TPU v7x, 32 devices: a whole 2x2x4 slice. The times are simulated.
32 devices in a mesh: dom: 8 (over y, x, core), feat: 4 (over z).
Axes of the slice: x: 2, y: 2, z: 4, core: 2. Of those that a mesh axis runs over, the one named last changes fastest.
Arguments:
- node_state: bfloat16 [49152, 128], P(('dom', 'feat')), may hold values from -6 to 6
- w_msg: bfloat16 [128, 128], replicated, may hold values from -0.5 to 0.5
- w_first: bfloat16 [256, 128], replicated, may hold values from -0.375 to 0.375
- b_first: float32 [128], replicated, may hold values from -3 to 3
- w_second: bfloat16 [128, 128], replicated, may hold values from -0.5 to 0.5
- b_second: float32 [128], replicated, may hold values from -3 to 3
- ln_gain: float32 [128], replicated, may hold values from 0.5 to 1.5
- col_index: int32 [384, 4], P(('dom', 'feat')), may hold values from 0 to 383, as said below
- edge_counts: int32 [384, 4, 128, 128], P(('dom', 'feat')), may hold values from 0 to 3, as said below
- cotangent: bfloat16 [49152, 128], P(('dom', 'feat')), may hold values from -14 to 14
Outputs:
- updated: bfloat16 [49152, 128], P(('dom', 'feat'))
- grad_state: bfloat16 [49152, 128], P(('dom', 'feat'))
- grad_w_msg: float32 [128, 128], replicated
- grad_w_first: float32 [256, 128], replicated
- grad_b_first: float32 [128], replicated
- grad_w_second: float32 [128, 128], replicated
- grad_b_second: float32 [128], replicated
- grad_gain: float32 [128], replicated
Inputs may be any that keep to these rules, and one draw needn't show every extreme that they name: `col_index`: tile 0 of block row b is block b itself; every other tile's column lies within 2 blocks of b, reflected at the two ends of the curve; columns of one block row may repeat. `edge_counts`: most entries are zero.
All inputs are finite; a program needn't handle non-finite values.
Results may differ from a plain program's by a relative error of at most 0.0093.
Values may be sent and summed in bfloat16 or wider, within the bound.
No kernel may reach another device: no remote copies, remote signals or barrier semaphores. Data moves between devices by JAX's collectives and lax.ppermute only.
A program may use at most 64 MiB of HBM per device.

v0:
```python
import math

import jax
import jax.numpy as jnp
from jax import lax
from jax.sharding import PartitionSpec as P

WIN = 2


epsilon = 1e-05


def with_halo(cells, sides, width):
    for axis, dim in sides:
        count = lax.axis_size(axis)
        ends = count - 1
        head = lax.slice_in_dim(cells, 0, width, axis=dim)
        tail = lax.slice_in_dim(cells, cells.shape[dim] - width, cells.shape[dim], axis=dim)
        cells = jnp.concatenate(
            [
                lax.ppermute(tail, axis, [(i, (i + 1) % count) for i in range(ends)]),
                cells,
                lax.ppermute(head, axis, [((i + 1) % count, i) for i in range(ends)]),
            ],
            axis=dim,
        )
    return cells


def passed_along(block, axis, distance):
    devices = range(lax.axis_size(axis))
    route = [(i - distance, i) for i in devices if i - distance in devices]
    return lax.ppermute(block, axis, route)


def inner_rows(left, right):
    return lax.dot_general(
        left, right, (((0,), (0,)), ((), ())), preferred_element_type=jnp.float32
    )


def times_transposed(left, right):
    return lax.dot_general(
        left, right, (((1,), (1,)), ((), ())), preferred_element_type=jnp.float32
    )


def shards(
    node_state,
    w_msg,
    w_first,
    b_first,
    w_second,
    b_second,
    ln_gain,
    col_index,
    edge_counts,
    cotangent,
):
    node_rows, features = node_state.shape
    block_count, tile_count, block_size, _ = edge_counts.shape
    span_blocks = WIN
    devices = lax.axis_size("dom") * lax.axis_size("feat")
    grad_scale = 1.0 / math.sqrt(node_rows * devices)
    messages = jnp.dot(node_state, w_msg, preferred_element_type=jnp.float32).astype(jnp.bfloat16)
    extended = with_halo(messages, ((("dom", "feat"), 0),), span_blocks * block_size)
    ext_blocks = extended.reshape(block_count + 2 * span_blocks, block_size, features)
    first_block = lax.axis_index(("dom", "feat")) * block_count
    local_col = col_index - first_block + span_blocks
    gathered = ext_blocks[local_col]
    tile_weights = edge_counts.astype(jnp.bfloat16)
    aggregate = jnp.einsum(
        "btij,btjh->bih", tile_weights, gathered, preferred_element_type=jnp.float32
    )
    aggregate = aggregate.reshape(node_rows, features).astype(jnp.bfloat16)
    joined = jnp.concatenate([node_state, aggregate], axis=1)
    pre_hidden = jnp.dot(joined, w_first, preferred_element_type=jnp.float32) + b_first
    activated = jax.nn.silu(pre_hidden).astype(jnp.bfloat16)
    pre_norm = jnp.dot(activated, w_second, preferred_element_type=jnp.float32) + b_second
    row_mean = jnp.mean(pre_norm, axis=-1, keepdims=True)
    centred = pre_norm - row_mean
    inv_std = lax.rsqrt(jnp.mean(centred * centred, axis=-1, keepdims=True) + epsilon)
    normed = centred * inv_std
    updated = (node_state.astype(jnp.float32) + ln_gain * normed).astype(jnp.bfloat16)
    cot_f32 = cotangent.astype(jnp.float32)
    d_normed = cot_f32 * ln_gain
    d_pre_norm = (
        inv_std
        * (
            d_normed
            - jnp.mean(d_normed, axis=-1, keepdims=True)
            - normed * jnp.mean(d_normed * normed, axis=-1, keepdims=True)
        )
    ).astype(jnp.bfloat16)
    sigmoid_z = jax.nn.sigmoid(pre_hidden)
    d_pre_hidden = (
        times_transposed(d_pre_norm, w_second) * sigmoid_z * (1.0 + pre_hidden * (1.0 - sigmoid_z))
    ).astype(jnp.bfloat16)
    d_joined = times_transposed(d_pre_hidden, w_first)
    d_aggregate = (
        d_joined[:, features:].astype(jnp.bfloat16).reshape(block_count, block_size, features)
    )
    contribution = jnp.einsum(
        "btij,bih->btjh", tile_weights, d_aggregate, preferred_element_type=jnp.float32
    )
    slot_ids = jnp.arange(block_count + 2 * span_blocks, dtype=jnp.int32)
    one_hot = (local_col[:, :, None] == slot_ids[None, None, :]).astype(jnp.float32)
    ext_grad = jnp.einsum("btc,btjh->cjh", one_hot, contribution, precision=lax.Precision.HIGHEST)
    lower_part = ext_grad[:span_blocks]
    upper_part = ext_grad[block_count + span_blocks :]
    own_part = ext_grad[span_blocks : block_count + span_blocks]
    from_below = passed_along(upper_part.astype(jnp.bfloat16), ("dom", "feat"), 1).astype(
        upper_part.dtype
    )
    from_above = passed_along(lower_part.astype(jnp.bfloat16), ("dom", "feat"), -1).astype(
        lower_part.dtype
    )
    summed_grad = own_part.at[:span_blocks].add(from_below)
    summed_grad = summed_grad.at[block_count - span_blocks :].add(from_above)
    d_messages = summed_grad.reshape(node_rows, features).astype(jnp.bfloat16)
    grad_state = (cot_f32 + d_joined[:, :features] + times_transposed(d_messages, w_msg)).astype(
        jnp.bfloat16
    )
    terms = (
        inner_rows(node_state, d_messages) * grad_scale,
        inner_rows(joined, d_pre_hidden) * grad_scale,
        jnp.sum(d_pre_hidden, axis=0, dtype=jnp.float32) * grad_scale,
        inner_rows(activated, d_pre_norm) * grad_scale,
        jnp.sum(d_pre_norm, axis=0, dtype=jnp.float32) * grad_scale,
        jnp.sum(cot_f32 * normed, axis=0) * grad_scale,
    )
    totals = lax.psum((terms[0], terms[1], terms[2], terms[3], terms[4], terms[5]), ("dom", "feat"))
    return (updated, grad_state, totals[0], totals[1], totals[2], totals[3], totals[4], totals[5])


def solution(mesh):
    return jax.shard_map(
        shards,
        mesh=mesh,
        in_specs=(
            P(("dom", "feat"), None),
            P(),
            P(),
            P(),
            P(),
            P(),
            P(),
            P(("dom", "feat"), None),
            P(("dom", "feat"), None, None, None),
            P(("dom", "feat"), None),
        ),
        out_specs=(
            P(("dom", "feat"), None),
            P(("dom", "feat"), None),
            P(),
            P(),
            P(),
            P(),
            P(),
            P(),
        ),
        check_vma=False,
    )
```

profile of v0, /device:TPU:0, one launch (start us, length us, event | category | flops | bytes accessed | tf_op | source)
XLA Modules:
  0.0 235.1 jit_solution(18420462372009894152)
XLA Ops:
  7.2 1.3 convolution_convert_fusion
  8.6 4.9 %collective-permute-start = (bf16[256,128]{1,0:T(8,128)(2,1)S(1)}, bf16[256,128]{1,0:T(8,128)(2,1)S(1)}, u32[]{:S(2)}, u32[]{:S(2)}) collective-permute-start(bf16[256,128]{1,0:T(8,128)(2,1)S(1)} %get-tuple-element.70), channel_id=1, source_target_pairs={{0,1},{1,2},{2,3},{3,4},{4,5},{5,6},{6,7},{7,8},{8,9},{9,10},{10,1... | collective-permute-start | bytes 196616 | tf_op jit(solution)/shard_map/ppermute | solution.py:22
  13.5 1.3 collective-permute-start.1
  14.8 1.9 copy.35
  16.9 0.9 copy.37
  17.9 2.0 collective-permute-done.1
  19.9 0.8 pad_maximum_fusion.1
  20.7 3.1 %gather_fusion = bf16[48,128,128]{2,1,0:T(8,128)(2,1)} fusion(bf16[16,128,128]{2,1,0:T(8,128)(2,1)} %bitcast.45, s32[1024]{0:T(1024)S(1)} %pad_clamp_fusion), kind=kCustom, calls=%fused_computation | custom fusion | bytes 3145920 | tf_op jit(solution)/shard_map/gather | solution.py:71
  23.9 2.0 fusion.3
  25.9 0.4 multiply_convert_fusion
  27.7 1.2 convert_reduce_fusion
  28.9 0.9 convolution_multiply_fusion.2
  29.8 0.5 convert_reduce_fusion.1
  30.3 1.1 convolution_multiply_fusion.1
  31.8 1.1 copy-done.5
  32.9 0.6 convolution_bitcast_fusion
  33.5 3.5 %copy.40 = f32[12,4,128,128]{3,0,1,2:T(8,128)} copy(f32[12,4,128,128]{2,3,1,0:T(8,128)S(1)} %convolution_bitcast_fusion) | data formatting | bytes 6291456 | tf_op jit(solution)/shard_map/btij,bih->btjh/dot_general | solution.py:104
  37.0 4.3 %convolution_bitcast_fusion.1 = f32[16,128,128]{2,0,1:T(8,128)S(1)} fusion(f32[12,4,128,128]{3,0,1,2:T(8,128)} %copy.40, s32[12,4]{0,1:T(4,128)S(1)} %get-tuple-element.72), kind=kOutput, calls=%fused_computation.10 | convolution fusion | flops 150995712 | bytes 4194496 | tf_op jit(solution)/shard_map/btc,btjh->cjh/dot_general | solution.py:109
  41.6 0.7 fusion.23
  42.3 3.9 %collective-permute-start.2 = (bf16[2,128,128]{2,1,0:T(8,128)(2,1)}, bf16[2,128,128]{2,1,0:T(8,128)(2,1)}, u32[]{:S(2)}, u32[]{:S(2)}) collective-permute-start(bf16[2,128,128]{2,1,0:T(8,128)(2,1)} %get-tuple-element.69), channel_id=1, source_target_pairs={{0,1},{1,2},{2,3},{3,4},{4,5},{5,6},{6,7},{7,8},{8,9},{9,10},{10,1... | collective-permute-start | bytes 196616 | tf_op jit(solution)/shard_map/ppermute | solution.py:34
  46.6 0.7 copy-done.9
  47.2 0.9 copy.45
  48.4 1.4 collective-permute-start.3
  49.9 42.8 %all-reduce = (f32[128]{0:T(128)}, f32[128]{0:T(128)}, f32[128]{0:T(128)}) all-reduce(f32[128]{0:T(128)S(1)} %broadcast_multiply_fusion.5, f32[128]{0:T(128)S(1)} %broadcast_multiply_fusion.4, f32[128]{0:T(128)S(1)} %broadcast_multiply_fusion.3), channel_id=1, replica_groups=mesh['dom'=8,'feat'=4] {'dom','feat'}, use_global_device_ids=true, to_apply=%region_7.8 | all-reduce | flops 384 | bytes 3072 | tf_op jit(solution)/shard_map/psum | solution.py:133
  92.7 0.9 fusion.16
  93.6 0.9 fusion.15
  94.6 0.9 fusion.4
  95.8 0.9 copy.46
  96.7 126.9 %all-reduce.4.cloned.1.call-done = (f32[128,128]{0,1:T(8,128)}, f32[256,128]{1,0:T(8,128)}, f32[128,128]{1,0:T(8,128)}) async-done(((f32[128,128]{0,1:T(8,128)}, f32[256,128]{1,0:T(8,128)}, f32[128,128]{1,0:T(8,128)}), (f32[128,128]{0,1:T(8,128)}, f32[256,128]{1,0:T(8,128)}, f32[128,128]{1,0:T(8,128)})) %all-reduce.4.cloned.1.call-update) | async-done | bytes 262160 | tf_op jit(solution)/shard_map/psum | solution.py:133
  223.6 1.6 copy.47
  225.2 1.6 copy.62
  226.8 1.5 copy.63
  (61 shorter events, 3.4 us)
Async XLA Ops:
  7.2 18.7 %copy-start = (bf16[256,128]{1,0:T(8,128)(2,1)S(1)}, bf16[256,128]{1,0:T(8,128)(2,1)}, u32[]{:S(2)}) copy-start(bf16[256,128]{1,0:T(8,128)(2,1)} %param.16) | copy-start | bytes 196612
  7.2 9.6 %copy-start.14 = (s32[12,4]{0,1:T(4,128)S(1)}, s32[12,4]{0,1:T(4,128)}, u32[]{:S(2)}) copy-start(s32[12,4]{0,1:T(4,128)} %param.21) | copy-start | bytes 580
  7.2 9.7 %copy-start.10 = (bf16[1536,128]{1,0:T(8,128)(2,1)S(1)}, bf16[1536,128]{1,0:T(8,128)(2,1)}, u32[]{:S(2)}) copy-start(bf16[1536,128]{1,0:T(8,128)(2,1)} %param.23) | copy-start | bytes 1179652
  7.2 216.4 %all-reduce.4.cloned.1.call-start = ((), (), s32[]{:S(2)}) async-start(), calls=%async_computation | async-start | bytes 524288 | tf_op jit(solution)/shard_map/psum | solution.py:133
  8.6 9.3 %collective-permute-start = (bf16[256,128]{1,0:T(8,128)(2,1)S(1)}, bf16[256,128]{1,0:T(8,128)(2,1)S(1)}, u32[]{:S(2)}, u32[]{:S(2)}) collective-permute-start(bf16[256,128]{1,0:T(8,128)(2,1)S(1)} %get-tuple-element.70), channel_id=1, source_target_pairs={{0,1},{1,2},{2,3},{3,4},{4,5},{5,6},{6,7},{7,8},{8,9},{9,10},{10,1... | collective-permute-start | bytes 196616 | tf_op jit(solution)/shard_map/ppermute | solution.py:22
  13.5 6.4 %collective-permute-start.1 = (bf16[256,128]{1,0:T(8,128)(2,1)S(1)}, bf16[256,128]{1,0:T(8,128)(2,1)S(1)}, u32[]{:S(2)}, u32[]{:S(2)}) collective-permute-start(bf16[256,128]{1,0:T(8,128)(2,1)S(1)} %get-tuple-element.71), channel_id=1, source_target_pairs={{1,0},{2,1},{3,2},{4,3},{5,4},{6,5},{7,6},{8,7},{9,8},{10,9},{11,1... | collective-permute-start | bytes 196616 | tf_op jit(solution)/shard_map/ppermute | solution.py:24
  20.7 3.1 %copy-start.1 = (s32[12,4,128,128]{3,2,1,0:T(8,128)S(1)}, s32[12,4,128,128]{3,2,1,0:T(8,128)}, u32[]{:S(2)}) copy-start(s32[12,4,128,128]{3,2,1,0:T(8,128)} %param.22) | copy-start | bytes 9437188
  23.9 2.0 copy-start.6
  23.9 2.0 copy-start.16
  25.9 0.8 copy-start.12
  25.9 0.8 copy-start.15
  26.3 1.0 copy-start.3
  26.3 1.0 copy-start.13
  26.7 1.0 copy-start.8
  30.2 2.6 %copy-start.2 = (s32[12,4,128,128]{3,2,1,0:T(8,128)S(1)}, s32[12,4,128,128]{3,2,1,0:T(8,128)}, u32[]{:S(2)}) copy-start(s32[12,4,128,128]{3,2,1,0:T(8,128)} %param.22) | copy-start | bytes 9437188
  31.7 1.2 copy-start.5
  42.3 50.4 %collective-permute-start.2 = (bf16[2,128,128]{2,1,0:T(8,128)(2,1)}, bf16[2,128,128]{2,1,0:T(8,128)(2,1)}, u32[]{:S(2)}, u32[]{:S(2)}) collective-permute-start(bf16[2,128,128]{2,1,0:T(8,128)(2,1)} %get-tuple-element.69), channel_id=1, source_target_pairs={{0,1},{1,2},{2,3},{3,4},{4,5},{5,6},{6,7},{7,8},{8,9},{9,10},{10,1... | collective-permute-start | bytes 196616 | tf_op jit(solution)/shard_map/ppermute | solution.py:34
  46.2 1.0 copy-start.9
  46.2 1.9 slice-start
  48.4 46.2 %copy-start.7 = (bf16[1536,128]{1,0:T(8,128)(2,1)S(1)}, bf16[1536,128]{1,0:T(8,128)(2,1)}, u32[]{:S(2)}) copy-start(bf16[1536,128]{1,0:T(8,128)(2,1)} %param.14) | copy-start | bytes 1179652
  48.4 45.2 %collective-permute-start.3 = (bf16[2,128,128]{2,1,0:T(8,128)(2,1)}, bf16[2,128,128]{2,1,0:T(8,128)(2,1)}, u32[]{:S(2)}, u32[]{:S(2)}) collective-permute-start(bf16[2,128,128]{2,1,0:T(8,128)(2,1)} %get-tuple-element.68), channel_id=1, source_target_pairs={{1,0},{2,1},{3,2},{4,3},{5,4},{6,5},{7,6},{8,7},{9,8},{10,9},{11,1... | collective-permute-start | bytes 196616 | tf_op jit(solution)/shard_map/ppermute | solution.py:34
  49.9 45.6 %copy-start.4 = (bf16[1536,128]{0,1:T(8,128)(2,1)S(1)}, bf16[1536,128]{0,1:T(8,128)(2,1)}, u32[]{:S(2)}) copy-start(bf16[1536,128]{0,1:T(8,128)(2,1)} %copy.37) | copy-start | bytes 1179652
  49.9 45.6 %copy-start.11 = (bf16[128,128]{1,0:T(8,128)(2,1)S(1)}, bf16[128,128]{1,0:T(8,128)(2,1)}, u32[]{:S(2)}) copy-start(bf16[128,128]{1,0:T(8,128)(2,1)} %param.15) | copy-start | bytes 98308
Sparse Core Ops, SparseCore 0:
  95.6 127.9 all-reduce.3
where the time goes:
time: 236 us; the launch traced here: 235 us
  waiting for transfers between devices  129 us (55%)
  blocking collectives  42.8 us (18%)
  local copies, waits for them, and re-layouts  20.1 us (9%)
  between operations  14.4 us (6%)
  matrix products  13 us (6%)
  starting transfers between devices  11.6 us (5%)
  other arithmetic  4.26 us (2%)
    psum x1, waiting for transfers between devices, shards(): lax.psum((terms[0], terms[1], terms[2], terms[3], terms[4], terms[5]), ('...  127 us
    psum x1, blocking collectives, shards(): lax.psum((terms[0], terms[1], terms[2], terms[3], terms[4], terms[5]), ('...  42.8 us
    unnamed x42, local copies, waits for them, and re-layouts  11.9 us
    ppermute x2, starting transfers between devices, passed_along(): return lax.ppermute(block, axis, route)  5.32 us
    ppermute x1, starting transfers between devices, with_halo(): lax.ppermute(tail, axis, [(i, (i + 1) % count) for i in range(ends)])  4.92 us
  transfers between devices with their start and end apart: 5, of which 2 were waited for; matrix products, arithmetic and copies ran while one was open for 3% of the time, Pallas kernels for 0%

commit v1 on v0

--- a/solution.py
+++ b/solution.py
@@ -44,6 +44,24 @@
     return lax.dot_general(
         left, right, (((1,), (1,)), ((), ())), preferred_element_type=jnp.float32
     )
+
+
+def summed_over_devices(terms, axes):
+    devices = lax.axis_size(axes)
+    sizes = [math.prod(term.shape) for term in terms]
+    total = sum(sizes)
+    rows = -(-total // (devices * 128))
+    flat = jnp.concatenate([term.reshape(-1) for term in terms])
+    flat = jnp.pad(flat, (0, rows * devices * 128 - total))
+    parts = lax.all_to_all(flat.reshape(devices, rows, 128), axes, 0, 0, tiled=True)
+    own = jnp.sum(parts, axis=0)
+    spread = jnp.broadcast_to(own[None], (devices, rows, 128))
+    whole = lax.all_to_all(spread, axes, 0, 0, tiled=True).reshape(-1)
+    results, start = [], 0
+    for term, size in zip(terms, sizes):
+        results.append(whole[start : start + size].reshape(term.shape))
+        start += size
+    return results
 
 
 def shards(
@@ -130,7 +148,7 @@
         jnp.sum(d_pre_norm, axis=0, dtype=jnp.float32) * grad_scale,
         jnp.sum(cot_f32 * normed, axis=0) * grad_scale,
     )
-    totals = lax.psum((terms[0], terms[1], terms[2], terms[3], terms[4], terms[5]), ("dom", "feat"))
+    totals = summed_over_devices(terms, ("dom", "feat"))
     return (updated, grad_state, totals[0], totals[1], totals[2], totals[3], totals[4], totals[5])
 
 

time: 236 us -> 86.6 us (0.37)
  waiting for transfers between devices: 129 us -> 16.4 us
  blocking collectives: 42.8 us -> 21.2 us
  between operations: 14.4 us -> 1.16 us
  starting transfers between devices: 11.6 us -> 14.8 us
    psum x1 -> x0, waiting for transfers between devices: 127 us -> none  [shards(): lax.psum((terms[0], terms[1], terms[2], terms[3], terms[4], terms[5]), ('...]
    psum x1 -> x0, blocking collectives: 42.8 us -> none  [shards(): lax.psum((terms[0], terms[1], terms[2], terms[3], terms[4], terms[5]), ('...]
    all_to_all x0 -> x1, blocking collectives: none -> 21.2 us  [summed_over_devices(): lax.all_to_all(flat.reshape(devices, rows, 128), axes, 0, 0, tiled=True)]
    all_to_all x0 -> x1, waiting for transfers between devices: none -> 9.39 us  [summed_over_devices(): whole = lax.all_to_all(spread, axes, 0, 0, tiled=True).reshape(-1)]
    ppermute x2, waiting for transfers between devices: 0.01 us -> 5 us  [passed_along(): return lax.ppermute(block, axis, route)]
    unnamed x42 -> x57, local copies, waits for them, and re-layouts: 11.9 us -> 7.79 us
    all_to_all x0 -> x1, starting transfers between devices: none -> 3.86 us  [summed_over_devices(): whole = lax.all_to_all(spread, axes, 0, 0, tiled=True).reshape(-1)]
  transfers between devices with their start and end apart: 5 -> 5, of which waited for: 2 -> 3; matrix products, arithmetic and copies ran while one was open for 3% -> 7% of each run, Pallas kernels for 0% -> 0%
where the time goes in v1:
time: 86.6 us; the launch traced here: 85.4 us
  blocking collectives  21.2 us (24%)
  local copies, waits for them, and re-layouts  18.2 us (21%)
  waiting for transfers between devices  16.4 us (19%)
  starting transfers between devices  14.8 us (17%)
  matrix products  11 us (13%)
  other arithmetic  2.66 us (3%)
  between operations  1.16 us (1%)
    all_to_all x1, blocking collectives, summed_over_devices(): lax.all_to_all(flat.reshape(devices, rows, 128), axes, 0, 0, tiled=True)  21.2 us
    all_to_all x1, waiting for transfers between devices, summed_over_devices(): whole = lax.all_to_all(spread, axes, 0, 0, tiled=True).reshape(-1)  9.39 us
    unnamed x57, local copies, waits for them, and re-layouts  7.79 us
    ppermute x2, waiting for transfers between devices, passed_along(): return lax.ppermute(block, axis, route)  5 us
    ppermute x1, starting transfers between devices, with_halo(): lax.ppermute(tail, axis, [(i, (i + 1) % count) for i in range(ends)])  4.93 us
    ppermute x2, starting transfers between devices, passed_along(): return lax.ppermute(block, axis, route)  4.7 us
    dot_general x1, matrix products, shards(): jnp.einsum('btc,btjh->cjh', one_hot, contribution, precision=lax.Precisio...  4.34 us
    all_to_all x1, starting transfers between devices, summed_over_devices(): whole = lax.all_to_all(spread, axes, 0, 0, tiled=True).reshape(-1)  3.86 us
  transfers between devices with their start and end apart: 5, of which 3 were waited for; matrix products, arithmetic and copies ran while one was open for 7% of the time, Pallas kernels for 0%

profile of v1, /device:TPU:0, one launch (start us, length us, event | category | flops | bytes accessed | tf_op | source)
XLA Modules:
  0.0 85.4 jit_solution(3886874901326124177)
XLA Ops:
  0.7 1.3 %convolution_convert_fusion = bf16[1536,128]{1,0:T(8,128)(2,1)S(1)} fusion(bf16[1536,128]{1,0:T(8,128)(2,1)} %param.14, bf16[128,128]{1,0:T(8,128)(2,1)} %param.15), kind=kOutput, calls=%fused_computation.8 | convolution fusion | flops 50528256 | bytes 819200 | tf_op jit(solution)/shard_map/dot_general | solution.py:84
  2.0 4.9 %collective-permute-start = (bf16[256,128]{1,0:T(8,128)(2,1)S(1)}, bf16[256,128]{1,0:T(8,128)(2,1)S(1)}, u32[]{:S(2)}, u32[]{:S(2)}) collective-permute-start(bf16[256,128]{1,0:T(8,128)(2,1)S(1)} %get-tuple-element.64), channel_id=1, source_target_pairs={{0,1},{1,2},{2,3},{3,4},{4,5},{5,6},{6,7},{7,8},{8,9},{9,10},{10,1... | collective-permute-start | bytes 196616 | tf_op jit(solution)/shard_map/ppermute | solution.py:22
  6.9 1.3 %collective-permute-start.1 = (bf16[256,128]{1,0:T(8,128)(2,1)S(1)}, bf16[256,128]{1,0:T(8,128)(2,1)S(1)}, u32[]{:S(2)}, u32[]{:S(2)}) collective-permute-start(bf16[256,128]{1,0:T(8,128)(2,1)S(1)} %get-tuple-element.65), channel_id=1, source_target_pairs={{1,0},{2,1},{3,2},{4,3},{5,4},{6,5},{7,6},{8,7},{9,8},{10,9},{11,1... | collective-permute-start | bytes 196616 | tf_op jit(solution)/shard_map/ppermute | solution.py:24
  8.2 1.9 %copy.34 = bf16[1536,128]{0,1:T(8,128)(2,1)} copy(bf16[1536,128]{1,0:T(8,128)(2,1)} %param.14) | data formatting | bytes 786432 | tf_op args[0]
  10.3 0.9 %copy.36 = bf16[1536,128]{0,1:T(8,128)(2,1)} copy(bf16[1536,128]{1,0:T(8,128)(2,1)S(1)} %copy-done.16) | data formatting | bytes 786432 | tf_op args[9]
  11.3 2.0 %collective-permute-done.1 = bf16[256,128]{1,0:T(8,128)(2,1)S(1)} collective-permute-done((bf16[256,128]{1,0:T(8,128)(2,1)S(1)}, bf16[256,128]{1,0:T(8,128)(2,1)S(1)}, u32[]{:S(2)}, u32[]{:S(2)}) %collective-permute-start.1) | collective-permute-done | bytes 65568 | tf_op jit(solution)/shard_map/ppermute | solution.py:24
  13.3 0.9 %pad_maximum_fusion.1 = bf16[2048,128]{1,0:T(8,128)(2,1)} fusion(bf16[256,128]{1,0:T(8,128)(2,1)S(1)} %collective-permute-done.1, bf16[1536,128]{1,0:T(8,128)(2,1)S(1)} %convolution_convert_fusion, bf16[256,128]{1,0:T(8,128)(2,1)S(1)} %collective-permute-done), kind=kLoop, calls=%fused_computation.42 | loop fusion | flops 1572864 | bytes 1048576 | tf_op jit(solution)/shard_map/concatenate | solution.py:20
  14.2 3.2 %gather_fusion = bf16[48,128,128]{2,1,0:T(8,128)(2,1)} fusion(bf16[16,128,128]{2,1,0:T(8,128)(2,1)} %bitcast.53, s32[1024]{0:T(1024)S(1)} %pad_clamp_fusion), kind=kCustom, calls=%fused_computation | custom fusion | bytes 3145920 | tf_op jit(solution)/shard_map/gather | solution.py:89
  17.3 2.0 %fusion.3 = bf16[12,128,128]{1,2,0:T(8,128)(2,1)S(1)} fusion(bf16[12,4,128,128]{3,2,1,0:T(8,128)(2,1)} %bitcast.54, s32[12,4,128,128]{3,2,1,0:T(8,128)S(1)} %copy-done.1), kind=kOutput, calls=%fused_computation.12 | convolution fusion | flops 202309632 | bytes 5111808 | tf_op jit(solution)/shard_map/btij,btjh->bih/dot_general | solution.py:91
  19.4 0.4 multiply_convert_fusion
  20.1 0.8 copy-done.8
  21.3 0.4 fusion.15
  21.9 1.1 %convert_reduce_fusion = (f32[128]{0:T(128)S(1)}, bf16[1536,128]{0,1:T(8,128)(2,1)S(1)}, bf16[1536,128]{0,1:T(8,128)(2,1)}) fusion(f32[1536]{0:T(1024)S(1)} %get-tuple-element.79, f32[1536,128]{0,1:T(8,128)S(1)} %get-tuple-element.76, f32[1536]{0:T(1024)S(1)} %broadcast_multiply_fusion.2, f32[1536]{0:T(1024)S(1)} %get-tuple-element.80, ...), kind=kLoop, calls=%fused_computation.33 | loop fusion | flops 2948992 | bytes 2384896 | tf_op jit(solution)/shard_map/reduce_sum | solution.py:148
  23.0 0.5 convert_reduce_fusion.1
  23.8 0.4 fusion.31
  24.6 0.8 copy-done.5
  25.4 0.6 convolution_bitcast_fusion
  26.0 3.4 %copy.39 = f32[12,4,128,128]{3,0,1,2:T(8,128)} copy(f32[12,4,128,128]{2,3,1,0:T(8,128)S(1)} %convolution_bitcast_fusion) | data formatting | bytes 6291456 | tf_op jit(solution)/shard_map/btij,bih->btjh/dot_general | solution.py:122
  29.5 4.3 %convolution_bitcast_fusion.1 = f32[16,128,128]{2,0,1:T(8,128)S(1)} fusion(f32[12,4,128,128]{3,0,1,2:T(8,128)} %copy.39, s32[12,4]{0,1:T(4,128)S(1)} %get-tuple-element.71), kind=kOutput, calls=%fused_computation.10 | convolution fusion | flops 150995712 | bytes 4194496 | tf_op jit(solution)/shard_map/btc,btjh->cjh/dot_general | solution.py:127
  34.2 3.3 %collective-permute-start.2 = (bf16[2,128,128]{2,1,0:T(8,128)(2,1)S(1)}, bf16[2,128,128]{2,1,0:T(8,128)(2,1)S(1)}, u32[]{:S(2)}, u32[]{:S(2)}) collective-permute-start(bf16[2,128,128]{2,1,0:T(8,128)(2,1)S(1)} %get-tuple-element.63), channel_id=1, source_target_pairs={{0,1},{1,2},{2,3},{3,4},{4,5},{5,6},{6,7},{7,8},{8,9},{9,10},{10,1... | collective-permute-start | bytes 196616 | tf_op jit(solution)/shard_map/ppermute | solution.py:34
  38.2 1.4 %collective-permute-start.3 = (bf16[2,128,128]{2,1,0:T(8,128)(2,1)S(1)}, bf16[2,128,128]{2,1,0:T(8,128)(2,1)S(1)}, u32[]{:S(2)}, u32[]{:S(2)}) collective-permute-start(bf16[2,128,128]{2,1,0:T(8,128)(2,1)S(1)} %get-tuple-element.62), channel_id=1, source_target_pairs={{1,0},{2,1},{3,2},{4,3},{5,4},{6,5},{7,6},{8,7},{9,8},{10,9},{11,1... | collective-permute-start | bytes 196616 | tf_op jit(solution)/shard_map/ppermute | solution.py:34
  39.7 5.0 %collective-permute-done.3 = bf16[2,128,128]{2,1,0:T(8,128)(2,1)S(1)} collective-permute-done((bf16[2,128,128]{2,1,0:T(8,128)(2,1)S(1)}, bf16[2,128,128]{2,1,0:T(8,128)(2,1)S(1)}, u32[]{:S(2)}, u32[]{:S(2)}) %collective-permute-start.3) | collective-permute-done | bytes 65568 | tf_op jit(solution)/shard_map/ppermute | solution.py:34
  45.3 0.4 fusion.5
  45.8 21.2 %all_to_all.10 = f32[32,17,128]{2,1,0:T(8,128)S(1)} all-to-all(f32[32,17,128]{2,1,0:T(8,128)S(1)} %reshape.140), channel_id=1, replica_groups=mesh['dom'=8,'feat'=4] {'dom','feat'}, dimensions={0} | all-to-all | bytes 557056 | tf_op jit(solution)/shard_map/all_to_all | solution.py:56
  67.0 0.8 broadcast_in_dim.5
  67.8 3.9 %all-to-all-start.1 = ((f32[32,17,128]{2,1,0:T(8,128)}), f32[32,17,128]{2,1,0:T(8,128)S(1)}, u32[]{:S(2)}, u32[]{:S(2)}) async-start(f32[32,17,128]{2,1,0:T(8,128)} %broadcast_in_dim.5), calls=%async_computation.1 | async-start | bytes 786432 | tf_op jit(solution)/shard_map/all_to_all | solution.py:59
  71.7 0.9 %copy.45 = bf16[1536,128]{1,0:T(8,128)(2,1)} copy(bf16[1536,128]{0,1:T(8,128)(2,1)S(1)} %copy-done.10) | data formatting | bytes 786432
  73.2 0.9 %copy.46 = bf16[1536,128]{1,0:T(8,128)(2,1)} copy(bf16[1536,128]{0,1:T(8,128)(2,1)S(1)} %fusion.2) | data formatting | bytes 786432
  74.1 9.4 %all-to-all-done.1 = f32[32,17,128]{2,1,0:T(8,128)S(1)} async-done(((f32[32,17,128]{2,1,0:T(8,128)}), f32[32,17,128]{2,1,0:T(8,128)S(1)}, u32[]{:S(2)}, u32[]{:S(2)}) %all-to-all-start.1) | async-done | bytes 278560 | tf_op jit(solution)/shard_map/all_to_all | solution.py:59
  83.6 0.7 slice.124
  84.2 0.7 fusion.29
  84.9 0.5 fusion.28
  (85 shorter events, 4.2 us)
Async XLA Ops:
  0.6 18.7 %copy-start = (bf16[256,128]{1,0:T(8,128)(2,1)S(1)}, bf16[256,128]{1,0:T(8,128)(2,1)}, u32[]{:S(2)}) copy-start(bf16[256,128]{1,0:T(8,128)(2,1)} %param.16) | copy-start | bytes 196612
  0.6 9.5 %copy-start.22 = (s32[12,4]{0,1:T(4,128)S(1)}, s32[12,4]{0,1:T(4,128)}, u32[]{:S(2)}) copy-start(s32[12,4]{0,1:T(4,128)} %param.21) | copy-start | bytes 580
  0.7 9.7 %copy-start.16 = (bf16[1536,128]{1,0:T(8,128)(2,1)S(1)}, bf16[1536,128]{1,0:T(8,128)(2,1)}, u32[]{:S(2)}) copy-start(bf16[1536,128]{1,0:T(8,128)(2,1)} %param.23) | copy-start | bytes 1179652
  2.0 9.3 %collective-permute-start = (bf16[256,128]{1,0:T(8,128)(2,1)S(1)}, bf16[256,128]{1,0:T(8,128)(2,1)S(1)}, u32[]{:S(2)}, u32[]{:S(2)}) collective-permute-start(bf16[256,128]{1,0:T(8,128)(2,1)S(1)} %get-tuple-element.64), channel_id=1, source_target_pairs={{0,1},{1,2},{2,3},{3,4},{4,5},{5,6},{6,7},{7,8},{8,9},{9,10},{10,1... | collective-permute-start | bytes 196616 | tf_op jit(solution)/shard_map/ppermute | solution.py:22
  6.9 6.4 %collective-permute-start.1 = (bf16[256,128]{1,0:T(8,128)(2,1)S(1)}, bf16[256,128]{1,0:T(8,128)(2,1)S(1)}, u32[]{:S(2)}, u32[]{:S(2)}) collective-permute-start(bf16[256,128]{1,0:T(8,128)(2,1)S(1)} %get-tuple-element.65), channel_id=1, source_target_pairs={{1,0},{2,1},{3,2},{4,3},{5,4},{6,5},{7,6},{8,7},{9,8},{10,9},{11,1... | collective-permute-start | bytes 196616 | tf_op jit(solution)/shard_map/ppermute | solution.py:24
  14.1 3.2 %copy-start.1 = (s32[12,4,128,128]{3,2,1,0:T(8,128)S(1)}, s32[12,4,128,128]{3,2,1,0:T(8,128)}, u32[]{:S(2)}) copy-start(s32[12,4,128,128]{3,2,1,0:T(8,128)} %param.22) | copy-start | bytes 9437188
  17.3 2.0 %copy-start.6 = (bf16[1536,128]{1,0:T(8,128)(2,1)S(1)}, bf16[1536,128]{1,0:T(8,128)(2,1)}, u32[]{:S(2)}) copy-start(bf16[1536,128]{1,0:T(8,128)(2,1)} %param.14) | copy-start | bytes 1179652
  17.3 2.1 %copy-start.24 = (f32[128]{0:T(128)S(1)}, f32[128]{0:T(128)}, u32[]{:S(2)}) copy-start(f32[128]{0:T(128)} %param.17) | copy-start | bytes 1540
  19.3 0.7 copy-start.14
  19.4 1.5 %copy-start.20 = (bf16[128,128]{1,0:T(8,128)(2,1)S(1)}, bf16[128,128]{1,0:T(8,128)(2,1)}, u32[]{:S(2)}) copy-start(bf16[128,128]{1,0:T(8,128)(2,1)} %param.18) | copy-start | bytes 98308
  19.4 1.5 %copy-start.23 = (f32[128]{0:T(128)S(1)}, f32[128]{0:T(128)}, u32[]{:S(2)}) copy-start(f32[128]{0:T(128)} %param.19) | copy-start | bytes 1540
  20.1 0.8 copy-start.8
  20.1 1.2 %copy-start.3 = (bf16[1536,128]{0,1:T(8,128)(2,1)S(1)}, bf16[1536,128]{0,1:T(8,128)(2,1)}, u32[]{:S(2)}) copy-start(bf16[1536,128]{0,1:T(8,128)(2,1)} %copy.36) | copy-start | bytes 1179652
  20.1 1.2 %copy-start.21 = (f32[128]{0:T(128)S(1)}, f32[128]{0:T(128)}, u32[]{:S(2)}) copy-start(f32[128]{0:T(128)} %param.20) | copy-start | bytes 1540
  20.9 1.0 %copy-start.11 = (bf16[1536,128]{0,1:T(8,128)(2,1)S(1)}, bf16[1536,128]{0,1:T(8,128)(2,1)}, u32[]{:S(2)}) copy-start(bf16[1536,128]{0,1:T(8,128)(2,1)} %copy.34) | copy-start | bytes 1179652
  23.0 0.8 copy-start.12
  23.0 2.4 %copy-start.2 = (s32[12,4,128,128]{3,2,1,0:T(8,128)S(1)}, s32[12,4,128,128]{3,2,1,0:T(8,128)}, u32[]{:S(2)}) copy-start(s32[12,4,128,128]{3,2,1,0:T(8,128)} %param.22) | copy-start | bytes 9437188
  23.8 0.8 copy-start.17
  24.2 1.2 %copy-start.5 = (f32[1536,256]{1,0:T(8,128)}, f32[1536,256]{1,0:T(8,128)S(1)}, u32[]{:S(2)}) copy-start(f32[1536,256]{1,0:T(8,128)S(1)} %fusion.31) | copy-start | bytes 4718596
  33.8 3.7 %copy-start.9 = (bf16[1536,128]{1,0:T(8,128)(2,1)S(1)}, bf16[1536,128]{1,0:T(8,128)(2,1)}, u32[]{:S(2)}) copy-start(bf16[1536,128]{1,0:T(8,128)(2,1)} %copy-done.8) | copy-start | bytes 1179652
  33.8 3.7 %copy-start.13 = (bf16[1536,128]{0,1:T(8,128)(2,1)S(1)}, bf16[1536,128]{0,1:T(8,128)(2,1)}, u32[]{:S(2)}) copy-start(bf16[1536,128]{0,1:T(8,128)(2,1)} %copy-done.12) | copy-start | bytes 1179652
  34.2 5.5 %collective-permute-start.2 = (bf16[2,128,128]{2,1,0:T(8,128)(2,1)S(1)}, bf16[2,128,128]{2,1,0:T(8,128)(2,1)S(1)}, u32[]{:S(2)}, u32[]{:S(2)}) collective-permute-start(bf16[2,128,128]{2,1,0:T(8,128)(2,1)S(1)} %get-tuple-element.63), channel_id=1, source_target_pairs={{0,1},{1,2},{2,3},{3,4},{4,5},{5,6},{6,7},{7,8},{8,9},{9,10},{10,1... | collective-permute-start | bytes 196616 | tf_op jit(solution)/shard_map/ppermute | solution.py:34
  38.2 6.7 %copy-start.7 = (bf16[1536,128]{1,0:T(8,128)(2,1)S(1)}, bf16[1536,128]{1,0:T(8,128)(2,1)}, u32[]{:S(2)}) copy-start(bf16[1536,128]{1,0:T(8,128)(2,1)} %param.14) | copy-start | bytes 1179652
  38.2 6.5 %collective-permute-start.3 = (bf16[2,128,128]{2,1,0:T(8,128)(2,1)S(1)}, bf16[2,128,128]{2,1,0:T(8,128)(2,1)S(1)}, u32[]{:S(2)}, u32[]{:S(2)}) collective-permute-start(bf16[2,128,128]{2,1,0:T(8,128)(2,1)S(1)} %get-tuple-element.62), channel_id=1, source_target_pairs={{1,0},{2,1},{3,2},{4,3},{5,4},{6,5},{7,6},{8,7},{9,8},{10,9},{11,1... | collective-permute-start | bytes 196616 | tf_op jit(solution)/shard_map/ppermute | solution.py:34
  39.7 5.6 %copy-start.15 = (bf16[12,128,128]{1,2,0:T(8,128)(2,1)S(1)}, bf16[12,128,128]{1,2,0:T(8,128)(2,1)}, u32[]{:S(2)}) copy-start(bf16[12,128,128]{1,2,0:T(8,128)(2,1)} %copy-done.14) | copy-start | bytes 1179652
  39.7 5.6 %copy-start.18 = (bf16[1536,128]{1,0:T(8,128)(2,1)S(1)}, bf16[1536,128]{1,0:T(8,128)(2,1)}, u32[]{:S(2)}) copy-start(bf16[1536,128]{1,0:T(8,128)(2,1)} %copy-done.17) | copy-start | bytes 1179652
  67.0 4.7 %copy-start.10 = (bf16[1536,128]{0,1:T(8,128)(2,1)S(1)}, bf16[1536,128]{0,1:T(8,128)(2,1)}, u32[]{:S(2)}) copy-start(bf16[1536,128]{0,1:T(8,128)(2,1)} %get-tuple-element.61) | copy-start | bytes 1179652
  67.8 4.8 %slice-start = ((f32[1536,256]{1,0:T(8,128)}), f32[1536,128]{1,0:T(8,128)S(1)}, s32[]{:S(2)}) async-start(f32[1536,256]{1,0:T(8,128)} %copy-done.5), calls=%async_computation.2 | async-start | bytes 1572864 | tf_op jit(solution)/shard_map/slice | solution.py:140
  67.8 15.7 %all-to-all-start.1 = ((f32[32,17,128]{2,1,0:T(8,128)}), f32[32,17,128]{2,1,0:T(8,128)S(1)}, u32[]{:S(2)}, u32[]{:S(2)}) async-start(f32[32,17,128]{2,1,0:T(8,128)} %broadcast_in_dim.5), calls=%async_computation.1 | async-start | bytes 786432 | tf_op jit(solution)/shard_map/all_to_all | solution.py:59
  71.7 1.2 %copy-start.4 = (bf16[1536,128]{0,1:T(8,128)(2,1)S(1)}, bf16[1536,128]{0,1:T(8,128)(2,1)}, u32[]{:S(2)}) copy-start(bf16[1536,128]{0,1:T(8,128)(2,1)} %copy.36) | copy-start | bytes 1179652
  71.7 1.2 %copy-start.19 = (bf16[128,128]{1,0:T(8,128)(2,1)S(1)}, bf16[128,128]{1,0:T(8,128)(2,1)}, u32[]{:S(2)}) copy-start(bf16[128,128]{1,0:T(8,128)(2,1)} %param.15) | copy-start | bytes 98308

commit v2 on v0

v2 whole, which is shorter than its diff:
```python
import functools
import math

import jax
import jax.numpy as jnp
from jax import lax
from jax.experimental import pallas as pl
from jax.experimental.pallas import tpu as pltpu
from jax.sharding import PartitionSpec as P

WIN = 2
epsilon = 1e-05
AXES = ("dom", "feat")
SENT = jnp.bfloat16
BIAS_ROWS = 16


def dot(left, right):
    return jnp.dot(left, right, preferred_element_type=jnp.float32)


def dot_nt(left, right):
    return lax.dot_general(
        left, right, (((1,), (1,)), ((), ())), preferred_element_type=jnp.float32
    )


def column(row_ref, width):
    features = row_ref.shape[1]
    return jnp.broadcast_to(row_ref[...], (width, features)).T


def layer_kernel(
    grad_scale,
    chunk,
    col_ref,
    state_ref,
    below_ref,
    above_ref,
    cot_ref,
    counts_ref,
    w_msg_ref,
    w_first_ref,
    b_first_ref,
    w_second_ref,
    b_second_ref,
    gain_ref,
    updated_ref,
    grad_state_ref,
    grads_ref,
    to_below_ref,
    to_above_ref,
    edge_msg_ref,
    edge_state_ref,
    states,
    messages,
    counts,
    ext_grad,
    direct,
    joined,
    d_hidden,
    active,
    d_norm,
):
    blocks, tiles, size, _ = counts_ref.shape
    features = state_ref.shape[1]
    ext = blocks + 2 * WIN
    group = 2
    width = group * size

    w_msg = w_msg_ref[...]
    w_msg_t = w_msg.T
    w_first = w_first_ref[...]
    w_first_t = jnp.concatenate([w_first[:features].T, w_first[features:].T], axis=1)
    w_second = w_second_ref[...]
    w_second_t = w_second.T
    b_first = column(b_first_ref, width)
    b_second = column(b_second_ref, width)
    gain = column(gain_ref, width)

    for slot in range(ext):
        if slot < WIN:
            block = below_ref[pl.ds(slot * size, size), :]
        elif slot < blocks + WIN:
            block = state_ref[pl.ds((slot - WIN) * size, size), :]
        else:
            block = above_ref[pl.ds((slot - WIN - blocks) * size, size), :]
        state_t = block.T
        states[:, pl.ds(slot * size, size)] = state_t
        messages[slot] = dot(w_msg_t, state_t).astype(jnp.bfloat16)
    ext_grad[...] = jnp.zeros_like(ext_grad)
    joined[pl.ds(2 * features, BIAS_ROWS), :] = jnp.ones((BIAS_ROWS, blocks * size), jnp.bfloat16)
    active[pl.ds(features, BIAS_ROWS), :] = jnp.ones((BIAS_ROWS, blocks * size), jnp.bfloat16)

    gain_terms = jnp.zeros((features, size), jnp.float32)
    for first in range(0, blocks, group):
        rows = range(first, first + group)
        place = pl.ds(first * size, width)
        slots = {}
        parts = []
        for b in rows:
            own = col_ref[b, 0]
            slots[b] = [b + WIN] + [col_ref[b, t] - own + (b + WIN) for t in range(1, tiles)]
            tile_row = jnp.concatenate(
                [counts_ref[b, t].astype(jnp.float32).astype(jnp.bfloat16) for t in range(tiles)],
                axis=1,
            )
            counts[b] = tile_row
            picked = jnp.concatenate([messages[slot] for slot in slots[b]], axis=1)
            parts.append(dot_nt(picked, tile_row).astype(jnp.bfloat16))
        state_t = states[:, pl.ds((first + WIN) * size, width)]
        joined_t = jnp.concatenate([state_t, jnp.concatenate(parts, axis=1)], axis=0)
        joined[pl.ds(0, 2 * features), place] = joined_t
        pre_hidden = dot(w_first_t, joined_t) + b_first
        sigmoid = 1.0 / (1.0 + jnp.exp(-pre_hidden))
        active_t = (pre_hidden * sigmoid).astype(jnp.bfloat16)
        active[pl.ds(0, features), place] = active_t
        slope = sigmoid * (1.0 + pre_hidden * (1.0 - sigmoid))
        pre_norm = dot(w_second_t, active_t) + b_second
        centred = pre_norm - jnp.mean(pre_norm, axis=0, keepdims=True)
        inv_std = lax.rsqrt(jnp.mean(centred * centred, axis=0, keepdims=True) + epsilon)
        normed = centred * inv_std
        updated_t = (state_t.astype(jnp.float32) + gain * normed).astype(jnp.bfloat16)
        cot_t = jnp.concatenate(
            [cot_ref[pl.ds(b * size, size), :].T for b in rows], axis=1
        ).astype(jnp.float32)
        terms = cot_t * normed
        q = cot_t * gain
        mean_q = jnp.mean(q, axis=0, keepdims=True)
        mean_qn = jnp.mean(q * normed, axis=0, keepdims=True)
        d_norm_t = (inv_std * (q - mean_q - normed * mean_qn)).astype(jnp.bfloat16)
        d_norm[:, place] = d_norm_t
        d_hidden_t = (dot(w_second, d_norm_t) * slope).astype(jnp.bfloat16)
        d_hidden[:, place] = d_hidden_t
        d_joined = dot(w_first, d_hidden_t)
        direct[:, place] = cot_t + d_joined[:features]
        d_aggregate = d_joined[features:].astype(jnp.bfloat16)
        for k, b in enumerate(rows):
            lanes = slice(k * size, (k + 1) * size)
            updated_ref[pl.ds(b * size, size), :] = updated_t[:, lanes].T
            gain_terms = gain_terms + terms[:, lanes]
            owed = dot(d_aggregate[:, lanes], counts[b])
            for t, slot in enumerate(slots[b]):
                ext_grad[slot] += owed[:, t * size : (t + 1) * size]

    d_msg = [ext_grad[slot].astype(jnp.bfloat16) for slot in range(ext)]
    for k in range(WIN):
        to_below_ref[k] = d_msg[k]
        to_above_ref[k] = d_msg[blocks + WIN + k]
        for e, b in ((k, k), (WIN + k, blocks - WIN + k)):
            edge_msg_ref[e] = ext_grad[b + WIN]
            edge_state_ref[e] = direct[:, pl.ds(b * size, size)]
    for b in range(WIN, blocks - WIN):
        total = direct[:, pl.ds(b * size, size)] + dot(w_msg, d_msg[b + WIN])
        grad_state_ref[pl.ds(b * size, size), :] = total.astype(jnp.bfloat16).T

    sent = grads_ref.dtype
    first_sums = dot_nt(joined[...], d_hidden[...]) * grad_scale
    second_sums = dot_nt(active[...], d_norm[...]) * grad_scale
    msg_sums = dot_nt(states[...], jnp.concatenate(d_msg, axis=1)) * grad_scale
    gain_sum = jnp.sum(gain_terms.T, axis=0, keepdims=True) * grad_scale
    bias = jnp.concatenate(
        [
            first_sums[2 * features : 2 * features + 1],
            second_sums[features : features + 1],
            gain_sum,
            jnp.zeros((BIAS_ROWS - 3, features), jnp.float32),
        ],
        axis=0,
    )
    sums = jnp.concatenate(
        [first_sums[: 2 * features], second_sums[:features], msg_sums], axis=0
    ).astype(sent)
    for k in range(grads_ref.shape[0]):
        have = max(0, min(chunk, sums.shape[0] - k * chunk))
        if have > 0:
            grads_ref[k, pl.ds(0, have), :] = sums[k * chunk : k * chunk + have]
        if have < chunk:
            grads_ref[k, pl.ds(have, chunk - have), :] = jnp.zeros((chunk - have, features), sent)
        tail = bias if k == 0 else jnp.zeros_like(bias)
        grads_ref[k, pl.ds(chunk, BIAS_ROWS), :] = tail.astype(sent)


def edge_kernel(
    grad_state_ref, msg_ref, state_ref, below_ref, above_ref, w_msg_ref, out_ref
):
    del grad_state_ref
    size = msg_ref.shape[2]
    side = pl.program_id(0)
    w_msg = w_msg_ref[...]
    for k in range(WIN):
        arrived = jnp.where(side == 0, below_ref[k], above_ref[k]).astype(jnp.float32)
        d_msg = (msg_ref[k] + arrived).astype(jnp.bfloat16)
        total = state_ref[k] + dot(w_msg, d_msg)
        out_ref[pl.ds(k * size, size), :] = total.astype(jnp.bfloat16).T


def sum_kernel(parts_ref, spread_ref):
    total = parts_ref[0].astype(jnp.float32)
    for k in range(1, parts_ref.shape[0]):
        total = total + parts_ref[k].astype(jnp.float32)
    total = total.astype(spread_ref.dtype)
    for k in range(spread_ref.shape[0]):
        spread_ref[k] = total


def unpack_kernel(chunk, parts_ref, msg_ref, first_ref, b_first_ref, second_ref, b_second_ref, gain_ref):
    place = 0
    for ref in (first_ref, second_ref, msg_ref):
        done = 0
        while done < ref.shape[0]:
            k, row = divmod(place, chunk)
            count = min(chunk - row, ref.shape[0] - done)
            ref[pl.ds(done, count), :] = parts_ref[k, pl.ds(row, count), :].astype(jnp.float32)
            done += count
            place += count
    bias = parts_ref[0, pl.ds(chunk, BIAS_ROWS), :].astype(jnp.float32)
    b_first_ref[...] = bias[0:1]
    b_second_ref[...] = bias[1:2]
    gain_ref[...] = bias[2:3]


def passed_along(block, distance):
    devices = range(lax.axis_size(AXES))
    route = [(i - distance, i) for i in devices if i - distance in devices]
    return lax.ppermute(block, AXES, route)


def in_vmem():
    return pl.BlockSpec(memory_space=pltpu.VMEM)


def shards(
    node_state,
    w_msg,
    w_first,
    b_first,
    w_second,
    b_second,
    ln_gain,
    col_index,
    edge_counts,
    cotangent,
):
    nodes, features = node_state.shape
    blocks, tiles, size, _ = edge_counts.shape
    ext = blocks + 2 * WIN
    devices = lax.axis_size(AXES)
    dom, feat = lax.axis_size("dom"), lax.axis_size("feat")
    grad_scale = 1.0 / math.sqrt(nodes * devices)
    chunk = -(-4 * features // (dom * 16)) * 16
    bf16, f32 = jnp.bfloat16, jnp.float32
    shape = jax.ShapeDtypeStruct

    from_below = passed_along(node_state[nodes - WIN * size :], 1)
    from_above = passed_along(node_state[: WIN * size], -1)
    row = lambda vector: vector.reshape(1, features)

    updated, grad_state, grads, to_below, to_above, edge_msg, edge_state = pl.pallas_call(
        functools.partial(layer_kernel, grad_scale, chunk),
        out_shape=(
            shape((nodes, features), bf16),
            shape((nodes, features), bf16),
            shape((dom, chunk + BIAS_ROWS, features), SENT),
            shape((WIN, features, size), bf16),
            shape((WIN, features, size), bf16),
            shape((2 * WIN, features, size), f32),
            shape((2 * WIN, features, size), f32),
        ),
        in_specs=[pl.BlockSpec(memory_space=pltpu.SMEM)] + [in_vmem()] * 11,
        out_specs=(in_vmem(),) * 7,
        scratch_shapes=[
            pltpu.VMEM((features, ext * size), bf16),
            pltpu.VMEM((ext, features, size), bf16),
            pltpu.VMEM((blocks, size, tiles * size), bf16),
            pltpu.VMEM((ext, features, size), f32),
            pltpu.VMEM((features, nodes), f32),
            pltpu.VMEM((2 * features + BIAS_ROWS, nodes), bf16),
            pltpu.VMEM((features, nodes), bf16),
            pltpu.VMEM((features + BIAS_ROWS, nodes), bf16),
            pltpu.VMEM((features, nodes), bf16),
        ],
        compiler_params=pltpu.CompilerParams(vmem_limit_bytes=32 * 1024 * 1024),
        cost_estimate=pl.CostEstimate(
            flops=1_000_000_000, bytes_accessed=5_000_000, transcendentals=200_000
        ),
        name="layer",
    )(
        col_index,
        node_state,
        from_below,
        from_above,
        cotangent,
        edge_counts,
        w_msg,
        w_first,
        row(b_first),
        w_second,
        row(b_second),
        row(ln_gain),
    )

    def summed(parts, count, name):
        return pl.pallas_call(
            sum_kernel,
            out_shape=shape((count,) + parts.shape[1:], parts.dtype),
            in_specs=[in_vmem()],
            out_specs=in_vmem(),
            name=name,
        )(parts)

    plane = lax.all_to_all(grads, "dom", 0, 0, tiled=True)
    owed_above = passed_along(to_above, 1)
    owed_below = passed_along(to_below, -1)
    line = lax.all_to_all(summed(plane, feat, "sum_dom"), "feat", 0, 0, tiled=True)

    edge_rows = WIN * size
    grad_state = pl.pallas_call(
        edge_kernel,
        grid=(2,),
        out_shape=shape((nodes, features), bf16),
        in_specs=[
            pl.BlockSpec(memory_space=pl.ANY),
            pl.BlockSpec((WIN, features, size), lambda side: (side, 0, 0)),
            pl.BlockSpec((WIN, features, size), lambda side: (side, 0, 0)),
            pl.BlockSpec((WIN, features, size), lambda side: (0, 0, 0)),
            pl.BlockSpec((WIN, features, size), lambda side: (0, 0, 0)),
            pl.BlockSpec((features, features), lambda side: (0, 0)),
        ],
        out_specs=pl.BlockSpec(
            (edge_rows, features), lambda side: (side * (nodes // edge_rows - 1), 0)
        ),
        input_output_aliases={0: 0},
        name="edge_state",
    )(grad_state, edge_msg, edge_state, owed_above, owed_below, w_msg)

    whole = lax.all_to_all(summed(line, dom, "sum_feat"), "dom", 0, 0, tiled=True)
    g_msg, g_first, g_b_first, g_second, g_b_second, g_gain = pl.pallas_call(
        functools.partial(unpack_kernel, chunk),
        out_shape=(
            shape((features, features), f32),
            shape((2 * features, features), f32),
            shape((1, features), f32),
            shape((features, features), f32),
            shape((1, features), f32),
            shape((1, features), f32),
        ),
        in_specs=[in_vmem()],
        out_specs=(in_vmem(),) * 6,
        name="unpack",
    )(whole)
    flat = lambda vector: vector.reshape(features)
    return (
        updated,
        grad_state,
        g_msg,
        g_first,
        flat(g_b_first),
        g_second,
        flat(g_b_second),
        flat(g_gain),
    )


def solution(mesh):
    split = P(AXES, None)
    return jax.shard_map(
        shards,
        mesh=mesh,
        in_specs=(split, P(), P(), P(), P(), P(), P(), split, P(AXES, None, None, None), split),
        out_specs=(split, split, P(), P(), P(), P(), P(), P()),
        check_vma=False,
    )
```

time: 236 us -> 78.8 us (0.33)
  the two profiles are of different devices: /device:TPU:0 before, /device:TPU:27 now
where the time goes in v2:
time: 78.8 us; the launch traced here: 77.8 us
  starting transfers between devices  22.6 us (29%)
  blocking collectives  18.5 us (23%)
  Pallas kernels  15.8 us (20%)
  local copies, waits for them, and re-layouts  12.5 us (16%)
  waiting for transfers between devices  7.77 us (10%)
    ppermute x4, starting transfers between devices, passed_along(): return lax.ppermute(block, AXES, route)  16.8 us
    unnamed x29, local copies, waits for them, and re-layouts  11.7 us
    all_to_all x1, blocking collectives, shards(): lax.all_to_all(summed(plane, feat, 'sum_dom'), 'feat', 0, 0, tiled=True)  11.3 us
    pallas_call x1, Pallas kernels, shards(): pl.pallas_call(functools.partial(layer_kernel, grad_scale, chunk), out_sh...  8.88 us
    ppermute x4, waiting for transfers between devices, passed_along(): return lax.ppermute(block, AXES, route)  7.77 us
    all_to_all x1, blocking collectives, shards(): plane = lax.all_to_all(grads, 'dom', 0, 0, tiled=True)  7.19 us
    all_to_all x1, starting transfers between devices, shards(): lax.all_to_all(summed(line, dom, 'sum_feat'), 'dom', 0, 0, tiled=True)  5.8 us
    pallas_call x2, Pallas kernels, summed(): pl.pallas_call(sum_kernel, out_shape=shape((count,) + parts.shape[1:], pa...  3.14 us
  transfers between devices with their start and end apart: 5, of which 2 were waited for; matrix products, arithmetic and copies ran while one was open for 1% of the time, Pallas kernels for 3%

profile of v2, /device:TPU:27, one launch (start us, length us, event | category | flops | bytes accessed | tf_op | source)
XLA Modules:
  0.0 77.8 jit_solution(7507595878582261508)
XLA Ops:
  0.6 0.9 %fusion = (bf16[256,128]{1,0:T(8,128)(2,1)S(1)}, bf16[256,128]{1,0:T(8,128)(2,1)S(1)}) fusion(bf16[1536,128]{1,0:T(8,128)(2,1)} %state_ref.1), kind=kLoop, calls=%fused_computation | loop fusion | bytes 262144 | tf_op jit(solution)/shard_map/slice | solution.py:256
  1.5 2.1 %collective-permute-start.1 = (bf16[256,128]{1,0:T(8,128)(2,1)S(1)}, bf16[256,128]{1,0:T(8,128)(2,1)S(1)}, u32[]{:S(2)}, u32[]{:S(2)}) collective-permute-start(bf16[256,128]{1,0:T(8,128)(2,1)S(1)} %get-tuple-element.34), channel_id=1, source_target_pairs={{1,0},{2,1},{3,2},{4,3},{5,4},{6,5},{7,6},{8,7},{9,8},{10,9},{11,1... | collective-permute-start | bytes 196616 | tf_op jit(solution)/shard_map/ppermute | solution.py:226
  3.6 7.1 %collective-permute-start = (bf16[256,128]{1,0:T(8,128)(2,1)S(1)}, bf16[256,128]{1,0:T(8,128)(2,1)S(1)}, u32[]{:S(2)}, u32[]{:S(2)}) collective-permute-start(bf16[256,128]{1,0:T(8,128)(2,1)S(1)} %get-tuple-element.35), channel_id=1, source_target_pairs={{0,1},{1,2},{2,3},{3,4},{4,5},{5,6},{6,7},{7,8},{8,9},{9,10},{10,1... | collective-permute-start | bytes 196616 | tf_op jit(solution)/shard_map/ppermute | solution.py:226
  10.7 0.8 copy.19.col_ref
  11.5 0.0 collective-permute-done.1.above_ref
  11.5 0.5 collective-permute-done.below_ref
  12.0 1.9 %copy-done = s32[12,4,128,128]{3,2,1,0:T(8,128)S(1)} copy-done((s32[12,4,128,128]{3,2,1,0:T(8,128)S(1)}, s32[12,4,128,128]{3,2,1,0:T(8,128)}, u32[]{:S(2)}) %copy-start) | copy-done | bytes 3145752
  13.9 1.0 %copy-done.1 = bf16[1536,128]{1,0:T(8,128)(2,1)S(1)} copy-done((bf16[1536,128]{1,0:T(8,128)(2,1)S(1)}, bf16[1536,128]{1,0:T(8,128)(2,1)}, u32[]{:S(2)}) %copy-start.1) | copy-done | bytes 393240
  14.9 1.0 %copy-done.2 = bf16[1536,128]{1,0:T(8,128)(2,1)S(1)} copy-done((bf16[1536,128]{1,0:T(8,128)(2,1)S(1)}, bf16[1536,128]{1,0:T(8,128)(2,1)}, u32[]{:S(2)}) %copy-start.2) | copy-done | bytes 393240
  15.9 0.8 copy-done.5
  16.6 0.8 %copy-done.6 = bf16[256,128]{1,0:T(8,128)(2,1)S(1)} copy-done((bf16[256,128]{1,0:T(8,128)(2,1)S(1)}, bf16[256,128]{1,0:T(8,128)(2,1)}, u32[]{:S(2)}) %copy-start.6) | copy-done | bytes 65560
  17.5 0.8 copy-done.7
  18.2 0.7 copy-done.8
  18.9 0.7 copy-done.9
  19.6 0.7 copy-done.10
  20.2 8.9 %layer.1 = (bf16[1536,128]{1,0:T(8,128)(2,1)}, bf16[1536,128]{1,0:T(8,128)(2,1)}, bf16[8,80,128]{2,1,0:T(8,128)(2,1)S(1)}, bf16[2,128,128]{2,1,0:T(8,128)(2,1)S(...) custom-call(s32[12,4]{1,0:T(8,128)S(1)} %copy.19.col_ref, ...), custom_call_target="tpu_custom_call" | custom-call | flops 1000000000 | bytes 5000000 | tf_op jit(solution)/shard_map/layer/pallas_call | solution.py:259
  29.1 0.7 copy-done.3
  29.8 0.7 copy-done.4
  30.5 7.2 %all_to_all.15.parts_ref = bf16[8,80,128]{2,1,0:T(8,128)(2,1)} all-to-all(bf16[8,80,128]{2,1,0:T(8,128)(2,1)S(1)} %get-tuple-element.27), channel_id=1, replica_groups=mesh['dom'=8,'feat'=4] {'dom'}, dimensions={0} | all-to-all | bytes 327680 | tf_op jit(solution)/shard_map/all_to_all | solution.py:312
  37.7 1.6 %sum_dom.1 = bf16[4,80,128]{2,1,0:T(8,128)(2,1)} custom-call(bf16[8,80,128]{2,1,0:T(8,128)(2,1)} %all_to_all.15.parts_ref), custom_call_target="tpu_custom_call" | custom-call | tf_op jit(solution)/shard_map/sum_dom/pallas_call | solution.py:304
  39.2 11.3 %all_to_all.16.parts_ref = bf16[4,80,128]{2,1,0:T(8,128)(2,1)} all-to-all(bf16[4,80,128]{2,1,0:T(8,128)(2,1)} %sum_dom.1), channel_id=1, replica_groups=mesh['dom'=8,'feat'=4] {'feat'}, dimensions={0} | all-to-all | bytes 163840 | tf_op jit(solution)/shard_map/all_to_all | solution.py:315
  50.6 1.6 %sum_feat.1 = bf16[8,80,128]{2,1,0:T(8,128)(2,1)} custom-call(bf16[4,80,128]{2,1,0:T(8,128)(2,1)} %all_to_all.16.parts_ref), custom_call_target="tpu_custom_call" | custom-call | tf_op jit(solution)/shard_map/sum_feat/pallas_call | solution.py:304
  52.1 5.8 %all-to-all-start.2 = ((bf16[8,80,128]{2,1,0:T(8,128)(2,1)}), bf16[8,80,128]{2,1,0:T(8,128)(2,1)S(1)}, u32[]{:S(2)}, u32[]{:S(2)}) async-start(bf16[8,80,128]{2,1,0:T(8,128)(2,1)} %sum_feat.1), calls=%async_computation.2 | async-start | bytes 327680 | tf_op jit(solution)/shard_map/all_to_all | solution.py:337
  57.9 5.7 %collective-permute-start.2 = (bf16[2,128,128]{2,1,0:T(8,128)(2,1)S(1)}, bf16[2,128,128]{2,1,0:T(8,128)(2,1)S(1)}, u32[]{:S(2)}, u32[]{:S(2)}) collective-permute-start(bf16[2,128,128]{2,1,0:T(8,128)(2,1)S(1)} %get-tuple-element.25), channel_id=1, source_target_pairs={{0,1},{1,2},{2,3},{3,4},{4,5},{5,6},{6,7},{7,8},{8,9},{9,10},{10,1... | collective-permute-start | bytes 196616 | tf_op jit(solution)/shard_map/ppermute | solution.py:226
  63.6 1.9 %collective-permute-start.3 = (bf16[2,128,128]{2,1,0:T(8,128)(2,1)S(1)}, bf16[2,128,128]{2,1,0:T(8,128)(2,1)S(1)}, u32[]{:S(2)}, u32[]{:S(2)}) collective-permute-start(bf16[2,128,128]{2,1,0:T(8,128)(2,1)S(1)} %get-tuple-element.26), channel_id=1, source_target_pairs={{1,0},{2,1},{3,2},{4,3},{5,4},{6,5},{7,6},{8,7},{9,8},{10,9},{11,1... | collective-permute-start | bytes 196616 | tf_op jit(solution)/shard_map/ppermute | solution.py:226
  65.6 0.0 collective-permute-done.2.below_ref
  65.6 0.0 copy-start.12
  65.6 7.2 %collective-permute-done.3.above_ref = bf16[2,128,128]{2,1,0:T(8,128)(2,1)S(1)} collective-permute-done((bf16[2,128,128]{2,1,0:T(8,128)(2,1)S(1)}, bf16[2,128,128]{2,1,0:T(8,128)(2,1)S(1)}, u32[]{:S(2)}, u32[]{:S(2)}) %collective-permute-start.3) | collective-permute-done | bytes 65568 | tf_op jit(solution)/shard_map/ppermute | solution.py:226
  72.8 0.6 copy-done.13
  73.4 2.1 %edge_state.1 = bf16[1536,128]{1,0:T(8,128)(2,1)} custom-call(bf16[1536,128]{1,0:T(8,128)(2,1)} %get-tuple-element.22.grad_state_ref, f32[4,128,128]{2,1,0:T(8,128)} %copy-done.3, f32[4,128,128]{2,1,0:T(8,128)} %copy-done.4, bf16[2,128,128]{2,1,0:T(8,128)(2,1)} %copy-done.12, bf16[2,128,128]{2,1,0:T(8,128)(2,1)} %copy-done.13, ...), custom_call_target="tpu_custom_call", output_to_operand_aliasing={{}: (0, {})} | custom-call | tf_op jit(solution)/shard_map/edge_state/pallas_call | solution.py:318
  75.6 0.7 copy-done.11
  76.2 1.6 %unpack.1 = (f32[128,128]{1,0:T(8,128)}, f32[256,128]{1,0:T(8,128)}, f32[1,128]{1,0:T(1,128)}, f32[128,128]{1,0:T(8,128)}, f32[1,128]{1,0:T(1,128)}, /*index=5*/f32[1,128]{1,0:T(1,128)}) custom-call(bf16[8,80,128]{2,1,0:T(8,128)(2,1)} %copy-done.11), custom_call_target="tpu_custom_call" | custom-call | tf_op jit(solution)/shard_map/unpack/pallas_call | solution.py:338
  (15 shorter events, 0.0 us)
Async XLA Ops:
  1.5 9.9 %collective-permute-start.1 = (bf16[256,128]{1,0:T(8,128)(2,1)S(1)}, bf16[256,128]{1,0:T(8,128)(2,1)S(1)}, u32[]{:S(2)}, u32[]{:S(2)}) collective-permute-start(bf16[256,128]{1,0:T(8,128)(2,1)S(1)} %get-tuple-element.34), channel_id=1, source_target_pairs={{1,0},{2,1},{3,2},{4,3},{5,4},{6,5},{7,6},{8,7},{9,8},{10,9},{11,1... | collective-permute-start | bytes 196616 | tf_op jit(solution)/shard_map/ppermute | solution.py:226
  3.6 8.4 %collective-permute-start = (bf16[256,128]{1,0:T(8,128)(2,1)S(1)}, bf16[256,128]{1,0:T(8,128)(2,1)S(1)}, u32[]{:S(2)}, u32[]{:S(2)}) collective-permute-start(bf16[256,128]{1,0:T(8,128)(2,1)S(1)} %get-tuple-element.35), channel_id=1, source_target_pairs={{0,1},{1,2},{2,3},{3,4},{4,5},{5,6},{6,7},{7,8},{8,9},{9,10},{10,1... | collective-permute-start | bytes 196616 | tf_op jit(solution)/shard_map/ppermute | solution.py:226
  12.0 1.9 %copy-start = (s32[12,4,128,128]{3,2,1,0:T(8,128)S(1)}, s32[12,4,128,128]{3,2,1,0:T(8,128)}, u32[]{:S(2)}) copy-start(s32[12,4,128,128]{3,2,1,0:T(8,128)} %counts_ref.1) | copy-start | bytes 9437188
  13.9 1.0 %copy-start.1 = (bf16[1536,128]{1,0:T(8,128)(2,1)S(1)}, bf16[1536,128]{1,0:T(8,128)(2,1)}, u32[]{:S(2)}) copy-start(bf16[1536,128]{1,0:T(8,128)(2,1)} %state_ref.1) | copy-start | bytes 1179652
  14.9 1.0 %copy-start.2 = (bf16[1536,128]{1,0:T(8,128)(2,1)S(1)}, bf16[1536,128]{1,0:T(8,128)(2,1)}, u32[]{:S(2)}) copy-start(bf16[1536,128]{1,0:T(8,128)(2,1)} %cot_ref.1) | copy-start | bytes 1179652
  15.9 0.8 copy-start.5
  16.6 0.8 %copy-start.6 = (bf16[256,128]{1,0:T(8,128)(2,1)S(1)}, bf16[256,128]{1,0:T(8,128)(2,1)}, u32[]{:S(2)}) copy-start(bf16[256,128]{1,0:T(8,128)(2,1)} %w_first_ref.1) | copy-start | bytes 196612
  17.5 0.8 copy-start.7
  18.2 0.7 copy-start.8
  18.9 0.7 copy-start.9
  19.6 0.7 copy-start.10
  29.1 0.7 copy-start.3
  29.8 0.7 copy-start.4
  52.1 23.4 %all-to-all-start.2 = ((bf16[8,80,128]{2,1,0:T(8,128)(2,1)}), bf16[8,80,128]{2,1,0:T(8,128)(2,1)S(1)}, u32[]{:S(2)}, u32[]{:S(2)}) async-start(bf16[8,80,128]{2,1,0:T(8,128)(2,1)} %sum_feat.1), calls=%async_computation.2 | async-start | bytes 327680 | tf_op jit(solution)/shard_map/all_to_all | solution.py:337
  57.9 7.6 %collective-permute-start.2 = (bf16[2,128,128]{2,1,0:T(8,128)(2,1)S(1)}, bf16[2,128,128]{2,1,0:T(8,128)(2,1)S(1)}, u32[]{:S(2)}, u32[]{:S(2)}) collective-permute-start(bf16[2,128,128]{2,1,0:T(8,128)(2,1)S(1)} %get-tuple-element.25), channel_id=1, source_target_pairs={{0,1},{1,2},{2,3},{3,4},{4,5},{5,6},{6,7},{7,8},{8,9},{9,10},{10,1... | collective-permute-start | bytes 196616 | tf_op jit(solution)/shard_map/ppermute | solution.py:226
  63.6 9.2 %collective-permute-start.3 = (bf16[2,128,128]{2,1,0:T(8,128)(2,1)S(1)}, bf16[2,128,128]{2,1,0:T(8,128)(2,1)S(1)}, u32[]{:S(2)}, u32[]{:S(2)}) collective-permute-start(bf16[2,128,128]{2,1,0:T(8,128)(2,1)S(1)} %get-tuple-element.26), channel_id=1, source_target_pairs={{1,0},{2,1},{3,2},{4,3},{5,4},{6,5},{7,6},{8,7},{9,8},{10,9},{11,1... | collective-permute-start | bytes 196616 | tf_op jit(solution)/shard_map/ppermute | solution.py:226
  65.6 7.2 %copy-start.12 = (bf16[2,128,128]{2,1,0:T(8,128)(2,1)}, bf16[2,128,128]{2,1,0:T(8,128)(2,1)S(1)}, u32[]{:S(2)}) copy-start(bf16[2,128,128]{2,1,0:T(8,128)(2,1)S(1)} %collective-permute-done.2.below_ref) | copy-start | bytes 196612
  72.8 0.6 copy-start.13
  75.6 0.7 copy-start.11

commit v3 on v2

--- a/solution.py
+++ b/solution.py
@@ -12,7 +12,8 @@
 epsilon = 1e-05
 AXES = ("dom", "feat")
 SENT = jnp.bfloat16
-BIAS_ROWS = 16
+ONES_ROWS = 16
+BIAS_ROWS = 8
 
 
 def dot(left, right):
@@ -33,10 +34,26 @@
 def layer_kernel(
     grad_scale,
     chunk,
-    col_ref,
+    place_ref,
+    got_even_ref,
+    got_odd_ref,
+    state_hbm,
+    cot_hbm,
+    counts_hbm,
+    w_msg_hbm,
+    w_first_hbm,
+    b_first_hbm,
+    w_second_hbm,
+    b_second_hbm,
+    gain_hbm,
+    updated_hbm,
+    grad_state_hbm,
+    grads_ref,
+    send_even_ref,
+    send_odd_ref,
+    edge_msg_ref,
+    edge_state_ref,
     state_ref,
-    below_ref,
-    above_ref,
     cot_ref,
     counts_ref,
     w_msg_ref,
@@ -47,11 +64,6 @@
     gain_ref,
     updated_ref,
     grad_state_ref,
-    grads_ref,
-    to_below_ref,
-    to_above_ref,
-    edge_msg_ref,
-    edge_state_ref,
     states,
     messages,
     counts,
@@ -61,12 +73,46 @@
     d_hidden,
     active,
     d_norm,
+    arrived,
+    left,
 ):
     blocks, tiles, size, _ = counts_ref.shape
     features = state_ref.shape[1]
     ext = blocks + 2 * WIN
     group = 2
     width = group * size
+
+    smalls = (
+        (w_msg_hbm, w_msg_ref),
+        (w_first_hbm, w_first_ref),
+        (b_first_hbm, b_first_ref),
+        (w_second_hbm, w_second_ref),
+        (b_second_hbm, b_second_ref),
+        (gain_hbm, gain_ref),
+    )
+    state_copy = pltpu.make_async_copy(state_hbm, state_ref, arrived.at[0])
+    cot_copy = pltpu.make_async_copy(cot_hbm, cot_ref, arrived.at[1])
+    small_copies = [
+        pltpu.make_async_copy(source, target, arrived.at[2 + k])
+        for k, (source, target) in enumerate(smalls)
+    ]
+    count_copies = [
+        pltpu.make_async_copy(
+            counts_hbm.at[pl.ds(b, group)],
+            counts_ref.at[pl.ds(b, group)],
+            arrived.at[2 + len(smalls) + b // group],
+        )
+        for b in range(0, blocks, group)
+    ]
+    for copy in [state_copy] + small_copies + count_copies[:1] + [cot_copy] + count_copies[1:]:
+        copy.start()
+    odd = place_ref[blocks * tiles] == 1
+    got_even, got_odd = got_even_ref[...], got_odd_ref[...]
+    below = jnp.where(odd, got_even, got_odd)
+    above = jnp.where(odd, got_odd, got_even)
+    state_copy.wait()
+    for copy in small_copies:
+        copy.wait()
 
     w_msg = w_msg_ref[...]
     w_msg_t = w_msg.T
@@ -80,27 +126,32 @@
 
     for slot in range(ext):
         if slot < WIN:
-            block = below_ref[pl.ds(slot * size, size), :]
+            block = below[slot * size : (slot + 1) * size]
         elif slot < blocks + WIN:
             block = state_ref[pl.ds((slot - WIN) * size, size), :]
         else:
-            block = above_ref[pl.ds((slot - WIN - blocks) * size, size), :]
+            block = above[(slot - WIN - blocks) * size : (slot - WIN - blocks + 1) * size]
         state_t = block.T
         states[:, pl.ds(slot * size, size)] = state_t
         messages[slot] = dot(w_msg_t, state_t).astype(jnp.bfloat16)
     ext_grad[...] = jnp.zeros_like(ext_grad)
-    joined[pl.ds(2 * features, BIAS_ROWS), :] = jnp.ones((BIAS_ROWS, blocks * size), jnp.bfloat16)
-    active[pl.ds(features, BIAS_ROWS), :] = jnp.ones((BIAS_ROWS, blocks * size), jnp.bfloat16)
+    joined[pl.ds(2 * features, ONES_ROWS), :] = jnp.ones((ONES_ROWS, blocks * size), jnp.bfloat16)
+    active[pl.ds(features, ONES_ROWS), :] = jnp.ones((ONES_ROWS, blocks * size), jnp.bfloat16)
 
     gain_terms = jnp.zeros((features, size), jnp.float32)
     for first in range(0, blocks, group):
         rows = range(first, first + group)
         place = pl.ds(first * size, width)
+        count_copies[first // group].wait()
+        if first == 0:
+            cot_copy.wait()
         slots = {}
         parts = []
         for b in rows:
-            own = col_ref[b, 0]
-            slots[b] = [b + WIN] + [col_ref[b, t] - own + (b + WIN) for t in range(1, tiles)]
+            own = place_ref[b * tiles]
+            slots[b] = [b + WIN] + [
+                place_ref[b * tiles + t] - own + (b + WIN) for t in range(1, tiles)
+            ]
             tile_row = jnp.concatenate(
                 [counts_ref[b, t].astype(jnp.float32).astype(jnp.bfloat16) for t in range(tiles)],
                 axis=1,
@@ -143,16 +194,24 @@
             for t, slot in enumerate(slots[b]):
                 ext_grad[slot] += owed[:, t * size : (t + 1) * size]
 
+    updated_copy = pltpu.make_async_copy(updated_ref, updated_hbm, left.at[0])
+    updated_copy.start()
     d_msg = [ext_grad[slot].astype(jnp.bfloat16) for slot in range(ext)]
     for k in range(WIN):
-        to_below_ref[k] = d_msg[k]
-        to_above_ref[k] = d_msg[blocks + WIN + k]
+        to_below, to_above = d_msg[k], d_msg[blocks + WIN + k]
+        send_even_ref[k] = jnp.where(odd, to_below, to_above)
+        send_odd_ref[k] = jnp.where(odd, to_above, to_below)
         for e, b in ((k, k), (WIN + k, blocks - WIN + k)):
             edge_msg_ref[e] = ext_grad[b + WIN]
             edge_state_ref[e] = direct[:, pl.ds(b * size, size)]
+    inner = pl.ds(WIN * size, (blocks - 2 * WIN) * size)
     for b in range(WIN, blocks - WIN):
         total = direct[:, pl.ds(b * size, size)] + dot(w_msg, d_msg[b + WIN])
         grad_state_ref[pl.ds(b * size, size), :] = total.astype(jnp.bfloat16).T
+    grad_state_copy = pltpu.make_async_copy(
+        grad_state_ref.at[inner], grad_state_hbm.at[inner], left.at[1]
+    )
+    grad_state_copy.start()
 
     sent = grads_ref.dtype
     first_sums = dot_nt(joined[...], d_hidden[...]) * grad_scale
@@ -171,37 +230,28 @@
     sums = jnp.concatenate(
         [first_sums[: 2 * features], second_sums[:features], msg_sums], axis=0
     ).astype(sent)
+    bias = bias.astype(sent)
+    nothing = jnp.zeros((chunk, features), sent)
     for k in range(grads_ref.shape[0]):
-        have = max(0, min(chunk, sums.shape[0] - k * chunk))
-        if have > 0:
-            grads_ref[k, pl.ds(0, have), :] = sums[k * chunk : k * chunk + have]
-        if have < chunk:
-            grads_ref[k, pl.ds(have, chunk - have), :] = jnp.zeros((chunk - have, features), sent)
-        tail = bias if k == 0 else jnp.zeros_like(bias)
-        grads_ref[k, pl.ds(chunk, BIAS_ROWS), :] = tail.astype(sent)
+        part = sums[k * chunk : (k + 1) * chunk] if k * chunk < sums.shape[0] else nothing
+        tail = bias if k == 0 else nothing[:BIAS_ROWS]
+        grads_ref[k] = jnp.concatenate([part, tail], axis=0)
+    updated_copy.wait()
+    grad_state_copy.wait()
 
 
 def edge_kernel(
-    grad_state_ref, msg_ref, state_ref, below_ref, above_ref, w_msg_ref, out_ref
+    odd_ref, grad_state_ref, msg_ref, state_ref, even_ref, odd_part_ref, w_msg_ref, out_ref
 ):
     del grad_state_ref
     size = msg_ref.shape[2]
-    side = pl.program_id(0)
+    from_odd_pair = (pl.program_id(0) == 0) != (odd_ref[0] == 1)
     w_msg = w_msg_ref[...]
     for k in range(WIN):
-        arrived = jnp.where(side == 0, below_ref[k], above_ref[k]).astype(jnp.float32)
+        arrived = jnp.where(from_odd_pair, odd_part_ref[k], even_ref[k]).astype(jnp.float32)
         d_msg = (msg_ref[k] + arrived).astype(jnp.bfloat16)
         total = state_ref[k] + dot(w_msg, d_msg)
         out_ref[pl.ds(k * size, size), :] = total.astype(jnp.bfloat16).T
-
-
-def sum_kernel(parts_ref, spread_ref):
-    total = parts_ref[0].astype(jnp.float32)
-    for k in range(1, parts_ref.shape[0]):
-        total = total + parts_ref[k].astype(jnp.float32)
-    total = total.astype(spread_ref.dtype)
-    for k in range(spread_ref.shape[0]):
-        spread_ref[k] = total
 
 
 def unpack_kernel(chunk, parts_ref, msg_ref, first_ref, b_first_ref, second_ref, b_second_ref, gain_ref):
@@ -220,10 +270,13 @@
     gain_ref[...] = bias[2:3]
 
 
-def passed_along(block, distance):
-    devices = range(lax.axis_size(AXES))
-    route = [(i - distance, i) for i in devices if i - distance in devices]
-    return lax.ppermute(block, AXES, route)
+def swapped(block, parity):
+    last = lax.axis_size(AXES) - 1
+    lower = range(parity, last, 2)
+    return lax.ppermute(block, AXES, [(i, i + 1) for i in lower] + [(i + 1, i) for i in lower])
+
+
+kept = pltpu.with_memory_space_constraint
 
 
 def in_vmem():
@@ -246,95 +299,110 @@
     blocks, tiles, size, _ = edge_counts.shape
     ext = blocks + 2 * WIN
     devices = lax.axis_size(AXES)
-    dom, feat = lax.axis_size("dom"), lax.axis_size("feat")
     grad_scale = 1.0 / math.sqrt(nodes * devices)
-    chunk = -(-4 * features // (dom * 16)) * 16
+    chunk = -(-4 * features // (devices * 8)) * 8
     bf16, f32 = jnp.bfloat16, jnp.float32
     shape = jax.ShapeDtypeStruct
-
-    from_below = passed_along(node_state[nodes - WIN * size :], 1)
-    from_above = passed_along(node_state[: WIN * size], -1)
+    in_hbm = pl.BlockSpec(memory_space=pltpu.HBM)
+    in_smem = pl.BlockSpec(memory_space=pltpu.SMEM)
+
+    edge_rows = WIN * size
+    odd = lax.axis_index(AXES) % 2
+    side = lambda upper: lax.dynamic_slice_in_dim(
+        node_state, upper * (nodes - edge_rows), edge_rows, 0
+    )
+    got_odd = swapped(side(odd), 1)
+    got_even = swapped(side(1 - odd), 0)
+    odd = odd.astype(jnp.int32).reshape(1)
+    place = jnp.concatenate([col_index.reshape(-1), odd])
     row = lambda vector: vector.reshape(1, features)
 
-    updated, grad_state, grads, to_below, to_above, edge_msg, edge_state = pl.pallas_call(
+    updated, grad_state, grads, send_even, send_odd, edge_msg, edge_state = pl.pallas_call(
         functools.partial(layer_kernel, grad_scale, chunk),
         out_shape=(
-            shape((nodes, features), bf16),
-            shape((nodes, features), bf16),
-            shape((dom, chunk + BIAS_ROWS, features), SENT),
-            shape((WIN, features, size), bf16),
-            shape((WIN, features, size), bf16),
-            shape((2 * WIN, features, size), f32),
-            shape((2 * WIN, features, size), f32),
+            pltpu.HBM((nodes, features), bf16),
+            pltpu.HBM((nodes, features), bf16),
+            pltpu.VMEM((devices, chunk + BIAS_ROWS, features), SENT),
+            pltpu.VMEM((WIN, features, size), bf16),
+            pltpu.VMEM((WIN, features, size), bf16),
+            pltpu.VMEM((2 * WIN, features, size), f32),
+            pltpu.VMEM((2 * WIN, features, size), f32),
         ),
-        in_specs=[pl.BlockSpec(memory_space=pltpu.SMEM)] + [in_vmem()] * 11,
-        out_specs=(in_vmem(),) * 7,
+        in_specs=[in_smem] + [in_vmem()] * 2 + [in_hbm] * 9,
+        out_specs=(in_hbm,) * 2 + (in_vmem(),) * 5,
         scratch_shapes=[
+            pltpu.VMEM((nodes, features), bf16),
+            pltpu.VMEM((nodes, features), bf16),
+            pltpu.VMEM(edge_counts.shape, jnp.int32),
+            pltpu.VMEM((features, features), bf16),
+            pltpu.VMEM((2 * features, features), bf16),
+            pltpu.VMEM((1, features), f32),
+            pltpu.VMEM((features, features), bf16),
+            pltpu.VMEM((1, features), f32),
+            pltpu.VMEM((1, features), f32),
+            pltpu.VMEM((nodes, features), bf16),
+            pltpu.VMEM((nodes, features), bf16),
             pltpu.VMEM((features, ext * size), bf16),
             pltpu.VMEM((ext, features, size), bf16),
             pltpu.VMEM((blocks, size, tiles * size), bf16),
             pltpu.VMEM((ext, features, size), f32),
             pltpu.VMEM((features, nodes), f32),
-            pltpu.VMEM((2 * features + BIAS_ROWS, nodes), bf16),
+            pltpu.VMEM((2 * features + ONES_ROWS, nodes), bf16),
             pltpu.VMEM((features, nodes), bf16),
-            pltpu.VMEM((features + BIAS_ROWS, nodes), bf16),
+            pltpu.VMEM((features + ONES_ROWS, nodes), bf16),
             pltpu.VMEM((features, nodes), bf16),
+            pltpu.SemaphoreType.DMA((8 + blocks // 2,)),
+            pltpu.SemaphoreType.DMA((2,)),
         ],
-        compiler_params=pltpu.CompilerParams(vmem_limit_bytes=32 * 1024 * 1024),
+        compiler_params=pltpu.CompilerParams(vmem_limit_bytes=24 * 1024 * 1024),
         cost_estimate=pl.CostEstimate(
             flops=1_000_000_000, bytes_accessed=5_000_000, transcendentals=200_000
         ),
         name="layer",
     )(
-        col_index,
-        node_state,
-        from_below,
-        from_above,
-        cotangent,
-        edge_counts,
-        w_msg,
-        w_first,
-        row(b_first),
-        w_second,
-        row(b_second),
-        row(ln_gain),
-    )
-
-    def summed(parts, count, name):
-        return pl.pallas_call(
-            sum_kernel,
-            out_shape=shape((count,) + parts.shape[1:], parts.dtype),
-            in_specs=[in_vmem()],
-            out_specs=in_vmem(),
-            name=name,
-        )(parts)
-
-    plane = lax.all_to_all(grads, "dom", 0, 0, tiled=True)
-    owed_above = passed_along(to_above, 1)
-    owed_below = passed_along(to_below, -1)
-    line = lax.all_to_all(summed(plane, feat, "sum_dom"), "feat", 0, 0, tiled=True)
-
-    edge_rows = WIN * size
+        place,
+        kept(got_even, pltpu.VMEM),
+        kept(got_odd, pltpu.VMEM),
+        kept(node_state, pltpu.HBM),
+        kept(cotangent, pltpu.HBM),
+        kept(edge_counts, pltpu.HBM),
+        kept(w_msg, pltpu.HBM),
+        kept(w_first, pltpu.HBM),
+        kept(row(b_first), pltpu.HBM),
+        kept(w_second, pltpu.HBM),
+        kept(row(b_second), pltpu.HBM),
+        kept(row(ln_gain), pltpu.HBM),
+    )
+
+    parts = lax.all_to_all(grads, AXES, 0, 0, tiled=True)
+    owed_odd = swapped(send_odd, 1)
+    owed_even = swapped(send_even, 0)
+    own_sum = jnp.sum(parts.astype(f32), axis=0)
+    own_sum, owed_odd, owed_even = lax.optimization_barrier((own_sum, owed_odd, owed_even))
+    spread = jnp.broadcast_to(own_sum.astype(SENT)[None], parts.shape)
+
+    whole_block = lambda k: (0, 0, 0)
     grad_state = pl.pallas_call(
         edge_kernel,
         grid=(2,),
         out_shape=shape((nodes, features), bf16),
         in_specs=[
+            in_smem,
             pl.BlockSpec(memory_space=pl.ANY),
-            pl.BlockSpec((WIN, features, size), lambda side: (side, 0, 0)),
-            pl.BlockSpec((WIN, features, size), lambda side: (side, 0, 0)),
-            pl.BlockSpec((WIN, features, size), lambda side: (0, 0, 0)),
-            pl.BlockSpec((WIN, features, size), lambda side: (0, 0, 0)),
-            pl.BlockSpec((features, features), lambda side: (0, 0)),
+            pl.BlockSpec((WIN, features, size), lambda k: (k, 0, 0)),
+            pl.BlockSpec((WIN, features, size), lambda k: (k, 0, 0)),
+            pl.BlockSpec((WIN, features, size), whole_block),
+            pl.BlockSpec((WIN, features, size), whole_block),
+            pl.BlockSpec((features, features), lambda k: (0, 0)),
         ],
         out_specs=pl.BlockSpec(
-            (edge_rows, features), lambda side: (side * (nodes // edge_rows - 1), 0)
+            (edge_rows, features), lambda k: (k * (nodes // edge_rows - 1), 0)
         ),
-        input_output_aliases={0: 0},
+        input_output_aliases={1: 0},
         name="edge_state",
-    )(grad_state, edge_msg, edge_state, owed_above, owed_below, w_msg)
-
-    whole = lax.all_to_all(summed(line, dom, "sum_feat"), "dom", 0, 0, tiled=True)
+    )(odd, grad_state, edge_msg, edge_state, owed_even, owed_odd, w_msg)
+
+    whole = lax.all_to_all(spread, AXES, 0, 0, tiled=True)
     g_msg, g_first, g_b_first, g_second, g_b_second, g_gain = pl.pallas_call(
         functools.partial(unpack_kernel, chunk),
         out_shape=(

time: 78.8 us -> 56.7 us (0.72)
  the two profiles are of different devices: /device:TPU:27 before, /device:TPU:0 now
where the time goes in v3:
time: 56.7 us; the launch traced here: 56.3 us
  starting transfers between devices  21.5 us (38%)
  Pallas kernels  15.3 us (27%)
  waiting for transfers between devices  14.1 us (25%)
  local copies, waits for them, and re-layouts  4.52 us (8%)
  between operations  0.76 us (1%)
    ppermute x4, starting transfers between devices, swapped(): lax.ppermute(block, AXES, [(i, i + 1) for i in lower] + [(i + 1, i) for i...  11.8 us
    pallas_call x1, Pallas kernels, shards(): pl.pallas_call(functools.partial(layer_kernel, grad_scale, chunk), out_sh...  11.5 us
    all_to_all x1, waiting for transfers between devices, shards(): whole = lax.all_to_all(spread, AXES, 0, 0, tiled=True)  7.19 us
    all_to_all x1, starting transfers between devices, shards(): parts = lax.all_to_all(grads, AXES, 0, 0, tiled=True)  5.2 us
    all_to_all x1, starting transfers between devices, shards(): whole = lax.all_to_all(spread, AXES, 0, 0, tiled=True)  4.55 us
    all_to_all x1, waiting for transfers between devices, shards(): parts = lax.all_to_all(grads, AXES, 0, 0, tiled=True)  4.19 us
    unnamed x11, local copies, waits for them, and re-layouts  2.85 us
    ppermute x4, waiting for transfers between devices, swapped(): lax.ppermute(block, AXES, [(i, i + 1) for i in lower] + [(i + 1, i) for i...  2.77 us
  transfers between devices with their start and end apart: 6, of which 3 were waited for; matrix products, arithmetic and copies ran while one was open for 2% of the time, Pallas kernels for 4%

profile of v3, /device:TPU:0, one launch (start us, length us, event | category | flops | bytes accessed | tf_op | source)
XLA Modules:
  0.0 56.3 jit_solution(16307285544475618798)
XLA Ops:
  0.7 0.9 %constant_dynamic-slice_fusion = (bf16[256,128]{1,0:T(8,128)(2,1)S(1)}, bf16[256,128]{1,0:T(8,128)(2,1)S(1)}) fusion(bf16[1536,128]{1,0:T(8,128)(2,1)} %state_hbm.1, s32[]{:T(128)S(6)} %select_n.15, s32[]{:T(128)S(6)} %select_n.14), kind=kLoop, calls=%fused_computation.2 | loop fusion | bytes 262152 | tf_op jit(solution)/shard_map/dynamic_slice | solution.py:311
  1.5 0.7 %collective-permute-start.1 = (bf16[256,128]{1,0:T(8,128)(2,1)S(1)}, bf16[256,128]{1,0:T(8,128)(2,1)S(1)}, u32[]{:S(2)}, u32[]{:S(2)}) collective-permute-start(bf16[256,128]{1,0:T(8,128)(2,1)S(1)} %get-tuple-element.40), channel_id=1, source_target_pairs={{1,2},{3,4},{5,6},{7,8},{9,10},{11,12},{13,14},{15,16},{17,18},{19... | collective-permute-start | bytes 196616 | tf_op jit(solution)/shard_map/ppermute | solution.py:276
  2.2 5.9 %collective-permute-start = (bf16[256,128]{1,0:T(8,128)(2,1)S(1)}, bf16[256,128]{1,0:T(8,128)(2,1)S(1)}, u32[]{:S(2)}, u32[]{:S(2)}) collective-permute-start(bf16[256,128]{1,0:T(8,128)(2,1)S(1)} %get-tuple-element.41), channel_id=1, source_target_pairs={{0,1},{2,3},{4,5},{6,7},{8,9},{10,11},{12,13},{14,15},{16,17},{18,... | collective-permute-start | bytes 196616 | tf_op jit(solution)/shard_map/ppermute | solution.py:276
  8.1 0.8 %copy.20 = s32[12,4]{1,0:T(8,128)S(1)} copy(s32[12,4]{0,1:T(4,128)} %param.17) | data formatting | bytes 384 | tf_op args[7]
  8.9 0.1 reshape.41
  9.0 0.1 pad_add_fusion.place_ref
  9.1 0.0 collective-permute-done.1.got_odd_ref
  9.1 2.8 %collective-permute-done.got_even_ref = bf16[256,128]{1,0:T(8,128)(2,1)S(1)} collective-permute-done((bf16[256,128]{1,0:T(8,128)(2,1)S(1)}, bf16[256,128]{1,0:T(8,128)(2,1)S(1)}, u32[]{:S(2)}, u32[]{:S(2)}) %collective-permute-start) | collective-permute-done | bytes 65568 | tf_op jit(solution)/shard_map/ppermute | solution.py:276
  11.8 11.5 %layer.1 = (bf16[1536,128]{1,0:T(8,128)(2,1)}, bf16[1536,128]{1,0:T(8,128)(2,1)}, bf16[32,24,128]{2,1,0:T(8,128)(2,1)}, bf16[2,128,128]{2,1,0:T(8,128)(2,1)S(1)}...) custom-call(s32[49]{0:T(128)S(1)} %pad_add_fusion.place_ref, ...), custom_call_target="tpu_custom_call" | custom-call | flops 1000000000 | bytes 5000000 | tf_op jit(solution)/shard_map/layer/pallas_call | solution.py:320
  23.3 0.0 copy-start
  23.3 0.7 %copy-done = f32[4,128,128]{2,1,0:T(8,128)} copy-done((f32[4,128,128]{2,1,0:T(8,128)}, f32[4,128,128]{2,1,0:T(8,128)S(1)}, u32[]{:S(2)}) %copy-start) | copy-done | bytes 262168
  24.0 0.0 copy-start.1
  24.0 0.7 %copy-done.1 = f32[4,128,128]{2,1,0:T(8,128)} copy-done((f32[4,128,128]{2,1,0:T(8,128)}, f32[4,128,128]{2,1,0:T(8,128)S(1)}, u32[]{:S(2)}) %copy-start.1) | copy-done | bytes 262168
  24.7 5.2 %all-to-all-start = ((bf16[32,24,128]{2,1,0:T(8,128)(2,1)}), bf16[32,24,128]{2,1,0:T(8,128)(2,1)S(1)}, u32[]{:S(2)}, u32[]{:S(2)}) async-start(bf16[32,24,128]{2,1,0:T(8,128)(2,1)} %get-tuple-element.28), calls=%async_computation | async-start | bytes 393216 | tf_op jit(solution)/shard_map/all_to_all | solution.py:377
  29.9 0.7 %collective-permute-start.2 = (bf16[2,128,128]{2,1,0:T(8,128)(2,1)S(1)}, bf16[2,128,128]{2,1,0:T(8,128)(2,1)S(1)}, u32[]{:S(2)}, u32[]{:S(2)}) collective-permute-start(bf16[2,128,128]{2,1,0:T(8,128)(2,1)S(1)} %get-tuple-element.29), channel_id=1, source_target_pairs={{1,2},{3,4},{5,6},{7,8},{9,10},{11,12},{13,14},{15,16},{17,18},{19... | collective-permute-start | bytes 196616 | tf_op jit(solution)/shard_map/ppermute | solution.py:276
  30.6 4.5 %collective-permute-start.3 = (bf16[2,128,128]{2,1,0:T(8,128)(2,1)S(1)}, bf16[2,128,128]{2,1,0:T(8,128)(2,1)S(1)}, u32[]{:S(2)}, u32[]{:S(2)}) collective-permute-start(bf16[2,128,128]{2,1,0:T(8,128)(2,1)S(1)} %get-tuple-element.30), channel_id=1, source_target_pairs={{0,1},{2,3},{4,5},{6,7},{8,9},{10,11},{12,13},{14,15},{16,17},{18,... | collective-permute-start | bytes 196616 | tf_op jit(solution)/shard_map/ppermute | solution.py:276
  35.2 4.2 %all-to-all-done = bf16[32,24,128]{2,1,0:T(8,128)(2,1)S(1)} async-done(((bf16[32,24,128]{2,1,0:T(8,128)(2,1)}), bf16[32,24,128]{2,1,0:T(8,128)(2,1)S(1)}, u32[]{:S(2)}, u32[]{:S(2)}) %all-to-all-start) | async-done | bytes 196640 | tf_op jit(solution)/shard_map/all_to_all | solution.py:377
  39.4 0.0 collective-permute-done.2.odd_part_ref
  39.4 0.0 copy-start.3
  39.4 0.0 collective-permute-done.3.even_ref
  39.4 0.0 copy-start.4
  39.4 0.7 %broadcast_in_dim.2 = bf16[32,24,128]{2,1,0:T(8,128)(2,1)} broadcast(bf16[24,128]{1,0:T(8,128)(2,1)S(1)} %convert_reduce_fusion), dimensions={1,2} | broadcast | bytes 202752 | tf_op jit(solution)/shard_map/broadcast_in_dim | solution.py:382
  40.1 4.5 %all-to-all-start.1 = ((bf16[32,24,128]{2,1,0:T(8,128)(2,1)}), bf16[32,24,128]{2,1,0:T(8,128)(2,1)S(1)}, u32[]{:S(2)}, u32[]{:S(2)}) async-start(bf16[32,24,128]{2,1,0:T(8,128)(2,1)} %broadcast_in_dim.2), calls=%async_computation.1 | async-start | bytes 393216 | tf_op jit(solution)/shard_map/all_to_all | solution.py:405
  44.7 0.0 copy-done.3
  44.7 0.0 copy-done.4
  44.7 2.1 %edge_state.1 = bf16[1536,128]{1,0:T(8,128)(2,1)} custom-call(s32[1]{0:T(128)} %bitcast.odd_ref, bf16[1536,128]{1,0:T(8,128)(2,1)} %get-tuple-element.25.grad_state_ref, f32[4,128,128]{2,1,0:T(8,128)} %copy-done, f32[4,128,128]{2,1,0:T(8,128)} %copy-done.1, bf16[2,128,128]{2,1,0:T(8,128)(2,1)} %copy-done.4, ...), custom_call_target="tpu_custom_call", output_to_operand_aliasing={{}: (1, {})} | custom-call | tf_op jit(solution)/shard_map/edge_state/pallas_call | solution.py:385
  46.8 7.2 %all-to-all-done.1.parts_ref = bf16[32,24,128]{2,1,0:T(8,128)(2,1)S(1)} async-done(((bf16[32,24,128]{2,1,0:T(8,128)(2,1)}), bf16[32,24,128]{2,1,0:T(8,128)(2,1)S(1)}, u32[]{:S(2)}, u32[]{:S(2)}) %all-to-all-start.1) | async-done | bytes 196640 | tf_op jit(solution)/shard_map/all_to_all | solution.py:405
  54.0 0.0 copy-start.2
  54.0 0.7 %copy-done.2 = bf16[32,24,128]{2,1,0:T(8,128)(2,1)} copy-done((bf16[32,24,128]{2,1,0:T(8,128)(2,1)}, bf16[32,24,128]{2,1,0:T(8,128)(2,1)S(1)}, u32[]{:S(2)}) %copy-start.2) | copy-done | bytes 196632
  54.7 1.6 %unpack.1 = (f32[128,128]{1,0:T(8,128)}, f32[256,128]{1,0:T(8,128)}, f32[1,128]{1,0:T(1,128)}, f32[128,128]{1,0:T(8,128)}, f32[1,128]{1,0:T(1,128)}, /*index=5*/f32[1,128]{1,0:T(1,128)}) custom-call(bf16[32,24,128]{2,1,0:T(8,128)(2,1)} %copy-done.2), custom_call_target="tpu_custom_call" | custom-call | tf_op jit(solution)/shard_map/unpack/pallas_call | solution.py:406
  (1 shorter events, 0.0 us)
Async XLA Ops:
  1.5 7.5 %collective-permute-start.1 = (bf16[256,128]{1,0:T(8,128)(2,1)S(1)}, bf16[256,128]{1,0:T(8,128)(2,1)S(1)}, u32[]{:S(2)}, u32[]{:S(2)}) collective-permute-start(bf16[256,128]{1,0:T(8,128)(2,1)S(1)} %get-tuple-element.40), channel_id=1, source_target_pairs={{1,2},{3,4},{5,6},{7,8},{9,10},{11,12},{13,14},{15,16},{17,18},{19... | collective-permute-start | bytes 196616 | tf_op jit(solution)/shard_map/ppermute | solution.py:276
  2.2 9.6 %collective-permute-start = (bf16[256,128]{1,0:T(8,128)(2,1)S(1)}, bf16[256,128]{1,0:T(8,128)(2,1)S(1)}, u32[]{:S(2)}, u32[]{:S(2)}) collective-permute-start(bf16[256,128]{1,0:T(8,128)(2,1)S(1)} %get-tuple-element.41), channel_id=1, source_target_pairs={{0,1},{2,3},{4,5},{6,7},{8,9},{10,11},{12,13},{14,15},{16,17},{18,... | collective-permute-start | bytes 196616 | tf_op jit(solution)/shard_map/ppermute | solution.py:276
  23.3 0.7 %copy-start = (f32[4,128,128]{2,1,0:T(8,128)}, f32[4,128,128]{2,1,0:T(8,128)S(1)}, u32[]{:S(2)}) copy-start(f32[4,128,128]{2,1,0:T(8,128)S(1)} %get-tuple-element.26.msg_ref) | copy-start | bytes 786436
  24.0 0.7 %copy-start.1 = (f32[4,128,128]{2,1,0:T(8,128)}, f32[4,128,128]{2,1,0:T(8,128)S(1)}, u32[]{:S(2)}) copy-start(f32[4,128,128]{2,1,0:T(8,128)S(1)} %get-tuple-element.27.state_ref) | copy-start | bytes 786436
  24.7 14.6 %all-to-all-start = ((bf16[32,24,128]{2,1,0:T(8,128)(2,1)}), bf16[32,24,128]{2,1,0:T(8,128)(2,1)S(1)}, u32[]{:S(2)}, u32[]{:S(2)}) async-start(bf16[32,24,128]{2,1,0:T(8,128)(2,1)} %get-tuple-element.28), calls=%async_computation | async-start | bytes 393216 | tf_op jit(solution)/shard_map/all_to_all | solution.py:377
  29.9 9.5 %collective-permute-start.2 = (bf16[2,128,128]{2,1,0:T(8,128)(2,1)S(1)}, bf16[2,128,128]{2,1,0:T(8,128)(2,1)S(1)}, u32[]{:S(2)}, u32[]{:S(2)}) collective-permute-start(bf16[2,128,128]{2,1,0:T(8,128)(2,1)S(1)} %get-tuple-element.29), channel_id=1, source_target_pairs={{1,2},{3,4},{5,6},{7,8},{9,10},{11,12},{13,14},{15,16},{17,18},{19... | collective-permute-start | bytes 196616 | tf_op jit(solution)/shard_map/ppermute | solution.py:276
  30.6 8.8 %collective-permute-start.3 = (bf16[2,128,128]{2,1,0:T(8,128)(2,1)S(1)}, bf16[2,128,128]{2,1,0:T(8,128)(2,1)S(1)}, u32[]{:S(2)}, u32[]{:S(2)}) collective-permute-start(bf16[2,128,128]{2,1,0:T(8,128)(2,1)S(1)} %get-tuple-element.30), channel_id=1, source_target_pairs={{0,1},{2,3},{4,5},{6,7},{8,9},{10,11},{12,13},{14,15},{16,17},{18,... | collective-permute-start | bytes 196616 | tf_op jit(solution)/shard_map/ppermute | solution.py:276
  39.4 5.3 %copy-start.3 = (bf16[2,128,128]{2,1,0:T(8,128)(2,1)}, bf16[2,128,128]{2,1,0:T(8,128)(2,1)S(1)}, u32[]{:S(2)}) copy-start(bf16[2,128,128]{2,1,0:T(8,128)(2,1)S(1)} %collective-permute-done.2.odd_part_ref) | copy-start | bytes 196612
  39.4 5.3 %copy-start.4 = (bf16[2,128,128]{2,1,0:T(8,128)(2,1)}, bf16[2,128,128]{2,1,0:T(8,128)(2,1)S(1)}, u32[]{:S(2)}) copy-start(bf16[2,128,128]{2,1,0:T(8,128)(2,1)S(1)} %collective-permute-done.3.even_ref) | copy-start | bytes 196612
  40.1 13.9 %all-to-all-start.1 = ((bf16[32,24,128]{2,1,0:T(8,128)(2,1)}), bf16[32,24,128]{2,1,0:T(8,128)(2,1)S(1)}, u32[]{:S(2)}, u32[]{:S(2)}) async-start(bf16[32,24,128]{2,1,0:T(8,128)(2,1)} %broadcast_in_dim.2), calls=%async_computation.1 | async-start | bytes 393216 | tf_op jit(solution)/shard_map/all_to_all | solution.py:405
  54.0 0.7 %copy-start.2 = (bf16[32,24,128]{2,1,0:T(8,128)(2,1)}, bf16[32,24,128]{2,1,0:T(8,128)(2,1)S(1)}, u32[]{:S(2)}) copy-start(bf16[32,24,128]{2,1,0:T(8,128)(2,1)S(1)} %all-to-all-done.1.parts_ref) | copy-start | bytes 589828

commit v4 on v3

--- a/solution.py
+++ b/solution.py
@@ -223,25 +223,38 @@
             first_sums[2 * features : 2 * features + 1],
             second_sums[features : features + 1],
             gain_sum,
-            jnp.zeros((BIAS_ROWS - 3, features), jnp.float32),
         ],
         axis=0,
+    )
+    bias_high = bias.astype(sent)
+    bias_low = (bias - bias_high.astype(jnp.float32)).astype(sent)
+    bias = jnp.concatenate(
+        [bias_high, bias_low, jnp.zeros((BIAS_ROWS - 6, features), sent)], axis=0
     )
     sums = jnp.concatenate(
         [first_sums[: 2 * features], second_sums[:features], msg_sums], axis=0
     ).astype(sent)
-    bias = bias.astype(sent)
     nothing = jnp.zeros((chunk, features), sent)
     for k in range(grads_ref.shape[0]):
         part = sums[k * chunk : (k + 1) * chunk] if k * chunk < sums.shape[0] else nothing
-        tail = bias if k == 0 else nothing[:BIAS_ROWS]
-        grads_ref[k] = jnp.concatenate([part, tail], axis=0)
+        grads_ref[k] = jnp.concatenate([part, bias], axis=0)
     updated_copy.wait()
     grad_state_copy.wait()
 
 
 def edge_kernel(
-    odd_ref, grad_state_ref, msg_ref, state_ref, even_ref, odd_part_ref, w_msg_ref, out_ref
+    odd_ref,
+    grad_state_ref,
+    msg_ref,
+    state_ref,
+    even_ref,
+    odd_part_ref,
+    w_msg_ref,
+    bias_ref,
+    out_ref,
+    b_first_ref,
+    b_second_ref,
+    gain_ref,
 ):
     del grad_state_ref
     size = msg_ref.shape[2]
@@ -252,22 +265,27 @@
         d_msg = (msg_ref[k] + arrived).astype(jnp.bfloat16)
         total = state_ref[k] + dot(w_msg, d_msg)
         out_ref[pl.ds(k * size, size), :] = total.astype(jnp.bfloat16).T
-
-
-def unpack_kernel(chunk, parts_ref, msg_ref, first_ref, b_first_ref, second_ref, b_second_ref, gain_ref):
+    for k, ref in enumerate((b_first_ref, b_second_ref, gain_ref)):
+        ref[...] = bias_ref[pl.ds(k, 1), :] + bias_ref[pl.ds(k + 3, 1), :]
+
+
+def sum_kernel(parts_ref, spread_ref, bias_ref):
+    total = parts_ref[0].astype(jnp.float32)
+    for k in range(1, parts_ref.shape[0]):
+        total = total + parts_ref[k].astype(jnp.float32)
+    chunk = spread_ref.shape[1]
+    weights = total[:chunk].astype(spread_ref.dtype)
+    for k in range(spread_ref.shape[0]):
+        spread_ref[k] = weights
+    bias_ref[...] = total[chunk:]
+
+
+def unpack_kernel(rows_ref, msg_ref, first_ref, second_ref):
     place = 0
     for ref in (first_ref, second_ref, msg_ref):
-        done = 0
-        while done < ref.shape[0]:
-            k, row = divmod(place, chunk)
-            count = min(chunk - row, ref.shape[0] - done)
-            ref[pl.ds(done, count), :] = parts_ref[k, pl.ds(row, count), :].astype(jnp.float32)
-            done += count
-            place += count
-    bias = parts_ref[0, pl.ds(chunk, BIAS_ROWS), :].astype(jnp.float32)
-    b_first_ref[...] = bias[0:1]
-    b_second_ref[...] = bias[1:2]
-    gain_ref[...] = bias[2:3]
+        count = ref.shape[0]
+        ref[...] = rows_ref[pl.ds(place, count), :].astype(jnp.float32)
+        place += count
 
 
 def swapped(block, parity):
@@ -377,15 +395,31 @@
     parts = lax.all_to_all(grads, AXES, 0, 0, tiled=True)
     owed_odd = swapped(send_odd, 1)
     owed_even = swapped(send_even, 0)
-    own_sum = jnp.sum(parts.astype(f32), axis=0)
-    own_sum, owed_odd, owed_even = lax.optimization_barrier((own_sum, owed_odd, owed_even))
-    spread = jnp.broadcast_to(own_sum.astype(SENT)[None], parts.shape)
+    small_limit = pltpu.CompilerParams(vmem_limit_bytes=16 * 1024 * 1024)
+    spread, bias = pl.pallas_call(
+        sum_kernel,
+        out_shape=(
+            pltpu.VMEM((devices, chunk, features), SENT),
+            pltpu.VMEM((BIAS_ROWS, features), f32),
+        ),
+        in_specs=[in_vmem()],
+        out_specs=(in_vmem(),) * 2,
+        compiler_params=small_limit,
+        name="sum",
+    )(kept(parts, pltpu.VMEM))
+    spread, owed_odd, owed_even = lax.optimization_barrier((spread, owed_odd, owed_even))
 
     whole_block = lambda k: (0, 0, 0)
-    grad_state = pl.pallas_call(
+    one_row = pl.BlockSpec((1, features), lambda k: (0, 0))
+    grad_state, g_b_first, g_b_second, g_gain = pl.pallas_call(
         edge_kernel,
         grid=(2,),
-        out_shape=shape((nodes, features), bf16),
+        out_shape=(
+            shape((nodes, features), bf16),
+            shape((1, features), f32),
+            shape((1, features), f32),
+            shape((1, features), f32),
+        ),
         in_specs=[
             in_smem,
             pl.BlockSpec(memory_space=pl.ANY),
@@ -394,29 +428,42 @@
             pl.BlockSpec((WIN, features, size), whole_block),
             pl.BlockSpec((WIN, features, size), whole_block),
             pl.BlockSpec((features, features), lambda k: (0, 0)),
+            pl.BlockSpec((BIAS_ROWS, features), lambda k: (0, 0)),
         ],
-        out_specs=pl.BlockSpec(
-            (edge_rows, features), lambda k: (k * (nodes // edge_rows - 1), 0)
+        out_specs=(
+            pl.BlockSpec((edge_rows, features), lambda k: (k * (nodes // edge_rows - 1), 0)),
+            one_row,
+            one_row,
+            one_row,
         ),
         input_output_aliases={1: 0},
+        compiler_params=small_limit,
         name="edge_state",
-    )(odd, grad_state, edge_msg, edge_state, owed_even, owed_odd, w_msg)
+    )(
+        odd,
+        grad_state,
+        kept(edge_msg, pltpu.VMEM),
+        kept(edge_state, pltpu.VMEM),
+        kept(owed_even, pltpu.VMEM),
+        kept(owed_odd, pltpu.VMEM),
+        w_msg,
+        kept(bias, pltpu.VMEM),
+    )
 
     whole = lax.all_to_all(spread, AXES, 0, 0, tiled=True)
-    g_msg, g_first, g_b_first, g_second, g_b_second, g_gain = pl.pallas_call(
-        functools.partial(unpack_kernel, chunk),
+    rows = whole.reshape(devices * chunk, features)
+    g_msg, g_first, g_second = pl.pallas_call(
+        unpack_kernel,
         out_shape=(
             shape((features, features), f32),
             shape((2 * features, features), f32),
-            shape((1, features), f32),
             shape((features, features), f32),
-            shape((1, features), f32),
-            shape((1, features), f32),
         ),
         in_specs=[in_vmem()],
-        out_specs=(in_vmem(),) * 6,
+        out_specs=(in_vmem(),) * 3,
+        compiler_params=small_limit,
         name="unpack",
-    )(whole)
+    )(kept(rows, pltpu.VMEM))
     flat = lambda vector: vector.reshape(features)
     return (
         updated,

time: 56.7 us -> 52 us (0.917)
  local copies, waits for them, and re-layouts: 4.52 us -> 1.75 us
  Pallas kernels: 15.3 us -> 14 us
  starting transfers between devices: 21.5 us -> 20.9 us
    unnamed x11 -> x3, local copies, waits for them, and re-layouts: 2.85 us -> 0.78 us
    pallas_call x2 -> x3, Pallas kernels: 3.76 us -> 2.53 us  [the longest x1 1.12 us: shards(): pl.pallas_call(edge_kernel, grid=(2,), out_shape=(shape((nodes, features)...]
    broadcast_in_dim x1 -> x0, local copies, waits for them, and re-layouts: 0.71 us -> none  [shards(): spread = jnp.broadcast_to(own_sum.astype(SENT)[None], parts.shape)]
    all_to_all x1, starting transfers between devices: 4.55 us -> 3.92 us  [shards(): whole = lax.all_to_all(spread, AXES, 0, 0, tiled=True)]
where the time goes in v4:
time: 52 us; the launch traced here: 51.7 us
  starting transfers between devices  20.9 us (40%)
  waiting for transfers between devices  14.2 us (27%)
  Pallas kernels  14 us (27%)
  local copies, waits for them, and re-layouts  1.75 us (3%)
  between operations  0.72 us (1%)
    ppermute x4, starting transfers between devices, swapped(): lax.ppermute(block, AXES, [(i, i + 1) for i in lower] + [(i + 1, i) for i...  11.8 us
    pallas_call x1, Pallas kernels, shards(): pl.pallas_call(functools.partial(layer_kernel, grad_scale, chunk), out_sh...  11.5 us
    all_to_all x1, waiting for transfers between devices, shards(): whole = lax.all_to_all(spread, AXES, 0, 0, tiled=True)  7.27 us
    all_to_all x1, starting transfers between devices, shards(): parts = lax.all_to_all(grads, AXES, 0, 0, tiled=True)  5.2 us
    all_to_all x1, waiting for transfers between devices, shards(): parts = lax.all_to_all(grads, AXES, 0, 0, tiled=True)  4.19 us
    all_to_all x1, starting transfers between devices, shards(): whole = lax.all_to_all(spread, AXES, 0, 0, tiled=True)  3.92 us
    ppermute x4, waiting for transfers between devices, swapped(): lax.ppermute(block, AXES, [(i, i + 1) for i in lower] + [(i + 1, i) for i...  2.77 us
    pallas_call x1, Pallas kernels, shards(): pl.pallas_call(edge_kernel, grid=(2,), out_shape=(shape((nodes, features)...  1.12 us
  transfers between devices with their start and end apart: 6, of which 3 were waited for; matrix products, arithmetic and copies ran while one was open for 2% of the time, Pallas kernels for 4%

profile of v4, /device:TPU:0, one launch (start us, length us, event | category | flops | bytes accessed | tf_op | source)
XLA Modules:
  0.0 51.7 jit_solution(5817417087146886788)
XLA Ops:
  0.6 0.0 copy-start
  0.7 0.9 %constant_dynamic-slice_fusion = (bf16[256,128]{1,0:T(8,128)(2,1)S(1)}, bf16[256,128]{1,0:T(8,128)(2,1)S(1)}) fusion(bf16[1536,128]{1,0:T(8,128)(2,1)} %state_hbm.1, s32[]{:T(128)S(6)} %select_n.15, s32[]{:T(128)S(6)} %select_n.14), kind=kLoop, calls=%fused_computation.1 | loop fusion | bytes 262152 | tf_op jit(solution)/shard_map/dynamic_slice | solution.py:329
  1.6 0.7 %collective-permute-start.1 = (bf16[256,128]{1,0:T(8,128)(2,1)S(1)}, bf16[256,128]{1,0:T(8,128)(2,1)S(1)}, u32[]{:S(2)}, u32[]{:S(2)}) collective-permute-start(bf16[256,128]{1,0:T(8,128)(2,1)S(1)} %get-tuple-element.46), channel_id=1, source_target_pairs={{1,2},{3,4},{5,6},{7,8},{9,10},{11,12},{13,14},{15,16},{17,18},{19... | collective-permute-start | bytes 196616 | tf_op jit(solution)/shard_map/ppermute | solution.py:294
  2.2 5.9 %collective-permute-start = (bf16[256,128]{1,0:T(8,128)(2,1)S(1)}, bf16[256,128]{1,0:T(8,128)(2,1)S(1)}, u32[]{:S(2)}, u32[]{:S(2)}) collective-permute-start(bf16[256,128]{1,0:T(8,128)(2,1)S(1)} %get-tuple-element.47), channel_id=1, source_target_pairs={{0,1},{2,3},{4,5},{6,7},{8,9},{10,11},{12,13},{14,15},{16,17},{18,... | collective-permute-start | bytes 196616 | tf_op jit(solution)/shard_map/ppermute | solution.py:294
  8.1 0.8 %copy.20 = s32[12,4]{1,0:T(8,128)S(1)} copy(s32[12,4]{0,1:T(4,128)} %param.17) | data formatting | bytes 384 | tf_op args[7]
  8.9 0.1 reshape.43
  9.0 0.1 pad_add_fusion.place_ref
  9.1 0.0 collective-permute-done.1.got_odd_ref
  9.1 2.8 %collective-permute-done.got_even_ref = bf16[256,128]{1,0:T(8,128)(2,1)S(1)} collective-permute-done((bf16[256,128]{1,0:T(8,128)(2,1)S(1)}, bf16[256,128]{1,0:T(8,128)(2,1)S(1)}, u32[]{:S(2)}, u32[]{:S(2)}) %collective-permute-start) | collective-permute-done | bytes 65568 | tf_op jit(solution)/shard_map/ppermute | solution.py:294
  11.8 11.5 %layer.1 = (bf16[1536,128]{1,0:T(8,128)(2,1)}, bf16[1536,128]{1,0:T(8,128)(2,1)}, bf16[32,24,128]{2,1,0:T(8,128)(2,1)}, bf16[2,128,128]{2,1,0:T(8,128)(2,1)S(1)}...) custom-call(s32[49]{0:T(128)S(1)} %pad_add_fusion.place_ref, ...), custom_call_target="tpu_custom_call" | custom-call | flops 1000000000 | bytes 5000000 | tf_op jit(solution)/shard_map/layer/pallas_call | solution.py:338
  23.4 5.2 %all-to-all-start = ((bf16[32,24,128]{2,1,0:T(8,128)(2,1)}), bf16[32,24,128]{2,1,0:T(8,128)(2,1)S(1)}, u32[]{:S(2)}, u32[]{:S(2)}) async-start(bf16[32,24,128]{2,1,0:T(8,128)(2,1)} %get-tuple-element.31), calls=%async_computation | async-start | bytes 393216 | tf_op jit(solution)/shard_map/all_to_all | solution.py:395
  28.6 0.7 %collective-permute-start.2 = (bf16[2,128,128]{2,1,0:T(8,128)(2,1)S(1)}, bf16[2,128,128]{2,1,0:T(8,128)(2,1)S(1)}, u32[]{:S(2)}, u32[]{:S(2)}) collective-permute-start(bf16[2,128,128]{2,1,0:T(8,128)(2,1)S(1)} %get-tuple-element.33), channel_id=1, source_target_pairs={{1,2},{3,4},{5,6},{7,8},{9,10},{11,12},{13,14},{15,16},{17,18},{19... | collective-permute-start | bytes 196616 | tf_op jit(solution)/shard_map/ppermute | solution.py:294
  29.2 4.5 %collective-permute-start.3 = (bf16[2,128,128]{2,1,0:T(8,128)(2,1)S(1)}, bf16[2,128,128]{2,1,0:T(8,128)(2,1)S(1)}, u32[]{:S(2)}, u32[]{:S(2)}) collective-permute-start(bf16[2,128,128]{2,1,0:T(8,128)(2,1)S(1)} %get-tuple-element.34), channel_id=1, source_target_pairs={{0,1},{2,3},{4,5},{6,7},{8,9},{10,11},{12,13},{14,15},{16,17},{18,... | collective-permute-start | bytes 196616 | tf_op jit(solution)/shard_map/ppermute | solution.py:294
  33.8 4.2 %all-to-all-done.parts_ref = bf16[32,24,128]{2,1,0:T(8,128)(2,1)S(1)} async-done(((bf16[32,24,128]{2,1,0:T(8,128)(2,1)}), bf16[32,24,128]{2,1,0:T(8,128)(2,1)S(1)}, u32[]{:S(2)}, u32[]{:S(2)}) %all-to-all-start) | async-done | bytes 196640 | tf_op jit(solution)/shard_map/all_to_all | solution.py:395
  38.0 0.7 %sum.1 = (bf16[32,16,128]{2,1,0:T(8,128)(2,1)}, f32[8,128]{1,0:T(8,128)S(1)}) custom-call(bf16[32,24,128]{2,1,0:T(8,128)(2,1)S(1)} %all-to-all-done.parts_ref), custom_call_target="tpu_custom_call" | custom-call | tf_op jit(solution)/shard_map/sum/pallas_call | solution.py:399
  38.7 0.0 collective-permute-done.2.odd_part_ref
  38.7 0.0 collective-permute-done.3.even_ref
  38.7 3.9 %all-to-all-start.1 = ((bf16[32,16,128]{2,1,0:T(8,128)(2,1)}), bf16[32,16,128]{2,1,0:T(8,128)(2,1)S(1)}, u32[]{:S(2)}, u32[]{:S(2)}) async-start(bf16[32,16,128]{2,1,0:T(8,128)(2,1)} %get-tuple-element.39), calls=%async_computation.1 | async-start | bytes 262144 | tf_op jit(solution)/shard_map/all_to_all | solution.py:453
  42.6 0.0 copy-done
  42.6 1.1 %edge_state.1 = (bf16[1536,128]{1,0:T(8,128)(2,1)}, f32[1,128]{1,0:T(1,128)}, f32[1,128]{1,0:T(1,128)}, f32[1,128]{1,0:T(1,128)}) custom-call(s32[1]{0:T(128)} %bitcast.odd_ref, bf16[1536,128]{1,0:T(8,128)(2,1)} %get-tuple-element.28.grad_state_ref, f32[4,128,128]{2,1,0:T(8,128)S(1)} %get-tuple-element.29.msg_ref, ...), custom_call_target="tpu_custom_call", output_to_operand_aliasing={{0}: (1, {})} | custom-call | tf_op jit(solution)/shard_map/edge_state/pallas_call | solution.py:414
  43.7 7.3 %all-to-all-done.1 = bf16[32,16,128]{2,1,0:T(8,128)(2,1)S(1)} async-done(((bf16[32,16,128]{2,1,0:T(8,128)(2,1)}), bf16[32,16,128]{2,1,0:T(8,128)(2,1)S(1)}, u32[]{:S(2)}, u32[]{:S(2)}) %all-to-all-start.1) | async-done | bytes 131104 | tf_op jit(solution)/shard_map/all_to_all | solution.py:453
  51.0 0.7 %unpack.1 = (f32[128,128]{1,0:T(8,128)}, f32[256,128]{1,0:T(8,128)}, f32[128,128]{1,0:T(8,128)}) custom-call(bf16[512,128]{1,0:T(8,128)(2,1)S(1)} %bitcast.8), custom_call_target="tpu_custom_call" | custom-call | tf_op jit(solution)/shard_map/unpack/pallas_call | solution.py:455
Async XLA Ops:
  0.6 42.0 %copy-start = (bf16[128,128]{1,0:T(8,128)(2,1)S(1)}, bf16[128,128]{1,0:T(8,128)(2,1)}, u32[]{:S(2)}) copy-start(bf16[128,128]{1,0:T(8,128)(2,1)} %w_msg_ref.1) | copy-start | bytes 98308
  1.6 7.5 %collective-permute-start.1 = (bf16[256,128]{1,0:T(8,128)(2,1)S(1)}, bf16[256,128]{1,0:T(8,128)(2,1)S(1)}, u32[]{:S(2)}, u32[]{:S(2)}) collective-permute-start(bf16[256,128]{1,0:T(8,128)(2,1)S(1)} %get-tuple-element.46), channel_id=1, source_target_pairs={{1,2},{3,4},{5,6},{7,8},{9,10},{11,12},{13,14},{15,16},{17,18},{19... | collective-permute-start | bytes 196616 | tf_op jit(solution)/shard_map/ppermute | solution.py:294
  2.2 9.6 %collective-permute-start = (bf16[256,128]{1,0:T(8,128)(2,1)S(1)}, bf16[256,128]{1,0:T(8,128)(2,1)S(1)}, u32[]{:S(2)}, u32[]{:S(2)}) collective-permute-start(bf16[256,128]{1,0:T(8,128)(2,1)S(1)} %get-tuple-element.47), channel_id=1, source_target_pairs={{0,1},{2,3},{4,5},{6,7},{8,9},{10,11},{12,13},{14,15},{16,17},{18,... | collective-permute-start | bytes 196616 | tf_op jit(solution)/shard_map/ppermute | solution.py:294
  23.4 14.6 %all-to-all-start = ((bf16[32,24,128]{2,1,0:T(8,128)(2,1)}), bf16[32,24,128]{2,1,0:T(8,128)(2,1)S(1)}, u32[]{:S(2)}, u32[]{:S(2)}) async-start(bf16[32,24,128]{2,1,0:T(8,128)(2,1)} %get-tuple-element.31), calls=%async_computation | async-start | bytes 393216 | tf_op jit(solution)/shard_map/all_to_all | solution.py:395
  28.6 10.1 %collective-permute-start.2 = (bf16[2,128,128]{2,1,0:T(8,128)(2,1)S(1)}, bf16[2,128,128]{2,1,0:T(8,128)(2,1)S(1)}, u32[]{:S(2)}, u32[]{:S(2)}) collective-permute-start(bf16[2,128,128]{2,1,0:T(8,128)(2,1)S(1)} %get-tuple-element.33), channel_id=1, source_target_pairs={{1,2},{3,4},{5,6},{7,8},{9,10},{11,12},{13,14},{15,16},{17,18},{19... | collective-permute-start | bytes 196616 | tf_op jit(solution)/shard_map/ppermute | solution.py:294
  29.2 9.4 %collective-permute-start.3 = (bf16[2,128,128]{2,1,0:T(8,128)(2,1)S(1)}, bf16[2,128,128]{2,1,0:T(8,128)(2,1)S(1)}, u32[]{:S(2)}, u32[]{:S(2)}) collective-permute-start(bf16[2,128,128]{2,1,0:T(8,128)(2,1)S(1)} %get-tuple-element.34), channel_id=1, source_target_pairs={{0,1},{2,3},{4,5},{6,7},{8,9},{10,11},{12,13},{14,15},{16,17},{18,... | collective-permute-start | bytes 196616 | tf_op jit(solution)/shard_map/ppermute | solution.py:294
  38.7 12.3 %all-to-all-start.1 = ((bf16[32,16,128]{2,1,0:T(8,128)(2,1)}), bf16[32,16,128]{2,1,0:T(8,128)(2,1)S(1)}, u32[]{:S(2)}, u32[]{:S(2)}) async-start(bf16[32,16,128]{2,1,0:T(8,128)(2,1)} %get-tuple-element.39), calls=%async_computation.1 | async-start | bytes 262144 | tf_op jit(solution)/shard_map/all_to_all | solution.py:453

commit v5 on v0

v5 whole, which is shorter than its diff:
```python
import functools
import math

import jax
import jax.numpy as jnp
from jax import lax
from jax.experimental import pallas as pl
from jax.experimental.pallas import tpu as pltpu
from jax.sharding import PartitionSpec as P

WIN = 2
BAND = 2 * WIN + 1
GROUP = 4
epsilon = 1e-05
AXES = ("dom", "feat")
BF16, F32 = jnp.bfloat16, jnp.float32
SENT = BF16
ONES = 128
BIAS_ROWS = 8

kept = pltpu.with_memory_space_constraint


def dot(left, right):
    return jnp.dot(left, right, preferred_element_type=F32)


def dot_nt(left, right):
    return lax.dot_general(left, right, (((1,), (1,)), ((), ())), preferred_element_type=F32)


def joined_lanes(parts):
    return jnp.concatenate(parts, axis=1)


def device_is_odd():
    index = lax.axis_index("dom") * lax.axis_size("feat") + lax.axis_index("feat")
    return index % 2 == 1


def column(row_ref, width):
    return jnp.broadcast_to(row_ref[...], (width, row_ref.shape[1])).T


def node_layer(state_t, aggregate_t, cot_t, first_t, second_t, w_first, w_second, columns):
    features, width = state_t.shape
    b_first, b_second, gain = (
        joined_lanes([c] * (width // c.shape[1])) for c in columns
    )
    pre_hidden = dot(first_t, jnp.concatenate([state_t, aggregate_t], axis=0)) + b_first
    sigmoid = 1.0 / (1.0 + jnp.exp(-pre_hidden))
    active_t = (pre_hidden * sigmoid).astype(BF16)
    slope = sigmoid * (1.0 + pre_hidden * (1.0 - sigmoid))
    pre_norm = dot(second_t, active_t) + b_second
    centred = pre_norm - jnp.mean(pre_norm, axis=0, keepdims=True)
    inv_std = lax.rsqrt(jnp.mean(centred * centred, axis=0, keepdims=True) + epsilon)
    normed = centred * inv_std
    updated_t = (state_t.astype(F32) + gain * normed).astype(BF16)
    cot = cot_t.astype(F32)
    terms = cot * normed
    q = cot * gain
    mean_q = jnp.mean(q, axis=0, keepdims=True)
    mean_qn = jnp.mean(q * normed, axis=0, keepdims=True)
    d_norm_t = (inv_std * (q - mean_q - normed * mean_qn)).astype(BF16)
    d_hidden_t = (dot(w_second, d_norm_t) * slope).astype(BF16)
    d_joined = dot(w_first, d_hidden_t)
    direct = cot + d_joined[:features]
    d_aggregate_t = d_joined[features:].astype(BF16)
    return updated_t, terms, active_t, d_norm_t, d_hidden_t, direct, d_aggregate_t


def first_products(d_hidden_t, state, aggregate):
    ones = jnp.ones((state.shape[0], ONES), BF16)
    return dot(d_hidden_t, joined_lanes([state, aggregate, ones]))


def second_products(active_t, d_norm_t):
    ones = jnp.ones((16, active_t.shape[1]), BF16)
    return dot_nt(jnp.concatenate([active_t, ones], axis=0), d_norm_t)


def inner_kernel(
    col_ref,
    state_hbm,
    cot_hbm,
    counts_hbm,
    w_msg_hbm,
    w_first_hbm,
    b_first_hbm,
    w_second_hbm,
    b_second_hbm,
    gain_hbm,
    state_ref,
    w_msg_ref,
    w_first_ref,
    w_second_ref,
    first_t_ref,
    second_t_ref,
    columns_ref,
    edge_state_ref,
    edge_cot_ref,
    edge_band_ref,
    edge_msg_ref,
    updated_ref,
    direct_ref,
    owed_ref,
    first_sums_ref,
    second_sums_ref,
    msg_sums_ref,
    gain_sums_ref,
    cot_ref,
    counts_ref,
    b_first_ref,
    b_second_ref,
    gain_ref,
    messages,
    band,
    arrived,
):
    blocks, tiles, size, _ = counts_ref.shape
    features = state_ref.shape[1]
    edge_rows = [*range(WIN), *range(blocks - WIN, blocks)]
    inner_rows = range(WIN, blocks - WIN)
    part = blocks // 4

    copies = [
        (state_hbm, state_ref),
        (w_msg_hbm, w_msg_ref),
        (w_first_hbm, w_first_ref),
        (b_first_hbm, b_first_ref),
        (w_second_hbm, w_second_ref),
        (b_second_hbm, b_second_ref),
        (gain_hbm, gain_ref),
    ]
    early = len(copies)
    copies += [
        (counts_hbm.at[pl.ds(b, part)], counts_ref.at[pl.ds(b, part)])
        for b in range(0, blocks, part)
    ]
    copies.append((cot_hbm, cot_ref))
    copies = [
        pltpu.make_async_copy(source, target, arrived.at[k])
        for k, (source, target) in enumerate(copies)
    ]
    for copy in copies:
        copy.start()
    for copy in copies[:early]:
        copy.wait()

    def rows(block, count=1):
        return pl.ds(block * size, count * size)

    w_msg, w_first, w_second = w_msg_ref[...], w_first_ref[...], w_second_ref[...]
    first_t = joined_lanes([w_first[:features].T, w_first[features:].T])
    second_t = w_second.T
    columns = [column(ref, size) for ref in (b_first_ref, b_second_ref, gain_ref)]
    first_t_ref[...] = first_t
    second_t_ref[...] = second_t
    for k in range(3):
        columns_ref[k] = columns[k]
    messages[...] = dot(state_ref[...], w_msg).astype(BF16)
    edge_msg_ref[0] = messages[rows(0, 2 * WIN), :]
    edge_msg_ref[1] = messages[rows(blocks - 2 * WIN, 2 * WIN), :]
    state_t = [state_ref[rows(b), :].T for b in range(blocks)]
    for k, b in enumerate(edge_rows):
        edge_state_ref[:, rows(k)] = state_t[b]

    for copy in copies[early:]:
        copy.wait()
    for k, b in enumerate(edge_rows):
        edge_cot_ref[:, rows(k)] = cot_ref[rows(b), :].T
    nothing = jnp.zeros((size, size), BF16)
    places = [(band, k, b) for k, b in enumerate(inner_rows)]
    places += [(edge_band_ref, k, b) for k, b in enumerate(edge_rows)]
    for ref, k, b in places:
        for place in range(BAND):
            if place != WIN:
                ref[k, place] = nothing
        ref[k, WIN] = counts_ref[b, 0].astype(F32).astype(BF16)
        own = col_ref[0, b]
        for t in range(1, tiles):
            ref[k, col_ref[t, b] - own + WIN] += counts_ref[b, t].astype(F32).astype(BF16)

    gain_sums = jnp.zeros((features, size), F32)
    first_sums = second_sums = 0.0
    reached = set()
    for start in range(0, len(inner_rows), GROUP):
        group = inner_rows[start : start + GROUP]
        lanes = pl.ds(start * size, len(group) * size)
        aggregate = [
            dot(
                joined_lanes([band[b - WIN, place] for place in range(BAND)]),
                messages[rows(b - WIN, BAND), :],
            ).astype(BF16)
            for b in group
        ]
        updated_t, terms, active_t, d_norm_t, d_hidden_t, direct, d_aggregate_t = node_layer(
            joined_lanes([state_t[b] for b in group]),
            joined_lanes([block.T for block in aggregate]),
            joined_lanes([cot_ref[rows(b), :].T for b in group]),
            first_t,
            second_t,
            w_first,
            w_second,
            columns,
        )
        updated_ref[:, lanes] = updated_t
        direct_ref[:, lanes] = direct
        first_sums += first_products(
            d_hidden_t, state_ref[rows(group[0], len(group)), :], jnp.concatenate(aggregate, axis=0)
        )
        second_sums += second_products(active_t, d_norm_t)
        for k, b in enumerate(group):
            own = slice(k * size, (k + 1) * size)
            gain_sums += terms[:, own]
            owed = dot(
                d_aggregate_t[:, own],
                joined_lanes([band[b - WIN, place] for place in range(BAND)]),
            )
            for place in range(BAND):
                block = b - WIN + place
                value = owed[:, place * size : (place + 1) * size]
                if block in reached:
                    owed_ref[block] += value
                else:
                    owed_ref[block] = value
                reached.add(block)
    first_sums_ref[...] = first_sums
    second_sums_ref[...] = second_sums
    gain_sums_ref[...] = gain_sums
    done = range(2 * WIN, blocks - 2 * WIN)
    msg_sums_ref[...] = dot(
        joined_lanes([owed_ref[b].astype(BF16) for b in done]), state_ref[rows(2 * WIN, len(done)), :]
    )


def outer_kernel(
    grad_scale,
    got_even_ref,
    got_odd_ref,
    state_ref,
    w_msg_ref,
    w_first_ref,
    w_second_ref,
    first_t_ref,
    second_t_ref,
    columns_ref,
    edge_state_ref,
    edge_cot_ref,
    edge_band_ref,
    edge_msg_ref,
    owed_ref,
    first_sums_ref,
    second_sums_ref,
    msg_sums_ref,
    gain_sums_ref,
    grads_ref,
    send_even_ref,
    send_odd_ref,
    updated_ref,
    direct_ref,
    edge_owed_ref,
):
    blocks, features, size = owed_ref.shape
    width = WIN * size

    def rows(block, count=1):
        return pl.ds(block * size, count * size)

    odd = device_is_odd()
    got_even, got_odd = got_even_ref[...], got_odd_ref[...]
    halo = (jnp.where(odd, got_even, got_odd), jnp.where(odd, got_odd, got_even))
    w_msg = w_msg_ref[...]
    below, above = (dot(block, w_msg).astype(BF16) for block in halo)
    messages = (
        jnp.concatenate([below, edge_msg_ref[0]], axis=0),
        jnp.concatenate([edge_msg_ref[1], above], axis=0),
    )

    bands = [
        joined_lanes([edge_band_ref[k, place] for place in range(BAND)]) for k in range(2 * WIN)
    ]
    aggregate = [
        dot(bands[k], messages[k // WIN][(k % WIN) * size : (k % WIN + BAND) * size]).astype(BF16)
        for k in range(2 * WIN)
    ]
    updated_t, terms, active_t, d_norm_t, d_hidden_t, direct, d_aggregate_t = node_layer(
        edge_state_ref[...],
        joined_lanes([block.T for block in aggregate]),
        edge_cot_ref[...],
        first_t_ref[...],
        second_t_ref[...],
        w_first_ref[...],
        w_second_ref[...],
        [columns_ref[k] for k in range(3)],
    )
    updated_ref[...] = updated_t
    direct_ref[...] = direct

    ends = []
    for end in range(2):
        owed = [None] * (3 * WIN)
        for k in range(WIN):
            own = slice((end * WIN + k) * size, (end * WIN + k + 1) * size)
            value = dot(d_aggregate_t[:, own], bands[end * WIN + k])
            for place in range(BAND):
                term = value[:, place * size : (place + 1) * size]
                owed[k + place] = term if owed[k + place] is None else owed[k + place] + term
        ends.append(owed)
    to_below = [block.astype(BF16) for block in ends[0][:WIN]]
    to_above = [block.astype(BF16) for block in ends[1][2 * WIN :]]
    for k in range(WIN):
        send_even_ref[k] = jnp.where(odd, to_below[k], to_above[k])
        send_odd_ref[k] = jnp.where(odd, to_above[k], to_below[k])
    inside = []
    for k in range(2 * WIN):
        inside.append(owed_ref[k] + ends[0][WIN + k])
    for k in range(2 * WIN):
        inside.append(owed_ref[blocks - 2 * WIN + k] + ends[1][k])
    for k, block in enumerate(inside):
        edge_owed_ref[k] = block
    inside = [block.astype(BF16) for block in inside]

    state = state_ref[...]
    low, high = state[:width], state[(blocks - WIN) * size :]
    first_sums = first_sums_ref[...] + first_products(
        d_hidden_t, jnp.concatenate([low, high], axis=0), jnp.concatenate(aggregate, axis=0)
    )
    second_sums = second_sums_ref[...] + second_products(active_t, d_norm_t)
    msg_sums = msg_sums_ref[...] + dot(
        joined_lanes(to_below + inside + to_above),
        jnp.concatenate(
            [halo[0], state[: 2 * width], state[(blocks - 2 * WIN) * size :], halo[1]], axis=0
        ),
    )
    gain_sums = gain_sums_ref[...]
    for k in range(2 * WIN):
        gain_sums = gain_sums + terms[:, k * size : (k + 1) * size]

    chunk = grads_ref.shape[1] - BIAS_ROWS
    turned = [first_sums[:, k * size : (k + 1) * size].T for k in range(3)]
    sums = (
        jnp.concatenate([turned[0], turned[1], second_sums[:features], msg_sums.T], axis=0)
        * grad_scale
    ).astype(SENT)
    bias = (
        jnp.concatenate(
            [
                turned[2][:1],
                second_sums[features : features + 1],
                jnp.sum(gain_sums.T, axis=0, keepdims=True),
            ],
            axis=0,
        )
        * grad_scale
    )
    bias_high = bias.astype(SENT)
    bias_low = (bias - bias_high.astype(F32)).astype(SENT)
    bias = jnp.concatenate(
        [bias_high, bias_low, jnp.zeros((BIAS_ROWS - 6, features), SENT)], axis=0
    )
    nothing = jnp.zeros((chunk, features), SENT)
    for k in range(grads_ref.shape[0]):
        block = sums[k * chunk : (k + 1) * chunk] if k * chunk < sums.shape[0] else nothing
        grads_ref[k] = jnp.concatenate([block, bias], axis=0)


def sum_kernel(parts_ref, spread_ref, bias_ref):
    total = parts_ref[0].astype(F32)
    for k in range(1, parts_ref.shape[0]):
        total = total + parts_ref[k].astype(F32)
    chunk = spread_ref.shape[1]
    weights = total[:chunk].astype(spread_ref.dtype)
    for k in range(spread_ref.shape[0]):
        spread_ref[k] = weights
    bias_ref[...] = total[chunk:]


def result_kernel(
    even_ref,
    odd_ref,
    w_msg_ref,
    inner_updated_ref,
    outer_updated_ref,
    inner_direct_ref,
    outer_direct_ref,
    owed_ref,
    edge_owed_ref,
    bias_ref,
    updated_ref,
    grad_state_ref,
    b_first_ref,
    b_second_ref,
    gain_ref,
):
    blocks, _, size = owed_ref.shape
    odd = device_is_odd()
    even_part, odd_part = even_ref[...].astype(F32), odd_ref[...].astype(F32)
    from_below = jnp.where(odd, even_part, odd_part)
    from_above = jnp.where(odd, odd_part, even_part)
    w_msg = w_msg_ref[...]
    for b in range(blocks):
        if b < 2 * WIN:
            owed = edge_owed_ref[b]
        elif b < blocks - 2 * WIN:
            owed = owed_ref[b]
        else:
            owed = edge_owed_ref[b - blocks + 4 * WIN]
        if b < WIN:
            owed = owed + from_below[b]
        elif b >= blocks - WIN:
            owed = owed + from_above[b - blocks + WIN]
        if WIN <= b < blocks - WIN:
            k, updated, direct = b - WIN, inner_updated_ref, inner_direct_ref
        else:
            k = b if b < WIN else b - blocks + 2 * WIN
            updated, direct = outer_updated_ref, outer_direct_ref
        lanes, rows = pl.ds(k * size, size), pl.ds(b * size, size)
        total = direct[:, lanes] + dot(w_msg, owed.astype(BF16))
        grad_state_ref[rows, :] = total.astype(BF16).T
        updated_ref[rows, :] = updated[:, lanes].T
    for k, ref in enumerate((b_first_ref, b_second_ref, gain_ref)):
        ref[...] = bias_ref[pl.ds(k, 1), :] + bias_ref[pl.ds(k + 3, 1), :]


def unpack_kernel(rows_ref, msg_ref, first_ref, second_ref):
    place = 0
    for ref in (first_ref, second_ref, msg_ref):
        count = ref.shape[0]
        ref[...] = rows_ref[pl.ds(place, count), :].astype(F32)
        place += count


def swapped(block, parity):
    last = lax.axis_size(AXES) - 1
    lower = range(parity, last, 2)
    return lax.ppermute(block, AXES, [(i, i + 1) for i in lower] + [(i + 1, i) for i in lower])


def call(kernel, name, outs, operands, scratch=(), limit=16, smem=0, flops=0):
    specs = [pl.BlockSpec(memory_space=pltpu.SMEM)] * smem
    specs += [pl.BlockSpec(memory_space=space) for _, space in operands[smem:]]
    arrays = list(operands[:smem]) + [kept(array, space) for array, space in operands[smem:]]
    return pl.pallas_call(
        kernel,
        out_shape=tuple(outs),
        in_specs=specs,
        out_specs=tuple(pl.BlockSpec(memory_space=pltpu.VMEM) for _ in outs),
        scratch_shapes=list(scratch),
        compiler_params=pltpu.CompilerParams(vmem_limit_bytes=limit * 1024 * 1024),
        cost_estimate=pl.CostEstimate(
            flops=flops, bytes_accessed=1_000_000, transcendentals=0
        ),
        name=name,
    )(*arrays)


def shards(
    node_state,
    w_msg,
    w_first,
    b_first,
    w_second,
    b_second,
    ln_gain,
    col_index,
    edge_counts,
    cotangent,
):
    nodes, features = node_state.shape
    blocks, tiles, size, _ = edge_counts.shape
    devices = lax.axis_size(AXES)
    grad_scale = 1.0 / math.sqrt(nodes * devices)
    chunk = -(-4 * features // (devices * 8)) * 8
    inner = blocks - 2 * WIN
    edge = 2 * WIN
    vmem, hbm = pltpu.VMEM, pltpu.HBM
    result = jax.ShapeDtypeStruct

    edge_rows = WIN * size
    odd = lax.axis_index(AXES) % 2
    side = lambda upper: lax.dynamic_slice_in_dim(
        node_state, upper * (nodes - edge_rows), edge_rows, 0
    )
    got_odd = swapped(side(odd), 1)
    got_even = swapped(side(1 - odd), 0)
    row = lambda vector: vector.reshape(1, features)

    (
        state,
        w_msg_here,
        w_first_here,
        w_second_here,
        first_t,
        second_t,
        columns,
        edge_state,
        edge_cot,
        edge_band,
        edge_msg,
        inner_updated,
        inner_direct,
        owed,
        first_sums,
        second_sums,
        msg_sums,
        gain_sums,
    ) = call(
        inner_kernel,
        "inner_rows",
        (
            vmem((nodes, features), BF16),
            vmem((features, features), BF16),
            vmem((2 * features, features), BF16),
            vmem((features, features), BF16),
            vmem((features, 2 * features), BF16),
            vmem((features, features), BF16),
            vmem((3, features, size), F32),
            vmem((features, edge * size), BF16),
            vmem((features, edge * size), BF16),
            vmem((edge, BAND, size, size), BF16),
            vmem((2, edge * size, features), BF16),
            vmem((features, inner * size), BF16),
            vmem((features, inner * size), F32),
            vmem((blocks, features, size), F32),
            vmem((features, 2 * features + ONES), F32),
            vmem((features + 16, features), F32),
            vmem((features, features), F32),
            vmem((features, size), F32),
        ),
        (
            col_index.T,
            (node_state, hbm),
            (cotangent, hbm),
            (edge_counts, hbm),
            (w_msg, hbm),
            (w_first, hbm),
            (row(b_first), hbm),
            (w_second, hbm),
            (row(b_second), hbm),
            (row(ln_gain), hbm),
        ),
        scratch=(
            vmem((nodes, features), BF16),
            vmem(edge_counts.shape, jnp.int32),
            vmem((1, features), F32),
            vmem((1, features), F32),
            vmem((1, features), F32),
            vmem((nodes, features), BF16),
            vmem((inner, BAND, size, size), BF16),
            pltpu.SemaphoreType.DMA((12,)),
        ),
        limit=32,
        smem=1,
        flops=700_000_000,
    )

    grads, send_even, send_odd, outer_updated, outer_direct, edge_owed = call(
        functools.partial(outer_kernel, grad_scale),
        "outer_rows",
        (
            vmem((devices, chunk + BIAS_ROWS, features), SENT),
            vmem((WIN, features, size), BF16),
            vmem((WIN, features, size), BF16),
            vmem((features, edge * size), BF16),
            vmem((features, edge * size), F32),
            vmem((2 * edge, features, size), F32),
        ),
        [
            (array, vmem)
            for array in (
                got_even,
                got_odd,
                state,
                w_msg_here,
                w_first_here,
                w_second_here,
                first_t,
                second_t,
                columns,
                edge_state,
                edge_cot,
                edge_band,
                edge_msg,
                owed,
                first_sums,
                second_sums,
                msg_sums,
                gain_sums,
            )
        ],
        flops=300_000_000,
    )

    parts = lax.all_to_all(grads, AXES, 0, 0, tiled=True)
    owed_odd = swapped(send_odd, 1)
    owed_even = swapped(send_even, 0)
    spread, bias = call(
        sum_kernel,
        "sum",
        (vmem((devices, chunk, features), SENT), vmem((BIAS_ROWS, features), F32)),
        [(parts, vmem)],
    )
    spread, owed_odd, owed_even = lax.optimization_barrier((spread, owed_odd, owed_even))

    updated, grad_state, g_b_first, g_b_second, g_gain = call(
        result_kernel,
        "results",
        (
            result((nodes, features), BF16),
            result((nodes, features), BF16),
            result((1, features), F32),
            result((1, features), F32),
            result((1, features), F32),
        ),
        [
            (array, vmem)
            for array in (
                owed_even,
                owed_odd,
                w_msg_here,
                inner_updated,
                outer_updated,
                inner_direct,
                outer_direct,
                owed,
                edge_owed,
                bias,
            )
        ],
        flops=100_000_000,
    )

    whole = lax.all_to_all(spread, AXES, 0, 0, tiled=True)
    g_msg, g_first, g_second = call(
        unpack_kernel,
        "unpack",
        (
            result((features, features), F32),
            result((2 * features, features), F32),
            result((features, features), F32),
        ),
        [(whole.reshape(devices * chunk, features), vmem)],
    )
    flat = lambda vector: vector.reshape(features)
    return (
        updated,
        grad_state,
        g_msg,
        g_first,
        flat(g_b_first),
        g_second,
        flat(g_b_second),
        flat(g_gain),
    )


def solution(mesh):
    split = P(AXES, None)
    return jax.shard_map(
        shards,
        mesh=mesh,
        in_specs=(split, P(), P(), P(), P(), P(), P(), split, P(AXES, None, None, None), split),
        out_specs=(split, split, P(), P(), P(), P(), P(), P()),
        check_vma=False,
    )
```

time: 236 us -> 45.4 us (0.19)
  waiting for transfers between devices: 129 us -> 11.3 us
  blocking collectives: 42.8 us -> 0 us
  local copies, waits for them, and re-layouts: 20.1 us -> 1.57 us
  between operations: 14.4 us -> 0.72 us
  matrix products: 13 us -> 0 us
  Pallas kernels: 0 us -> 11.6 us
  starting transfers between devices: 11.6 us -> 19.9 us
  other arithmetic: 4.26 us -> 0 us
    psum x1 -> x0, waiting for transfers between devices: 127 us -> none  [shards(): lax.psum((terms[0], terms[1], terms[2], terms[3], terms[4], terms[5]), ('...]
    psum x1 -> x0, blocking collectives: 42.8 us -> none  [shards(): lax.psum((terms[0], terms[1], terms[2], terms[3], terms[4], terms[5]), ('...]
    dot_general x12 -> x0, matrix products: 13 us -> none  [the longest x1 4.34 us: shards(): jnp.einsum('btc,btjh->cjh', one_hot, contribution, precision=lax.Precisio...]
    pallas_call x0 -> x5, Pallas kernels: none -> 11.6 us  [call(): pl.pallas_call(kernel, out_shape=tuple(outs), in_specs=specs, out_specs=t...]
    all_to_all x0 -> x2, waiting for transfers between devices: none -> 11.3 us  [the longest x1 7.1 us: shards(): whole = lax.all_to_all(spread, AXES, 0, 0, tiled=True)]
    unnamed x42 -> x2, local copies, waits for them, and re-layouts: 11.9 us -> 0.68 us
    all_to_all x0 -> x2, starting transfers between devices: none -> 8.1 us  [the longest x1 4.18 us: shards(): parts = lax.all_to_all(grads, AXES, 0, 0, tiled=True)]
    dot_general x3 -> x0, local copies, waits for them, and re-layouts: 4.14 us -> none  [the longest x1 3.46 us: shards(): jnp.einsum('btij,bih->btjh', tile_weights, d_aggregate, preferred_element...]
  transfers between devices with their start and end apart: 5 -> 6, of which waited for: 2 -> 2; matrix products, arithmetic and copies ran while one was open for 3% -> 0% of each run, Pallas kernels for 0% -> 19%
where the time goes in v5:
time: 45.4 us; the launch traced here: 45.1 us
  starting transfers between devices  19.9 us (44%)
  Pallas kernels  11.6 us (26%)
  waiting for transfers between devices  11.3 us (25%)
  local copies, waits for them, and re-layouts  1.57 us (3%)
  between operations  0.72 us (2%)
    ppermute x4, starting transfers between devices, swapped(): lax.ppermute(block, AXES, [(i, i + 1) for i in lower] + [(i + 1, i) for i...  11.8 us
    pallas_call x5, Pallas kernels, call(): pl.pallas_call(kernel, out_shape=tuple(outs), in_specs=specs, out_specs=t...  11.6 us
    all_to_all x1, waiting for transfers between devices, shards(): whole = lax.all_to_all(spread, AXES, 0, 0, tiled=True)  7.1 us
    all_to_all x1, waiting for transfers between devices, shards(): parts = lax.all_to_all(grads, AXES, 0, 0, tiled=True)  4.19 us
    all_to_all x1, starting transfers between devices, shards(): parts = lax.all_to_all(grads, AXES, 0, 0, tiled=True)  4.18 us
    all_to_all x1, starting transfers between devices, shards(): whole = lax.all_to_all(spread, AXES, 0, 0, tiled=True)  3.92 us
  transfers between devices with their start and end apart: 6, of which 2 were waited for; matrix products, arithmetic and copies ran while one was open for 0% of the time, Pallas kernels for 19%

profile of v5, /device:TPU:0, one launch (start us, length us, event | category | flops | bytes accessed | tf_op | source)
XLA Modules:
  0.0 45.1 jit_solution(1285177142750944308)
XLA Ops:
  0.7 0.9 %constant_dynamic-slice_fusion = (bf16[256,128]{1,0:T(8,128)(2,1)S(1)}, bf16[256,128]{1,0:T(8,128)(2,1)S(1)}) fusion(bf16[1536,128]{1,0:T(8,128)(2,1)} %state_hbm.1, s32[]{:T(128)S(6)} %select_n.15, s32[]{:T(128)S(6)} %select_n.14), kind=kLoop, calls=%fused_computation | loop fusion | bytes 262152 | tf_op jit(solution)/shard_map/dynamic_slice | solution.py:482
  1.5 0.7 %collective-permute-start.1 = (bf16[256,128]{1,0:T(8,128)(2,1)S(1)}, bf16[256,128]{1,0:T(8,128)(2,1)S(1)}, u32[]{:S(2)}, u32[]{:S(2)}) collective-permute-start(bf16[256,128]{1,0:T(8,128)(2,1)S(1)} %get-tuple-element.82), channel_id=1, source_target_pairs={{1,2},{3,4},{5,6},{7,8},{9,10},{11,12},{13,14},{15,16},{17,18},{19... | collective-permute-start | bytes 196616 | tf_op jit(solution)/shard_map/ppermute | solution.py:437
  2.2 5.9 %collective-permute-start = (bf16[256,128]{1,0:T(8,128)(2,1)S(1)}, bf16[256,128]{1,0:T(8,128)(2,1)S(1)}, u32[]{:S(2)}, u32[]{:S(2)}) collective-permute-start(bf16[256,128]{1,0:T(8,128)(2,1)S(1)} %get-tuple-element.83), channel_id=1, source_target_pairs={{0,1},{2,3},{4,5},{6,7},{8,9},{10,11},{12,13},{14,15},{16,17},{18,... | collective-permute-start | bytes 196616 | tf_op jit(solution)/shard_map/ppermute | solution.py:437
  8.1 0.0 copy-start
  8.1 0.7 %copy-done = s32[12,4]{0,1:T(4,128)S(1)} copy-done((s32[12,4]{0,1:T(4,128)S(1)}, s32[12,4]{0,1:T(4,128)}, u32[]{:S(2)}) %copy-start) | copy-done | bytes 216
  8.8 6.4 %inner_rows.1 = (bf16[1536,128]{1,0:T(8,128)(2,1)S(1)}, bf16[128,128]{1,0:T(8,128)(2,1)S(1)}, bf16[256,128]{1,0:T(8,128)(2,1)S(1)}, bf16[128,128]{1,0:T(8,128)(2...) custom-call(s32[4,12]{1,0:T(4,128)S(1)} %bitcast.9, ...), custom_call_target="tpu_custom_call" | custom-call | flops 700000000 | bytes 1000000 | tf_op jit(solution)/shard_map/inner_rows/pallas_call | solution.py:444
  15.2 0.0 collective-permute-done.1.got_odd_ref
  15.2 0.0 collective-permute-done.got_even_ref
  15.2 2.5 %outer_rows.1 = (bf16[32,24,128]{2,1,0:T(8,128)(2,1)}, bf16[2,128,128]{2,1,0:T(8,128)(2,1)S(1)}, bf16[2,128,128]{2,1,0:T(8,128)(2,1)S(1)}, bf16[128,512]{1,0:T(8...) custom-call(bf16[256,128]{1,0:T(8,128)(2,1)S(1)} %collective-permute-done.got_even_ref, ...), custom_call_target="tpu_custom_call" | custom-call | flops 300000000 | bytes 1000000 | tf_op jit(solution)/shard_map/outer_rows/pallas_call | solution.py:444
  17.7 4.2 %all-to-all-start = ((bf16[32,24,128]{2,1,0:T(8,128)(2,1)}), bf16[32,24,128]{2,1,0:T(8,128)(2,1)S(1)}, u32[]{:S(2)}, u32[]{:S(2)}) async-start(bf16[32,24,128]{2,1,0:T(8,128)(2,1)} %get-tuple-element.61), calls=%async_computation | async-start | bytes 393216 | tf_op jit(solution)/shard_map/all_to_all | solution.py:595
  21.9 0.7 %collective-permute-start.2 = (bf16[2,128,128]{2,1,0:T(8,128)(2,1)S(1)}, bf16[2,128,128]{2,1,0:T(8,128)(2,1)S(1)}, u32[]{:S(2)}, u32[]{:S(2)}) collective-permute-start(bf16[2,128,128]{2,1,0:T(8,128)(2,1)S(1)} %get-tuple-element.63), channel_id=1, source_target_pairs={{1,2},{3,4},{5,6},{7,8},{9,10},{11,12},{13,14},{15,16},{17,18},{19... | collective-permute-start | bytes 196616 | tf_op jit(solution)/shard_map/ppermute | solution.py:437
  22.6 4.5 %collective-permute-start.3 = (bf16[2,128,128]{2,1,0:T(8,128)(2,1)S(1)}, bf16[2,128,128]{2,1,0:T(8,128)(2,1)S(1)}, u32[]{:S(2)}, u32[]{:S(2)}) collective-permute-start(bf16[2,128,128]{2,1,0:T(8,128)(2,1)S(1)} %get-tuple-element.64), channel_id=1, source_target_pairs={{0,1},{2,3},{4,5},{6,7},{8,9},{10,11},{12,13},{14,15},{16,17},{18,... | collective-permute-start | bytes 196616 | tf_op jit(solution)/shard_map/ppermute | solution.py:437
  27.2 4.2 %all-to-all-done.parts_ref = bf16[32,24,128]{2,1,0:T(8,128)(2,1)S(1)} async-done(((bf16[32,24,128]{2,1,0:T(8,128)(2,1)}), bf16[32,24,128]{2,1,0:T(8,128)(2,1)S(1)}, u32[]{:S(2)}, u32[]{:S(2)}) %all-to-all-start) | async-done | bytes 196640 | tf_op jit(solution)/shard_map/all_to_all | solution.py:595
  31.3 0.7 %sum.1 = (bf16[32,16,128]{2,1,0:T(8,128)(2,1)}, f32[8,128]{1,0:T(8,128)S(1)}) custom-call(bf16[32,24,128]{2,1,0:T(8,128)(2,1)S(1)} %all-to-all-done.parts_ref), custom_call_target="tpu_custom_call" | custom-call | bytes 1000000 | tf_op jit(solution)/shard_map/sum/pallas_call | solution.py:444
  32.0 0.0 collective-permute-done.2.odd_ref
  32.0 0.0 collective-permute-done.3.even_ref
  32.0 3.9 %all-to-all-start.1 = ((bf16[32,16,128]{2,1,0:T(8,128)(2,1)}), bf16[32,16,128]{2,1,0:T(8,128)(2,1)S(1)}, u32[]{:S(2)}, u32[]{:S(2)}) async-start(bf16[32,16,128]{2,1,0:T(8,128)(2,1)} %get-tuple-element.75), calls=%async_computation.1 | async-start | bytes 262144 | tf_op jit(solution)/shard_map/all_to_all | solution.py:634
  36.0 1.3 %results.1 = (bf16[1536,128]{1,0:T(8,128)(2,1)}, bf16[1536,128]{1,0:T(8,128)(2,1)}, f32[1,128]{1,0:T(1,128)}, f32[1,128]{1,0:T(1,128)}, f32[1,128]{1,0:T(1,128)}) custom-call(bf16[2,128,128]{2,1,0:T(8,128)(2,1)S(1)} %collective-permute-done.3.even_ref, bf16[2,128,128]{2,1,0:T(8,128)(2,1)S(1)} %collective-permute-done.2.odd_ref, ...), custom_call_target="tpu_custom_call" | custom-call | flops 100000000 | bytes 1000000 | tf_op jit(solution)/shard_map/results/pallas_call | solution.py:444
  37.3 7.1 %all-to-all-done.1 = bf16[32,16,128]{2,1,0:T(8,128)(2,1)S(1)} async-done(((bf16[32,16,128]{2,1,0:T(8,128)(2,1)}), bf16[32,16,128]{2,1,0:T(8,128)(2,1)S(1)}, u32[]{:S(2)}, u32[]{:S(2)}) %all-to-all-start.1) | async-done | bytes 131104 | tf_op jit(solution)/shard_map/all_to_all | solution.py:634
  44.4 0.7 %unpack.1 = (f32[128,128]{1,0:T(8,128)}, f32[256,128]{1,0:T(8,128)}, f32[128,128]{1,0:T(8,128)}) custom-call(bf16[512,128]{1,0:T(8,128)(2,1)S(1)} %bitcast.8), custom_call_target="tpu_custom_call" | custom-call | bytes 1000000 | tf_op jit(solution)/shard_map/unpack/pallas_call | solution.py:444
Async XLA Ops:
  1.5 13.7 %collective-permute-start.1 = (bf16[256,128]{1,0:T(8,128)(2,1)S(1)}, bf16[256,128]{1,0:T(8,128)(2,1)S(1)}, u32[]{:S(2)}, u32[]{:S(2)}) collective-permute-start(bf16[256,128]{1,0:T(8,128)(2,1)S(1)} %get-tuple-element.82), channel_id=1, source_target_pairs={{1,2},{3,4},{5,6},{7,8},{9,10},{11,12},{13,14},{15,16},{17,18},{19... | collective-permute-start | bytes 196616 | tf_op jit(solution)/shard_map/ppermute | solution.py:437
  2.2 13.0 %collective-permute-start = (bf16[256,128]{1,0:T(8,128)(2,1)S(1)}, bf16[256,128]{1,0:T(8,128)(2,1)S(1)}, u32[]{:S(2)}, u32[]{:S(2)}) collective-permute-start(bf16[256,128]{1,0:T(8,128)(2,1)S(1)} %get-tuple-element.83), channel_id=1, source_target_pairs={{0,1},{2,3},{4,5},{6,7},{8,9},{10,11},{12,13},{14,15},{16,17},{18,... | collective-permute-start | bytes 196616 | tf_op jit(solution)/shard_map/ppermute | solution.py:437
  8.1 0.7 %copy-start = (s32[12,4]{0,1:T(4,128)S(1)}, s32[12,4]{0,1:T(4,128)}, u32[]{:S(2)}) copy-start(s32[12,4]{0,1:T(4,128)} %param.17) | copy-start | bytes 580
  17.7 13.6 %all-to-all-start = ((bf16[32,24,128]{2,1,0:T(8,128)(2,1)}), bf16[32,24,128]{2,1,0:T(8,128)(2,1)S(1)}, u32[]{:S(2)}, u32[]{:S(2)}) async-start(bf16[32,24,128]{2,1,0:T(8,128)(2,1)} %get-tuple-element.61), calls=%async_computation | async-start | bytes 393216 | tf_op jit(solution)/shard_map/all_to_all | solution.py:595
  21.9 10.1 %collective-permute-start.2 = (bf16[2,128,128]{2,1,0:T(8,128)(2,1)S(1)}, bf16[2,128,128]{2,1,0:T(8,128)(2,1)S(1)}, u32[]{:S(2)}, u32[]{:S(2)}) collective-permute-start(bf16[2,128,128]{2,1,0:T(8,128)(2,1)S(1)} %get-tuple-element.63), channel_id=1, source_target_pairs={{1,2},{3,4},{5,6},{7,8},{9,10},{11,12},{13,14},{15,16},{17,18},{19... | collective-permute-start | bytes 196616 | tf_op jit(solution)/shard_map/ppermute | solution.py:437
  22.6 9.4 %collective-permute-start.3 = (bf16[2,128,128]{2,1,0:T(8,128)(2,1)S(1)}, bf16[2,128,128]{2,1,0:T(8,128)(2,1)S(1)}, u32[]{:S(2)}, u32[]{:S(2)}) collective-permute-start(bf16[2,128,128]{2,1,0:T(8,128)(2,1)S(1)} %get-tuple-element.64), channel_id=1, source_target_pairs={{0,1},{2,3},{4,5},{6,7},{8,9},{10,11},{12,13},{14,15},{16,17},{18,... | collective-permute-start | bytes 196616 | tf_op jit(solution)/shard_map/ppermute | solution.py:437
  32.0 12.3 %all-to-all-start.1 = ((bf16[32,16,128]{2,1,0:T(8,128)(2,1)}), bf16[32,16,128]{2,1,0:T(8,128)(2,1)S(1)}, u32[]{:S(2)}, u32[]{:S(2)}) async-start(bf16[32,16,128]{2,1,0:T(8,128)(2,1)} %get-tuple-element.75), calls=%async_computation.1 | async-start | bytes 262144 | tf_op jit(solution)/shard_map/all_to_all | solution.py:634

commit v6 on v5

--- a/solution.py
+++ b/solution.py
@@ -10,7 +10,7 @@
 
 WIN = 2
 BAND = 2 * WIN + 1
-GROUP = 4
+GROUP = 2
 epsilon = 1e-05
 AXES = ("dom", "feat")
 BF16, F32 = jnp.bfloat16, jnp.float32
@@ -79,21 +79,37 @@
     return dot_nt(jnp.concatenate([active_t, ones], axis=0), d_norm_t)
 
 
+def fetch_kernel(*refs):
+    count = (len(refs) - 3) // 2
+    sources, targets = refs[:count], refs[count : 2 * count]
+    even_side_ref, odd_side_ref, arrived = refs[2 * count :]
+    copies = [
+        pltpu.make_async_copy(source, target, arrived.at[k])
+        for k, (source, target) in enumerate(zip(sources, targets))
+    ]
+    for copy in copies:
+        copy.start()
+    copies[0].wait()
+    state, edge = targets[0], even_side_ref.shape[0]
+    odd = device_is_odd()
+    head, tail = state[pl.ds(0, edge), :], state[pl.ds(state.shape[0] - edge, edge), :]
+    even_side_ref[...] = jnp.where(odd, head, tail)
+    odd_side_ref[...] = jnp.where(odd, tail, head)
+    for copy in copies[1:]:
+        copy.wait()
+
+
 def inner_kernel(
-    col_ref,
-    state_hbm,
-    cot_hbm,
+    col_hbm,
     counts_hbm,
-    w_msg_hbm,
-    w_first_hbm,
-    b_first_hbm,
-    w_second_hbm,
-    b_second_hbm,
-    gain_hbm,
     state_ref,
+    cot_ref,
     w_msg_ref,
     w_first_ref,
     w_second_ref,
+    b_first_ref,
+    b_second_ref,
+    gain_ref,
     first_t_ref,
     second_t_ref,
     columns_ref,
@@ -108,11 +124,8 @@
     second_sums_ref,
     msg_sums_ref,
     gain_sums_ref,
-    cot_ref,
+    col_ref,
     counts_ref,
-    b_first_ref,
-    b_second_ref,
-    gain_ref,
     messages,
     band,
     arrived,
@@ -123,29 +136,17 @@
     inner_rows = range(WIN, blocks - WIN)
     part = blocks // 4
 
-    copies = [
-        (state_hbm, state_ref),
-        (w_msg_hbm, w_msg_ref),
-        (w_first_hbm, w_first_ref),
-        (b_first_hbm, b_first_ref),
-        (w_second_hbm, w_second_ref),
-        (b_second_hbm, b_second_ref),
-        (gain_hbm, gain_ref),
-    ]
-    early = len(copies)
+    copies = [(col_hbm, col_ref)]
     copies += [
         (counts_hbm.at[pl.ds(b, part)], counts_ref.at[pl.ds(b, part)])
         for b in range(0, blocks, part)
     ]
-    copies.append((cot_hbm, cot_ref))
     copies = [
         pltpu.make_async_copy(source, target, arrived.at[k])
         for k, (source, target) in enumerate(copies)
     ]
     for copy in copies:
         copy.start()
-    for copy in copies[:early]:
-        copy.wait()
 
     def rows(block, count=1):
         return pl.ds(block * size, count * size)
@@ -165,10 +166,10 @@
     for k, b in enumerate(edge_rows):
         edge_state_ref[:, rows(k)] = state_t[b]
 
-    for copy in copies[early:]:
-        copy.wait()
     for k, b in enumerate(edge_rows):
         edge_cot_ref[:, rows(k)] = cot_ref[rows(b), :].T
+    for copy in copies:
+        copy.wait()
     nothing = jnp.zeros((size, size), BF16)
     places = [(band, k, b) for k, b in enumerate(inner_rows)]
     places += [(edge_band_ref, k, b) for k, b in enumerate(edge_rows)]
@@ -437,10 +438,9 @@
     return lax.ppermute(block, AXES, [(i, i + 1) for i in lower] + [(i + 1, i) for i in lower])
 
 
-def call(kernel, name, outs, operands, scratch=(), limit=16, smem=0, flops=0):
-    specs = [pl.BlockSpec(memory_space=pltpu.SMEM)] * smem
-    specs += [pl.BlockSpec(memory_space=space) for _, space in operands[smem:]]
-    arrays = list(operands[:smem]) + [kept(array, space) for array, space in operands[smem:]]
+def call(kernel, name, outs, operands, scratch=(), limit=16, flops=0):
+    specs = [pl.BlockSpec(memory_space=space) for _, space in operands]
+    arrays = [kept(array, space) for array, space in operands]
     return pl.pallas_call(
         kernel,
         out_shape=tuple(outs),
@@ -477,20 +477,30 @@
     vmem, hbm = pltpu.VMEM, pltpu.HBM
     result = jax.ShapeDtypeStruct
 
-    edge_rows = WIN * size
-    odd = lax.axis_index(AXES) % 2
-    side = lambda upper: lax.dynamic_slice_in_dim(
-        node_state, upper * (nodes - edge_rows), edge_rows, 0
-    )
-    got_odd = swapped(side(odd), 1)
-    got_even = swapped(side(1 - odd), 0)
     row = lambda vector: vector.reshape(1, features)
+    sources = (
+        node_state,
+        cotangent,
+        w_msg,
+        w_first,
+        w_second,
+        row(b_first),
+        row(b_second),
+        row(ln_gain),
+    )
+    *fetched, even_side, odd_side = call(
+        fetch_kernel,
+        "fetch",
+        [vmem(array.shape, array.dtype) for array in sources]
+        + [vmem((WIN * size, features), BF16)] * 2,
+        [(array, hbm) for array in sources],
+        scratch=(pltpu.SemaphoreType.DMA((len(sources),)),),
+    )
+    state, cot_here, w_msg_here, w_first_here, w_second_here, *vectors = fetched
+    got_even = swapped(even_side, 0)
+    got_odd = swapped(odd_side, 1)
 
     (
-        state,
-        w_msg_here,
-        w_first_here,
-        w_second_here,
         first_t,
         second_t,
         columns,
@@ -509,10 +519,6 @@
         inner_kernel,
         "inner_rows",
         (
-            vmem((nodes, features), BF16),
-            vmem((features, features), BF16),
-            vmem((2 * features, features), BF16),
-            vmem((features, features), BF16),
             vmem((features, 2 * features), BF16),
             vmem((features, features), BF16),
             vmem((3, features, size), F32),
@@ -528,30 +534,19 @@
             vmem((features, features), F32),
             vmem((features, size), F32),
         ),
-        (
-            col_index.T,
-            (node_state, hbm),
-            (cotangent, hbm),
-            (edge_counts, hbm),
-            (w_msg, hbm),
-            (w_first, hbm),
-            (row(b_first), hbm),
-            (w_second, hbm),
-            (row(b_second), hbm),
-            (row(ln_gain), hbm),
-        ),
+        [(col_index.T, hbm), (edge_counts, hbm)]
+        + [
+            (array, vmem)
+            for array in (state, cot_here, w_msg_here, w_first_here, w_second_here, *vectors)
+        ],
         scratch=(
-            vmem((nodes, features), BF16),
+            pltpu.SMEM((tiles, blocks), jnp.int32),
             vmem(edge_counts.shape, jnp.int32),
-            vmem((1, features), F32),
-            vmem((1, features), F32),
-            vmem((1, features), F32),
             vmem((nodes, features), BF16),
             vmem((inner, BAND, size, size), BF16),
-            pltpu.SemaphoreType.DMA((12,)),
+            pltpu.SemaphoreType.DMA((5,)),
         ),
         limit=32,
-        smem=1,
         flops=700_000_000,
     )
 
@@ -593,16 +588,15 @@
     )
 
     parts = lax.all_to_all(grads, AXES, 0, 0, tiled=True)
+    owed_even = swapped(send_even, 0)
     owed_odd = swapped(send_odd, 1)
-    owed_even = swapped(send_even, 0)
     spread, bias = call(
         sum_kernel,
         "sum",
         (vmem((devices, chunk, features), SENT), vmem((BIAS_ROWS, features), F32)),
         [(parts, vmem)],
-    )
-    spread, owed_odd, owed_even = lax.optimization_barrier((spread, owed_odd, owed_even))
-
+        flops=10_000_000_000,
+    )
     updated, grad_state, g_b_first, g_b_second, g_gain = call(
         result_kernel,
         "results",
@@ -628,7 +622,7 @@
                 bias,
             )
         ],
-        flops=100_000_000,
+        flops=50_000_000_000,
     )
 
     whole = lax.all_to_all(spread, AXES, 0, 0, tiled=True)

time: 45.4 us -> 44.5 us (0.980)
  starting transfers between devices: 19.9 us -> 15.8 us
  waiting for transfers between devices: 11.3 us -> 14 us
  Pallas kernels: 11.6 us -> 13.7 us
  local copies, waits for them, and re-layouts: 1.57 us -> 0 us
    ppermute x4, starting transfers between devices: 11.8 us -> 6.23 us  [swapped(): lax.ppermute(block, AXES, [(i, i + 1) for i in lower] + [(i + 1, i) for i...]
    all_to_all x1, starting transfers between devices: 4.18 us -> 7.02 us  [shards(): parts = lax.all_to_all(grads, AXES, 0, 0, tiled=True)]
    all_to_all x1, waiting for transfers between devices: 4.19 us -> 6.91 us  [shards(): parts = lax.all_to_all(grads, AXES, 0, 0, tiled=True)]
    pallas_call x5 -> x6, Pallas kernels: 11.6 us -> 13.7 us  [call(): pl.pallas_call(kernel, out_shape=tuple(outs), in_specs=specs, out_specs=t...]
    all_to_all x1, starting transfers between devices: 3.92 us -> 2.58 us  [shards(): whole = lax.all_to_all(spread, AXES, 0, 0, tiled=True)]
    dynamic_slice x1 -> x0, local copies, waits for them, and re-layouts: 0.89 us -> none  [shards(): lax.dynamic_slice_in_dim(node_state, upper * (nodes - edge_rows), edge_ro...]
    unnamed x2 -> x0, local copies, waits for them, and re-layouts: 0.68 us -> none
  transfers between devices with their start and end apart: 6 -> 6, of which waited for: 2 -> 2; matrix products, arithmetic and copies ran while one was open for 0% -> 0% of each run, Pallas kernels for 19% -> 21%
where the time goes in v6:
time: 44.5 us; the launch traced here: 44.2 us
  starting transfers between devices  15.8 us (36%)
  waiting for transfers between devices  14 us (31%)
  Pallas kernels  13.7 us (31%)
  between operations  0.72 us (2%)
    pallas_call x6, Pallas kernels, call(): pl.pallas_call(kernel, out_shape=tuple(outs), in_specs=specs, out_specs=t...  13.7 us
    all_to_all x1, waiting for transfers between devices, shards(): whole = lax.all_to_all(spread, AXES, 0, 0, tiled=True)  7.08 us
    all_to_all x1, starting transfers between devices, shards(): parts = lax.all_to_all(grads, AXES, 0, 0, tiled=True)  7.02 us
    all_to_all x1, waiting for transfers between devices, shards(): parts = lax.all_to_all(grads, AXES, 0, 0, tiled=True)  6.91 us
    ppermute x4, starting transfers between devices, swapped(): lax.ppermute(block, AXES, [(i, i + 1) for i in lower] + [(i + 1, i) for i...  6.23 us
    all_to_all x1, starting transfers between devices, shards(): whole = lax.all_to_all(spread, AXES, 0, 0, tiled=True)  2.58 us
  transfers between devices with their start and end apart: 6, of which 2 were waited for; matrix products, arithmetic and copies ran while one was open for 0% of the time, Pallas kernels for 21%

profile of v6, /device:TPU:0, one launch (start us, length us, event | category | flops | bytes accessed | tf_op | source)
XLA Modules:
  0.0 44.2 jit_solution(269017143684809895)
XLA Ops:
  0.6 1.2 %fetch.1 = (bf16[1536,128]{1,0:T(8,128)(2,1)S(1)}, bf16[1536,128]{1,0:T(8,128)(2,1)S(1)}, bf16[128,128]{1,0:T(8,128)(2,1)S(1)}, bf16[256,128]{1,0:T(8,128)(2,1)S...) custom-call(bf16[1536,128]{1,0:T(8,128)(2,1)} %refs_0_.1, ...), custom_call_target="tpu_custom_call" | custom-call | bytes 1000000 | tf_op jit(solution)/shard_map/fetch/pallas_call | solution.py:444
  1.8 3.1 %collective-permute-start = (bf16[256,128]{1,0:T(8,128)(2,1)S(1)}, bf16[256,128]{1,0:T(8,128)(2,1)S(1)}, u32[]{:S(2)}, u32[]{:S(2)}) collective-permute-start(bf16[256,128]{1,0:T(8,128)(2,1)S(1)} %get-tuple-element.48), channel_id=1, source_target_pairs={{0,1},{2,3},{4,5},{6,7},{8,9},{10,11},{12,13},{14,15},{16,17},{18,... | collective-permute-start | bytes 196616 | tf_op jit(solution)/shard_map/ppermute | solution.py:438
  4.9 0.7 %collective-permute-start.1 = (bf16[256,128]{1,0:T(8,128)(2,1)S(1)}, bf16[256,128]{1,0:T(8,128)(2,1)S(1)}, u32[]{:S(2)}, u32[]{:S(2)}) collective-permute-start(bf16[256,128]{1,0:T(8,128)(2,1)S(1)} %get-tuple-element.49), channel_id=1, source_target_pairs={{1,2},{3,4},{5,6},{7,8},{9,10},{11,12},{13,14},{15,16},{17,18},{19... | collective-permute-start | bytes 196616 | tf_op jit(solution)/shard_map/ppermute | solution.py:438
  5.6 7.3 %inner_rows.1 = (bf16[128,256]{1,0:T(8,128)(2,1)S(1)}, bf16[128,128]{1,0:T(8,128)(2,1)S(1)}, f32[3,128,128]{2,1,0:T(8,128)S(1)}, bf16[128,512]{1,0:T(8,128)(2,1)...) custom-call(s32[4,12]{1,0:T(4,128)} %bitcast.9, ...), custom_call_target="tpu_custom_call" | custom-call | flops 700000000 | bytes 1000000 | tf_op jit(solution)/shard_map/inner_rows/pallas_call | solution.py:444
  12.9 0.0 collective-permute-done.got_even_ref
  12.9 0.0 collective-permute-done.1.got_odd_ref
  12.9 2.5 %outer_rows.1 = (bf16[32,24,128]{2,1,0:T(8,128)(2,1)}, bf16[2,128,128]{2,1,0:T(8,128)(2,1)S(1)}, bf16[2,128,128]{2,1,0:T(8,128)(2,1)S(1)}, bf16[128,512]{1,0:T(8...) custom-call(bf16[256,128]{1,0:T(8,128)(2,1)S(1)} %collective-permute-done.got_even_ref, ...), custom_call_target="tpu_custom_call" | custom-call | flops 300000000 | bytes 1000000 | tf_op jit(solution)/shard_map/outer_rows/pallas_call | solution.py:444
  15.4 7.0 %all-to-all-start = ((bf16[32,24,128]{2,1,0:T(8,128)(2,1)}), bf16[32,24,128]{2,1,0:T(8,128)(2,1)S(1)}, u32[]{:S(2)}, u32[]{:S(2)}) async-start(bf16[32,24,128]{2,1,0:T(8,128)(2,1)} %get-tuple-element.77), calls=%async_computation | async-start | bytes 393216 | tf_op jit(solution)/shard_map/all_to_all | solution.py:590
  22.4 1.8 %collective-permute-start.2 = (bf16[2,128,128]{2,1,0:T(8,128)(2,1)S(1)}, bf16[2,128,128]{2,1,0:T(8,128)(2,1)S(1)}, u32[]{:S(2)}, u32[]{:S(2)}) collective-permute-start(bf16[2,128,128]{2,1,0:T(8,128)(2,1)S(1)} %get-tuple-element.70), channel_id=1, source_target_pairs={{0,1},{2,3},{4,5},{6,7},{8,9},{10,11},{12,13},{14,15},{16,17},{18,... | collective-permute-start | bytes 196616 | tf_op jit(solution)/shard_map/ppermute | solution.py:438
  24.3 0.7 %collective-permute-start.3 = (bf16[2,128,128]{2,1,0:T(8,128)(2,1)S(1)}, bf16[2,128,128]{2,1,0:T(8,128)(2,1)S(1)}, u32[]{:S(2)}, u32[]{:S(2)}) collective-permute-start(bf16[2,128,128]{2,1,0:T(8,128)(2,1)S(1)} %get-tuple-element.71), channel_id=1, source_target_pairs={{1,2},{3,4},{5,6},{7,8},{9,10},{11,12},{13,14},{15,16},{17,18},{19... | collective-permute-start | bytes 196616 | tf_op jit(solution)/shard_map/ppermute | solution.py:438
  24.9 6.9 %all-to-all-done.parts_ref = bf16[32,24,128]{2,1,0:T(8,128)(2,1)S(1)} async-done(((bf16[32,24,128]{2,1,0:T(8,128)(2,1)}), bf16[32,24,128]{2,1,0:T(8,128)(2,1)S(1)}, u32[]{:S(2)}, u32[]{:S(2)}) %all-to-all-start) | async-done | bytes 196640 | tf_op jit(solution)/shard_map/all_to_all | solution.py:590
  31.8 0.7 %sum.1 = (bf16[32,16,128]{2,1,0:T(8,128)(2,1)}, f32[8,128]{1,0:T(8,128)S(1)}) custom-call(bf16[32,24,128]{2,1,0:T(8,128)(2,1)S(1)} %all-to-all-done.parts_ref), custom_call_target="tpu_custom_call" | custom-call | flops 10000000000 | bytes 1000000 | tf_op jit(solution)/shard_map/sum/pallas_call | solution.py:444
  32.5 2.6 %all-to-all-start.1 = ((bf16[32,16,128]{2,1,0:T(8,128)(2,1)}), bf16[32,16,128]{2,1,0:T(8,128)(2,1)S(1)}, u32[]{:S(2)}, u32[]{:S(2)}) async-start(bf16[32,16,128]{2,1,0:T(8,128)(2,1)} %get-tuple-element.81), calls=%async_computation.1 | async-start | bytes 262144 | tf_op jit(solution)/shard_map/all_to_all | solution.py:628
  35.1 0.0 collective-permute-done.2.even_ref
  35.1 0.0 collective-permute-done.3.odd_ref
  35.1 1.3 %results.1 = (bf16[1536,128]{1,0:T(8,128)(2,1)}, bf16[1536,128]{1,0:T(8,128)(2,1)}, f32[1,128]{1,0:T(1,128)}, f32[1,128]{1,0:T(1,128)}, f32[1,128]{1,0:T(1,128)}) custom-call(bf16[2,128,128]{2,1,0:T(8,128)(2,1)S(1)} %collective-permute-done.2.even_ref, bf16[2,128,128]{2,1,0:T(8,128)(2,1)S(1)} %collective-permute-done.3.odd_ref, ...), custom_call_target="tpu_custom_call" | custom-call | flops 49999998976 | bytes 1000000 | tf_op jit(solution)/shard_map/results/pallas_call | solution.py:444
  36.4 7.1 %all-to-all-done.1 = bf16[32,16,128]{2,1,0:T(8,128)(2,1)S(1)} async-done(((bf16[32,16,128]{2,1,0:T(8,128)(2,1)}), bf16[32,16,128]{2,1,0:T(8,128)(2,1)S(1)}, u32[]{:S(2)}, u32[]{:S(2)}) %all-to-all-start.1) | async-done | bytes 131104 | tf_op jit(solution)/shard_map/all_to_all | solution.py:628
  43.5 0.7 %unpack.1 = (f32[128,128]{1,0:T(8,128)}, f32[256,128]{1,0:T(8,128)}, f32[128,128]{1,0:T(8,128)}) custom-call(bf16[512,128]{1,0:T(8,128)(2,1)S(1)} %bitcast.8), custom_call_target="tpu_custom_call" | custom-call | bytes 1000000 | tf_op jit(solution)/shard_map/unpack/pallas_call | solution.py:444
Async XLA Ops:
  1.8 11.0 %collective-permute-start = (bf16[256,128]{1,0:T(8,128)(2,1)S(1)}, bf16[256,128]{1,0:T(8,128)(2,1)S(1)}, u32[]{:S(2)}, u32[]{:S(2)}) collective-permute-start(bf16[256,128]{1,0:T(8,128)(2,1)S(1)} %get-tuple-element.48), channel_id=1, source_target_pairs={{0,1},{2,3},{4,5},{6,7},{8,9},{10,11},{12,13},{14,15},{16,17},{18,... | collective-permute-start | bytes 196616 | tf_op jit(solution)/shard_map/ppermute | solution.py:438
  4.9 8.0 %collective-permute-start.1 = (bf16[256,128]{1,0:T(8,128)(2,1)S(1)}, bf16[256,128]{1,0:T(8,128)(2,1)S(1)}, u32[]{:S(2)}, u32[]{:S(2)}) collective-permute-start(bf16[256,128]{1,0:T(8,128)(2,1)S(1)} %get-tuple-element.49), channel_id=1, source_target_pairs={{1,2},{3,4},{5,6},{7,8},{9,10},{11,12},{13,14},{15,16},{17,18},{19... | collective-permute-start | bytes 196616 | tf_op jit(solution)/shard_map/ppermute | solution.py:438
  15.4 16.4 %all-to-all-start = ((bf16[32,24,128]{2,1,0:T(8,128)(2,1)}), bf16[32,24,128]{2,1,0:T(8,128)(2,1)S(1)}, u32[]{:S(2)}, u32[]{:S(2)}) async-start(bf16[32,24,128]{2,1,0:T(8,128)(2,1)} %get-tuple-element.77), calls=%async_computation | async-start | bytes 393216 | tf_op jit(solution)/shard_map/all_to_all | solution.py:590
  22.4 12.7 %collective-permute-start.2 = (bf16[2,128,128]{2,1,0:T(8,128)(2,1)S(1)}, bf16[2,128,128]{2,1,0:T(8,128)(2,1)S(1)}, u32[]{:S(2)}, u32[]{:S(2)}) collective-permute-start(bf16[2,128,128]{2,1,0:T(8,128)(2,1)S(1)} %get-tuple-element.70), channel_id=1, source_target_pairs={{0,1},{2,3},{4,5},{6,7},{8,9},{10,11},{12,13},{14,15},{16,17},{18,... | collective-permute-start | bytes 196616 | tf_op jit(solution)/shard_map/ppermute | solution.py:438
  24.3 10.9 %collective-permute-start.3 = (bf16[2,128,128]{2,1,0:T(8,128)(2,1)S(1)}, bf16[2,128,128]{2,1,0:T(8,128)(2,1)S(1)}, u32[]{:S(2)}, u32[]{:S(2)}) collective-permute-start(bf16[2,128,128]{2,1,0:T(8,128)(2,1)S(1)} %get-tuple-element.71), channel_id=1, source_target_pairs={{1,2},{3,4},{5,6},{7,8},{9,10},{11,12},{13,14},{15,16},{17,18},{19... | collective-permute-start | bytes 196616 | tf_op jit(solution)/shard_map/ppermute | solution.py:438
  32.5 11.0 %all-to-all-start.1 = ((bf16[32,16,128]{2,1,0:T(8,128)(2,1)}), bf16[32,16,128]{2,1,0:T(8,128)(2,1)S(1)}, u32[]{:S(2)}, u32[]{:S(2)}) async-start(bf16[32,16,128]{2,1,0:T(8,128)(2,1)} %get-tuple-element.81), calls=%async_computation.1 | async-start | bytes 262144 | tf_op jit(solution)/shard_map/all_to_all | solution.py:628

commit v7 on v6

--- a/solution.py
+++ b/solution.py
@@ -10,7 +10,7 @@
 
 WIN = 2
 BAND = 2 * WIN + 1
-GROUP = 2
+GROUP = 8
 epsilon = 1e-05
 AXES = ("dom", "feat")
 BF16, F32 = jnp.bfloat16, jnp.float32
@@ -102,8 +102,8 @@
 def inner_kernel(
     col_hbm,
     counts_hbm,
+    cot_hbm,
     state_ref,
-    cot_ref,
     w_msg_ref,
     w_first_ref,
     w_second_ref,
@@ -126,6 +126,7 @@
     gain_sums_ref,
     col_ref,
     counts_ref,
+    cot_ref,
     messages,
     band,
     arrived,
@@ -141,6 +142,7 @@
         (counts_hbm.at[pl.ds(b, part)], counts_ref.at[pl.ds(b, part)])
         for b in range(0, blocks, part)
     ]
+    copies.append((cot_hbm, cot_ref))
     copies = [
         pltpu.make_async_copy(source, target, arrived.at[k])
         for k, (source, target) in enumerate(copies)
@@ -166,10 +168,10 @@
     for k, b in enumerate(edge_rows):
         edge_state_ref[:, rows(k)] = state_t[b]
 
+    for copy in copies:
+        copy.wait()
     for k, b in enumerate(edge_rows):
         edge_cot_ref[:, rows(k)] = cot_ref[rows(b), :].T
-    for copy in copies:
-        copy.wait()
     nothing = jnp.zeros((size, size), BF16)
     places = [(band, k, b) for k, b in enumerate(inner_rows)]
     places += [(edge_band_ref, k, b) for k, b in enumerate(edge_rows)]
@@ -480,7 +482,6 @@
     row = lambda vector: vector.reshape(1, features)
     sources = (
         node_state,
-        cotangent,
         w_msg,
         w_first,
         w_second,
@@ -496,7 +497,7 @@
         [(array, hbm) for array in sources],
         scratch=(pltpu.SemaphoreType.DMA((len(sources),)),),
     )
-    state, cot_here, w_msg_here, w_first_here, w_second_here, *vectors = fetched
+    state, w_msg_here, w_first_here, w_second_here, *vectors = fetched
     got_even = swapped(even_side, 0)
     got_odd = swapped(odd_side, 1)
 
@@ -534,17 +535,18 @@
             vmem((features, features), F32),
             vmem((features, size), F32),
         ),
-        [(col_index.T, hbm), (edge_counts, hbm)]
+        [(col_index.T, hbm), (edge_counts, hbm), (cotangent, hbm)]
         + [
             (array, vmem)
-            for array in (state, cot_here, w_msg_here, w_first_here, w_second_here, *vectors)
+            for array in (state, w_msg_here, w_first_here, w_second_here, *vectors)
         ],
         scratch=(
             pltpu.SMEM((tiles, blocks), jnp.int32),
             vmem(edge_counts.shape, jnp.int32),
             vmem((nodes, features), BF16),
+            vmem((nodes, features), BF16),
             vmem((inner, BAND, size, size), BF16),
-            pltpu.SemaphoreType.DMA((5,)),
+            pltpu.SemaphoreType.DMA((6,)),
         ),
         limit=32,
         flops=700_000_000,

time: 44.5 us -> 42 us (0.944)
  Pallas kernels: 13.7 us -> 11.2 us
    pallas_call x6, Pallas kernels: 13.7 us -> 11.2 us  [call(): pl.pallas_call(kernel, out_shape=tuple(outs), in_specs=specs, out_specs=t...]
  transfers between devices with their start and end apart: 6 -> 6, of which waited for: 2 -> 2; matrix products, arithmetic and copies ran while one was open for 0% -> 0% of each run, Pallas kernels for 21% -> 16%
where the time goes in v7:
time: 42 us; the launch traced here: 41.8 us
  starting transfers between devices  15.8 us (38%)
  waiting for transfers between devices  14 us (33%)
  Pallas kernels  11.2 us (27%)
  between operations  0.72 us (2%)
    pallas_call x6, Pallas kernels, call(): pl.pallas_call(kernel, out_shape=tuple(outs), in_specs=specs, out_specs=t...  11.2 us
    all_to_all x1, waiting for transfers between devices, shards(): whole = lax.all_to_all(spread, AXES, 0, 0, tiled=True)  7.08 us
    all_to_all x1, starting transfers between devices, shards(): parts = lax.all_to_all(grads, AXES, 0, 0, tiled=True)  7.03 us
    all_to_all x1, waiting for transfers between devices, shards(): parts = lax.all_to_all(grads, AXES, 0, 0, tiled=True)  6.91 us
    ppermute x4, starting transfers between devices, swapped(): lax.ppermute(block, AXES, [(i, i + 1) for i in lower] + [(i + 1, i) for i...  6.23 us
    all_to_all x1, starting transfers between devices, shards(): whole = lax.all_to_all(spread, AXES, 0, 0, tiled=True)  2.58 us
  transfers between devices with their start and end apart: 6, of which 2 were waited for; matrix products, arithmetic and copies ran while one was open for 0% of the time, Pallas kernels for 16%

profile of v7, /device:TPU:0, one launch (start us, length us, event | category | flops | bytes accessed | tf_op | source)
XLA Modules:
  0.0 41.8 jit_solution(9070166901008259244)
XLA Ops:
  0.6 1.1 %fetch.1 = (bf16[1536,128]{1,0:T(8,128)(2,1)S(1)}, bf16[128,128]{1,0:T(8,128)(2,1)S(1)}, bf16[256,128]{1,0:T(8,128)(2,1)S(1)}, bf16[128,128]{1,0:T(8,128)(2,1)S(...) custom-call(bf16[1536,128]{1,0:T(8,128)(2,1)} %refs_0_.1, ...), custom_call_target="tpu_custom_call" | custom-call | bytes 1000000 | tf_op jit(solution)/shard_map/fetch/pallas_call | solution.py:446
  1.7 3.1 %collective-permute-start = (bf16[256,128]{1,0:T(8,128)(2,1)S(1)}, bf16[256,128]{1,0:T(8,128)(2,1)S(1)}, u32[]{:S(2)}, u32[]{:S(2)}) collective-permute-start(bf16[256,128]{1,0:T(8,128)(2,1)S(1)} %get-tuple-element.47), channel_id=1, source_target_pairs={{0,1},{2,3},{4,5},{6,7},{8,9},{10,11},{12,13},{14,15},{16,17},{18,... | collective-permute-start | bytes 196616 | tf_op jit(solution)/shard_map/ppermute | solution.py:440
  4.8 0.7 %collective-permute-start.1 = (bf16[256,128]{1,0:T(8,128)(2,1)S(1)}, bf16[256,128]{1,0:T(8,128)(2,1)S(1)}, u32[]{:S(2)}, u32[]{:S(2)}) collective-permute-start(bf16[256,128]{1,0:T(8,128)(2,1)S(1)} %get-tuple-element.48), channel_id=1, source_target_pairs={{1,2},{3,4},{5,6},{7,8},{9,10},{11,12},{13,14},{15,16},{17,18},{19... | collective-permute-start | bytes 196616 | tf_op jit(solution)/shard_map/ppermute | solution.py:440
  5.5 4.9 %inner_rows.1 = (bf16[128,256]{1,0:T(8,128)(2,1)S(1)}, bf16[128,128]{1,0:T(8,128)(2,1)S(1)}, f32[3,128,128]{2,1,0:T(8,128)S(1)}, bf16[128,512]{1,0:T(8,128)(2,1)...) custom-call(s32[4,12]{1,0:T(4,128)} %bitcast.9, ...), custom_call_target="tpu_custom_call" | custom-call | flops 700000000 | bytes 1000000 | tf_op jit(solution)/shard_map/inner_rows/pallas_call | solution.py:446
  10.4 0.0 collective-permute-done.got_even_ref
  10.4 0.0 collective-permute-done.1.got_odd_ref
  10.4 2.5 %outer_rows.1 = (bf16[32,24,128]{2,1,0:T(8,128)(2,1)}, bf16[2,128,128]{2,1,0:T(8,128)(2,1)S(1)}, bf16[2,128,128]{2,1,0:T(8,128)(2,1)S(1)}, bf16[128,512]{1,0:T(8...) custom-call(bf16[256,128]{1,0:T(8,128)(2,1)S(1)} %collective-permute-done.got_even_ref, ...), custom_call_target="tpu_custom_call" | custom-call | flops 300000000 | bytes 1000000 | tf_op jit(solution)/shard_map/outer_rows/pallas_call | solution.py:446
  12.9 7.0 %all-to-all-start = ((bf16[32,24,128]{2,1,0:T(8,128)(2,1)}), bf16[32,24,128]{2,1,0:T(8,128)(2,1)S(1)}, u32[]{:S(2)}, u32[]{:S(2)}) async-start(bf16[32,24,128]{2,1,0:T(8,128)(2,1)} %get-tuple-element.75), calls=%async_computation | async-start | bytes 393216 | tf_op jit(solution)/shard_map/all_to_all | solution.py:592
  20.0 1.8 %collective-permute-start.2 = (bf16[2,128,128]{2,1,0:T(8,128)(2,1)S(1)}, bf16[2,128,128]{2,1,0:T(8,128)(2,1)S(1)}, u32[]{:S(2)}, u32[]{:S(2)}) collective-permute-start(bf16[2,128,128]{2,1,0:T(8,128)(2,1)S(1)} %get-tuple-element.68), channel_id=1, source_target_pairs={{0,1},{2,3},{4,5},{6,7},{8,9},{10,11},{12,13},{14,15},{16,17},{18,... | collective-permute-start | bytes 196616 | tf_op jit(solution)/shard_map/ppermute | solution.py:440
  21.8 0.7 %collective-permute-start.3 = (bf16[2,128,128]{2,1,0:T(8,128)(2,1)S(1)}, bf16[2,128,128]{2,1,0:T(8,128)(2,1)S(1)}, u32[]{:S(2)}, u32[]{:S(2)}) collective-permute-start(bf16[2,128,128]{2,1,0:T(8,128)(2,1)S(1)} %get-tuple-element.69), channel_id=1, source_target_pairs={{1,2},{3,4},{5,6},{7,8},{9,10},{11,12},{13,14},{15,16},{17,18},{19... | collective-permute-start | bytes 196616 | tf_op jit(solution)/shard_map/ppermute | solution.py:440
  22.5 6.9 %all-to-all-done.parts_ref = bf16[32,24,128]{2,1,0:T(8,128)(2,1)S(1)} async-done(((bf16[32,24,128]{2,1,0:T(8,128)(2,1)}), bf16[32,24,128]{2,1,0:T(8,128)(2,1)S(1)}, u32[]{:S(2)}, u32[]{:S(2)}) %all-to-all-start) | async-done | bytes 196640 | tf_op jit(solution)/shard_map/all_to_all | solution.py:592
  29.4 0.7 %sum.1 = (bf16[32,16,128]{2,1,0:T(8,128)(2,1)}, f32[8,128]{1,0:T(8,128)S(1)}) custom-call(bf16[32,24,128]{2,1,0:T(8,128)(2,1)S(1)} %all-to-all-done.parts_ref), custom_call_target="tpu_custom_call" | custom-call | flops 10000000000 | bytes 1000000 | tf_op jit(solution)/shard_map/sum/pallas_call | solution.py:446
  30.1 2.6 %all-to-all-start.1 = ((bf16[32,16,128]{2,1,0:T(8,128)(2,1)}), bf16[32,16,128]{2,1,0:T(8,128)(2,1)S(1)}, u32[]{:S(2)}, u32[]{:S(2)}) async-start(bf16[32,16,128]{2,1,0:T(8,128)(2,1)} %get-tuple-element.79), calls=%async_computation.1 | async-start | bytes 262144 | tf_op jit(solution)/shard_map/all_to_all | solution.py:630
  32.6 0.0 collective-permute-done.2.even_ref
  32.7 0.0 collective-permute-done.3.odd_ref
  32.7 1.3 %results.1 = (bf16[1536,128]{1,0:T(8,128)(2,1)}, bf16[1536,128]{1,0:T(8,128)(2,1)}, f32[1,128]{1,0:T(1,128)}, f32[1,128]{1,0:T(1,128)}, f32[1,128]{1,0:T(1,128)}) custom-call(bf16[2,128,128]{2,1,0:T(8,128)(2,1)S(1)} %collective-permute-done.2.even_ref, bf16[2,128,128]{2,1,0:T(8,128)(2,1)S(1)} %collective-permute-done.3.odd_ref, ...), custom_call_target="tpu_custom_call" | custom-call | flops 49999998976 | bytes 1000000 | tf_op jit(solution)/shard_map/results/pallas_call | solution.py:446
  34.0 7.1 %all-to-all-done.1 = bf16[32,16,128]{2,1,0:T(8,128)(2,1)S(1)} async-done(((bf16[32,16,128]{2,1,0:T(8,128)(2,1)}), bf16[32,16,128]{2,1,0:T(8,128)(2,1)S(1)}, u32[]{:S(2)}, u32[]{:S(2)}) %all-to-all-start.1) | async-done | bytes 131104 | tf_op jit(solution)/shard_map/all_to_all | solution.py:630
  41.0 0.7 %unpack.1 = (f32[128,128]{1,0:T(8,128)}, f32[256,128]{1,0:T(8,128)}, f32[128,128]{1,0:T(8,128)}) custom-call(bf16[512,128]{1,0:T(8,128)(2,1)S(1)} %bitcast.8), custom_call_target="tpu_custom_call" | custom-call | bytes 1000000 | tf_op jit(solution)/shard_map/unpack/pallas_call | solution.py:446
Async XLA Ops:
  1.7 8.6 %collective-permute-start = (bf16[256,128]{1,0:T(8,128)(2,1)S(1)}, bf16[256,128]{1,0:T(8,128)(2,1)S(1)}, u32[]{:S(2)}, u32[]{:S(2)}) collective-permute-start(bf16[256,128]{1,0:T(8,128)(2,1)S(1)} %get-tuple-element.47), channel_id=1, source_target_pairs={{0,1},{2,3},{4,5},{6,7},{8,9},{10,11},{12,13},{14,15},{16,17},{18,... | collective-permute-start | bytes 196616 | tf_op jit(solution)/shard_map/ppermute | solution.py:440
  4.8 5.6 %collective-permute-start.1 = (bf16[256,128]{1,0:T(8,128)(2,1)S(1)}, bf16[256,128]{1,0:T(8,128)(2,1)S(1)}, u32[]{:S(2)}, u32[]{:S(2)}) collective-permute-start(bf16[256,128]{1,0:T(8,128)(2,1)S(1)} %get-tuple-element.48), channel_id=1, source_target_pairs={{1,2},{3,4},{5,6},{7,8},{9,10},{11,12},{13,14},{15,16},{17,18},{19... | collective-permute-start | bytes 196616 | tf_op jit(solution)/shard_map/ppermute | solution.py:440
  12.9 16.4 %all-to-all-start = ((bf16[32,24,128]{2,1,0:T(8,128)(2,1)}), bf16[32,24,128]{2,1,0:T(8,128)(2,1)S(1)}, u32[]{:S(2)}, u32[]{:S(2)}) async-start(bf16[32,24,128]{2,1,0:T(8,128)(2,1)} %get-tuple-element.75), calls=%async_computation | async-start | bytes 393216 | tf_op jit(solution)/shard_map/all_to_all | solution.py:592
  20.0 12.7 %collective-permute-start.2 = (bf16[2,128,128]{2,1,0:T(8,128)(2,1)S(1)}, bf16[2,128,128]{2,1,0:T(8,128)(2,1)S(1)}, u32[]{:S(2)}, u32[]{:S(2)}) collective-permute-start(bf16[2,128,128]{2,1,0:T(8,128)(2,1)S(1)} %get-tuple-element.68), channel_id=1, source_target_pairs={{0,1},{2,3},{4,5},{6,7},{8,9},{10,11},{12,13},{14,15},{16,17},{18,... | collective-permute-start | bytes 196616 | tf_op jit(solution)/shard_map/ppermute | solution.py:440
  21.8 10.9 %collective-permute-start.3 = (bf16[2,128,128]{2,1,0:T(8,128)(2,1)S(1)}, bf16[2,128,128]{2,1,0:T(8,128)(2,1)S(1)}, u32[]{:S(2)}, u32[]{:S(2)}) collective-permute-start(bf16[2,128,128]{2,1,0:T(8,128)(2,1)S(1)} %get-tuple-element.69), channel_id=1, source_target_pairs={{1,2},{3,4},{5,6},{7,8},{9,10},{11,12},{13,14},{15,16},{17,18},{19... | collective-permute-start | bytes 196616 | tf_op jit(solution)/shard_map/ppermute | solution.py:440
  30.1 11.0 %all-to-all-start.1 = ((bf16[32,16,128]{2,1,0:T(8,128)(2,1)}), bf16[32,16,128]{2,1,0:T(8,128)(2,1)S(1)}, u32[]{:S(2)}, u32[]{:S(2)}) async-start(bf16[32,16,128]{2,1,0:T(8,128)(2,1)} %get-tuple-element.79), calls=%async_computation.1 | async-start | bytes 262144 | tf_op jit(solution)/shard_map/all_to_all | solution.py:630

commit v8 on v7

--- a/solution.py
+++ b/solution.py
@@ -10,7 +10,6 @@
 
 WIN = 2
 BAND = 2 * WIN + 1
-GROUP = 8
 epsilon = 1e-05
 AXES = ("dom", "feat")
 BF16, F32 = jnp.bfloat16, jnp.float32
@@ -42,15 +41,21 @@
     return jnp.broadcast_to(row_ref[...], (width, row_ref.shape[1])).T
 
 
+def blocks_turned(array):
+    size = array.shape[1]
+    return [array[k : k + size].T for k in range(0, array.shape[0], size)]
+
+
 def node_layer(state_t, aggregate_t, cot_t, first_t, second_t, w_first, w_second, columns):
     features, width = state_t.shape
     b_first, b_second, gain = (
         joined_lanes([c] * (width // c.shape[1])) for c in columns
     )
     pre_hidden = dot(first_t, jnp.concatenate([state_t, aggregate_t], axis=0)) + b_first
-    sigmoid = 1.0 / (1.0 + jnp.exp(-pre_hidden))
-    active_t = (pre_hidden * sigmoid).astype(BF16)
-    slope = sigmoid * (1.0 + pre_hidden * (1.0 - sigmoid))
+    sigmoid = 0.5 * jnp.tanh(0.5 * pre_hidden) + 0.5
+    silu = pre_hidden * sigmoid
+    active_t = silu.astype(BF16)
+    slope = sigmoid + silu * (1.0 - sigmoid)
     pre_norm = dot(second_t, active_t) + b_second
     centred = pre_norm - jnp.mean(pre_norm, axis=0, keepdims=True)
     inv_std = lax.rsqrt(jnp.mean(centred * centred, axis=0, keepdims=True) + epsilon)
@@ -115,11 +120,11 @@
     columns_ref,
     edge_state_ref,
     edge_cot_ref,
-    edge_band_ref,
-    edge_msg_ref,
+    edge_sum_ref,
+    band_ref,
     updated_ref,
     direct_ref,
-    owed_ref,
+    d_aggregate_ref,
     first_sums_ref,
     second_sums_ref,
     msg_sums_ref,
@@ -127,8 +132,6 @@
     col_ref,
     counts_ref,
     cot_ref,
-    messages,
-    band,
     arrived,
 ):
     blocks, tiles, size, _ = counts_ref.shape
@@ -161,9 +164,6 @@
     second_t_ref[...] = second_t
     for k in range(3):
         columns_ref[k] = columns[k]
-    messages[...] = dot(state_ref[...], w_msg).astype(BF16)
-    edge_msg_ref[0] = messages[rows(0, 2 * WIN), :]
-    edge_msg_ref[1] = messages[rows(blocks - 2 * WIN, 2 * WIN), :]
     state_t = [state_ref[rows(b), :].T for b in range(blocks)]
     for k, b in enumerate(edge_rows):
         edge_state_ref[:, rows(k)] = state_t[b]
@@ -173,67 +173,44 @@
     for k, b in enumerate(edge_rows):
         edge_cot_ref[:, rows(k)] = cot_ref[rows(b), :].T
     nothing = jnp.zeros((size, size), BF16)
-    places = [(band, k, b) for k, b in enumerate(inner_rows)]
-    places += [(edge_band_ref, k, b) for k, b in enumerate(edge_rows)]
-    for ref, k, b in places:
+    for b in [*inner_rows, *edge_rows]:
         for place in range(BAND):
             if place != WIN:
-                ref[k, place] = nothing
-        ref[k, WIN] = counts_ref[b, 0].astype(F32).astype(BF16)
+                band_ref[b, place] = nothing
+        band_ref[b, WIN] = counts_ref[b, 0].astype(F32).astype(BF16)
         own = col_ref[0, b]
         for t in range(1, tiles):
-            ref[k, col_ref[t, b] - own + WIN] += counts_ref[b, t].astype(F32).astype(BF16)
-
-    gain_sums = jnp.zeros((features, size), F32)
-    first_sums = second_sums = 0.0
-    reached = set()
-    for start in range(0, len(inner_rows), GROUP):
-        group = inner_rows[start : start + GROUP]
-        lanes = pl.ds(start * size, len(group) * size)
-        aggregate = [
-            dot(
-                joined_lanes([band[b - WIN, place] for place in range(BAND)]),
-                messages[rows(b - WIN, BAND), :],
-            ).astype(BF16)
-            for b in group
-        ]
-        updated_t, terms, active_t, d_norm_t, d_hidden_t, direct, d_aggregate_t = node_layer(
-            joined_lanes([state_t[b] for b in group]),
-            joined_lanes([block.T for block in aggregate]),
-            joined_lanes([cot_ref[rows(b), :].T for b in group]),
-            first_t,
-            second_t,
-            w_first,
-            w_second,
-            columns,
-        )
-        updated_ref[:, lanes] = updated_t
-        direct_ref[:, lanes] = direct
-        first_sums += first_products(
-            d_hidden_t, state_ref[rows(group[0], len(group)), :], jnp.concatenate(aggregate, axis=0)
-        )
-        second_sums += second_products(active_t, d_norm_t)
-        for k, b in enumerate(group):
-            own = slice(k * size, (k + 1) * size)
-            gain_sums += terms[:, own]
-            owed = dot(
-                d_aggregate_t[:, own],
-                joined_lanes([band[b - WIN, place] for place in range(BAND)]),
-            )
-            for place in range(BAND):
-                block = b - WIN + place
-                value = owed[:, place * size : (place + 1) * size]
-                if block in reached:
-                    owed_ref[block] += value
-                else:
-                    owed_ref[block] = value
-                reached.add(block)
-    first_sums_ref[...] = first_sums
-    second_sums_ref[...] = second_sums
-    gain_sums_ref[...] = gain_sums
-    done = range(2 * WIN, blocks - 2 * WIN)
-    msg_sums_ref[...] = dot(
-        joined_lanes([owed_ref[b].astype(BF16) for b in done]), state_ref[rows(2 * WIN, len(done)), :]
+            band_ref[b, col_ref[t, b] - own + WIN] += counts_ref[b, t].astype(F32).astype(BF16)
+
+    def neighbour_sum(b):
+        first, last = max(b - WIN, 0), min(b + WIN, blocks - 1)
+        tiles_of = [band_ref[b, block - b + WIN] for block in range(first, last + 1)]
+        return dot(joined_lanes(tiles_of), state_ref[rows(first, last + 1 - first), :])
+
+    for k, b in enumerate(edge_rows):
+        edge_sum_ref[k] = neighbour_sum(b)
+    summed = jnp.concatenate([neighbour_sum(b).astype(BF16) for b in inner_rows], axis=0)
+    aggregate = dot(summed, w_msg).astype(BF16)
+    updated_t, terms, active_t, d_norm_t, d_hidden_t, direct, d_aggregate_t = node_layer(
+        joined_lanes([state_t[b] for b in inner_rows]),
+        joined_lanes(blocks_turned(aggregate)),
+        joined_lanes([cot_ref[rows(b), :].T for b in inner_rows]),
+        first_t,
+        second_t,
+        w_first,
+        w_second,
+        columns,
+    )
+    updated_ref[...] = updated_t
+    direct_ref[...] = direct
+    d_aggregate_ref[...] = d_aggregate_t
+    first_sums_ref[...] = first_products(
+        d_hidden_t, state_ref[rows(WIN, len(inner_rows)), :], aggregate
+    )
+    second_sums_ref[...] = second_products(active_t, d_norm_t)
+    msg_sums_ref[...] = dot(d_aggregate_t, summed)
+    gain_sums_ref[...] = sum(
+        terms[:, k * size : (k + 1) * size] for k in range(len(inner_rows))
     )
 
 
@@ -250,46 +227,35 @@
     columns_ref,
     edge_state_ref,
     edge_cot_ref,
-    edge_band_ref,
-    edge_msg_ref,
-    owed_ref,
+    edge_sum_ref,
+    band_ref,
     first_sums_ref,
     second_sums_ref,
     msg_sums_ref,
     gain_sums_ref,
     grads_ref,
-    send_even_ref,
-    send_odd_ref,
     updated_ref,
     direct_ref,
-    edge_owed_ref,
+    d_aggregate_ref,
 ):
-    blocks, features, size = owed_ref.shape
-    width = WIN * size
-
-    def rows(block, count=1):
-        return pl.ds(block * size, count * size)
-
+    blocks, _, size, _ = band_ref.shape
+    features = w_msg_ref.shape[0]
     odd = device_is_odd()
     got_even, got_odd = got_even_ref[...], got_odd_ref[...]
-    halo = (jnp.where(odd, got_even, got_odd), jnp.where(odd, got_odd, got_even))
-    w_msg = w_msg_ref[...]
-    below, above = (dot(block, w_msg).astype(BF16) for block in halo)
-    messages = (
-        jnp.concatenate([below, edge_msg_ref[0]], axis=0),
-        jnp.concatenate([edge_msg_ref[1], above], axis=0),
-    )
-
-    bands = [
-        joined_lanes([edge_band_ref[k, place] for place in range(BAND)]) for k in range(2 * WIN)
-    ]
-    aggregate = [
-        dot(bands[k], messages[k // WIN][(k % WIN) * size : (k % WIN + BAND) * size]).astype(BF16)
-        for k in range(2 * WIN)
-    ]
+    below, above = jnp.where(odd, got_even, got_odd), jnp.where(odd, got_odd, got_even)
+
+    summed = []
+    for k in range(WIN):
+        far = joined_lanes([band_ref[k, place] for place in range(WIN - k)])
+        summed.append(edge_sum_ref[k] + dot(far, below[k * size :]))
+    for k in range(WIN):
+        far = [band_ref[blocks - WIN + k, place] for place in range(2 * WIN - k, BAND)]
+        summed.append(edge_sum_ref[WIN + k] + dot(joined_lanes(far), above[: (k + 1) * size]))
+    summed = jnp.concatenate(summed, axis=0).astype(BF16)
+    aggregate = dot(summed, w_msg_ref[...]).astype(BF16)
     updated_t, terms, active_t, d_norm_t, d_hidden_t, direct, d_aggregate_t = node_layer(
         edge_state_ref[...],
-        joined_lanes([block.T for block in aggregate]),
+        joined_lanes(blocks_turned(aggregate)),
         edge_cot_ref[...],
         first_t_ref[...],
         second_t_ref[...],
@@ -299,43 +265,15 @@
     )
     updated_ref[...] = updated_t
     direct_ref[...] = direct
-
-    ends = []
-    for end in range(2):
-        owed = [None] * (3 * WIN)
-        for k in range(WIN):
-            own = slice((end * WIN + k) * size, (end * WIN + k + 1) * size)
-            value = dot(d_aggregate_t[:, own], bands[end * WIN + k])
-            for place in range(BAND):
-                term = value[:, place * size : (place + 1) * size]
-                owed[k + place] = term if owed[k + place] is None else owed[k + place] + term
-        ends.append(owed)
-    to_below = [block.astype(BF16) for block in ends[0][:WIN]]
-    to_above = [block.astype(BF16) for block in ends[1][2 * WIN :]]
-    for k in range(WIN):
-        send_even_ref[k] = jnp.where(odd, to_below[k], to_above[k])
-        send_odd_ref[k] = jnp.where(odd, to_above[k], to_below[k])
-    inside = []
-    for k in range(2 * WIN):
-        inside.append(owed_ref[k] + ends[0][WIN + k])
-    for k in range(2 * WIN):
-        inside.append(owed_ref[blocks - 2 * WIN + k] + ends[1][k])
-    for k, block in enumerate(inside):
-        edge_owed_ref[k] = block
-    inside = [block.astype(BF16) for block in inside]
-
-    state = state_ref[...]
-    low, high = state[:width], state[(blocks - WIN) * size :]
+    d_aggregate_ref[...] = d_aggregate_t
+
+    width = WIN * size
+    ends = [state_ref[pl.ds(0, width), :], state_ref[pl.ds((blocks - WIN) * size, width), :]]
     first_sums = first_sums_ref[...] + first_products(
-        d_hidden_t, jnp.concatenate([low, high], axis=0), jnp.concatenate(aggregate, axis=0)
+        d_hidden_t, jnp.concatenate(ends, axis=0), aggregate
     )
     second_sums = second_sums_ref[...] + second_products(active_t, d_norm_t)
-    msg_sums = msg_sums_ref[...] + dot(
-        joined_lanes(to_below + inside + to_above),
-        jnp.concatenate(
-            [halo[0], state[: 2 * width], state[(blocks - 2 * WIN) * size :], halo[1]], axis=0
-        ),
-    )
+    msg_sums = msg_sums_ref[...] + dot(d_aggregate_t, summed)
     gain_sums = gain_sums_ref[...]
     for k in range(2 * WIN):
         gain_sums = gain_sums + terms[:, k * size : (k + 1) * size]
@@ -368,6 +306,34 @@
         grads_ref[k] = jnp.concatenate([block, bias], axis=0)
 
 
+def owed_kernel(
+    band_ref, inner_ref, outer_ref, owed_ref, send_even_ref, send_odd_ref
+):
+    blocks, _, size, _ = band_ref.shape
+    odd = device_is_odd()
+
+    def d_aggregate(b):
+        if WIN <= b < blocks - WIN:
+            return inner_ref[:, pl.ds((b - WIN) * size, size)]
+        k = b if b < WIN else b - blocks + 2 * WIN
+        return outer_ref[:, pl.ds(k * size, size)]
+
+    def owed(block):
+        near = range(max(block - WIN, 0), min(block + WIN, blocks - 1) + 1)
+        tiles_of = [band_ref[b, block - b + WIN] for b in near]
+        return dot(
+            joined_lanes([d_aggregate(b) for b in near]), jnp.concatenate(tiles_of, axis=0)
+        )
+
+    for k in range(WIN):
+        to_below = owed(k - WIN).astype(BF16)
+        to_above = owed(blocks + k).astype(BF16)
+        send_even_ref[k] = jnp.where(odd, to_below, to_above)
+        send_odd_ref[k] = jnp.where(odd, to_above, to_below)
+    for b in range(blocks):
+        owed_ref[b] = owed(b)
+
+
 def sum_kernel(parts_ref, spread_ref, bias_ref):
     total = parts_ref[0].astype(F32)
     for k in range(1, parts_ref.shape[0]):
@@ -388,7 +354,6 @@
     inner_direct_ref,
     outer_direct_ref,
     owed_ref,
-    edge_owed_ref,
     bias_ref,
     updated_ref,
     grad_state_ref,
@@ -403,12 +368,7 @@
     from_above = jnp.where(odd, odd_part, even_part)
     w_msg = w_msg_ref[...]
     for b in range(blocks):
-        if b < 2 * WIN:
-            owed = edge_owed_ref[b]
-        elif b < blocks - 2 * WIN:
-            owed = owed_ref[b]
-        else:
-            owed = edge_owed_ref[b - blocks + 4 * WIN]
+        owed = owed_ref[b]
         if b < WIN:
             owed = owed + from_below[b]
         elif b >= blocks - WIN:
@@ -507,11 +467,11 @@
         columns,
         edge_state,
         edge_cot,
-        edge_band,
-        edge_msg,
+        edge_sum,
+        band,
         inner_updated,
         inner_direct,
-        owed,
+        inner_d_aggregate,
         first_sums,
         second_sums,
         msg_sums,
@@ -525,11 +485,11 @@
             vmem((3, features, size), F32),
             vmem((features, edge * size), BF16),
             vmem((features, edge * size), BF16),
-            vmem((edge, BAND, size, size), BF16),
-            vmem((2, edge * size, features), BF16),
+            vmem((edge, size, features), F32),
+            vmem((blocks, BAND, size, size), BF16),
             vmem((features, inner * size), BF16),
             vmem((features, inner * size), F32),
-            vmem((blocks, features, size), F32),
+            vmem((features, inner * size), BF16),
             vmem((features, 2 * features + ONES), F32),
             vmem((features + 16, features), F32),
             vmem((features, features), F32),
@@ -544,24 +504,20 @@
             pltpu.SMEM((tiles, blocks), jnp.int32),
             vmem(edge_counts.shape, jnp.int32),
             vmem((nodes, features), BF16),
-            vmem((nodes, features), BF16),
-            vmem((inner, BAND, size, size), BF16),
             pltpu.SemaphoreType.DMA((6,)),
         ),
         limit=32,
         flops=700_000_000,
     )
 
-    grads, send_even, send_odd, outer_updated, outer_direct, edge_owed = call(
+    grads, outer_updated, outer_direct, outer_d_aggregate = call(
         functools.partial(outer_kernel, grad_scale),
         "outer_rows",
         (
             vmem((devices, chunk + BIAS_ROWS, features), SENT),
-            vmem((WIN, features, size), BF16),
-            vmem((WIN, features, size), BF16),
             vmem((features, edge * size), BF16),
             vmem((features, edge * size), F32),
-            vmem((2 * edge, features, size), F32),
+            vmem((features, edge * size), BF16),
         ),
         [
             (array, vmem)
@@ -577,9 +533,8 @@
                 columns,
                 edge_state,
                 edge_cot,
-                edge_band,
-                edge_msg,
-                owed,
+                edge_sum,
+                band,
                 first_sums,
                 second_sums,
                 msg_sums,
@@ -590,6 +545,17 @@
     )
 
     parts = lax.all_to_all(grads, AXES, 0, 0, tiled=True)
+    owed, send_even, send_odd = call(
+        owed_kernel,
+        "owed",
+        (
+            vmem((blocks, features, size), F32),
+            vmem((WIN, features, size), BF16),
+            vmem((WIN, features, size), BF16),
+        ),
+        [(band, vmem), (inner_d_aggregate, vmem), (outer_d_aggregate, vmem)],
+        flops=200_000_000,
+    )
     owed_even = swapped(send_even, 0)
     owed_odd = swapped(send_odd, 1)
     spread, bias = call(
@@ -620,7 +586,6 @@
                 inner_direct,
                 outer_direct,
                 owed,
-                edge_owed,
                 bias,
             )
         ],

time: 42 us -> 42.4 us (level)
  waiting for transfers between devices: 14 us -> 12.8 us
  local copies, waits for them, and re-layouts: 0 us -> 0.72 us
  Pallas kernels: 11.2 us -> 11.7 us
    all_to_all x1, waiting for transfers between devices: 6.91 us -> 5.77 us  [shards(): parts = lax.all_to_all(grads, AXES, 0, 0, tiled=True)]
    unnamed x0 -> x12, local copies, waits for them, and re-layouts: none -> 0.72 us
    pallas_call x6 -> x7, Pallas kernels: 11.2 us -> 11.7 us  [call(): pl.pallas_call(kernel, out_shape=tuple(outs), in_specs=specs, out_specs=t...]
  transfers between devices with their start and end apart: 6 -> 6, of which waited for: 2 -> 2; matrix products, arithmetic and copies ran while one was open for 0% -> 0% of each run, Pallas kernels for 16% -> 18%
where the time goes in v8:
time: 42.4 us; the launch traced here: 42.1 us
  starting transfers between devices  16 us (38%)
  waiting for transfers between devices  12.8 us (30%)
  Pallas kernels  11.7 us (28%)
  between operations  0.76 us (2%)
  local copies, waits for them, and re-layouts  0.72 us (2%)
    pallas_call x7, Pallas kernels, call(): pl.pallas_call(kernel, out_shape=tuple(outs), in_specs=specs, out_specs=t...  11.7 us
    all_to_all x1, starting transfers between devices, shards(): parts = lax.all_to_all(grads, AXES, 0, 0, tiled=True)  7.16 us
    all_to_all x1, waiting for transfers between devices, shards(): whole = lax.all_to_all(spread, AXES, 0, 0, tiled=True)  7.05 us
    ppermute x4, starting transfers between devices, swapped(): lax.ppermute(block, AXES, [(i, i + 1) for i in lower] + [(i + 1, i) for i...  6.3 us
    all_to_all x1, waiting for transfers between devices, shards(): parts = lax.all_to_all(grads, AXES, 0, 0, tiled=True)  5.77 us
    all_to_all x1, starting transfers between devices, shards(): whole = lax.all_to_all(spread, AXES, 0, 0, tiled=True)  2.58 us
  transfers between devices with their start and end apart: 6, of which 2 were waited for; matrix products, arithmetic and copies ran while one was open for 0% of the time, Pallas kernels for 18%

profile of v8, /device:TPU:0, one launch (start us, length us, event | category | flops | bytes accessed | tf_op | source)
XLA Modules:
  0.0 42.1 jit_solution(8267372368728283863)
XLA Ops:
  0.6 1.1 %fetch.1 = (bf16[1536,128]{1,0:T(8,128)(2,1)S(1)}, bf16[128,128]{1,0:T(8,128)(2,1)S(1)}, bf16[256,128]{1,0:T(8,128)(2,1)S(1)}, bf16[128,128]{1,0:T(8,128)(2,1)S(...) custom-call(bf16[1536,128]{1,0:T(8,128)(2,1)} %refs_0_.1, ...), custom_call_target="tpu_custom_call" | custom-call | bytes 1000000 | tf_op jit(solution)/shard_map/fetch/pallas_call | solution.py:406
  1.7 3.1 %collective-permute-start = (bf16[256,128]{1,0:T(8,128)(2,1)S(1)}, bf16[256,128]{1,0:T(8,128)(2,1)S(1)}, u32[]{:S(2)}, u32[]{:S(2)}) collective-permute-start(bf16[256,128]{1,0:T(8,128)(2,1)S(1)} %get-tuple-element.57), channel_id=1, source_target_pairs={{0,1},{2,3},{4,5},{6,7},{8,9},{10,11},{12,13},{14,15},{16,17},{18,... | collective-permute-start | bytes 196616 | tf_op jit(solution)/shard_map/ppermute | solution.py:400
  4.8 0.7 %collective-permute-start.1 = (bf16[256,128]{1,0:T(8,128)(2,1)S(1)}, bf16[256,128]{1,0:T(8,128)(2,1)S(1)}, u32[]{:S(2)}, u32[]{:S(2)}) collective-permute-start(bf16[256,128]{1,0:T(8,128)(2,1)S(1)} %get-tuple-element.58), channel_id=1, source_target_pairs={{1,2},{3,4},{5,6},{7,8},{9,10},{11,12},{13,14},{15,16},{17,18},{19... | collective-permute-start | bytes 196616 | tf_op jit(solution)/shard_map/ppermute | solution.py:400
  5.5 4.7 %inner_rows.1 = (bf16[128,256]{1,0:T(8,128)(2,1)S(1)}, bf16[128,128]{1,0:T(8,128)(2,1)S(1)}, f32[3,128,128]{2,1,0:T(8,128)S(1)}, bf16[128,512]{1,0:T(8,128)(2,1)...) custom-call(s32[4,12]{1,0:T(4,128)} %bitcast.9, ...), custom_call_target="tpu_custom_call" | custom-call | flops 700000000 | bytes 1000000 | tf_op jit(solution)/shard_map/inner_rows/pallas_call | solution.py:406
  10.2 0.0 copy-start
  10.2 0.0 copy-start.2
  10.2 0.0 collective-permute-done.got_even_ref
  10.2 0.0 collective-permute-done.1.got_odd_ref
  10.3 2.2 %outer_rows.1 = (bf16[32,24,128]{2,1,0:T(8,128)(2,1)}, bf16[128,512]{1,0:T(8,128)(2,1)S(1)}, f32[128,512]{1,0:T(8,128)S(1)}, bf16[128,512]{1,0:T(8,128)(2,1)S(1)}) custom-call(bf16[256,128]{1,0:T(8,128)(2,1)S(1)} %collective-permute-done.got_even_ref, bf16[256,128]{1,0:T(8,128)(2,1)S(1)} %collective-permute-done.1.got_odd_ref, ...), custom_call_target="tpu_custom_call" | custom-call | flops 300000000 | bytes 1000000 | tf_op jit(solution)/shard_map/outer_rows/pallas_call | solution.py:406
  12.4 0.0 copy-done
  12.4 0.0 copy-done.2
  12.4 0.0 copy-start.4
  12.4 0.7 %copy-done.4 = f32[128,512]{1,0:T(8,128)} copy-done((f32[128,512]{1,0:T(8,128)}, f32[128,512]{1,0:T(8,128)S(1)}, u32[]{:S(2)}) %copy-start.4) | copy-done | bytes 262168
  13.1 7.2 %all-to-all-start = ((bf16[32,24,128]{2,1,0:T(8,128)(2,1)}), bf16[32,24,128]{2,1,0:T(8,128)(2,1)S(1)}, u32[]{:S(2)}, u32[]{:S(2)}) async-start(bf16[32,24,128]{2,1,0:T(8,128)(2,1)} %get-tuple-element.77), calls=%async_computation | async-start | bytes 393216 | tf_op jit(solution)/shard_map/all_to_all | solution.py:547
  20.3 1.1 %owed.1 = (f32[12,128,128]{2,1,0:T(8,128)S(1)}, bf16[2,128,128]{2,1,0:T(8,128)(2,1)}, bf16[2,128,128]{2,1,0:T(8,128)(2,1)}) custom-call(bf16[12,5,128,128]{3,2,1,0:T(8,128)(2,1)S(1)} %get-tuple-element.55.band_ref, bf16[128,1024]{1,0:T(8,128)(2,1)S(1)} %get-tuple-element.56.inner_ref, bf16[128,512]{1,0:T(8,128)(2,1)S(1)} %get-tuple-element.69.outer_ref), custom_call_target="tpu_custom_call" | custom-call | flops 200000000 | bytes 1000000 | tf_op jit(solution)/shard_map/owed/pallas_call | solution.py:406
  21.4 1.8 %collective-permute-start.2 = (bf16[2,128,128]{2,1,0:T(8,128)(2,1)}, bf16[2,128,128]{2,1,0:T(8,128)(2,1)S(1)}, u32[]{:S(2)}, u32[]{:S(2)}) collective-permute-start(bf16[2,128,128]{2,1,0:T(8,128)(2,1)} %get-tuple-element.70), channel_id=1, source_target_pairs={{0,1},{2,3},{4,5},{6,7},{8,9},{10,11},{12,13},{14,15},{16,17},{18,... | collective-permute-start | bytes 196616 | tf_op jit(solution)/shard_map/ppermute | solution.py:400
  23.1 0.0 copy-start.1
  23.1 0.0 copy-start.3
  23.1 0.0 copy-start.5
  23.1 0.8 %collective-permute-start.3 = (bf16[2,128,128]{2,1,0:T(8,128)(2,1)}, bf16[2,128,128]{2,1,0:T(8,128)(2,1)S(1)}, u32[]{:S(2)}, u32[]{:S(2)}) collective-permute-start(bf16[2,128,128]{2,1,0:T(8,128)(2,1)} %get-tuple-element.71), channel_id=1, source_target_pairs={{1,2},{3,4},{5,6},{7,8},{9,10},{11,12},{13,14},{15,16},{17,18},{19... | collective-permute-start | bytes 196616 | tf_op jit(solution)/shard_map/ppermute | solution.py:400
  23.9 5.8 %all-to-all-done.parts_ref = bf16[32,24,128]{2,1,0:T(8,128)(2,1)S(1)} async-done(((bf16[32,24,128]{2,1,0:T(8,128)(2,1)}), bf16[32,24,128]{2,1,0:T(8,128)(2,1)S(1)}, u32[]{:S(2)}, u32[]{:S(2)}) %all-to-all-start) | async-done | bytes 196640 | tf_op jit(solution)/shard_map/all_to_all | solution.py:547
  29.7 0.7 %sum.1 = (bf16[32,16,128]{2,1,0:T(8,128)(2,1)}, f32[8,128]{1,0:T(8,128)S(1)}) custom-call(bf16[32,24,128]{2,1,0:T(8,128)(2,1)S(1)} %all-to-all-done.parts_ref), custom_call_target="tpu_custom_call" | custom-call | flops 10000000000 | bytes 1000000 | tf_op jit(solution)/shard_map/sum/pallas_call | solution.py:406
  30.4 2.6 %all-to-all-start.1 = ((bf16[32,16,128]{2,1,0:T(8,128)(2,1)}), bf16[32,16,128]{2,1,0:T(8,128)(2,1)S(1)}, u32[]{:S(2)}, u32[]{:S(2)}) async-start(bf16[32,16,128]{2,1,0:T(8,128)(2,1)} %get-tuple-element.81), calls=%async_computation.1 | async-start | bytes 262144 | tf_op jit(solution)/shard_map/all_to_all | solution.py:595
  33.0 0.0 collective-permute-done.2.even_ref
  33.0 0.0 collective-permute-done.3.odd_ref
  33.0 0.0 copy-done.1
  33.0 0.0 copy-done.3
  33.0 0.0 copy-done.5
  33.0 1.3 %results.1 = (bf16[1536,128]{1,0:T(8,128)(2,1)}, bf16[1536,128]{1,0:T(8,128)(2,1)}, f32[1,128]{1,0:T(1,128)}, f32[1,128]{1,0:T(1,128)}, f32[1,128]{1,0:T(1,128)}) custom-call(bf16[2,128,128]{2,1,0:T(8,128)(2,1)S(1)} %collective-permute-done.2.even_ref, bf16[2,128,128]{2,1,0:T(8,128)(2,1)S(1)} %collective-permute-done.3.odd_ref, ...), custom_call_target="tpu_custom_call" | custom-call | flops 49999998976 | bytes 1000000 | tf_op jit(solution)/shard_map/results/pallas_call | solution.py:406
  34.3 7.0 %all-to-all-done.1 = bf16[32,16,128]{2,1,0:T(8,128)(2,1)S(1)} async-done(((bf16[32,16,128]{2,1,0:T(8,128)(2,1)}), bf16[32,16,128]{2,1,0:T(8,128)(2,1)S(1)}, u32[]{:S(2)}, u32[]{:S(2)}) %all-to-all-start.1) | async-done | bytes 131104 | tf_op jit(solution)/shard_map/all_to_all | solution.py:595
  41.4 0.7 %unpack.1 = (f32[128,128]{1,0:T(8,128)}, f32[256,128]{1,0:T(8,128)}, f32[128,128]{1,0:T(8,128)}) custom-call(bf16[512,128]{1,0:T(8,128)(2,1)S(1)} %bitcast.8), custom_call_target="tpu_custom_call" | custom-call | bytes 1000000 | tf_op jit(solution)/shard_map/unpack/pallas_call | solution.py:406
Async XLA Ops:
  1.7 8.5 %collective-permute-start = (bf16[256,128]{1,0:T(8,128)(2,1)S(1)}, bf16[256,128]{1,0:T(8,128)(2,1)S(1)}, u32[]{:S(2)}, u32[]{:S(2)}) collective-permute-start(bf16[256,128]{1,0:T(8,128)(2,1)S(1)} %get-tuple-element.57), channel_id=1, source_target_pairs={{0,1},{2,3},{4,5},{6,7},{8,9},{10,11},{12,13},{14,15},{16,17},{18,... | collective-permute-start | bytes 196616 | tf_op jit(solution)/shard_map/ppermute | solution.py:400
  4.8 5.4 %collective-permute-start.1 = (bf16[256,128]{1,0:T(8,128)(2,1)S(1)}, bf16[256,128]{1,0:T(8,128)(2,1)S(1)}, u32[]{:S(2)}, u32[]{:S(2)}) collective-permute-start(bf16[256,128]{1,0:T(8,128)(2,1)S(1)} %get-tuple-element.58), channel_id=1, source_target_pairs={{1,2},{3,4},{5,6},{7,8},{9,10},{11,12},{13,14},{15,16},{17,18},{19... | collective-permute-start | bytes 196616 | tf_op jit(solution)/shard_map/ppermute | solution.py:400
  10.2 2.2 %copy-start = (f32[128,1024]{1,0:T(8,128)}, f32[128,1024]{1,0:T(8,128)S(1)}, u32[]{:S(2)}) copy-start(f32[128,1024]{1,0:T(8,128)S(1)} %get-tuple-element.74.inner_direct_ref) | copy-start | bytes 1572868
  10.2 2.2 %copy-start.2 = (bf16[128,1024]{1,0:T(8,128)(2,1)}, bf16[128,1024]{1,0:T(8,128)(2,1)S(1)}, u32[]{:S(2)}) copy-start(bf16[128,1024]{1,0:T(8,128)(2,1)S(1)} %get-tuple-element.72.inner_updated_ref) | copy-start | bytes 786436
  12.4 0.7 %copy-start.4 = (f32[128,512]{1,0:T(8,128)}, f32[128,512]{1,0:T(8,128)S(1)}, u32[]{:S(2)}) copy-start(f32[128,512]{1,0:T(8,128)S(1)} %get-tuple-element.75.outer_direct_ref) | copy-start | bytes 786436
  13.1 16.6 %all-to-all-start = ((bf16[32,24,128]{2,1,0:T(8,128)(2,1)}), bf16[32,24,128]{2,1,0:T(8,128)(2,1)S(1)}, u32[]{:S(2)}, u32[]{:S(2)}) async-start(bf16[32,24,128]{2,1,0:T(8,128)(2,1)} %get-tuple-element.77), calls=%async_computation | async-start | bytes 393216 | tf_op jit(solution)/shard_map/all_to_all | solution.py:547
  21.4 11.6 %collective-permute-start.2 = (bf16[2,128,128]{2,1,0:T(8,128)(2,1)}, bf16[2,128,128]{2,1,0:T(8,128)(2,1)S(1)}, u32[]{:S(2)}, u32[]{:S(2)}) collective-permute-start(bf16[2,128,128]{2,1,0:T(8,128)(2,1)} %get-tuple-element.70), channel_id=1, source_target_pairs={{0,1},{2,3},{4,5},{6,7},{8,9},{10,11},{12,13},{14,15},{16,17},{18,... | collective-permute-start | bytes 196616 | tf_op jit(solution)/shard_map/ppermute | solution.py:400
  23.1 9.9 %copy-start.1 = (f32[128,1024]{1,0:T(8,128)S(1)}, f32[128,1024]{1,0:T(8,128)}, u32[]{:S(2)}) copy-start(f32[128,1024]{1,0:T(8,128)} %copy-done) | copy-start | bytes 1572868
  23.1 9.9 %copy-start.3 = (bf16[128,1024]{1,0:T(8,128)(2,1)S(1)}, bf16[128,1024]{1,0:T(8,128)(2,1)}, u32[]{:S(2)}) copy-start(bf16[128,1024]{1,0:T(8,128)(2,1)} %copy-done.2) | copy-start | bytes 786436
  23.1 9.9 %copy-start.5 = (f32[128,512]{1,0:T(8,128)S(1)}, f32[128,512]{1,0:T(8,128)}, u32[]{:S(2)}) copy-start(f32[128,512]{1,0:T(8,128)} %copy-done.4) | copy-start | bytes 786436
  23.1 9.9 %collective-permute-start.3 = (bf16[2,128,128]{2,1,0:T(8,128)(2,1)}, bf16[2,128,128]{2,1,0:T(8,128)(2,1)S(1)}, u32[]{:S(2)}, u32[]{:S(2)}) collective-permute-start(bf16[2,128,128]{2,1,0:T(8,128)(2,1)} %get-tuple-element.71), channel_id=1, source_target_pairs={{1,2},{3,4},{5,6},{7,8},{9,10},{11,12},{13,14},{15,16},{17,18},{19... | collective-permute-start | bytes 196616 | tf_op jit(solution)/shard_map/ppermute | solution.py:400
  30.4 11.0 %all-to-all-start.1 = ((bf16[32,16,128]{2,1,0:T(8,128)(2,1)}), bf16[32,16,128]{2,1,0:T(8,128)(2,1)S(1)}, u32[]{:S(2)}, u32[]{:S(2)}) async-start(bf16[32,16,128]{2,1,0:T(8,128)(2,1)} %get-tuple-element.81), calls=%async_computation.1 | async-start | bytes 262144 | tf_op jit(solution)/shard_map/all_to_all | solution.py:595

commit v9 on v8

--- a/solution.py
+++ b/solution.py
@@ -46,7 +46,7 @@
     return [array[k : k + size].T for k in range(0, array.shape[0], size)]
 
 
-def node_layer(state_t, aggregate_t, cot_t, first_t, second_t, w_first, w_second, columns):
+def node_layer(state_t, aggregate_t, cot_t, first_t, second_t, w_second, columns):
     features, width = state_t.shape
     b_first, b_second, gain = (
         joined_lanes([c] * (width // c.shape[1])) for c in columns
@@ -68,10 +68,11 @@
     mean_qn = jnp.mean(q * normed, axis=0, keepdims=True)
     d_norm_t = (inv_std * (q - mean_q - normed * mean_qn)).astype(BF16)
     d_hidden_t = (dot(w_second, d_norm_t) * slope).astype(BF16)
-    d_joined = dot(w_first, d_hidden_t)
-    direct = cot + d_joined[:features]
-    d_aggregate_t = d_joined[features:].astype(BF16)
-    return updated_t, terms, active_t, d_norm_t, d_hidden_t, direct, d_aggregate_t
+    return updated_t, terms, active_t, d_norm_t, d_hidden_t
+
+
+def d_aggregate_of(w_first, d_hidden_t):
+    return dot(w_first[w_first.shape[1] :], d_hidden_t).astype(BF16)
 
 
 def first_products(d_hidden_t, state, aggregate):
@@ -123,8 +124,7 @@
     edge_sum_ref,
     band_ref,
     updated_ref,
-    direct_ref,
-    d_aggregate_ref,
+    d_hidden_ref,
     first_sums_ref,
     second_sums_ref,
     msg_sums_ref,
@@ -182,28 +182,30 @@
         for t in range(1, tiles):
             band_ref[b, col_ref[t, b] - own + WIN] += counts_ref[b, t].astype(F32).astype(BF16)
 
+    state = state_ref[...]
+    wide = joined_lanes([dot(state, w_msg).astype(BF16), state])
+
     def neighbour_sum(b):
         first, last = max(b - WIN, 0), min(b + WIN, blocks - 1)
         tiles_of = [band_ref[b, block - b + WIN] for block in range(first, last + 1)]
-        return dot(joined_lanes(tiles_of), state_ref[rows(first, last + 1 - first), :])
+        return dot(joined_lanes(tiles_of), wide[first * size : (last + 1) * size])
 
     for k, b in enumerate(edge_rows):
         edge_sum_ref[k] = neighbour_sum(b)
     summed = jnp.concatenate([neighbour_sum(b).astype(BF16) for b in inner_rows], axis=0)
-    aggregate = dot(summed, w_msg).astype(BF16)
-    updated_t, terms, active_t, d_norm_t, d_hidden_t, direct, d_aggregate_t = node_layer(
+    aggregate, summed = summed[:, :features], summed[:, features:]
+    updated_t, terms, active_t, d_norm_t, d_hidden_t = node_layer(
         joined_lanes([state_t[b] for b in inner_rows]),
         joined_lanes(blocks_turned(aggregate)),
         joined_lanes([cot_ref[rows(b), :].T for b in inner_rows]),
         first_t,
         second_t,
-        w_first,
         w_second,
         columns,
     )
     updated_ref[...] = updated_t
-    direct_ref[...] = direct
-    d_aggregate_ref[...] = d_aggregate_t
+    d_hidden_ref[...] = d_hidden_t
+    d_aggregate_t = d_aggregate_of(w_first, d_hidden_t)
     first_sums_ref[...] = first_products(
         d_hidden_t, state_ref[rows(WIN, len(inner_rows)), :], aggregate
     )
@@ -235,8 +237,7 @@
     gain_sums_ref,
     grads_ref,
     updated_ref,
-    direct_ref,
-    d_aggregate_ref,
+    d_hidden_ref,
 ):
     blocks, _, size, _ = band_ref.shape
     features = w_msg_ref.shape[0]
@@ -244,6 +245,10 @@
     got_even, got_odd = got_even_ref[...], got_odd_ref[...]
     below, above = jnp.where(odd, got_even, got_odd), jnp.where(odd, got_odd, got_even)
 
+    w_msg = w_msg_ref[...]
+    below, above = (
+        joined_lanes([dot(halo, w_msg).astype(BF16), halo]) for halo in (below, above)
+    )
     summed = []
     for k in range(WIN):
         far = joined_lanes([band_ref[k, place] for place in range(WIN - k)])
@@ -252,20 +257,19 @@
         far = [band_ref[blocks - WIN + k, place] for place in range(2 * WIN - k, BAND)]
         summed.append(edge_sum_ref[WIN + k] + dot(joined_lanes(far), above[: (k + 1) * size]))
     summed = jnp.concatenate(summed, axis=0).astype(BF16)
-    aggregate = dot(summed, w_msg_ref[...]).astype(BF16)
-    updated_t, terms, active_t, d_norm_t, d_hidden_t, direct, d_aggregate_t = node_layer(
+    aggregate, summed = summed[:, :features], summed[:, features:]
+    updated_t, terms, active_t, d_norm_t, d_hidden_t = node_layer(
         edge_state_ref[...],
         joined_lanes(blocks_turned(aggregate)),
         edge_cot_ref[...],
         first_t_ref[...],
         second_t_ref[...],
-        w_first_ref[...],
         w_second_ref[...],
         [columns_ref[k] for k in range(3)],
     )
     updated_ref[...] = updated_t
-    direct_ref[...] = direct
-    d_aggregate_ref[...] = d_aggregate_t
+    d_hidden_ref[...] = d_hidden_t
+    d_aggregate_t = d_aggregate_of(w_first_ref[...], d_hidden_t)
 
     width = WIN * size
     ends = [state_ref[pl.ds(0, width), :], state_ref[pl.ds((blocks - WIN) * size, width), :]]
@@ -307,16 +311,19 @@
 
 
 def owed_kernel(
-    band_ref, inner_ref, outer_ref, owed_ref, send_even_ref, send_odd_ref
+    band_ref, w_first_ref, inner_ref, outer_ref, owed_ref, send_even_ref, send_odd_ref
 ):
     blocks, _, size, _ = band_ref.shape
     odd = device_is_odd()
+    w_first = w_first_ref[...]
+    inner = d_aggregate_of(w_first, inner_ref[...])
+    outer = d_aggregate_of(w_first, outer_ref[...])
 
     def d_aggregate(b):
         if WIN <= b < blocks - WIN:
-            return inner_ref[:, pl.ds((b - WIN) * size, size)]
+            return inner[:, (b - WIN) * size : (b - WIN + 1) * size]
         k = b if b < WIN else b - blocks + 2 * WIN
-        return outer_ref[:, pl.ds(k * size, size)]
+        return outer[:, k * size : (k + 1) * size]
 
     def owed(block):
         near = range(max(block - WIN, 0), min(block + WIN, blocks - 1) + 1)
@@ -348,11 +355,13 @@
 def result_kernel(
     even_ref,
     odd_ref,
+    cot_hbm,
     w_msg_ref,
+    w_first_ref,
     inner_updated_ref,
     outer_updated_ref,
-    inner_direct_ref,
-    outer_direct_ref,
+    inner_d_hidden_ref,
+    outer_d_hidden_ref,
     owed_ref,
     bias_ref,
     updated_ref,
@@ -360,13 +369,18 @@
     b_first_ref,
     b_second_ref,
     gain_ref,
+    cot_ref,
+    arrived,
 ):
-    blocks, _, size = owed_ref.shape
+    blocks, features, size = owed_ref.shape
+    copy = pltpu.make_async_copy(cot_hbm, cot_ref, arrived)
+    copy.start()
     odd = device_is_odd()
     even_part, odd_part = even_ref[...].astype(F32), odd_ref[...].astype(F32)
     from_below = jnp.where(odd, even_part, odd_part)
     from_above = jnp.where(odd, odd_part, even_part)
-    w_msg = w_msg_ref[...]
+    weights = joined_lanes([w_first_ref[pl.ds(0, features), :], w_msg_ref[...]])
+    copy.wait()
     for b in range(blocks):
         owed = owed_ref[b]
         if b < WIN:
@@ -374,13 +388,13 @@
         elif b >= blocks - WIN:
             owed = owed + from_above[b - blocks + WIN]
         if WIN <= b < blocks - WIN:
-            k, updated, direct = b - WIN, inner_updated_ref, inner_direct_ref
+            k, updated, d_hidden = b - WIN, inner_updated_ref, inner_d_hidden_ref
         else:
             k = b if b < WIN else b - blocks + 2 * WIN
-            updated, direct = outer_updated_ref, outer_direct_ref
+            updated, d_hidden = outer_updated_ref, outer_d_hidden_ref
         lanes, rows = pl.ds(k * size, size), pl.ds(b * size, size)
-        total = direct[:, lanes] + dot(w_msg, owed.astype(BF16))
-        grad_state_ref[rows, :] = total.astype(BF16).T
+        change = dot(weights, jnp.concatenate([d_hidden[:, lanes], owed.astype(BF16)], axis=0))
+        grad_state_ref[rows, :] = (cot_ref[rows, :].astype(F32) + change.T).astype(BF16)
         updated_ref[rows, :] = updated[:, lanes].T
     for k, ref in enumerate((b_first_ref, b_second_ref, gain_ref)):
         ref[...] = bias_ref[pl.ds(k, 1), :] + bias_ref[pl.ds(k + 3, 1), :]
@@ -470,8 +484,7 @@
         edge_sum,
         band,
         inner_updated,
-        inner_direct,
-        inner_d_aggregate,
+        inner_d_hidden,
         first_sums,
         second_sums,
         msg_sums,
@@ -485,10 +498,9 @@
             vmem((3, features, size), F32),
             vmem((features, edge * size), BF16),
             vmem((features, edge * size), BF16),
-            vmem((edge, size, features), F32),
+            vmem((edge, size, 2 * features), F32),
             vmem((blocks, BAND, size, size), BF16),
             vmem((features, inner * size), BF16),
-            vmem((features, inner * size), F32),
             vmem((features, inner * size), BF16),
             vmem((features, 2 * features + ONES), F32),
             vmem((features + 16, features), F32),
@@ -510,13 +522,12 @@
         flops=700_000_000,
     )
 
-    grads, outer_updated, outer_direct, outer_d_aggregate = call(
+    grads, outer_updated, outer_d_hidden = call(
         functools.partial(outer_kernel, grad_scale),
         "outer_rows",
         (
             vmem((devices, chunk + BIAS_ROWS, features), SENT),
             vmem((features, edge * size), BF16),
-            vmem((features, edge * size), F32),
             vmem((features, edge * size), BF16),
         ),
         [
@@ -553,7 +564,7 @@
             vmem((WIN, features, size), BF16),
             vmem((WIN, features, size), BF16),
         ),
-        [(band, vmem), (inner_d_aggregate, vmem), (outer_d_aggregate, vmem)],
+        [(array, vmem) for array in (band, w_first_here, inner_d_hidden, outer_d_hidden)],
         flops=200_000_000,
     )
     owed_even = swapped(send_even, 0)
@@ -575,20 +586,21 @@
             result((1, features), F32),
             result((1, features), F32),
         ),
-        [
+        [(owed_even, vmem), (owed_odd, vmem), (cotangent, hbm)]
+        + [
             (array, vmem)
             for array in (
-                owed_even,
-                owed_odd,
                 w_msg_here,
+                w_first_here,
                 inner_updated,
                 outer_updated,
-                inner_direct,
-                outer_direct,
+                inner_d_hidden,
+                outer_d_hidden,
                 owed,
                 bias,
             )
         ],
+        scratch=(vmem((nodes, features), BF16), pltpu.SemaphoreType.DMA),
         flops=50_000_000_000,
     )
 

time: 42.4 us -> 42.4 us (level)
  Pallas kernels: 11.7 us -> 13.1 us
  waiting for transfers between devices: 12.8 us -> 11.5 us
    pallas_call x7, Pallas kernels: 11.7 us -> 13.1 us  [call(): pl.pallas_call(kernel, out_shape=tuple(outs), in_specs=specs, out_specs=t...]
    all_to_all x1, waiting for transfers between devices: 7.05 us -> 6 us  [shards(): whole = lax.all_to_all(spread, AXES, 0, 0, tiled=True)]
  transfers between devices with their start and end apart: 6 -> 6, of which waited for: 2 -> 2; matrix products, arithmetic and copies ran while one was open for 0% -> 0% of each run, Pallas kernels for 18% -> 22%
where the time goes in v9:
time: 42.4 us; the launch traced here: 42 us
  starting transfers between devices  16 us (38%)
  Pallas kernels  13.1 us (31%)
  waiting for transfers between devices  11.5 us (27%)
  between operations  0.75 us (2%)
  local copies, waits for them, and re-layouts  0.67 us (2%)
    pallas_call x7, Pallas kernels, call(): pl.pallas_call(kernel, out_shape=tuple(outs), in_specs=specs, out_specs=t...  13.1 us
    all_to_all x1, starting transfers between devices, shards(): parts = lax.all_to_all(grads, AXES, 0, 0, tiled=True)  7.15 us
    ppermute x4, starting transfers between devices, swapped(): lax.ppermute(block, AXES, [(i, i + 1) for i in lower] + [(i + 1, i) for i...  6.3 us
    all_to_all x1, waiting for transfers between devices, shards(): whole = lax.all_to_all(spread, AXES, 0, 0, tiled=True)  6 us
    all_to_all x1, waiting for transfers between devices, shards(): parts = lax.all_to_all(grads, AXES, 0, 0, tiled=True)  5.47 us
    all_to_all x1, starting transfers between devices, shards(): whole = lax.all_to_all(spread, AXES, 0, 0, tiled=True)  2.56 us
  transfers between devices with their start and end apart: 6, of which 2 were waited for; matrix products, arithmetic and copies ran while one was open for 0% of the time, Pallas kernels for 22%

profile of v9, /device:TPU:0, one launch (start us, length us, event | category | flops | bytes accessed | tf_op | source)
XLA Modules:
  0.0 42.0 jit_solution(8136818833827479063)
XLA Ops:
  0.6 1.1 %fetch.1 = (bf16[1536,128]{1,0:T(8,128)(2,1)S(1)}, bf16[128,128]{1,0:T(8,128)(2,1)S(1)}, bf16[256,128]{1,0:T(8,128)(2,1)S(1)}, bf16[128,128]{1,0:T(8,128)(2,1)S(...) custom-call(bf16[1536,128]{1,0:T(8,128)(2,1)} %refs_0_.1, ...), custom_call_target="tpu_custom_call" | custom-call | bytes 1000000 | tf_op jit(solution)/shard_map/fetch/pallas_call | solution.py:420
  1.7 3.1 %collective-permute-start = (bf16[256,128]{1,0:T(8,128)(2,1)S(1)}, bf16[256,128]{1,0:T(8,128)(2,1)S(1)}, u32[]{:S(2)}, u32[]{:S(2)}) collective-permute-start(bf16[256,128]{1,0:T(8,128)(2,1)S(1)} %get-tuple-element.55), channel_id=1, source_target_pairs={{0,1},{2,3},{4,5},{6,7},{8,9},{10,11},{12,13},{14,15},{16,17},{18,... | collective-permute-start | bytes 196616 | tf_op jit(solution)/shard_map/ppermute | solution.py:414
  4.8 0.7 %collective-permute-start.1 = (bf16[256,128]{1,0:T(8,128)(2,1)S(1)}, bf16[256,128]{1,0:T(8,128)(2,1)S(1)}, u32[]{:S(2)}, u32[]{:S(2)}) collective-permute-start(bf16[256,128]{1,0:T(8,128)(2,1)S(1)} %get-tuple-element.56), channel_id=1, source_target_pairs={{1,2},{3,4},{5,6},{7,8},{9,10},{11,12},{13,14},{15,16},{17,18},{19... | collective-permute-start | bytes 196616 | tf_op jit(solution)/shard_map/ppermute | solution.py:414
  5.5 4.7 %inner_rows.1 = (bf16[128,256]{1,0:T(8,128)(2,1)S(1)}, bf16[128,128]{1,0:T(8,128)(2,1)S(1)}, f32[3,128,128]{2,1,0:T(8,128)S(1)}, bf16[128,512]{1,0:T(8,128)(2,1)...) custom-call(s32[4,12]{1,0:T(4,128)} %bitcast.9, ...), custom_call_target="tpu_custom_call" | custom-call | flops 700000000 | bytes 1000000 | tf_op jit(solution)/shard_map/inner_rows/pallas_call | solution.py:420
  10.2 0.0 copy-start
  10.3 0.0 collective-permute-done.got_even_ref
  10.3 0.0 collective-permute-done.1.got_odd_ref
  10.3 2.1 %outer_rows.1 = (bf16[32,24,128]{2,1,0:T(8,128)(2,1)}, bf16[128,512]{1,0:T(8,128)(2,1)S(1)}, bf16[128,512]{1,0:T(8,128)(2,1)S(1)}) custom-call(bf16[256,128]{1,0:T(8,128)(2,1)S(1)} %collective-permute-done.got_even_ref, bf16[256,128]{1,0:T(8,128)(2,1)S(1)} %collective-permute-done.1.got_odd_ref, bf16[1536,128]{1,0:T(8,128)(2,1)S(1)} %get-tuple-element.46.state_ref, ...), custom_call_target="tpu_custom_call" | custom-call | flops 300000000 | bytes 1000000 | tf_op jit(solution)/shard_map/outer_rows/pallas_call | solution.py:420
  12.4 0.0 copy-done
  12.4 0.0 copy-start.2
  12.4 0.7 %copy-done.2 = bf16[128,512]{1,0:T(8,128)(2,1)} copy-done((bf16[128,512]{1,0:T(8,128)(2,1)}, bf16[128,512]{1,0:T(8,128)(2,1)S(1)}, u32[]{:S(2)}) %copy-start.2) | copy-done | bytes 131096
  13.1 7.2 %all-to-all-start = ((bf16[32,24,128]{2,1,0:T(8,128)(2,1)}), bf16[32,24,128]{2,1,0:T(8,128)(2,1)S(1)}, u32[]{:S(2)}, u32[]{:S(2)}) async-start(bf16[32,24,128]{2,1,0:T(8,128)(2,1)} %get-tuple-element.73), calls=%async_computation | async-start | bytes 393216 | tf_op jit(solution)/shard_map/all_to_all | solution.py:558
  20.2 1.4 %owed.1 = (f32[12,128,128]{2,1,0:T(8,128)S(1)}, bf16[2,128,128]{2,1,0:T(8,128)(2,1)}, bf16[2,128,128]{2,1,0:T(8,128)(2,1)S(1)}) custom-call(bf16[12,5,128,128]{3,2,1,0:T(8,128)(2,1)S(1)} %get-tuple-element.53.band_ref, bf16[256,128]{1,0:T(8,128)(2,1)S(1)} %get-tuple-element.48.w_first_ref, ...), custom_call_target="tpu_custom_call" | custom-call | flops 200000000 | bytes 1000000 | tf_op jit(solution)/shard_map/owed/pallas_call | solution.py:420
  21.6 1.8 %collective-permute-start.2 = (bf16[2,128,128]{2,1,0:T(8,128)(2,1)}, bf16[2,128,128]{2,1,0:T(8,128)(2,1)S(1)}, u32[]{:S(2)}, u32[]{:S(2)}) collective-permute-start(bf16[2,128,128]{2,1,0:T(8,128)(2,1)} %get-tuple-element.68), channel_id=1, source_target_pairs={{0,1},{2,3},{4,5},{6,7},{8,9},{10,11},{12,13},{14,15},{16,17},{18,... | collective-permute-start | bytes 196616 | tf_op jit(solution)/shard_map/ppermute | solution.py:414
  23.4 0.0 copy-start.1
  23.4 0.0 copy-start.3
  23.4 0.8 %collective-permute-start.3 = (bf16[2,128,128]{2,1,0:T(8,128)(2,1)S(1)}, bf16[2,128,128]{2,1,0:T(8,128)(2,1)S(1)}, u32[]{:S(2)}, u32[]{:S(2)}) collective-permute-start(bf16[2,128,128]{2,1,0:T(8,128)(2,1)S(1)} %get-tuple-element.69), channel_id=1, source_target_pairs={{1,2},{3,4},{5,6},{7,8},{9,10},{11,12},{13,14},{15,16},{17,18},{19... | collective-permute-start | bytes 196616 | tf_op jit(solution)/shard_map/ppermute | solution.py:414
  24.2 5.5 %all-to-all-done.parts_ref = bf16[32,24,128]{2,1,0:T(8,128)(2,1)S(1)} async-done(((bf16[32,24,128]{2,1,0:T(8,128)(2,1)}), bf16[32,24,128]{2,1,0:T(8,128)(2,1)S(1)}, u32[]{:S(2)}, u32[]{:S(2)}) %all-to-all-start) | async-done | bytes 196640 | tf_op jit(solution)/shard_map/all_to_all | solution.py:558
  29.6 0.7 %sum.1 = (bf16[32,16,128]{2,1,0:T(8,128)(2,1)}, f32[8,128]{1,0:T(8,128)S(1)}) custom-call(bf16[32,24,128]{2,1,0:T(8,128)(2,1)S(1)} %all-to-all-done.parts_ref), custom_call_target="tpu_custom_call" | custom-call | flops 10000000000 | bytes 1000000 | tf_op jit(solution)/shard_map/sum/pallas_call | solution.py:420
  30.4 2.6 %all-to-all-start.1 = ((bf16[32,16,128]{2,1,0:T(8,128)(2,1)}), bf16[32,16,128]{2,1,0:T(8,128)(2,1)S(1)}, u32[]{:S(2)}, u32[]{:S(2)}) async-start(bf16[32,16,128]{2,1,0:T(8,128)(2,1)} %get-tuple-element.77), calls=%async_computation.1 | async-start | bytes 262144 | tf_op jit(solution)/shard_map/all_to_all | solution.py:607
  32.9 0.0 collective-permute-done.2.even_ref
  32.9 0.0 collective-permute-done.3.odd_ref
  32.9 0.0 copy-done.1
  33.0 0.0 copy-done.3
  33.0 2.4 %results.1 = (bf16[1536,128]{1,0:T(8,128)(2,1)}, bf16[1536,128]{1,0:T(8,128)(2,1)}, f32[1,128]{1,0:T(1,128)}, f32[1,128]{1,0:T(1,128)}, f32[1,128]{1,0:T(1,128)}) custom-call(bf16[2,128,128]{2,1,0:T(8,128)(2,1)S(1)} %collective-permute-done.2.even_ref, bf16[2,128,128]{2,1,0:T(8,128)(2,1)S(1)} %collective-permute-done.3.odd_ref, bf16[1536,128]{1,0:T(8,128)(2,1)} %cot_hbm.3, ...), custom_call_target="tpu_custom_call" | custom-call | flops 49999998976 | bytes 1000000 | tf_op jit(solution)/shard_map/results/pallas_call | solution.py:420
  35.3 6.0 %all-to-all-done.1 = bf16[32,16,128]{2,1,0:T(8,128)(2,1)S(1)} async-done(((bf16[32,16,128]{2,1,0:T(8,128)(2,1)}), bf16[32,16,128]{2,1,0:T(8,128)(2,1)S(1)}, u32[]{:S(2)}, u32[]{:S(2)}) %all-to-all-start.1) | async-done | bytes 131104 | tf_op jit(solution)/shard_map/all_to_all | solution.py:607
  41.3 0.7 %unpack.1 = (f32[128,128]{1,0:T(8,128)}, f32[256,128]{1,0:T(8,128)}, f32[128,128]{1,0:T(8,128)}) custom-call(bf16[512,128]{1,0:T(8,128)(2,1)S(1)} %bitcast.8), custom_call_target="tpu_custom_call" | custom-call | bytes 1000000 | tf_op jit(solution)/shard_map/unpack/pallas_call | solution.py:420
Async XLA Ops:
  1.7 8.5 %collective-permute-start = (bf16[256,128]{1,0:T(8,128)(2,1)S(1)}, bf16[256,128]{1,0:T(8,128)(2,1)S(1)}, u32[]{:S(2)}, u32[]{:S(2)}) collective-permute-start(bf16[256,128]{1,0:T(8,128)(2,1)S(1)} %get-tuple-element.55), channel_id=1, source_target_pairs={{0,1},{2,3},{4,5},{6,7},{8,9},{10,11},{12,13},{14,15},{16,17},{18,... | collective-permute-start | bytes 196616 | tf_op jit(solution)/shard_map/ppermute | solution.py:414
  4.8 5.4 %collective-permute-start.1 = (bf16[256,128]{1,0:T(8,128)(2,1)S(1)}, bf16[256,128]{1,0:T(8,128)(2,1)S(1)}, u32[]{:S(2)}, u32[]{:S(2)}) collective-permute-start(bf16[256,128]{1,0:T(8,128)(2,1)S(1)} %get-tuple-element.56), channel_id=1, source_target_pairs={{1,2},{3,4},{5,6},{7,8},{9,10},{11,12},{13,14},{15,16},{17,18},{19... | collective-permute-start | bytes 196616 | tf_op jit(solution)/shard_map/ppermute | solution.py:414
  10.2 2.2 %copy-start = (bf16[128,1024]{1,0:T(8,128)(2,1)}, bf16[128,1024]{1,0:T(8,128)(2,1)S(1)}, u32[]{:S(2)}) copy-start(bf16[128,1024]{1,0:T(8,128)(2,1)S(1)} %get-tuple-element.70.inner_updated_ref) | copy-start | bytes 786436
  12.4 0.7 %copy-start.2 = (bf16[128,512]{1,0:T(8,128)(2,1)}, bf16[128,512]{1,0:T(8,128)(2,1)S(1)}, u32[]{:S(2)}) copy-start(bf16[128,512]{1,0:T(8,128)(2,1)S(1)} %get-tuple-element.71.outer_updated_ref) | copy-start | bytes 393220
  13.1 16.6 %all-to-all-start = ((bf16[32,24,128]{2,1,0:T(8,128)(2,1)}), bf16[32,24,128]{2,1,0:T(8,128)(2,1)S(1)}, u32[]{:S(2)}, u32[]{:S(2)}) async-start(bf16[32,24,128]{2,1,0:T(8,128)(2,1)} %get-tuple-element.73), calls=%async_computation | async-start | bytes 393216 | tf_op jit(solution)/shard_map/all_to_all | solution.py:558
  21.6 11.3 %collective-permute-start.2 = (bf16[2,128,128]{2,1,0:T(8,128)(2,1)}, bf16[2,128,128]{2,1,0:T(8,128)(2,1)S(1)}, u32[]{:S(2)}, u32[]{:S(2)}) collective-permute-start(bf16[2,128,128]{2,1,0:T(8,128)(2,1)} %get-tuple-element.68), channel_id=1, source_target_pairs={{0,1},{2,3},{4,5},{6,7},{8,9},{10,11},{12,13},{14,15},{16,17},{18,... | collective-permute-start | bytes 196616 | tf_op jit(solution)/shard_map/ppermute | solution.py:414
  23.4 9.6 %copy-start.1 = (bf16[128,1024]{1,0:T(8,128)(2,1)S(1)}, bf16[128,1024]{1,0:T(8,128)(2,1)}, u32[]{:S(2)}) copy-start(bf16[128,1024]{1,0:T(8,128)(2,1)} %copy-done) | copy-start | bytes 786436
  23.4 9.6 %copy-start.3 = (bf16[128,512]{1,0:T(8,128)(2,1)S(1)}, bf16[128,512]{1,0:T(8,128)(2,1)}, u32[]{:S(2)}) copy-start(bf16[128,512]{1,0:T(8,128)(2,1)} %copy-done.2) | copy-start | bytes 393220
  23.4 9.6 %collective-permute-start.3 = (bf16[2,128,128]{2,1,0:T(8,128)(2,1)S(1)}, bf16[2,128,128]{2,1,0:T(8,128)(2,1)S(1)}, u32[]{:S(2)}, u32[]{:S(2)}) collective-permute-start(bf16[2,128,128]{2,1,0:T(8,128)(2,1)S(1)} %get-tuple-element.69), channel_id=1, source_target_pairs={{1,2},{3,4},{5,6},{7,8},{9,10},{11,12},{13,14},{15,16},{17,18},{19... | collective-permute-start | bytes 196616 | tf_op jit(solution)/shard_map/ppermute | solution.py:414
  30.4 11.0 %all-to-all-start.1 = ((bf16[32,16,128]{2,1,0:T(8,128)(2,1)}), bf16[32,16,128]{2,1,0:T(8,128)(2,1)S(1)}, u32[]{:S(2)}, u32[]{:S(2)}) async-start(bf16[32,16,128]{2,1,0:T(8,128)(2,1)} %get-tuple-element.77), calls=%async_computation.1 | async-start | bytes 262144 | tf_op jit(solution)/shard_map/all_to_all | solution.py:607

commit v10 on v9

--- a/solution.py
+++ b/solution.py
@@ -14,7 +14,7 @@
 AXES = ("dom", "feat")
 BF16, F32 = jnp.bfloat16, jnp.float32
 SENT = BF16
-ONES = 128
+ONES = 16
 BIAS_ROWS = 8
 
 kept = pltpu.with_memory_space_constraint
@@ -75,14 +75,9 @@
     return dot(w_first[w_first.shape[1] :], d_hidden_t).astype(BF16)
 
 
-def first_products(d_hidden_t, state, aggregate):
-    ones = jnp.ones((state.shape[0], ONES), BF16)
-    return dot(d_hidden_t, joined_lanes([state, aggregate, ones]))
-
-
-def second_products(active_t, d_norm_t):
-    ones = jnp.ones((16, active_t.shape[1]), BF16)
-    return dot_nt(jnp.concatenate([active_t, ones], axis=0), d_norm_t)
+def node_products(parts, right):
+    ones = jnp.ones((ONES, right.shape[1]), BF16)
+    return dot_nt(jnp.concatenate([*parts, ones], axis=0), right)
 
 
 def fetch_kernel(*refs):
@@ -123,7 +118,7 @@
     edge_cot_ref,
     edge_sum_ref,
     band_ref,
-    updated_ref,
+    updated_hbm,
     d_hidden_ref,
     first_sums_ref,
     second_sums_ref,
@@ -132,7 +127,9 @@
     col_ref,
     counts_ref,
     cot_ref,
+    updated_ref,
     arrived,
+    left,
 ):
     blocks, tiles, size, _ = counts_ref.shape
     features = state_ref.shape[1]
@@ -168,12 +165,11 @@
     for k, b in enumerate(edge_rows):
         edge_state_ref[:, rows(k)] = state_t[b]
 
-    for copy in copies:
-        copy.wait()
-    for k, b in enumerate(edge_rows):
-        edge_cot_ref[:, rows(k)] = cot_ref[rows(b), :].T
     nothing = jnp.zeros((size, size), BF16)
-    for b in [*inner_rows, *edge_rows]:
+    copies[0].wait()
+    for b in range(blocks):
+        if b % part == 0:
+            copies[1 + b // part].wait()
         for place in range(BAND):
             if place != WIN:
                 band_ref[b, place] = nothing
@@ -181,6 +177,9 @@
         own = col_ref[0, b]
         for t in range(1, tiles):
             band_ref[b, col_ref[t, b] - own + WIN] += counts_ref[b, t].astype(F32).astype(BF16)
+    copies[-1].wait()
+    for k, b in enumerate(edge_rows):
+        edge_cot_ref[:, rows(k)] = cot_ref[rows(b), :].T
 
     state = state_ref[...]
     wide = joined_lanes([dot(state, w_msg).astype(BF16), state])
@@ -194,9 +193,11 @@
         edge_sum_ref[k] = neighbour_sum(b)
     summed = jnp.concatenate([neighbour_sum(b).astype(BF16) for b in inner_rows], axis=0)
     aggregate, summed = summed[:, :features], summed[:, features:]
+    inner_state_t = joined_lanes([state_t[b] for b in inner_rows])
+    aggregate_t = joined_lanes(blocks_turned(aggregate))
     updated_t, terms, active_t, d_norm_t, d_hidden_t = node_layer(
-        joined_lanes([state_t[b] for b in inner_rows]),
-        joined_lanes(blocks_turned(aggregate)),
+        inner_state_t,
+        aggregate_t,
         joined_lanes([cot_ref[rows(b), :].T for b in inner_rows]),
         first_t,
         second_t,
@@ -204,23 +205,23 @@
         columns,
     )
     updated_ref[...] = updated_t
+    updated_copy = pltpu.make_async_copy(updated_ref, updated_hbm, left)
+    updated_copy.start()
     d_hidden_ref[...] = d_hidden_t
     d_aggregate_t = d_aggregate_of(w_first, d_hidden_t)
-    first_sums_ref[...] = first_products(
-        d_hidden_t, state_ref[rows(WIN, len(inner_rows)), :], aggregate
-    )
-    second_sums_ref[...] = second_products(active_t, d_norm_t)
+    first_sums_ref[...] = node_products([inner_state_t, aggregate_t], d_hidden_t)
+    second_sums_ref[...] = node_products([active_t], d_norm_t)
     msg_sums_ref[...] = dot(d_aggregate_t, summed)
     gain_sums_ref[...] = sum(
         terms[:, k * size : (k + 1) * size] for k in range(len(inner_rows))
     )
+    updated_copy.wait()
 
 
 def outer_kernel(
     grad_scale,
     got_even_ref,
     got_odd_ref,
-    state_ref,
     w_msg_ref,
     w_first_ref,
     w_second_ref,
@@ -236,8 +237,10 @@
     msg_sums_ref,
     gain_sums_ref,
     grads_ref,
+    updated_hbm,
+    d_hidden_ref,
     updated_ref,
-    d_hidden_ref,
+    left,
 ):
     blocks, _, size, _ = band_ref.shape
     features = w_msg_ref.shape[0]
@@ -258,9 +261,10 @@
         summed.append(edge_sum_ref[WIN + k] + dot(joined_lanes(far), above[: (k + 1) * size]))
     summed = jnp.concatenate(summed, axis=0).astype(BF16)
     aggregate, summed = summed[:, :features], summed[:, features:]
+    aggregate_t = joined_lanes(blocks_turned(aggregate))
     updated_t, terms, active_t, d_norm_t, d_hidden_t = node_layer(
         edge_state_ref[...],
-        joined_lanes(blocks_turned(aggregate)),
+        aggregate_t,
         edge_cot_ref[...],
         first_t_ref[...],
         second_t_ref[...],
@@ -268,30 +272,31 @@
         [columns_ref[k] for k in range(3)],
     )
     updated_ref[...] = updated_t
+    updated_copy = pltpu.make_async_copy(updated_ref, updated_hbm, left)
+    updated_copy.start()
     d_hidden_ref[...] = d_hidden_t
     d_aggregate_t = d_aggregate_of(w_first_ref[...], d_hidden_t)
 
-    width = WIN * size
-    ends = [state_ref[pl.ds(0, width), :], state_ref[pl.ds((blocks - WIN) * size, width), :]]
-    first_sums = first_sums_ref[...] + first_products(
-        d_hidden_t, jnp.concatenate(ends, axis=0), aggregate
-    )
-    second_sums = second_sums_ref[...] + second_products(active_t, d_norm_t)
+    first_sums = first_sums_ref[...] + node_products(
+        [edge_state_ref[...], aggregate_t], d_hidden_t
+    )
+    second_sums = second_sums_ref[...] + node_products([active_t], d_norm_t)
     msg_sums = msg_sums_ref[...] + dot(d_aggregate_t, summed)
     gain_sums = gain_sums_ref[...]
     for k in range(2 * WIN):
         gain_sums = gain_sums + terms[:, k * size : (k + 1) * size]
 
     chunk = grads_ref.shape[1] - BIAS_ROWS
-    turned = [first_sums[:, k * size : (k + 1) * size].T for k in range(3)]
     sums = (
-        jnp.concatenate([turned[0], turned[1], second_sums[:features], msg_sums.T], axis=0)
+        jnp.concatenate(
+            [first_sums[: 2 * features], second_sums[:features], msg_sums.T], axis=0
+        )
         * grad_scale
     ).astype(SENT)
     bias = (
         jnp.concatenate(
             [
-                turned[2][:1],
+                first_sums[2 * features : 2 * features + 1],
                 second_sums[features : features + 1],
                 jnp.sum(gain_sums.T, axis=0, keepdims=True),
             ],
@@ -308,6 +313,7 @@
     for k in range(grads_ref.shape[0]):
         block = sums[k * chunk : (k + 1) * chunk] if k * chunk < sums.shape[0] else nothing
         grads_ref[k] = jnp.concatenate([block, bias], axis=0)
+    updated_copy.wait()
 
 
 def owed_kernel(
@@ -358,8 +364,8 @@
     cot_hbm,
     w_msg_ref,
     w_first_ref,
-    inner_updated_ref,
-    outer_updated_ref,
+    inner_updated_hbm,
+    outer_updated_hbm,
     inner_d_hidden_ref,
     outer_d_hidden_ref,
     owed_ref,
@@ -370,17 +376,30 @@
     b_second_ref,
     gain_ref,
     cot_ref,
+    inner_updated_ref,
+    outer_updated_ref,
     arrived,
 ):
     blocks, features, size = owed_ref.shape
-    copy = pltpu.make_async_copy(cot_hbm, cot_ref, arrived)
-    copy.start()
+    copies = [
+        pltpu.make_async_copy(source, target, arrived.at[k])
+        for k, (source, target) in enumerate(
+            (
+                (cot_hbm, cot_ref),
+                (inner_updated_hbm, inner_updated_ref),
+                (outer_updated_hbm, outer_updated_ref),
+            )
+        )
+    ]
+    for copy in copies:
+        copy.start()
     odd = device_is_odd()
     even_part, odd_part = even_ref[...].astype(F32), odd_ref[...].astype(F32)
     from_below = jnp.where(odd, even_part, odd_part)
     from_above = jnp.where(odd, odd_part, even_part)
     weights = joined_lanes([w_first_ref[pl.ds(0, features), :], w_msg_ref[...]])
-    copy.wait()
+    for copy in copies:
+        copy.wait()
     for b in range(blocks):
         owed = owed_ref[b]
         if b < WIN:
@@ -421,7 +440,9 @@
         kernel,
         out_shape=tuple(outs),
         in_specs=specs,
-        out_specs=tuple(pl.BlockSpec(memory_space=pltpu.VMEM) for _ in outs),
+        out_specs=tuple(
+            pl.BlockSpec(memory_space=getattr(out, "memory_space", pltpu.VMEM)) for out in outs
+        ),
         scratch_shapes=list(scratch),
         compiler_params=pltpu.CompilerParams(vmem_limit_bytes=limit * 1024 * 1024),
         cost_estimate=pl.CostEstimate(
@@ -500,10 +521,10 @@
             vmem((features, edge * size), BF16),
             vmem((edge, size, 2 * features), F32),
             vmem((blocks, BAND, size, size), BF16),
+            hbm((features, inner * size), BF16),
             vmem((features, inner * size), BF16),
-            vmem((features, inner * size), BF16),
-            vmem((features, 2 * features + ONES), F32),
-            vmem((features + 16, features), F32),
+            vmem((2 * features + ONES, features), F32),
+            vmem((features + ONES, features), F32),
             vmem((features, features), F32),
             vmem((features, size), F32),
         ),
@@ -516,7 +537,9 @@
             pltpu.SMEM((tiles, blocks), jnp.int32),
             vmem(edge_counts.shape, jnp.int32),
             vmem((nodes, features), BF16),
+            vmem((features, inner * size), BF16),
             pltpu.SemaphoreType.DMA((6,)),
+            pltpu.SemaphoreType.DMA,
         ),
         limit=32,
         flops=700_000_000,
@@ -527,7 +550,7 @@
         "outer_rows",
         (
             vmem((devices, chunk + BIAS_ROWS, features), SENT),
-            vmem((features, edge * size), BF16),
+            hbm((features, edge * size), BF16),
             vmem((features, edge * size), BF16),
         ),
         [
@@ -535,7 +558,6 @@
             for array in (
                 got_even,
                 got_odd,
-                state,
                 w_msg_here,
                 w_first_here,
                 w_second_here,
@@ -552,6 +574,7 @@
                 gain_sums,
             )
         ],
+        scratch=(vmem((features, edge * size), BF16), pltpu.SemaphoreType.DMA),
         flops=300_000_000,
     )
 
@@ -587,20 +610,14 @@
             result((1, features), F32),
         ),
         [(owed_even, vmem), (owed_odd, vmem), (cotangent, hbm)]
-        + [
-            (array, vmem)
-            for array in (
-                w_msg_here,
-                w_first_here,
-                inner_updated,
-                outer_updated,
-                inner_d_hidden,
-                outer_d_hidden,
-                owed,
-                bias,
-            )
-        ],
-        scratch=(vmem((nodes, features), BF16), pltpu.SemaphoreType.DMA),
+        + [(w_msg_here, vmem), (w_first_here, vmem), (inner_updated, hbm), (outer_updated, hbm)]
+        + [(array, vmem) for array in (inner_d_hidden, outer_d_hidden, owed, bias)],
+        scratch=(
+            vmem((nodes, features), BF16),
+            vmem((features, inner * size), BF16),
+            vmem((features, edge * size), BF16),
+            pltpu.SemaphoreType.DMA((3,)),
+        ),
         flops=50_000_000_000,
     )
 

time: 42.4 us -> 41.8 us (0.986)
  local copies, waits for them, and re-layouts: 0.67 us -> 0 us
    unnamed x8 -> x0, local copies, waits for them, and re-layouts: 0.67 us -> none
  transfers between devices with their start and end apart: 6 -> 6, of which waited for: 2 -> 2; matrix products, arithmetic and copies ran while one was open for 0% -> 0% of each run, Pallas kernels for 22% -> 23%
where the time goes in v10:
time: 41.8 us; the launch traced here: 41.5 us
  starting transfers between devices  15.8 us (38%)
  Pallas kernels  13.5 us (32%)
  waiting for transfers between devices  11.5 us (28%)
  between operations  0.73 us (2%)
    pallas_call x7, Pallas kernels, call(): pl.pallas_call(kernel, out_shape=tuple(outs), in_specs=specs, out_specs=t...  13.5 us
    all_to_all x1, starting transfers between devices, shards(): parts = lax.all_to_all(grads, AXES, 0, 0, tiled=True)  7.04 us
    ppermute x4, starting transfers between devices, swapped(): lax.ppermute(block, AXES, [(i, i + 1) for i in lower] + [(i + 1, i) for i...  6.16 us
    all_to_all x1, waiting for transfers between devices, shards(): whole = lax.all_to_all(spread, AXES, 0, 0, tiled=True)  5.9 us
    all_to_all x1, waiting for transfers between devices, shards(): parts = lax.all_to_all(grads, AXES, 0, 0, tiled=True)  5.61 us
    all_to_all x1, starting transfers between devices, shards(): whole = lax.all_to_all(spread, AXES, 0, 0, tiled=True)  2.56 us
  transfers between devices with their start and end apart: 6, of which 2 were waited for; matrix products, arithmetic and copies ran while one was open for 0% of the time, Pallas kernels for 23%

profile of v10, /device:TPU:0, one launch (start us, length us, event | category | flops | bytes accessed | tf_op | source)
XLA Modules:
  0.0 41.5 jit_solution(7663102000241760283)
XLA Ops:
  0.6 1.1 %fetch.1 = (bf16[1536,128]{1,0:T(8,128)(2,1)S(1)}, bf16[128,128]{1,0:T(8,128)(2,1)S(1)}, bf16[256,128]{1,0:T(8,128)(2,1)S(1)}, bf16[128,128]{1,0:T(8,128)(2,1)S(...) custom-call(bf16[1536,128]{1,0:T(8,128)(2,1)} %refs_0_.1, ...), custom_call_target="tpu_custom_call" | custom-call | bytes 1000000 | tf_op jit(solution)/shard_map/fetch/pallas_call | solution.py:439
  1.7 3.1 %collective-permute-start = (bf16[256,128]{1,0:T(8,128)(2,1)S(1)}, bf16[256,128]{1,0:T(8,128)(2,1)S(1)}, u32[]{:S(2)}, u32[]{:S(2)}) collective-permute-start(bf16[256,128]{1,0:T(8,128)(2,1)S(1)} %get-tuple-element.55), channel_id=1, source_target_pairs={{0,1},{2,3},{4,5},{6,7},{8,9},{10,11},{12,13},{14,15},{16,17},{18,... | collective-permute-start | bytes 196616 | tf_op jit(solution)/shard_map/ppermute | solution.py:433
  4.8 0.7 %collective-permute-start.1 = (bf16[256,128]{1,0:T(8,128)(2,1)S(1)}, bf16[256,128]{1,0:T(8,128)(2,1)S(1)}, u32[]{:S(2)}, u32[]{:S(2)}) collective-permute-start(bf16[256,128]{1,0:T(8,128)(2,1)S(1)} %get-tuple-element.56), channel_id=1, source_target_pairs={{1,2},{3,4},{5,6},{7,8},{9,10},{11,12},{13,14},{15,16},{17,18},{19... | collective-permute-start | bytes 196616 | tf_op jit(solution)/shard_map/ppermute | solution.py:433
  5.5 4.9 %inner_rows.1 = (bf16[128,256]{1,0:T(8,128)(2,1)S(1)}, bf16[128,128]{1,0:T(8,128)(2,1)S(1)}, f32[3,128,128]{2,1,0:T(8,128)S(1)}, bf16[128,512]{1,0:T(8,128)(2,1)...) custom-call(s32[4,12]{1,0:T(4,128)} %bitcast.9, ...), custom_call_target="tpu_custom_call" | custom-call | flops 700000000 | bytes 1000000 | tf_op jit(solution)/shard_map/inner_rows/pallas_call | solution.py:439
  10.4 0.0 collective-permute-done.got_even_ref
  10.4 0.0 collective-permute-done.1.got_odd_ref
  10.4 2.3 %outer_rows.1 = (bf16[32,24,128]{2,1,0:T(8,128)(2,1)}, bf16[128,512]{1,0:T(8,128)(2,1)}, bf16[128,512]{1,0:T(8,128)(2,1)S(1)}) custom-call(bf16[256,128]{1,0:T(8,128)(2,1)S(1)} %collective-permute-done.got_even_ref, bf16[256,128]{1,0:T(8,128)(2,1)S(1)} %collective-permute-done.1.got_odd_ref, bf16[128,128]{1,0:T(8,128)(2,1)S(1)} %get-tuple-element.47.w_msg_ref, ...), custom_call_target="tpu_custom_call" | custom-call | flops 300000000 | bytes 1000000 | tf_op jit(solution)/shard_map/outer_rows/pallas_call | solution.py:439
  12.7 7.0 %all-to-all-start = ((bf16[32,24,128]{2,1,0:T(8,128)(2,1)}), bf16[32,24,128]{2,1,0:T(8,128)(2,1)S(1)}, u32[]{:S(2)}, u32[]{:S(2)}) async-start(bf16[32,24,128]{2,1,0:T(8,128)(2,1)} %get-tuple-element.73), calls=%async_computation | async-start | bytes 393216 | tf_op jit(solution)/shard_map/all_to_all | solution.py:581
  19.8 1.4 %owed.1 = (f32[12,128,128]{2,1,0:T(8,128)S(1)}, bf16[2,128,128]{2,1,0:T(8,128)(2,1)}, bf16[2,128,128]{2,1,0:T(8,128)(2,1)S(1)}) custom-call(bf16[12,5,128,128]{3,2,1,0:T(8,128)(2,1)S(1)} %get-tuple-element.53.band_ref, bf16[256,128]{1,0:T(8,128)(2,1)S(1)} %get-tuple-element.48.w_first_ref, ...), custom_call_target="tpu_custom_call" | custom-call | flops 200000000 | bytes 1000000 | tf_op jit(solution)/shard_map/owed/pallas_call | solution.py:439
  21.1 1.8 %collective-permute-start.2 = (bf16[2,128,128]{2,1,0:T(8,128)(2,1)}, bf16[2,128,128]{2,1,0:T(8,128)(2,1)S(1)}, u32[]{:S(2)}, u32[]{:S(2)}) collective-permute-start(bf16[2,128,128]{2,1,0:T(8,128)(2,1)} %get-tuple-element.68), channel_id=1, source_target_pairs={{0,1},{2,3},{4,5},{6,7},{8,9},{10,11},{12,13},{14,15},{16,17},{18,... | collective-permute-start | bytes 196616 | tf_op jit(solution)/shard_map/ppermute | solution.py:433
  22.9 0.7 %collective-permute-start.3 = (bf16[2,128,128]{2,1,0:T(8,128)(2,1)S(1)}, bf16[2,128,128]{2,1,0:T(8,128)(2,1)S(1)}, u32[]{:S(2)}, u32[]{:S(2)}) collective-permute-start(bf16[2,128,128]{2,1,0:T(8,128)(2,1)S(1)} %get-tuple-element.69), channel_id=1, source_target_pairs={{1,2},{3,4},{5,6},{7,8},{9,10},{11,12},{13,14},{15,16},{17,18},{19... | collective-permute-start | bytes 196616 | tf_op jit(solution)/shard_map/ppermute | solution.py:433
  23.6 5.6 %all-to-all-done.parts_ref = bf16[32,24,128]{2,1,0:T(8,128)(2,1)S(1)} async-done(((bf16[32,24,128]{2,1,0:T(8,128)(2,1)}), bf16[32,24,128]{2,1,0:T(8,128)(2,1)S(1)}, u32[]{:S(2)}, u32[]{:S(2)}) %all-to-all-start) | async-done | bytes 196640 | tf_op jit(solution)/shard_map/all_to_all | solution.py:581
  29.2 0.7 %sum.1 = (bf16[32,16,128]{2,1,0:T(8,128)(2,1)}, f32[8,128]{1,0:T(8,128)S(1)}) custom-call(bf16[32,24,128]{2,1,0:T(8,128)(2,1)S(1)} %all-to-all-done.parts_ref), custom_call_target="tpu_custom_call" | custom-call | flops 10000000000 | bytes 1000000 | tf_op jit(solution)/shard_map/sum/pallas_call | solution.py:439
  29.9 2.6 %all-to-all-start.1 = ((bf16[32,16,128]{2,1,0:T(8,128)(2,1)}), bf16[32,16,128]{2,1,0:T(8,128)(2,1)S(1)}, u32[]{:S(2)}, u32[]{:S(2)}) async-start(bf16[32,16,128]{2,1,0:T(8,128)(2,1)} %get-tuple-element.77), calls=%async_computation.1 | async-start | bytes 262144 | tf_op jit(solution)/shard_map/all_to_all | solution.py:624
  32.4 0.0 collective-permute-done.2.even_ref
  32.4 0.0 collective-permute-done.3.odd_ref
  32.5 2.5 %results.1 = (bf16[1536,128]{1,0:T(8,128)(2,1)}, bf16[1536,128]{1,0:T(8,128)(2,1)}, f32[1,128]{1,0:T(1,128)}, f32[1,128]{1,0:T(1,128)}, f32[1,128]{1,0:T(1,128)}) custom-call(bf16[2,128,128]{2,1,0:T(8,128)(2,1)S(1)} %collective-permute-done.2.even_ref, bf16[2,128,128]{2,1,0:T(8,128)(2,1)S(1)} %collective-permute-done.3.odd_ref, bf16[1536,128]{1,0:T(8,128)(2,1)} %cot_hbm.3, ...), custom_call_target="tpu_custom_call" | custom-call | flops 49999998976 | bytes 1000000 | tf_op jit(solution)/shard_map/results/pallas_call | solution.py:439
  34.9 5.9 %all-to-all-done.1 = bf16[32,16,128]{2,1,0:T(8,128)(2,1)S(1)} async-done(((bf16[32,16,128]{2,1,0:T(8,128)(2,1)}), bf16[32,16,128]{2,1,0:T(8,128)(2,1)S(1)}, u32[]{:S(2)}, u32[]{:S(2)}) %all-to-all-start.1) | async-done | bytes 131104 | tf_op jit(solution)/shard_map/all_to_all | solution.py:624
  40.8 0.7 %unpack.1 = (f32[128,128]{1,0:T(8,128)}, f32[256,128]{1,0:T(8,128)}, f32[128,128]{1,0:T(8,128)}) custom-call(bf16[512,128]{1,0:T(8,128)(2,1)S(1)} %bitcast.8), custom_call_target="tpu_custom_call" | custom-call | bytes 1000000 | tf_op jit(solution)/shard_map/unpack/pallas_call | solution.py:439
Async XLA Ops:
  1.7 8.7 %collective-permute-start = (bf16[256,128]{1,0:T(8,128)(2,1)S(1)}, bf16[256,128]{1,0:T(8,128)(2,1)S(1)}, u32[]{:S(2)}, u32[]{:S(2)}) collective-permute-start(bf16[256,128]{1,0:T(8,128)(2,1)S(1)} %get-tuple-element.55), channel_id=1, source_target_pairs={{0,1},{2,3},{4,5},{6,7},{8,9},{10,11},{12,13},{14,15},{16,17},{18,... | collective-permute-start | bytes 196616 | tf_op jit(solution)/shard_map/ppermute | solution.py:433
  4.8 5.6 %collective-permute-start.1 = (bf16[256,128]{1,0:T(8,128)(2,1)S(1)}, bf16[256,128]{1,0:T(8,128)(2,1)S(1)}, u32[]{:S(2)}, u32[]{:S(2)}) collective-permute-start(bf16[256,128]{1,0:T(8,128)(2,1)S(1)} %get-tuple-element.56), channel_id=1, source_target_pairs={{1,2},{3,4},{5,6},{7,8},{9,10},{11,12},{13,14},{15,16},{17,18},{19... | collective-permute-start | bytes 196616 | tf_op jit(solution)/shard_map/ppermute | solution.py:433
  12.7 16.5 %all-to-all-start = ((bf16[32,24,128]{2,1,0:T(8,128)(2,1)}), bf16[32,24,128]{2,1,0:T(8,128)(2,1)S(1)}, u32[]{:S(2)}, u32[]{:S(2)}) async-start(bf16[32,24,128]{2,1,0:T(8,128)(2,1)} %get-tuple-element.73), calls=%async_computation | async-start | bytes 393216 | tf_op jit(solution)/shard_map/all_to_all | solution.py:581
  21.1 11.3 %collective-permute-start.2 = (bf16[2,128,128]{2,1,0:T(8,128)(2,1)}, bf16[2,128,128]{2,1,0:T(8,128)(2,1)S(1)}, u32[]{:S(2)}, u32[]{:S(2)}) collective-permute-start(bf16[2,128,128]{2,1,0:T(8,128)(2,1)} %get-tuple-element.68), channel_id=1, source_target_pairs={{0,1},{2,3},{4,5},{6,7},{8,9},{10,11},{12,13},{14,15},{16,17},{18,... | collective-permute-start | bytes 196616 | tf_op jit(solution)/shard_map/ppermute | solution.py:433
  22.9 9.5 %collective-permute-start.3 = (bf16[2,128,128]{2,1,0:T(8,128)(2,1)S(1)}, bf16[2,128,128]{2,1,0:T(8,128)(2,1)S(1)}, u32[]{:S(2)}, u32[]{:S(2)}) collective-permute-start(bf16[2,128,128]{2,1,0:T(8,128)(2,1)S(1)} %get-tuple-element.69), channel_id=1, source_target_pairs={{1,2},{3,4},{5,6},{7,8},{9,10},{11,12},{13,14},{15,16},{17,18},{19... | collective-permute-start | bytes 196616 | tf_op jit(solution)/shard_map/ppermute | solution.py:433
  29.9 11.0 %all-to-all-start.1 = ((bf16[32,16,128]{2,1,0:T(8,128)(2,1)}), bf16[32,16,128]{2,1,0:T(8,128)(2,1)S(1)}, u32[]{:S(2)}, u32[]{:S(2)}) async-start(bf16[32,16,128]{2,1,0:T(8,128)(2,1)} %get-tuple-element.77), calls=%async_computation.1 | async-start | bytes 262144 | tf_op jit(solution)/shard_map/all_to_all | solution.py:624

commit v11 on v10

--- a/solution.py
+++ b/solution.py
@@ -14,7 +14,7 @@
 AXES = ("dom", "feat")
 BF16, F32 = jnp.bfloat16, jnp.float32
 SENT = BF16
-ONES = 16
+ONES = 128
 BIAS_ROWS = 8
 
 kept = pltpu.with_memory_space_constraint
@@ -75,9 +75,14 @@
     return dot(w_first[w_first.shape[1] :], d_hidden_t).astype(BF16)
 
 
-def node_products(parts, right):
-    ones = jnp.ones((ONES, right.shape[1]), BF16)
-    return dot_nt(jnp.concatenate([*parts, ones], axis=0), right)
+def first_products(d_hidden_t, state, aggregate):
+    ones = jnp.ones((state.shape[0], ONES), BF16)
+    return dot(d_hidden_t, joined_lanes([state, aggregate, ones]))
+
+
+def second_products(active_t, d_norm_t):
+    ones = jnp.ones((16, active_t.shape[1]), BF16)
+    return dot_nt(jnp.concatenate([active_t, ones], axis=0), d_norm_t)
 
 
 def fetch_kernel(*refs):
@@ -102,8 +107,8 @@
 
 def inner_kernel(
     col_hbm,
-    counts_hbm,
-    cot_hbm,
+    counts_ref,
+    cot_ref,
     state_ref,
     w_msg_ref,
     w_first_ref,
@@ -125,8 +130,6 @@
     msg_sums_ref,
     gain_sums_ref,
     col_ref,
-    counts_ref,
-    cot_ref,
     updated_ref,
     arrived,
     left,
@@ -135,20 +138,8 @@
     features = state_ref.shape[1]
     edge_rows = [*range(WIN), *range(blocks - WIN, blocks)]
     inner_rows = range(WIN, blocks - WIN)
-    part = blocks // 4
-
-    copies = [(col_hbm, col_ref)]
-    copies += [
-        (counts_hbm.at[pl.ds(b, part)], counts_ref.at[pl.ds(b, part)])
-        for b in range(0, blocks, part)
-    ]
-    copies.append((cot_hbm, cot_ref))
-    copies = [
-        pltpu.make_async_copy(source, target, arrived.at[k])
-        for k, (source, target) in enumerate(copies)
-    ]
-    for copy in copies:
-        copy.start()
+    col_copy = pltpu.make_async_copy(col_hbm, col_ref, arrived)
+    col_copy.start()
 
     def rows(block, count=1):
         return pl.ds(block * size, count * size)
@@ -166,10 +157,8 @@
         edge_state_ref[:, rows(k)] = state_t[b]
 
     nothing = jnp.zeros((size, size), BF16)
-    copies[0].wait()
+    col_copy.wait()
     for b in range(blocks):
-        if b % part == 0:
-            copies[1 + b // part].wait()
         for place in range(BAND):
             if place != WIN:
                 band_ref[b, place] = nothing
@@ -177,7 +166,6 @@
         own = col_ref[0, b]
         for t in range(1, tiles):
             band_ref[b, col_ref[t, b] - own + WIN] += counts_ref[b, t].astype(F32).astype(BF16)
-    copies[-1].wait()
     for k, b in enumerate(edge_rows):
         edge_cot_ref[:, rows(k)] = cot_ref[rows(b), :].T
 
@@ -209,8 +197,10 @@
     updated_copy.start()
     d_hidden_ref[...] = d_hidden_t
     d_aggregate_t = d_aggregate_of(w_first, d_hidden_t)
-    first_sums_ref[...] = node_products([inner_state_t, aggregate_t], d_hidden_t)
-    second_sums_ref[...] = node_products([active_t], d_norm_t)
+    first_sums_ref[...] = first_products(
+        d_hidden_t, state[WIN * size : (blocks - WIN) * size], aggregate
+    )
+    second_sums_ref[...] = second_products(active_t, d_norm_t)
     msg_sums_ref[...] = dot(d_aggregate_t, summed)
     gain_sums_ref[...] = sum(
         terms[:, k * size : (k + 1) * size] for k in range(len(inner_rows))
@@ -222,6 +212,7 @@
     grad_scale,
     got_even_ref,
     got_odd_ref,
+    state_ref,
     w_msg_ref,
     w_first_ref,
     w_second_ref,
@@ -277,26 +268,27 @@
     d_hidden_ref[...] = d_hidden_t
     d_aggregate_t = d_aggregate_of(w_first_ref[...], d_hidden_t)
 
-    first_sums = first_sums_ref[...] + node_products(
-        [edge_state_ref[...], aggregate_t], d_hidden_t
-    )
-    second_sums = second_sums_ref[...] + node_products([active_t], d_norm_t)
+    width = WIN * size
+    ends = [state_ref[pl.ds(0, width), :], state_ref[pl.ds((blocks - WIN) * size, width), :]]
+    first_sums = first_sums_ref[...] + first_products(
+        d_hidden_t, jnp.concatenate(ends, axis=0), aggregate
+    )
+    second_sums = second_sums_ref[...] + second_products(active_t, d_norm_t)
     msg_sums = msg_sums_ref[...] + dot(d_aggregate_t, summed)
     gain_sums = gain_sums_ref[...]
     for k in range(2 * WIN):
         gain_sums = gain_sums + terms[:, k * size : (k + 1) * size]
 
     chunk = grads_ref.shape[1] - BIAS_ROWS
+    turned = [first_sums[:, k * size : (k + 1) * size].T for k in range(3)]
     sums = (
-        jnp.concatenate(
-            [first_sums[: 2 * features], second_sums[:features], msg_sums.T], axis=0
-        )
+        jnp.concatenate([turned[0], turned[1], second_sums[:features], msg_sums.T], axis=0)
         * grad_scale
     ).astype(SENT)
     bias = (
         jnp.concatenate(
             [
-                first_sums[2 * features : 2 * features + 1],
+                turned[2][:1],
                 second_sums[features : features + 1],
                 jnp.sum(gain_sums.T, axis=0, keepdims=True),
             ],
@@ -491,6 +483,7 @@
         + [vmem((WIN * size, features), BF16)] * 2,
         [(array, hbm) for array in sources],
         scratch=(pltpu.SemaphoreType.DMA((len(sources),)),),
+        flops=50_000_000_000,
     )
     state, w_msg_here, w_first_here, w_second_here, *vectors = fetched
     got_even = swapped(even_side, 0)
@@ -523,22 +516,20 @@
             vmem((blocks, BAND, size, size), BF16),
             hbm((features, inner * size), BF16),
             vmem((features, inner * size), BF16),
-            vmem((2 * features + ONES, features), F32),
-            vmem((features + ONES, features), F32),
+            vmem((features, 2 * features + ONES), F32),
+            vmem((features + 16, features), F32),
             vmem((features, features), F32),
             vmem((features, size), F32),
         ),
-        [(col_index.T, hbm), (edge_counts, hbm), (cotangent, hbm)]
+        [(col_index.T, hbm), (edge_counts, vmem), (cotangent, vmem)]
         + [
             (array, vmem)
             for array in (state, w_msg_here, w_first_here, w_second_here, *vectors)
         ],
         scratch=(
             pltpu.SMEM((tiles, blocks), jnp.int32),
-            vmem(edge_counts.shape, jnp.int32),
-            vmem((nodes, features), BF16),
             vmem((features, inner * size), BF16),
-            pltpu.SemaphoreType.DMA((6,)),
+            pltpu.SemaphoreType.DMA,
             pltpu.SemaphoreType.DMA,
         ),
         limit=32,
@@ -558,6 +549,7 @@
             for array in (
                 got_even,
                 got_odd,
+                state,
                 w_msg_here,
                 w_first_here,
                 w_second_here,

time: 41.8 us -> 41.9 us (level)
  starting transfers between devices: 15.8 us -> 16.7 us
  Pallas kernels: 13.5 us -> 12.7 us
    all_to_all x1, starting transfers between devices: 7.04 us -> 7.98 us  [shards(): parts = lax.all_to_all(grads, AXES, 0, 0, tiled=True)]
    pallas_call x7, Pallas kernels: 13.5 us -> 12.7 us  [call(): pl.pallas_call(kernel, out_shape=tuple(outs), in_specs=specs, out_specs=t...]
  transfers between devices with their start and end apart: 6 -> 6, of which waited for: 2 -> 2; matrix products, arithmetic and copies ran while one was open for 0% -> 0% of each run, Pallas kernels for 23% -> 20%
where the time goes in v11:
time: 41.9 us; the launch traced here: 41.7 us
  starting transfers between devices  16.7 us (40%)
  Pallas kernels  12.7 us (30%)
  waiting for transfers between devices  11.5 us (27%)
  between operations  0.77 us (2%)
    pallas_call x7, Pallas kernels, call(): pl.pallas_call(kernel, out_shape=tuple(outs), in_specs=specs, out_specs=t...  12.7 us
    all_to_all x1, starting transfers between devices, shards(): parts = lax.all_to_all(grads, AXES, 0, 0, tiled=True)  7.98 us
    ppermute x4, starting transfers between devices, swapped(): lax.ppermute(block, AXES, [(i, i + 1) for i in lower] + [(i + 1, i) for i...  6.16 us
    all_to_all x1, waiting for transfers between devices, shards(): whole = lax.all_to_all(spread, AXES, 0, 0, tiled=True)  5.9 us
    all_to_all x1, waiting for transfers between devices, shards(): parts = lax.all_to_all(grads, AXES, 0, 0, tiled=True)  5.61 us
    all_to_all x1, starting transfers between devices, shards(): whole = lax.all_to_all(spread, AXES, 0, 0, tiled=True)  2.56 us
  transfers between devices with their start and end apart: 6, of which 2 were waited for; matrix products, arithmetic and copies ran while one was open for 0% of the time, Pallas kernels for 20%

profile of v11, /device:TPU:0, one launch (start us, length us, event | category | flops | bytes accessed | tf_op | source)
XLA Modules:
  0.0 41.7 jit_solution(3277802009228239355)
XLA Ops:
  0.6 0.0 copy-start
  0.6 0.0 copy-start.1
  0.7 1.3 %fetch.1 = (bf16[1536,128]{1,0:T(8,128)(2,1)S(1)}, bf16[128,128]{1,0:T(8,128)(2,1)S(1)}, bf16[256,128]{1,0:T(8,128)(2,1)S(1)}, bf16[128,128]{1,0:T(8,128)(2,1)S(...) custom-call(bf16[1536,128]{1,0:T(8,128)(2,1)} %refs_0_.1, ...), custom_call_target="tpu_custom_call" | custom-call | flops 49999998976 | bytes 1000000 | tf_op jit(solution)/shard_map/fetch/pallas_call | solution.py:431
  1.9 3.1 %collective-permute-start = (bf16[256,128]{1,0:T(8,128)(2,1)S(1)}, bf16[256,128]{1,0:T(8,128)(2,1)S(1)}, u32[]{:S(2)}, u32[]{:S(2)}) collective-permute-start(bf16[256,128]{1,0:T(8,128)(2,1)S(1)} %get-tuple-element.55), channel_id=1, source_target_pairs={{0,1},{2,3},{4,5},{6,7},{8,9},{10,11},{12,13},{14,15},{16,17},{18,... | collective-permute-start | bytes 196616 | tf_op jit(solution)/shard_map/ppermute | solution.py:425
  5.0 0.7 %collective-permute-start.1 = (bf16[256,128]{1,0:T(8,128)(2,1)S(1)}, bf16[256,128]{1,0:T(8,128)(2,1)S(1)}, u32[]{:S(2)}, u32[]{:S(2)}) collective-permute-start(bf16[256,128]{1,0:T(8,128)(2,1)S(1)} %get-tuple-element.56), channel_id=1, source_target_pairs={{1,2},{3,4},{5,6},{7,8},{9,10},{11,12},{13,14},{15,16},{17,18},{19... | collective-permute-start | bytes 196616 | tf_op jit(solution)/shard_map/ppermute | solution.py:425
  5.7 0.0 copy-done
  5.7 0.0 copy-done.1
  5.7 3.9 %inner_rows.1 = (bf16[128,256]{1,0:T(8,128)(2,1)S(1)}, bf16[128,128]{1,0:T(8,128)(2,1)S(1)}, f32[3,128,128]{2,1,0:T(8,128)S(1)}, bf16[128,512]{1,0:T(8,128)(2,1)...) custom-call(s32[4,12]{1,0:T(4,128)} %bitcast.9, ...), custom_call_target="tpu_custom_call" | custom-call | flops 700000000 | bytes 1000000 | tf_op jit(solution)/shard_map/inner_rows/pallas_call | solution.py:431
  9.6 0.0 collective-permute-done.got_even_ref
  9.6 0.0 collective-permute-done.1.got_odd_ref
  9.6 2.2 %outer_rows.1 = (bf16[32,24,128]{2,1,0:T(8,128)(2,1)}, bf16[128,512]{1,0:T(8,128)(2,1)}, bf16[128,512]{1,0:T(8,128)(2,1)S(1)}) custom-call(bf16[256,128]{1,0:T(8,128)(2,1)S(1)} %collective-permute-done.got_even_ref, bf16[256,128]{1,0:T(8,128)(2,1)S(1)} %collective-permute-done.1.got_odd_ref, bf16[1536,128]{1,0:T(8,128)(2,1)S(1)} %get-tuple-element.46.state_ref, ...), custom_call_target="tpu_custom_call" | custom-call | flops 300000000 | bytes 1000000 | tf_op jit(solution)/shard_map/outer_rows/pallas_call | solution.py:431
  11.9 8.0 %all-to-all-start = ((bf16[32,24,128]{2,1,0:T(8,128)(2,1)}), bf16[32,24,128]{2,1,0:T(8,128)(2,1)S(1)}, u32[]{:S(2)}, u32[]{:S(2)}) async-start(bf16[32,24,128]{2,1,0:T(8,128)(2,1)} %get-tuple-element.73), calls=%async_computation | async-start | bytes 393216 | tf_op jit(solution)/shard_map/all_to_all | solution.py:573
  19.9 1.4 %owed.1 = (f32[12,128,128]{2,1,0:T(8,128)S(1)}, bf16[2,128,128]{2,1,0:T(8,128)(2,1)}, bf16[2,128,128]{2,1,0:T(8,128)(2,1)}) custom-call(bf16[12,5,128,128]{3,2,1,0:T(8,128)(2,1)S(1)} %get-tuple-element.53.band_ref, bf16[256,128]{1,0:T(8,128)(2,1)S(1)} %get-tuple-element.48.w_first_ref, bf16[128,1024]{1,0:T(8,128)(2,1)S(1)} %get-tuple-element.54.inner_ref.inner_d_hidden_ref, ...), custom_call_target="tpu_custom_call" | custom-call | flops 200000000 | bytes 1000000 | tf_op jit(solution)/shard_map/owed/pallas_call | solution.py:431
  21.2 1.8 %collective-permute-start.2 = (bf16[2,128,128]{2,1,0:T(8,128)(2,1)}, bf16[2,128,128]{2,1,0:T(8,128)(2,1)S(1)}, u32[]{:S(2)}, u32[]{:S(2)}) collective-permute-start(bf16[2,128,128]{2,1,0:T(8,128)(2,1)} %get-tuple-element.68), channel_id=1, source_target_pairs={{0,1},{2,3},{4,5},{6,7},{8,9},{10,11},{12,13},{14,15},{16,17},{18,... | collective-permute-start | bytes 196616 | tf_op jit(solution)/shard_map/ppermute | solution.py:425
  23.0 0.7 %collective-permute-start.3 = (bf16[2,128,128]{2,1,0:T(8,128)(2,1)}, bf16[2,128,128]{2,1,0:T(8,128)(2,1)S(1)}, u32[]{:S(2)}, u32[]{:S(2)}) collective-permute-start(bf16[2,128,128]{2,1,0:T(8,128)(2,1)} %get-tuple-element.69), channel_id=1, source_target_pairs={{1,2},{3,4},{5,6},{7,8},{9,10},{11,12},{13,14},{15,16},{17,18},{19... | collective-permute-start | bytes 196616 | tf_op jit(solution)/shard_map/ppermute | solution.py:425
  23.7 5.6 %all-to-all-done.parts_ref = bf16[32,24,128]{2,1,0:T(8,128)(2,1)S(1)} async-done(((bf16[32,24,128]{2,1,0:T(8,128)(2,1)}), bf16[32,24,128]{2,1,0:T(8,128)(2,1)S(1)}, u32[]{:S(2)}, u32[]{:S(2)}) %all-to-all-start) | async-done | bytes 196640 | tf_op jit(solution)/shard_map/all_to_all | solution.py:573
  29.3 0.7 %sum.1 = (bf16[32,16,128]{2,1,0:T(8,128)(2,1)}, f32[8,128]{1,0:T(8,128)S(1)}) custom-call(bf16[32,24,128]{2,1,0:T(8,128)(2,1)S(1)} %all-to-all-done.parts_ref), custom_call_target="tpu_custom_call" | custom-call | flops 10000000000 | bytes 1000000 | tf_op jit(solution)/shard_map/sum/pallas_call | solution.py:431
  30.0 2.6 %all-to-all-start.1 = ((bf16[32,16,128]{2,1,0:T(8,128)(2,1)}), bf16[32,16,128]{2,1,0:T(8,128)(2,1)S(1)}, u32[]{:S(2)}, u32[]{:S(2)}) async-start(bf16[32,16,128]{2,1,0:T(8,128)(2,1)} %get-tuple-element.77), calls=%async_computation.1 | async-start | bytes 262144 | tf_op jit(solution)/shard_map/all_to_all | solution.py:616
  32.5 0.0 collective-permute-done.2.even_ref
  32.6 0.0 collective-permute-done.3.odd_ref
  32.6 2.5 %results.1 = (bf16[1536,128]{1,0:T(8,128)(2,1)}, bf16[1536,128]{1,0:T(8,128)(2,1)}, f32[1,128]{1,0:T(1,128)}, f32[1,128]{1,0:T(1,128)}, f32[1,128]{1,0:T(1,128)}) custom-call(bf16[2,128,128]{2,1,0:T(8,128)(2,1)S(1)} %collective-permute-done.2.even_ref, bf16[2,128,128]{2,1,0:T(8,128)(2,1)S(1)} %collective-permute-done.3.odd_ref, bf16[1536,128]{1,0:T(8,128)(2,1)} %cot_hbm.1, ...), custom_call_target="tpu_custom_call" | custom-call | flops 49999998976 | bytes 1000000 | tf_op jit(solution)/shard_map/results/pallas_call | solution.py:431
  35.0 5.9 %all-to-all-done.1 = bf16[32,16,128]{2,1,0:T(8,128)(2,1)S(1)} async-done(((bf16[32,16,128]{2,1,0:T(8,128)(2,1)}), bf16[32,16,128]{2,1,0:T(8,128)(2,1)S(1)}, u32[]{:S(2)}, u32[]{:S(2)}) %all-to-all-start.1) | async-done | bytes 131104 | tf_op jit(solution)/shard_map/all_to_all | solution.py:616
  40.9 0.7 %unpack.1 = (f32[128,128]{1,0:T(8,128)}, f32[256,128]{1,0:T(8,128)}, f32[128,128]{1,0:T(8,128)}) custom-call(bf16[512,128]{1,0:T(8,128)(2,1)S(1)} %bitcast.8), custom_call_target="tpu_custom_call" | custom-call | bytes 1000000 | tf_op jit(solution)/shard_map/unpack/pallas_call | solution.py:431
Async XLA Ops:
  0.6 5.0 %copy-start = (s32[12,4,128,128]{3,2,1,0:T(8,128)S(1)}, s32[12,4,128,128]{3,2,1,0:T(8,128)}, u32[]{:S(2)}) copy-start(s32[12,4,128,128]{3,2,1,0:T(8,128)} %counts_ref.1) | copy-start | bytes 9437188
  0.6 5.0 %copy-start.1 = (bf16[1536,128]{1,0:T(8,128)(2,1)S(1)}, bf16[1536,128]{1,0:T(8,128)(2,1)}, u32[]{:S(2)}) copy-start(bf16[1536,128]{1,0:T(8,128)(2,1)} %cot_hbm.1) | copy-start | bytes 1179652
  1.9 7.7 %collective-permute-start = (bf16[256,128]{1,0:T(8,128)(2,1)S(1)}, bf16[256,128]{1,0:T(8,128)(2,1)S(1)}, u32[]{:S(2)}, u32[]{:S(2)}) collective-permute-start(bf16[256,128]{1,0:T(8,128)(2,1)S(1)} %get-tuple-element.55), channel_id=1, source_target_pairs={{0,1},{2,3},{4,5},{6,7},{8,9},{10,11},{12,13},{14,15},{16,17},{18,... | collective-permute-start | bytes 196616 | tf_op jit(solution)/shard_map/ppermute | solution.py:425
  5.0 4.6 %collective-permute-start.1 = (bf16[256,128]{1,0:T(8,128)(2,1)S(1)}, bf16[256,128]{1,0:T(8,128)(2,1)S(1)}, u32[]{:S(2)}, u32[]{:S(2)}) collective-permute-start(bf16[256,128]{1,0:T(8,128)(2,1)S(1)} %get-tuple-element.56), channel_id=1, source_target_pairs={{1,2},{3,4},{5,6},{7,8},{9,10},{11,12},{13,14},{15,16},{17,18},{19... | collective-permute-start | bytes 196616 | tf_op jit(solution)/shard_map/ppermute | solution.py:425
  11.9 17.4 %all-to-all-start = ((bf16[32,24,128]{2,1,0:T(8,128)(2,1)}), bf16[32,24,128]{2,1,0:T(8,128)(2,1)S(1)}, u32[]{:S(2)}, u32[]{:S(2)}) async-start(bf16[32,24,128]{2,1,0:T(8,128)(2,1)} %get-tuple-element.73), calls=%async_computation | async-start | bytes 393216 | tf_op jit(solution)/shard_map/all_to_all | solution.py:573
  21.2 11.3 %collective-permute-start.2 = (bf16[2,128,128]{2,1,0:T(8,128)(2,1)}, bf16[2,128,128]{2,1,0:T(8,128)(2,1)S(1)}, u32[]{:S(2)}, u32[]{:S(2)}) collective-permute-start(bf16[2,128,128]{2,1,0:T(8,128)(2,1)} %get-tuple-element.68), channel_id=1, source_target_pairs={{0,1},{2,3},{4,5},{6,7},{8,9},{10,11},{12,13},{14,15},{16,17},{18,... | collective-permute-start | bytes 196616 | tf_op jit(solution)/shard_map/ppermute | solution.py:425
  23.0 9.5 %collective-permute-start.3 = (bf16[2,128,128]{2,1,0:T(8,128)(2,1)}, bf16[2,128,128]{2,1,0:T(8,128)(2,1)S(1)}, u32[]{:S(2)}, u32[]{:S(2)}) collective-permute-start(bf16[2,128,128]{2,1,0:T(8,128)(2,1)} %get-tuple-element.69), channel_id=1, source_target_pairs={{1,2},{3,4},{5,6},{7,8},{9,10},{11,12},{13,14},{15,16},{17,18},{19... | collective-permute-start | bytes 196616 | tf_op jit(solution)/shard_map/ppermute | solution.py:425
  30.0 11.0 %all-to-all-start.1 = ((bf16[32,16,128]{2,1,0:T(8,128)(2,1)}), bf16[32,16,128]{2,1,0:T(8,128)(2,1)S(1)}, u32[]{:S(2)}, u32[]{:S(2)}) async-start(bf16[32,16,128]{2,1,0:T(8,128)(2,1)} %get-tuple-element.77), calls=%async_computation.1 | async-start | bytes 262144 | tf_op jit(solution)/shard_map/all_to_all | solution.py:616

commit v12 on v11

--- a/solution.py
+++ b/solution.py
@@ -85,23 +85,27 @@
     return dot_nt(jnp.concatenate([active_t, ones], axis=0), d_norm_t)
 
 
-def fetch_kernel(*refs):
+def fetch_kernel(state_hbm, *refs):
     count = (len(refs) - 3) // 2
     sources, targets = refs[:count], refs[count : 2 * count]
     even_side_ref, odd_side_ref, arrived = refs[2 * count :]
+    edge = even_side_ref.shape[0]
+    odd = device_is_odd()
+    last = state_hbm.shape[0] - edge
+    even_start = pl.multiple_of(jnp.where(odd, 0, last), edge)
+    odd_start = pl.multiple_of(jnp.where(odd, last, 0), edge)
+    pairs = [
+        (state_hbm.at[pl.ds(even_start, edge)], even_side_ref),
+        (state_hbm.at[pl.ds(odd_start, edge)], odd_side_ref),
+        *zip(sources, targets),
+    ]
     copies = [
         pltpu.make_async_copy(source, target, arrived.at[k])
-        for k, (source, target) in enumerate(zip(sources, targets))
+        for k, (source, target) in enumerate(pairs)
     ]
     for copy in copies:
         copy.start()
-    copies[0].wait()
-    state, edge = targets[0], even_side_ref.shape[0]
-    odd = device_is_odd()
-    head, tail = state[pl.ds(0, edge), :], state[pl.ds(state.shape[0] - edge, edge), :]
-    even_side_ref[...] = jnp.where(odd, head, tail)
-    odd_side_ref[...] = jnp.where(odd, tail, head)
-    for copy in copies[1:]:
+    for copy in copies:
         copy.wait()
 
 
@@ -110,6 +114,7 @@
     counts_ref,
     cot_ref,
     state_ref,
+    got_even_ref,
     w_msg_ref,
     w_first_ref,
     w_second_ref,
@@ -119,9 +124,11 @@
     first_t_ref,
     second_t_ref,
     columns_ref,
-    edge_state_ref,
-    edge_cot_ref,
-    edge_sum_ref,
+    side_state_ref,
+    side_state_t_ref,
+    side_cot_ref,
+    side_sum_ref,
+    side_far_ref,
     band_ref,
     updated_hbm,
     d_hidden_ref,
@@ -136,8 +143,16 @@
 ):
     blocks, tiles, size, _ = counts_ref.shape
     features = state_ref.shape[1]
-    edge_rows = [*range(WIN), *range(blocks - WIN, blocks)]
     inner_rows = range(WIN, blocks - WIN)
+    low_rows, high_rows = range(WIN), range(blocks - WIN, blocks)
+    odd = device_is_odd()
+
+    def even_side(low, high):
+        return jnp.where(odd, low, high)
+
+    def odd_side(low, high):
+        return jnp.where(odd, high, low)
+
     col_copy = pltpu.make_async_copy(col_hbm, col_ref, arrived)
     col_copy.start()
 
@@ -152,9 +167,9 @@
     second_t_ref[...] = second_t
     for k in range(3):
         columns_ref[k] = columns[k]
-    state_t = [state_ref[rows(b), :].T for b in range(blocks)]
-    for k, b in enumerate(edge_rows):
-        edge_state_ref[:, rows(k)] = state_t[b]
+    state = state_ref[...]
+    state_t = [state[b * size : (b + 1) * size].T for b in range(blocks)]
+    cot_t = [cot_ref[rows(b), :].T for b in range(blocks)]
 
     nothing = jnp.zeros((size, size), BF16)
     col_copy.wait()
@@ -166,10 +181,7 @@
         own = col_ref[0, b]
         for t in range(1, tiles):
             band_ref[b, col_ref[t, b] - own + WIN] += counts_ref[b, t].astype(F32).astype(BF16)
-    for k, b in enumerate(edge_rows):
-        edge_cot_ref[:, rows(k)] = cot_ref[rows(b), :].T
-
-    state = state_ref[...]
+
     wide = joined_lanes([dot(state, w_msg).astype(BF16), state])
 
     def neighbour_sum(b):
@@ -177,16 +189,33 @@
         tiles_of = [band_ref[b, block - b + WIN] for block in range(first, last + 1)]
         return dot(joined_lanes(tiles_of), wide[first * size : (last + 1) * size])
 
-    for k, b in enumerate(edge_rows):
-        edge_sum_ref[k] = neighbour_sum(b)
-    summed = jnp.concatenate([neighbour_sum(b).astype(BF16) for b in inner_rows], axis=0)
+    def far(b, first):
+        places = [block - b + WIN for block in range(first, first + WIN)]
+        return joined_lanes([band_ref[b, p] if 0 <= p < BAND else nothing for p in places])
+
+    def stacked(parts):
+        return jnp.concatenate(list(parts), axis=0)
+
+    ends = (stacked(map(neighbour_sum, low_rows)), stacked(map(neighbour_sum, high_rows)))
+    fars = (stacked(far(b, -WIN) for b in low_rows), stacked(far(b, blocks) for b in high_rows))
+    end_states = (state[: WIN * size], state[(blocks - WIN) * size :])
+    end_states_t = (joined_lanes(state_t[:WIN]), joined_lanes(state_t[blocks - WIN :]))
+    end_cots_t = (joined_lanes(cot_t[:WIN]), joined_lanes(cot_t[blocks - WIN :]))
+    side_sum_ref[...] = odd_side(*ends)
+    side_far_ref[...] = odd_side(*fars)
+    side_state_ref[...] = odd_side(*end_states)
+    side_state_t_ref[...] = odd_side(*end_states_t)
+    side_cot_ref[...] = odd_side(*end_cots_t)
+
+    halo = got_even_ref[...]
+    wide_halo = joined_lanes([dot(halo, w_msg).astype(BF16), halo])
+    end_sum = even_side(*ends) + dot(even_side(*fars), wide_halo)
+    summed = stacked([*map(neighbour_sum, inner_rows), end_sum]).astype(BF16)
     aggregate, summed = summed[:, :features], summed[:, features:]
-    inner_state_t = joined_lanes([state_t[b] for b in inner_rows])
-    aggregate_t = joined_lanes(blocks_turned(aggregate))
     updated_t, terms, active_t, d_norm_t, d_hidden_t = node_layer(
-        inner_state_t,
-        aggregate_t,
-        joined_lanes([cot_ref[rows(b), :].T for b in inner_rows]),
+        joined_lanes([*state_t[WIN : blocks - WIN], even_side(*end_states_t)]),
+        joined_lanes(blocks_turned(aggregate)),
+        joined_lanes([*cot_t[WIN : blocks - WIN], even_side(*end_cots_t)]),
         first_t,
         second_t,
         w_second,
@@ -198,31 +227,32 @@
     d_hidden_ref[...] = d_hidden_t
     d_aggregate_t = d_aggregate_of(w_first, d_hidden_t)
     first_sums_ref[...] = first_products(
-        d_hidden_t, state[WIN * size : (blocks - WIN) * size], aggregate
+        d_hidden_t,
+        stacked([state[WIN * size : (blocks - WIN) * size], even_side(*end_states)]),
+        aggregate,
     )
     second_sums_ref[...] = second_products(active_t, d_norm_t)
     msg_sums_ref[...] = dot(d_aggregate_t, summed)
     gain_sums_ref[...] = sum(
-        terms[:, k * size : (k + 1) * size] for k in range(len(inner_rows))
+        terms[:, k * size : (k + 1) * size] for k in range(blocks - WIN)
     )
     updated_copy.wait()
 
 
 def outer_kernel(
     grad_scale,
-    got_even_ref,
     got_odd_ref,
-    state_ref,
     w_msg_ref,
     w_first_ref,
     w_second_ref,
     first_t_ref,
     second_t_ref,
     columns_ref,
-    edge_state_ref,
-    edge_cot_ref,
-    edge_sum_ref,
-    band_ref,
+    side_state_ref,
+    side_state_t_ref,
+    side_cot_ref,
+    side_sum_ref,
+    side_far_ref,
     first_sums_ref,
     second_sums_ref,
     msg_sums_ref,
@@ -233,30 +263,15 @@
     updated_ref,
     left,
 ):
-    blocks, _, size, _ = band_ref.shape
-    features = w_msg_ref.shape[0]
-    odd = device_is_odd()
-    got_even, got_odd = got_even_ref[...], got_odd_ref[...]
-    below, above = jnp.where(odd, got_even, got_odd), jnp.where(odd, got_odd, got_even)
-
-    w_msg = w_msg_ref[...]
-    below, above = (
-        joined_lanes([dot(halo, w_msg).astype(BF16), halo]) for halo in (below, above)
-    )
-    summed = []
-    for k in range(WIN):
-        far = joined_lanes([band_ref[k, place] for place in range(WIN - k)])
-        summed.append(edge_sum_ref[k] + dot(far, below[k * size :]))
-    for k in range(WIN):
-        far = [band_ref[blocks - WIN + k, place] for place in range(2 * WIN - k, BAND)]
-        summed.append(edge_sum_ref[WIN + k] + dot(joined_lanes(far), above[: (k + 1) * size]))
-    summed = jnp.concatenate(summed, axis=0).astype(BF16)
+    features, size = w_msg_ref.shape[0], columns_ref.shape[2]
+    halo = got_odd_ref[...]
+    wide_halo = joined_lanes([dot(halo, w_msg_ref[...]).astype(BF16), halo])
+    summed = (side_sum_ref[...] + dot(side_far_ref[...], wide_halo)).astype(BF16)
     aggregate, summed = summed[:, :features], summed[:, features:]
-    aggregate_t = joined_lanes(blocks_turned(aggregate))
     updated_t, terms, active_t, d_norm_t, d_hidden_t = node_layer(
-        edge_state_ref[...],
-        aggregate_t,
-        edge_cot_ref[...],
+        side_state_t_ref[...],
+        joined_lanes(blocks_turned(aggregate)),
+        side_cot_ref[...],
         first_t_ref[...],
         second_t_ref[...],
         w_second_ref[...],
@@ -268,15 +283,11 @@
     d_hidden_ref[...] = d_hidden_t
     d_aggregate_t = d_aggregate_of(w_first_ref[...], d_hidden_t)
 
-    width = WIN * size
-    ends = [state_ref[pl.ds(0, width), :], state_ref[pl.ds((blocks - WIN) * size, width), :]]
-    first_sums = first_sums_ref[...] + first_products(
-        d_hidden_t, jnp.concatenate(ends, axis=0), aggregate
-    )
+    first_sums = first_sums_ref[...] + first_products(d_hidden_t, side_state_ref[...], aggregate)
     second_sums = second_sums_ref[...] + second_products(active_t, d_norm_t)
     msg_sums = msg_sums_ref[...] + dot(d_aggregate_t, summed)
     gain_sums = gain_sums_ref[...]
-    for k in range(2 * WIN):
+    for k in range(WIN):
         gain_sums = gain_sums + terms[:, k * size : (k + 1) * size]
 
     chunk = grads_ref.shape[1] - BIAS_ROWS
@@ -320,8 +331,10 @@
     def d_aggregate(b):
         if WIN <= b < blocks - WIN:
             return inner[:, (b - WIN) * size : (b - WIN + 1) * size]
-        k = b if b < WIN else b - blocks + 2 * WIN
-        return outer[:, k * size : (k + 1) * size]
+        k = b if b < WIN else b - blocks + WIN
+        even_end = inner[:, (blocks - 2 * WIN + k) * size : (blocks - 2 * WIN + k + 1) * size]
+        odd_end = outer[:, k * size : (k + 1) * size]
+        return jnp.where(odd == (b < WIN), even_end, odd_end)
 
     def owed(block):
         near = range(max(block - WIN, 0), min(block + WIN, blocks - 1) + 1)
@@ -399,14 +412,22 @@
         elif b >= blocks - WIN:
             owed = owed + from_above[b - blocks + WIN]
         if WIN <= b < blocks - WIN:
-            k, updated, d_hidden = b - WIN, inner_updated_ref, inner_d_hidden_ref
+            lanes = pl.ds((b - WIN) * size, size)
+            updated, d_hidden = inner_updated_ref[:, lanes], inner_d_hidden_ref[:, lanes]
         else:
-            k = b if b < WIN else b - blocks + 2 * WIN
-            updated, d_hidden = outer_updated_ref, outer_d_hidden_ref
-        lanes, rows = pl.ds(k * size, size), pl.ds(b * size, size)
-        change = dot(weights, jnp.concatenate([d_hidden[:, lanes], owed.astype(BF16)], axis=0))
+            k = b if b < WIN else b - blocks + WIN
+            even_end = odd == (b < WIN)
+            lanes, outer_lanes = pl.ds((blocks - 2 * WIN + k) * size, size), pl.ds(k * size, size)
+            updated = jnp.where(
+                even_end, inner_updated_ref[:, lanes], outer_updated_ref[:, outer_lanes]
+            )
+            d_hidden = jnp.where(
+                even_end, inner_d_hidden_ref[:, lanes], outer_d_hidden_ref[:, outer_lanes]
+            )
+        rows = pl.ds(b * size, size)
+        change = dot(weights, jnp.concatenate([d_hidden, owed.astype(BF16)], axis=0))
         grad_state_ref[rows, :] = (cot_ref[rows, :].astype(F32) + change.T).astype(BF16)
-        updated_ref[rows, :] = updated[:, lanes].T
+        updated_ref[rows, :] = updated.T
     for k, ref in enumerate((b_first_ref, b_second_ref, gain_ref)):
         ref[...] = bias_ref[pl.ds(k, 1), :] + bias_ref[pl.ds(k + 3, 1), :]
 
@@ -461,79 +482,63 @@
     devices = lax.axis_size(AXES)
     grad_scale = 1.0 / math.sqrt(nodes * devices)
     chunk = -(-4 * features // (devices * 8)) * 8
-    inner = blocks - 2 * WIN
-    edge = 2 * WIN
+    side = WIN * size
+    most = nodes - side
     vmem, hbm = pltpu.VMEM, pltpu.HBM
     result = jax.ShapeDtypeStruct
 
     row = lambda vector: vector.reshape(1, features)
-    sources = (
-        node_state,
-        w_msg,
-        w_first,
-        w_second,
-        row(b_first),
-        row(b_second),
-        row(ln_gain),
-    )
+    sources = (w_msg, w_first, w_second, row(b_first), row(b_second), row(ln_gain))
     *fetched, even_side, odd_side = call(
         fetch_kernel,
         "fetch",
         [vmem(array.shape, array.dtype) for array in sources]
-        + [vmem((WIN * size, features), BF16)] * 2,
-        [(array, hbm) for array in sources],
-        scratch=(pltpu.SemaphoreType.DMA((len(sources),)),),
+        + [vmem((side, features), BF16)] * 2,
+        [(array, hbm) for array in (node_state, *sources)],
+        scratch=(pltpu.SemaphoreType.DMA((len(sources) + 2,)),),
         flops=50_000_000_000,
     )
-    state, w_msg_here, w_first_here, w_second_here, *vectors = fetched
+    w_msg_here, w_first_here, w_second_here, *vectors = fetched
     got_even = swapped(even_side, 0)
     got_odd = swapped(odd_side, 1)
 
-    (
-        first_t,
-        second_t,
-        columns,
-        edge_state,
-        edge_cot,
-        edge_sum,
-        band,
-        inner_updated,
-        inner_d_hidden,
-        first_sums,
-        second_sums,
-        msg_sums,
-        gain_sums,
-    ) = call(
-        inner_kernel,
-        "inner_rows",
-        (
-            vmem((features, 2 * features), BF16),
-            vmem((features, features), BF16),
-            vmem((3, features, size), F32),
-            vmem((features, edge * size), BF16),
-            vmem((features, edge * size), BF16),
-            vmem((edge, size, 2 * features), F32),
-            vmem((blocks, BAND, size, size), BF16),
-            hbm((features, inner * size), BF16),
-            vmem((features, inner * size), BF16),
-            vmem((features, 2 * features + ONES), F32),
-            vmem((features + 16, features), F32),
-            vmem((features, features), F32),
-            vmem((features, size), F32),
-        ),
-        [(col_index.T, hbm), (edge_counts, vmem), (cotangent, vmem)]
-        + [
-            (array, vmem)
-            for array in (state, w_msg_here, w_first_here, w_second_here, *vectors)
-        ],
-        scratch=(
-            pltpu.SMEM((tiles, blocks), jnp.int32),
-            vmem((features, inner * size), BF16),
-            pltpu.SemaphoreType.DMA,
-            pltpu.SemaphoreType.DMA,
-        ),
-        limit=32,
-        flops=700_000_000,
+    *outer_operands, band, inner_updated, inner_d_hidden = (
+        lambda *outs: (*outs[:8], *outs[11:], *outs[8:11])
+    )(
+        *call(
+            inner_kernel,
+            "inner_rows",
+            (
+                vmem((features, 2 * features), BF16),
+                vmem((features, features), BF16),
+                vmem((3, features, size), F32),
+                vmem((side, features), BF16),
+                vmem((features, side), BF16),
+                vmem((features, side), BF16),
+                vmem((side, 2 * features), F32),
+                vmem((side, side), BF16),
+                vmem((blocks, BAND, size, size), BF16),
+                hbm((features, most), BF16),
+                vmem((features, most), BF16),
+                vmem((features, 2 * features + ONES), F32),
+                vmem((features + 16, features), F32),
+                vmem((features, features), F32),
+                vmem((features, size), F32),
+            ),
+            [(col_index.T, hbm)]
+            + [
+                (array, vmem)
+                for array in (edge_counts, cotangent, node_state, got_even, *fetched)
+            ],
+            scratch=(
+                pltpu.SMEM((tiles, blocks), jnp.int32),
+                vmem((features, most), BF16),
+                pltpu.SemaphoreType.DMA,
+                pltpu.SemaphoreType.DMA,
+            ),
+            limit=32,
+            flops=700_000_000,
+        )
     )
 
     grads, outer_updated, outer_d_hidden = call(
@@ -541,32 +546,14 @@
         "outer_rows",
         (
             vmem((devices, chunk + BIAS_ROWS, features), SENT),
-            hbm((features, edge * size), BF16),
-            vmem((features, edge * size), BF16),
+            hbm((features, side), BF16),
+            vmem((features, side), BF16),
         ),
         [
             (array, vmem)
-            for array in (
-                got_even,
-                got_odd,
-                state,
-                w_msg_here,
-                w_first_here,
-                w_second_here,
-                first_t,
-                second_t,
-                columns,
-                edge_state,
-                edge_cot,
-                edge_sum,
-                band,
-                first_sums,
-                second_sums,
-                msg_sums,
-                gain_sums,
-            )
+            for array in (got_odd, w_msg_here, w_first_here, w_second_here, *outer_operands)
         ],
-        scratch=(vmem((features, edge * size), BF16), pltpu.SemaphoreType.DMA),
+        scratch=(vmem((features, side), BF16), pltpu.SemaphoreType.DMA),
         flops=300_000_000,
     )
 
@@ -606,8 +593,8 @@
         + [(array, vmem) for array in (inner_d_hidden, outer_d_hidden, owed, bias)],
         scratch=(
             vmem((nodes, features), BF16),
-            vmem((features, inner * size), BF16),
-            vmem((features, edge * size), BF16),
+            vmem((features, most), BF16),
+            vmem((features, side), BF16),
             pltpu.SemaphoreType.DMA((3,)),
         ),
         flops=50_000_000_000,

time: 41.9 us -> 41.8 us (level)
  starting transfers between devices: 16.7 us -> 15.3 us
  waiting for transfers between devices: 11.5 us -> 12.5 us
  local copies, waits for them, and re-layouts: 0.01 us -> 0.9 us
  Pallas kernels: 12.7 us -> 11.9 us
    ppermute x4, waiting for transfers between devices: 0.01 us -> 1.59 us  [swapped(): lax.ppermute(block, AXES, [(i, i + 1) for i in lower] + [(i + 1, i) for i...]
    all_to_all x1, starting transfers between devices: 7.98 us -> 6.46 us  [shards(): parts = lax.all_to_all(grads, AXES, 0, 0, tiled=True)]
    unnamed x4 -> x10, local copies, waits for them, and re-layouts: 0.01 us -> 0.9 us
    pallas_call x7, Pallas kernels: 12.7 us -> 11.9 us  [call(): pl.pallas_call(kernel, out_shape=tuple(outs), in_specs=specs, out_specs=t...]
    all_to_all x1, waiting for transfers between devices: 5.61 us -> 5.06 us  [shards(): parts = lax.all_to_all(grads, AXES, 0, 0, tiled=True)]
  transfers between devices with their start and end apart: 6 -> 6, of which waited for: 2 -> 3; matrix products, arithmetic and copies ran while one was open for 0% -> 0% of each run, Pallas kernels for 20% -> 19%
where the time goes in v12:
time: 41.8 us; the launch traced here: 41.5 us
  starting transfers between devices  15.3 us (37%)
  waiting for transfers between devices  12.5 us (30%)
  Pallas kernels  11.9 us (28%)
  local copies, waits for them, and re-layouts  0.9 us (2%)
  between operations  0.78 us (2%)
    pallas_call x7, Pallas kernels, call(): pl.pallas_call(kernel, out_shape=tuple(outs), in_specs=specs, out_specs=t...  11.9 us
    all_to_all x1, starting transfers between devices, shards(): parts = lax.all_to_all(grads, AXES, 0, 0, tiled=True)  6.46 us
    ppermute x4, starting transfers between devices, swapped(): lax.ppermute(block, AXES, [(i, i + 1) for i in lower] + [(i + 1, i) for i...  6.31 us
    all_to_all x1, waiting for transfers between devices, shards(): whole = lax.all_to_all(spread, AXES, 0, 0, tiled=True)  5.89 us
    all_to_all x1, waiting for transfers between devices, shards(): parts = lax.all_to_all(grads, AXES, 0, 0, tiled=True)  5.06 us
    all_to_all x1, starting transfers between devices, shards(): whole = lax.all_to_all(spread, AXES, 0, 0, tiled=True)  2.58 us
    ppermute x4, waiting for transfers between devices, swapped(): lax.ppermute(block, AXES, [(i, i + 1) for i in lower] + [(i + 1, i) for i...  1.59 us
    unnamed x10, local copies, waits for them, and re-layouts  0.9 us
  transfers between devices with their start and end apart: 6, of which 3 were waited for; matrix products, arithmetic and copies ran while one was open for 0% of the time, Pallas kernels for 19%

profile of v12, /device:TPU:0, one launch (start us, length us, event | category | flops | bytes accessed | tf_op | source)
XLA Modules:
  0.0 41.5 jit_solution(10503997645738725729)
XLA Ops:
  0.6 0.0 copy-start
  0.6 0.0 copy-start.1
  0.7 0.0 copy-start.2
  0.7 1.2 %fetch.1 = (bf16[128,128]{1,0:T(8,128)(2,1)S(1)}, bf16[256,128]{1,0:T(8,128)(2,1)S(1)}, bf16[128,128]{1,0:T(8,128)(2,1)S(1)}, f32[1,128]{1,0:T(1,128)S(1)}, f32[...) custom-call(bf16[1536,128]{1,0:T(8,128)(2,1)} %state_ref.1, ...), custom_call_target="tpu_custom_call" | custom-call | flops 49999998976 | bytes 1000000 | tf_op jit(solution)/shard_map/fetch/pallas_call | solution.py:452
  1.8 3.1 %collective-permute-start = (bf16[256,128]{1,0:T(8,128)(2,1)S(1)}, bf16[256,128]{1,0:T(8,128)(2,1)S(1)}, u32[]{:S(2)}, u32[]{:S(2)}) collective-permute-start(bf16[256,128]{1,0:T(8,128)(2,1)S(1)} %get-tuple-element.47), channel_id=1, source_target_pairs={{0,1},{2,3},{4,5},{6,7},{8,9},{10,11},{12,13},{14,15},{16,17},{18,... | collective-permute-start | bytes 196616 | tf_op jit(solution)/shard_map/ppermute | solution.py:446
  4.9 0.7 %collective-permute-start.1 = (bf16[256,128]{1,0:T(8,128)(2,1)S(1)}, bf16[256,128]{1,0:T(8,128)(2,1)S(1)}, u32[]{:S(2)}, u32[]{:S(2)}) collective-permute-start(bf16[256,128]{1,0:T(8,128)(2,1)S(1)} %get-tuple-element.56), channel_id=1, source_target_pairs={{1,2},{3,4},{5,6},{7,8},{9,10},{11,12},{13,14},{15,16},{17,18},{19... | collective-permute-start | bytes 196616 | tf_op jit(solution)/shard_map/ppermute | solution.py:446
  5.6 1.6 %collective-permute-done.got_even_ref = bf16[256,128]{1,0:T(8,128)(2,1)S(1)} collective-permute-done((bf16[256,128]{1,0:T(8,128)(2,1)S(1)}, bf16[256,128]{1,0:T(8,128)(2,1)S(1)}, u32[]{:S(2)}, u32[]{:S(2)}) %collective-permute-start) | collective-permute-done | bytes 65568 | tf_op jit(solution)/shard_map/ppermute | solution.py:446
  7.2 0.0 copy-done
  7.2 0.0 copy-done.1
  7.2 0.0 copy-done.2
  7.2 3.9 %inner_rows.1 = (bf16[128,256]{1,0:T(8,128)(2,1)S(1)}, bf16[128,128]{1,0:T(8,128)(2,1)S(1)}, f32[3,128,128]{2,1,0:T(8,128)S(1)}, bf16[256,128]{1,0:T(8,128)(2,1)...) custom-call(s32[4,12]{1,0:T(4,128)} %bitcast.9, ...), custom_call_target="tpu_custom_call" | custom-call | flops 700000000 | bytes 1000000 | tf_op jit(solution)/shard_map/inner_rows/pallas_call | solution.py:452
  11.1 0.0 collective-permute-done.1.got_odd_ref
  11.1 2.2 %outer_rows.1 = (bf16[32,24,128]{2,1,0:T(8,128)(2,1)}, bf16[128,256]{1,0:T(8,128)(2,1)}, bf16[128,256]{1,0:T(8,128)(2,1)S(1)}) custom-call(bf16[256,128]{1,0:T(8,128)(2,1)S(1)} %collective-permute-done.1.got_odd_ref, bf16[128,128]{1,0:T(8,128)(2,1)S(1)} %get-tuple-element.48.w_msg_ref, bf16[256,128]{1,0:T(8,128)(2,1)S(1)} %get-tuple-element.49.w_first_ref, ...), custom_call_target="tpu_custom_call" | custom-call | flops 300000000 | bytes 1000000 | tf_op jit(solution)/shard_map/outer_rows/pallas_call | solution.py:452
  13.2 6.5 %all-to-all-start = ((bf16[32,24,128]{2,1,0:T(8,128)(2,1)}), bf16[32,24,128]{2,1,0:T(8,128)(2,1)S(1)}, u32[]{:S(2)}, u32[]{:S(2)}) async-start(bf16[32,24,128]{2,1,0:T(8,128)(2,1)} %get-tuple-element.75), calls=%async_computation | async-start | bytes 393216 | tf_op jit(solution)/shard_map/all_to_all | solution.py:560
  19.7 0.9 %owed.1 = (f32[12,128,128]{2,1,0:T(8,128)S(1)}, bf16[2,128,128]{2,1,0:T(8,128)(2,1)S(1)}, bf16[2,128,128]{2,1,0:T(8,128)(2,1)S(1)}) custom-call(bf16[12,5,128,128]{3,2,1,0:T(8,128)(2,1)S(1)} %get-tuple-element.54.band_ref, bf16[256,128]{1,0:T(8,128)(2,1)S(1)} %get-tuple-element.49.w_first_ref, ...), custom_call_target="tpu_custom_call" | custom-call | flops 200000000 | bytes 1000000 | tf_op jit(solution)/shard_map/owed/pallas_call | solution.py:452
  20.6 0.0 copy-start.3
  20.6 0.9 %copy-done.3 = f32[12,128,128]{2,1,0:T(8,128)} copy-done((f32[12,128,128]{2,1,0:T(8,128)}, f32[12,128,128]{2,1,0:T(8,128)S(1)}, u32[]{:S(2)}) %copy-start.3) | copy-done | bytes 786456
  21.5 1.8 %collective-permute-start.2 = (bf16[2,128,128]{2,1,0:T(8,128)(2,1)S(1)}, bf16[2,128,128]{2,1,0:T(8,128)(2,1)S(1)}, u32[]{:S(2)}, u32[]{:S(2)}) collective-permute-start(bf16[2,128,128]{2,1,0:T(8,128)(2,1)S(1)} %get-tuple-element.70), channel_id=1, source_target_pairs={{0,1},{2,3},{4,5},{6,7},{8,9},{10,11},{12,13},{14,15},{16,17},{18,... | collective-permute-start | bytes 196616 | tf_op jit(solution)/shard_map/ppermute | solution.py:446
  23.3 0.0 copy-start.4
  23.3 0.8 %collective-permute-start.3 = (bf16[2,128,128]{2,1,0:T(8,128)(2,1)S(1)}, bf16[2,128,128]{2,1,0:T(8,128)(2,1)S(1)}, u32[]{:S(2)}, u32[]{:S(2)}) collective-permute-start(bf16[2,128,128]{2,1,0:T(8,128)(2,1)S(1)} %get-tuple-element.71), channel_id=1, source_target_pairs={{1,2},{3,4},{5,6},{7,8},{9,10},{11,12},{13,14},{15,16},{17,18},{19... | collective-permute-start | bytes 196616 | tf_op jit(solution)/shard_map/ppermute | solution.py:446
  24.1 5.1 %all-to-all-done.parts_ref = bf16[32,24,128]{2,1,0:T(8,128)(2,1)S(1)} async-done(((bf16[32,24,128]{2,1,0:T(8,128)(2,1)}), bf16[32,24,128]{2,1,0:T(8,128)(2,1)S(1)}, u32[]{:S(2)}, u32[]{:S(2)}) %all-to-all-start) | async-done | bytes 196640 | tf_op jit(solution)/shard_map/all_to_all | solution.py:560
  29.1 0.7 %sum.1 = (bf16[32,16,128]{2,1,0:T(8,128)(2,1)}, f32[8,128]{1,0:T(8,128)S(1)}) custom-call(bf16[32,24,128]{2,1,0:T(8,128)(2,1)S(1)} %all-to-all-done.parts_ref), custom_call_target="tpu_custom_call" | custom-call | flops 10000000000 | bytes 1000000 | tf_op jit(solution)/shard_map/sum/pallas_call | solution.py:452
  29.8 2.6 %all-to-all-start.1 = ((bf16[32,16,128]{2,1,0:T(8,128)(2,1)}), bf16[32,16,128]{2,1,0:T(8,128)(2,1)S(1)}, u32[]{:S(2)}, u32[]{:S(2)}) async-start(bf16[32,16,128]{2,1,0:T(8,128)(2,1)} %get-tuple-element.79), calls=%async_computation.1 | async-start | bytes 262144 | tf_op jit(solution)/shard_map/all_to_all | solution.py:603
  32.4 0.0 collective-permute-done.2.even_ref
  32.4 0.0 collective-permute-done.3.odd_ref
  32.4 0.0 copy-done.4
  32.4 2.5 %results.1 = (bf16[1536,128]{1,0:T(8,128)(2,1)}, bf16[1536,128]{1,0:T(8,128)(2,1)}, f32[1,128]{1,0:T(1,128)}, f32[1,128]{1,0:T(1,128)}, f32[1,128]{1,0:T(1,128)}) custom-call(bf16[2,128,128]{2,1,0:T(8,128)(2,1)S(1)} %collective-permute-done.2.even_ref, bf16[2,128,128]{2,1,0:T(8,128)(2,1)S(1)} %collective-permute-done.3.odd_ref, bf16[1536,128]{1,0:T(8,128)(2,1)} %cot_hbm.1, ...), custom_call_target="tpu_custom_call" | custom-call | flops 49999998976 | bytes 1000000 | tf_op jit(solution)/shard_map/results/pallas_call | solution.py:452
  34.9 5.9 %all-to-all-done.1 = bf16[32,16,128]{2,1,0:T(8,128)(2,1)S(1)} async-done(((bf16[32,16,128]{2,1,0:T(8,128)(2,1)}), bf16[32,16,128]{2,1,0:T(8,128)(2,1)S(1)}, u32[]{:S(2)}, u32[]{:S(2)}) %all-to-all-start.1) | async-done | bytes 131104 | tf_op jit(solution)/shard_map/all_to_all | solution.py:603
  40.8 0.7 %unpack.1 = (f32[128,128]{1,0:T(8,128)}, f32[256,128]{1,0:T(8,128)}, f32[128,128]{1,0:T(8,128)}) custom-call(bf16[512,128]{1,0:T(8,128)(2,1)S(1)} %bitcast.8), custom_call_target="tpu_custom_call" | custom-call | bytes 1000000 | tf_op jit(solution)/shard_map/unpack/pallas_call | solution.py:452
Async XLA Ops:
  0.6 6.5 %copy-start = (s32[12,4,128,128]{3,2,1,0:T(8,128)S(1)}, s32[12,4,128,128]{3,2,1,0:T(8,128)}, u32[]{:S(2)}) copy-start(s32[12,4,128,128]{3,2,1,0:T(8,128)} %counts_ref.1) | copy-start | bytes 9437188
  0.6 6.5 %copy-start.1 = (bf16[1536,128]{1,0:T(8,128)(2,1)S(1)}, bf16[1536,128]{1,0:T(8,128)(2,1)}, u32[]{:S(2)}) copy-start(bf16[1536,128]{1,0:T(8,128)(2,1)} %state_ref.1) | copy-start | bytes 1179652
  0.7 6.5 %copy-start.2 = (bf16[1536,128]{1,0:T(8,128)(2,1)S(1)}, bf16[1536,128]{1,0:T(8,128)(2,1)}, u32[]{:S(2)}) copy-start(bf16[1536,128]{1,0:T(8,128)(2,1)} %cot_hbm.1) | copy-start | bytes 1179652
  1.8 5.3 %collective-permute-start = (bf16[256,128]{1,0:T(8,128)(2,1)S(1)}, bf16[256,128]{1,0:T(8,128)(2,1)S(1)}, u32[]{:S(2)}, u32[]{:S(2)}) collective-permute-start(bf16[256,128]{1,0:T(8,128)(2,1)S(1)} %get-tuple-element.47), channel_id=1, source_target_pairs={{0,1},{2,3},{4,5},{6,7},{8,9},{10,11},{12,13},{14,15},{16,17},{18,... | collective-permute-start | bytes 196616 | tf_op jit(solution)/shard_map/ppermute | solution.py:446
  4.9 6.1 %collective-permute-start.1 = (bf16[256,128]{1,0:T(8,128)(2,1)S(1)}, bf16[256,128]{1,0:T(8,128)(2,1)S(1)}, u32[]{:S(2)}, u32[]{:S(2)}) collective-permute-start(bf16[256,128]{1,0:T(8,128)(2,1)S(1)} %get-tuple-element.56), channel_id=1, source_target_pairs={{1,2},{3,4},{5,6},{7,8},{9,10},{11,12},{13,14},{15,16},{17,18},{19... | collective-permute-start | bytes 196616 | tf_op jit(solution)/shard_map/ppermute | solution.py:446
  13.2 15.9 %all-to-all-start = ((bf16[32,24,128]{2,1,0:T(8,128)(2,1)}), bf16[32,24,128]{2,1,0:T(8,128)(2,1)S(1)}, u32[]{:S(2)}, u32[]{:S(2)}) async-start(bf16[32,24,128]{2,1,0:T(8,128)(2,1)} %get-tuple-element.75), calls=%async_computation | async-start | bytes 393216 | tf_op jit(solution)/shard_map/all_to_all | solution.py:560
  20.6 0.9 %copy-start.3 = (f32[12,128,128]{2,1,0:T(8,128)}, f32[12,128,128]{2,1,0:T(8,128)S(1)}, u32[]{:S(2)}) copy-start(f32[12,128,128]{2,1,0:T(8,128)S(1)} %get-tuple-element.74.owed_ref) | copy-start | bytes 2359300
  21.5 10.9 %collective-permute-start.2 = (bf16[2,128,128]{2,1,0:T(8,128)(2,1)S(1)}, bf16[2,128,128]{2,1,0:T(8,128)(2,1)S(1)}, u32[]{:S(2)}, u32[]{:S(2)}) collective-permute-start(bf16[2,128,128]{2,1,0:T(8,128)(2,1)S(1)} %get-tuple-element.70), channel_id=1, source_target_pairs={{0,1},{2,3},{4,5},{6,7},{8,9},{10,11},{12,13},{14,15},{16,17},{18,... | collective-permute-start | bytes 196616 | tf_op jit(solution)/shard_map/ppermute | solution.py:446
  23.3 9.2 %copy-start.4 = (f32[12,128,128]{2,1,0:T(8,128)S(1)}, f32[12,128,128]{2,1,0:T(8,128)}, u32[]{:S(2)}) copy-start(f32[12,128,128]{2,1,0:T(8,128)} %copy-done.3) | copy-start | bytes 2359300
  23.3 9.1 %collective-permute-start.3 = (bf16[2,128,128]{2,1,0:T(8,128)(2,1)S(1)}, bf16[2,128,128]{2,1,0:T(8,128)(2,1)S(1)}, u32[]{:S(2)}, u32[]{:S(2)}) collective-permute-start(bf16[2,128,128]{2,1,0:T(8,128)(2,1)S(1)} %get-tuple-element.71), channel_id=1, source_target_pairs={{1,2},{3,4},{5,6},{7,8},{9,10},{11,12},{13,14},{15,16},{17,18},{19... | collective-permute-start | bytes 196616 | tf_op jit(solution)/shard_map/ppermute | solution.py:446
  29.8 11.0 %all-to-all-start.1 = ((bf16[32,16,128]{2,1,0:T(8,128)(2,1)}), bf16[32,16,128]{2,1,0:T(8,128)(2,1)S(1)}, u32[]{:S(2)}, u32[]{:S(2)}) async-start(bf16[32,16,128]{2,1,0:T(8,128)(2,1)} %get-tuple-element.79), calls=%async_computation.1 | async-start | bytes 262144 | tf_op jit(solution)/shard_map/all_to_all | solution.py:603

commit v13 on v12

--- a/solution.py
+++ b/solution.py
@@ -80,28 +80,22 @@
     return dot(d_hidden_t, joined_lanes([state, aggregate, ones]))
 
 
-def second_products(active_t, d_norm_t):
-    ones = jnp.ones((16, active_t.shape[1]), BF16)
-    return dot_nt(jnp.concatenate([active_t, ones], axis=0), d_norm_t)
-
-
-def fetch_kernel(state_hbm, *refs):
-    count = (len(refs) - 3) // 2
-    sources, targets = refs[:count], refs[count : 2 * count]
-    even_side_ref, odd_side_ref, arrived = refs[2 * count :]
-    edge = even_side_ref.shape[0]
+def sums_over_nodes(lefts, right):
+    ones = jnp.ones((16, right.shape[1]), BF16)
+    return dot_nt(jnp.concatenate([*lefts, ones], axis=0), right)
+
+
+def cut_kernel(state_hbm, even_side_ref, odd_side_ref, arrived):
+    side = even_side_ref.shape[0]
     odd = device_is_odd()
-    last = state_hbm.shape[0] - edge
-    even_start = pl.multiple_of(jnp.where(odd, 0, last), edge)
-    odd_start = pl.multiple_of(jnp.where(odd, last, 0), edge)
-    pairs = [
-        (state_hbm.at[pl.ds(even_start, edge)], even_side_ref),
-        (state_hbm.at[pl.ds(odd_start, edge)], odd_side_ref),
-        *zip(sources, targets),
-    ]
+    last = state_hbm.shape[0] - side
+    even_start = pl.multiple_of(jnp.where(odd, 0, last), side)
+    odd_start = pl.multiple_of(jnp.where(odd, last, 0), side)
     copies = [
-        pltpu.make_async_copy(source, target, arrived.at[k])
-        for k, (source, target) in enumerate(pairs)
+        pltpu.make_async_copy(state_hbm.at[pl.ds(start, side)], target, arrived.at[k])
+        for k, (start, target) in enumerate(
+            ((even_start, even_side_ref), (odd_start, odd_side_ref))
+        )
     ]
     for copy in copies:
         copy.start()
@@ -121,10 +115,12 @@
     b_first_ref,
     b_second_ref,
     gain_ref,
+    w_msg_here_ref,
+    w_first_here_ref,
+    w_second_here_ref,
     first_t_ref,
     second_t_ref,
     columns_ref,
-    side_state_ref,
     side_state_t_ref,
     side_cot_ref,
     side_sum_ref,
@@ -163,6 +159,9 @@
     first_t = joined_lanes([w_first[:features].T, w_first[features:].T])
     second_t = w_second.T
     columns = [column(ref, size) for ref in (b_first_ref, b_second_ref, gain_ref)]
+    w_msg_here_ref[...] = w_msg
+    w_first_here_ref[...] = w_first
+    w_second_here_ref[...] = w_second
     first_t_ref[...] = first_t
     second_t_ref[...] = second_t
     for k in range(3):
@@ -203,7 +202,6 @@
     end_cots_t = (joined_lanes(cot_t[:WIN]), joined_lanes(cot_t[blocks - WIN :]))
     side_sum_ref[...] = odd_side(*ends)
     side_far_ref[...] = odd_side(*fars)
-    side_state_ref[...] = odd_side(*end_states)
     side_state_t_ref[...] = odd_side(*end_states_t)
     side_cot_ref[...] = odd_side(*end_cots_t)
 
@@ -231,7 +229,7 @@
         stacked([state[WIN * size : (blocks - WIN) * size], even_side(*end_states)]),
         aggregate,
     )
-    second_sums_ref[...] = second_products(active_t, d_norm_t)
+    second_sums_ref[...] = sums_over_nodes([active_t], d_norm_t)
     msg_sums_ref[...] = dot(d_aggregate_t, summed)
     gain_sums_ref[...] = sum(
         terms[:, k * size : (k + 1) * size] for k in range(blocks - WIN)
@@ -248,7 +246,6 @@
     first_t_ref,
     second_t_ref,
     columns_ref,
-    side_state_ref,
     side_state_t_ref,
     side_cot_ref,
     side_sum_ref,
@@ -264,13 +261,18 @@
     left,
 ):
     features, size = w_msg_ref.shape[0], columns_ref.shape[2]
+    first_before = [first_sums_ref[:, pl.ds(k * size, size)].T for k in range(3)]
+    msg_before = msg_sums_ref[...].T
     halo = got_odd_ref[...]
     wide_halo = joined_lanes([dot(halo, w_msg_ref[...]).astype(BF16), halo])
     summed = (side_sum_ref[...] + dot(side_far_ref[...], wide_halo)).astype(BF16)
     aggregate, summed = summed[:, :features], summed[:, features:]
+    state_t = side_state_t_ref[...]
+    aggregate_t = joined_lanes(blocks_turned(aggregate))
+    summed_t = joined_lanes(blocks_turned(summed))
     updated_t, terms, active_t, d_norm_t, d_hidden_t = node_layer(
-        side_state_t_ref[...],
-        joined_lanes(blocks_turned(aggregate)),
+        state_t,
+        aggregate_t,
         side_cot_ref[...],
         first_t_ref[...],
         second_t_ref[...],
@@ -283,23 +285,30 @@
     d_hidden_ref[...] = d_hidden_t
     d_aggregate_t = d_aggregate_of(w_first_ref[...], d_hidden_t)
 
-    first_sums = first_sums_ref[...] + first_products(d_hidden_t, side_state_ref[...], aggregate)
-    second_sums = second_sums_ref[...] + second_products(active_t, d_norm_t)
-    msg_sums = msg_sums_ref[...] + dot(d_aggregate_t, summed)
+    second_sums = second_sums_ref[...] + sums_over_nodes([active_t], d_norm_t)
+    first_sums = sums_over_nodes([state_t, aggregate_t], d_hidden_t)
+    msg_sums = msg_before + dot_nt(summed_t, d_aggregate_t)
     gain_sums = gain_sums_ref[...]
     for k in range(WIN):
         gain_sums = gain_sums + terms[:, k * size : (k + 1) * size]
 
     chunk = grads_ref.shape[1] - BIAS_ROWS
-    turned = [first_sums[:, k * size : (k + 1) * size].T for k in range(3)]
     sums = (
-        jnp.concatenate([turned[0], turned[1], second_sums[:features], msg_sums.T], axis=0)
+        jnp.concatenate(
+            [
+                first_before[0] + first_sums[:features],
+                first_before[1] + first_sums[features : 2 * features],
+                second_sums[:features],
+                msg_sums,
+            ],
+            axis=0,
+        )
         * grad_scale
     ).astype(SENT)
     bias = (
         jnp.concatenate(
             [
-                turned[2][:1],
+                first_before[2][:1] + first_sums[2 * features : 2 * features + 1],
                 second_sums[features : features + 1],
                 jnp.sum(gain_sums.T, axis=0, keepdims=True),
             ],
@@ -320,7 +329,7 @@
 
 
 def owed_kernel(
-    band_ref, w_first_ref, inner_ref, outer_ref, owed_ref, send_even_ref, send_odd_ref
+    band_ref, w_first_ref, inner_ref, outer_ref, done_ref, ends_ref, send_even_ref, send_odd_ref
 ):
     blocks, _, size, _ = band_ref.shape
     odd = device_is_odd()
@@ -348,8 +357,11 @@
         to_above = owed(blocks + k).astype(BF16)
         send_even_ref[k] = jnp.where(odd, to_below, to_above)
         send_odd_ref[k] = jnp.where(odd, to_above, to_below)
-    for b in range(blocks):
-        owed_ref[b] = owed(b)
+    for b in range(WIN, blocks - WIN):
+        done_ref[b - WIN] = owed(b).astype(BF16)
+    for k in range(WIN):
+        ends_ref[k] = owed(k)
+        ends_ref[WIN + k] = owed(blocks - WIN + k)
 
 
 def sum_kernel(parts_ref, spread_ref, bias_ref):
@@ -374,6 +386,7 @@
     inner_d_hidden_ref,
     outer_d_hidden_ref,
     owed_ref,
+    ends_ref,
     bias_ref,
     updated_ref,
     grad_state_ref,
@@ -385,7 +398,8 @@
     outer_updated_ref,
     arrived,
 ):
-    blocks, features, size = owed_ref.shape
+    inner, features, size = owed_ref.shape
+    blocks = inner + 2 * WIN
     copies = [
         pltpu.make_async_copy(source, target, arrived.at[k])
         for k, (source, target) in enumerate(
@@ -406,11 +420,13 @@
     for copy in copies:
         copy.wait()
     for b in range(blocks):
-        owed = owed_ref[b]
         if b < WIN:
-            owed = owed + from_below[b]
-        elif b >= blocks - WIN:
-            owed = owed + from_above[b - blocks + WIN]
+            owed = (ends_ref[b] + from_below[b]).astype(BF16)
+        elif b < blocks - WIN:
+            owed = owed_ref[b - WIN]
+        else:
+            k = b - blocks + WIN
+            owed = (ends_ref[WIN + k] + from_above[k]).astype(BF16)
         if WIN <= b < blocks - WIN:
             lanes = pl.ds((b - WIN) * size, size)
             updated, d_hidden = inner_updated_ref[:, lanes], inner_d_hidden_ref[:, lanes]
@@ -425,7 +441,7 @@
                 even_end, inner_d_hidden_ref[:, lanes], outer_d_hidden_ref[:, outer_lanes]
             )
         rows = pl.ds(b * size, size)
-        change = dot(weights, jnp.concatenate([d_hidden, owed.astype(BF16)], axis=0))
+        change = dot(weights, jnp.concatenate([d_hidden, owed], axis=0))
         grad_state_ref[rows, :] = (cot_ref[rows, :].astype(F32) + change.T).astype(BF16)
         updated_ref[rows, :] = updated.T
     for k, ref in enumerate((b_first_ref, b_second_ref, gain_ref)):
@@ -488,31 +504,27 @@
     result = jax.ShapeDtypeStruct
 
     row = lambda vector: vector.reshape(1, features)
-    sources = (w_msg, w_first, w_second, row(b_first), row(b_second), row(ln_gain))
-    *fetched, even_side, odd_side = call(
-        fetch_kernel,
-        "fetch",
-        [vmem(array.shape, array.dtype) for array in sources]
-        + [vmem((side, features), BF16)] * 2,
-        [(array, hbm) for array in (node_state, *sources)],
-        scratch=(pltpu.SemaphoreType.DMA((len(sources) + 2,)),),
+    even_side, odd_side = call(
+        cut_kernel,
+        "cut",
+        [vmem((side, features), BF16)] * 2,
+        [(node_state, hbm)],
+        scratch=(pltpu.SemaphoreType.DMA((2,)),),
         flops=50_000_000_000,
     )
-    w_msg_here, w_first_here, w_second_here, *vectors = fetched
     got_even = swapped(even_side, 0)
     got_odd = swapped(odd_side, 1)
 
-    *outer_operands, band, inner_updated, inner_d_hidden = (
-        lambda *outs: (*outs[:8], *outs[11:], *outs[8:11])
-    )(
-        *call(
+    inner_results = call(
             inner_kernel,
             "inner_rows",
             (
+                vmem((features, features), BF16),
+                vmem((2 * features, features), BF16),
+                vmem((features, features), BF16),
                 vmem((features, 2 * features), BF16),
                 vmem((features, features), BF16),
                 vmem((3, features, size), F32),
-                vmem((side, features), BF16),
                 vmem((features, side), BF16),
                 vmem((features, side), BF16),
                 vmem((side, 2 * features), F32),
@@ -528,9 +540,20 @@
             [(col_index.T, hbm)]
             + [
                 (array, vmem)
-                for array in (edge_counts, cotangent, node_state, got_even, *fetched)
+                for array in (
+                    edge_counts,
+                    cotangent,
+                    node_state,
+                    got_even,
+                    w_msg,
+                    w_first,
+                    w_second,
+                    row(b_first),
+                    row(b_second),
+                    row(ln_gain),
+                )
             ],
-            scratch=(
+        scratch=(
                 pltpu.SMEM((tiles, blocks), jnp.int32),
                 vmem((features, most), BF16),
                 pltpu.SemaphoreType.DMA,
@@ -538,8 +561,13 @@
             ),
             limit=32,
             flops=700_000_000,
-        )
-    )
+    )
+    for_outer, (band, inner_updated, inner_d_hidden), sums = (
+        inner_results[:10],
+        inner_results[10:13],
+        inner_results[13:],
+    )
+    w_msg_here, w_first_here = inner_results[:2]
 
     grads, outer_updated, outer_d_hidden = call(
         functools.partial(outer_kernel, grad_scale),
@@ -551,18 +579,19 @@
         ),
         [
             (array, vmem)
-            for array in (got_odd, w_msg_here, w_first_here, w_second_here, *outer_operands)
+            for array in (got_odd, *for_outer, *sums)
         ],
         scratch=(vmem((features, side), BF16), pltpu.SemaphoreType.DMA),
         flops=300_000_000,
     )
 
     parts = lax.all_to_all(grads, AXES, 0, 0, tiled=True)
-    owed, send_even, send_odd = call(
+    owed, owed_ends, send_even, send_odd = call(
         owed_kernel,
         "owed",
         (
-            vmem((blocks, features, size), F32),
+            vmem((blocks - 2 * WIN, features, size), BF16),
+            vmem((2 * WIN, features, size), F32),
             vmem((WIN, features, size), BF16),
             vmem((WIN, features, size), BF16),
         ),
@@ -590,7 +619,7 @@
         ),
         [(owed_even, vmem), (owed_odd, vmem), (cotangent, hbm)]
         + [(w_msg_here, vmem), (w_first_here, vmem), (inner_updated, hbm), (outer_updated, hbm)]
-        + [(array, vmem) for array in (inner_d_hidden, outer_d_hidden, owed, bias)],
+        + [(array, vmem) for array in (inner_d_hidden, outer_d_hidden, owed, owed_ends, bias)],
         scratch=(
             vmem((nodes, features), BF16),
             vmem((features, most), BF16),

time: 41.8 us -> 42.1 us (level)
  waiting for transfers between devices: 12.5 us -> 13.5 us
  local copies, waits for them, and re-layouts: 0.9 us -> 0.04 us
    all_to_all x1, waiting for transfers between devices: 5.06 us -> 6.01 us  [shards(): parts = lax.all_to_all(grads, AXES, 0, 0, tiled=True)]
    unnamed x10 -> x18, local copies, waits for them, and re-layouts: 0.9 us -> 0.04 us
where the time goes in v13:
time: 42.1 us; the launch traced here: 41.8 us
  starting transfers between devices  15.1 us (36%)
  waiting for transfers between devices  13.5 us (32%)
  Pallas kernels  12.3 us (29%)
  between operations  0.86 us (2%)
    pallas_call x7, Pallas kernels, call(): pl.pallas_call(kernel, out_shape=tuple(outs), in_specs=specs, out_specs=t...  12.3 us
    all_to_all x1, starting transfers between devices, shards(): parts = lax.all_to_all(grads, AXES, 0, 0, tiled=True)  6.3 us
    ppermute x4, starting transfers between devices, swapped(): lax.ppermute(block, AXES, [(i, i + 1) for i in lower] + [(i + 1, i) for i...  6.24 us
    all_to_all x1, waiting for transfers between devices, shards(): parts = lax.all_to_all(grads, AXES, 0, 0, tiled=True)  6.01 us
    all_to_all x1, waiting for transfers between devices, shards(): whole = lax.all_to_all(spread, AXES, 0, 0, tiled=True)  5.91 us
    all_to_all x1, starting transfers between devices, shards(): whole = lax.all_to_all(spread, AXES, 0, 0, tiled=True)  2.58 us
    ppermute x4, waiting for transfers between devices, swapped(): lax.ppermute(block, AXES, [(i, i + 1) for i in lower] + [(i + 1, i) for i...  1.59 us
  transfers between devices with their start and end apart: 6, of which 3 were waited for; matrix products, arithmetic and copies ran while one was open for 0% of the time, Pallas kernels for 19%

profile of v13, /device:TPU:0, one launch (start us, length us, event | category | flops | bytes accessed | tf_op | source)
XLA Modules:
  0.0 41.8 jit_solution(9772463562212758629)
XLA Ops:
  0.6 0.0 copy-start.1
  0.6 0.0 copy-start.2
  0.7 0.0 copy-start
  0.7 0.0 copy-start.8
  0.7 0.0 copy-start.7
  0.7 0.0 copy-start.5
  0.7 0.0 copy-start.6
  0.7 0.0 copy-start.3
  0.7 0.0 copy-start.4
  0.7 1.1 %cut.1 = (bf16[256,128]{1,0:T(8,128)(2,1)S(1)}, bf16[256,128]{1,0:T(8,128)(2,1)S(1)}) custom-call(bf16[1536,128]{1,0:T(8,128)(2,1)} %state_ref.1), custom_call_target="tpu_custom_call" | custom-call | flops 49999998976 | bytes 1000000 | tf_op jit(solution)/shard_map/cut/pallas_call | solution.py:468
  1.8 3.1 %collective-permute-start = (bf16[256,128]{1,0:T(8,128)(2,1)S(1)}, bf16[256,128]{1,0:T(8,128)(2,1)S(1)}, u32[]{:S(2)}, u32[]{:S(2)}) collective-permute-start(bf16[256,128]{1,0:T(8,128)(2,1)S(1)} %get-tuple-element.44), channel_id=1, source_target_pairs={{0,1},{2,3},{4,5},{6,7},{8,9},{10,11},{12,13},{14,15},{16,17},{18,... | collective-permute-start | bytes 196616 | tf_op jit(solution)/shard_map/ppermute | solution.py:462
  4.9 0.7 %collective-permute-start.1 = (bf16[256,128]{1,0:T(8,128)(2,1)S(1)}, bf16[256,128]{1,0:T(8,128)(2,1)S(1)}, u32[]{:S(2)}, u32[]{:S(2)}) collective-permute-start(bf16[256,128]{1,0:T(8,128)(2,1)S(1)} %get-tuple-element.48), channel_id=1, source_target_pairs={{1,2},{3,4},{5,6},{7,8},{9,10},{11,12},{13,14},{15,16},{17,18},{19... | collective-permute-start | bytes 196616 | tf_op jit(solution)/shard_map/ppermute | solution.py:462
  5.5 1.6 %collective-permute-done.got_even_ref = bf16[256,128]{1,0:T(8,128)(2,1)S(1)} collective-permute-done((bf16[256,128]{1,0:T(8,128)(2,1)S(1)}, bf16[256,128]{1,0:T(8,128)(2,1)S(1)}, u32[]{:S(2)}, u32[]{:S(2)}) %collective-permute-start) | collective-permute-done | bytes 65568 | tf_op jit(solution)/shard_map/ppermute | solution.py:462
  7.1 0.0 copy-done.1
  7.1 0.0 copy-done.2
  7.1 0.0 copy-done
  7.1 0.0 copy-done.8
  7.2 4.0 %inner_rows.1 = (bf16[128,128]{1,0:T(8,128)(2,1)S(1)}, bf16[256,128]{1,0:T(8,128)(2,1)S(1)}, bf16[128,128]{1,0:T(8,128)(2,1)S(1)}, bf16[128,256]{1,0:T(8,128)(2,...) custom-call(s32[4,12]{1,0:T(4,128)} %bitcast.12, ...), custom_call_target="tpu_custom_call" | custom-call | flops 700000000 | bytes 1000000 | tf_op jit(solution)/shard_map/inner_rows/pallas_call | solution.py:468
  11.2 0.0 collective-permute-done.1.got_odd_ref
  11.2 2.5 %outer_rows.1 = (bf16[32,24,128]{2,1,0:T(8,128)(2,1)}, bf16[128,256]{1,0:T(8,128)(2,1)}, bf16[128,256]{1,0:T(8,128)(2,1)S(1)}) custom-call(bf16[256,128]{1,0:T(8,128)(2,1)S(1)} %collective-permute-done.1.got_odd_ref, bf16[128,128]{1,0:T(8,128)(2,1)S(1)} %get-tuple-element.49.w_msg_ref, bf16[256,128]{1,0:T(8,128)(2,1)S(1)} %get-tuple-element.46.w_first_ref, ...), custom_call_target="tpu_custom_call" | custom-call | flops 300000000 | bytes 1000000 | tf_op jit(solution)/shard_map/outer_rows/pallas_call | solution.py:468
  13.7 6.3 %all-to-all-start = ((bf16[32,24,128]{2,1,0:T(8,128)(2,1)}), bf16[32,24,128]{2,1,0:T(8,128)(2,1)S(1)}, u32[]{:S(2)}, u32[]{:S(2)}) async-start(bf16[32,24,128]{2,1,0:T(8,128)(2,1)} %get-tuple-element.69), calls=%async_computation | async-start | bytes 393216 | tf_op jit(solution)/shard_map/all_to_all | solution.py:588
  20.0 0.9 %owed.1 = (bf16[8,128,128]{2,1,0:T(8,128)(2,1)S(1)}, f32[4,128,128]{2,1,0:T(8,128)S(1)}, bf16[2,128,128]{2,1,0:T(8,128)(2,1)S(1)}, bf16[2,128,128]{2,1,0:T(8,128)(2,1)S(1)}) custom-call(bf16[12,5,128,128]{3,2,1,0:T(8,128)(2,1)S(1)} %get-tuple-element.45.band_ref, bf16[256,128]{1,0:T(8,128)(2,1)S(1)} %get-tuple-element.46.w_first_ref, ...), custom_call_target="tpu_custom_call" | custom-call | flops 200000000 | bytes 1000000 | tf_op jit(solution)/shard_map/owed/pallas_call | solution.py:468
  20.9 1.8 %collective-permute-start.2 = (bf16[2,128,128]{2,1,0:T(8,128)(2,1)S(1)}, bf16[2,128,128]{2,1,0:T(8,128)(2,1)S(1)}, u32[]{:S(2)}, u32[]{:S(2)}) collective-permute-start(bf16[2,128,128]{2,1,0:T(8,128)(2,1)S(1)} %get-tuple-element.63), channel_id=1, source_target_pairs={{0,1},{2,3},{4,5},{6,7},{8,9},{10,11},{12,13},{14,15},{16,17},{18,... | collective-permute-start | bytes 196616 | tf_op jit(solution)/shard_map/ppermute | solution.py:462
  22.7 0.7 %collective-permute-start.3 = (bf16[2,128,128]{2,1,0:T(8,128)(2,1)S(1)}, bf16[2,128,128]{2,1,0:T(8,128)(2,1)S(1)}, u32[]{:S(2)}, u32[]{:S(2)}) collective-permute-start(bf16[2,128,128]{2,1,0:T(8,128)(2,1)S(1)} %get-tuple-element.64), channel_id=1, source_target_pairs={{1,2},{3,4},{5,6},{7,8},{9,10},{11,12},{13,14},{15,16},{17,18},{19... | collective-permute-start | bytes 196616 | tf_op jit(solution)/shard_map/ppermute | solution.py:462
  23.4 6.0 %all-to-all-done.parts_ref = bf16[32,24,128]{2,1,0:T(8,128)(2,1)S(1)} async-done(((bf16[32,24,128]{2,1,0:T(8,128)(2,1)}), bf16[32,24,128]{2,1,0:T(8,128)(2,1)S(1)}, u32[]{:S(2)}, u32[]{:S(2)}) %all-to-all-start) | async-done | bytes 196640 | tf_op jit(solution)/shard_map/all_to_all | solution.py:588
  29.4 0.7 %sum.1 = (bf16[32,16,128]{2,1,0:T(8,128)(2,1)}, f32[8,128]{1,0:T(8,128)S(1)}) custom-call(bf16[32,24,128]{2,1,0:T(8,128)(2,1)S(1)} %all-to-all-done.parts_ref), custom_call_target="tpu_custom_call" | custom-call | flops 10000000000 | bytes 1000000 | tf_op jit(solution)/shard_map/sum/pallas_call | solution.py:468
  30.1 2.6 %all-to-all-start.1 = ((bf16[32,16,128]{2,1,0:T(8,128)(2,1)}), bf16[32,16,128]{2,1,0:T(8,128)(2,1)S(1)}, u32[]{:S(2)}, u32[]{:S(2)}) async-start(bf16[32,16,128]{2,1,0:T(8,128)(2,1)} %get-tuple-element.73), calls=%async_computation.1 | async-start | bytes 262144 | tf_op jit(solution)/shard_map/all_to_all | solution.py:632
  32.7 0.0 collective-permute-done.2.even_ref
  32.7 0.0 collective-permute-done.3.odd_ref
  32.7 2.5 %results.1 = (bf16[1536,128]{1,0:T(8,128)(2,1)}, bf16[1536,128]{1,0:T(8,128)(2,1)}, f32[1,128]{1,0:T(1,128)}, f32[1,128]{1,0:T(1,128)}, f32[1,128]{1,0:T(1,128)}) custom-call(bf16[2,128,128]{2,1,0:T(8,128)(2,1)S(1)} %collective-permute-done.2.even_ref, bf16[2,128,128]{2,1,0:T(8,128)(2,1)S(1)} %collective-permute-done.3.odd_ref, bf16[1536,128]{1,0:T(8,128)(2,1)} %cot_hbm.1, ...), custom_call_target="tpu_custom_call" | custom-call | flops 49999998976 | bytes 1000000 | tf_op jit(solution)/shard_map/results/pallas_call | solution.py:468
  35.2 5.9 %all-to-all-done.1 = bf16[32,16,128]{2,1,0:T(8,128)(2,1)S(1)} async-done(((bf16[32,16,128]{2,1,0:T(8,128)(2,1)}), bf16[32,16,128]{2,1,0:T(8,128)(2,1)S(1)}, u32[]{:S(2)}, u32[]{:S(2)}) %all-to-all-start.1) | async-done | bytes 131104 | tf_op jit(solution)/shard_map/all_to_all | solution.py:632
  41.1 0.7 %unpack.1 = (f32[128,128]{1,0:T(8,128)}, f32[256,128]{1,0:T(8,128)}, f32[128,128]{1,0:T(8,128)}) custom-call(bf16[512,128]{1,0:T(8,128)(2,1)S(1)} %bitcast.8), custom_call_target="tpu_custom_call" | custom-call | bytes 1000000 | tf_op jit(solution)/shard_map/unpack/pallas_call | solution.py:468
  (5 shorter events, 0.0 us)
Async XLA Ops:
  0.6 6.5 %copy-start.1 = (bf16[1536,128]{1,0:T(8,128)(2,1)S(1)}, bf16[1536,128]{1,0:T(8,128)(2,1)}, u32[]{:S(2)}) copy-start(bf16[1536,128]{1,0:T(8,128)(2,1)} %state_ref.1) | copy-start | bytes 1179652
  0.6 6.5 %copy-start.2 = (bf16[1536,128]{1,0:T(8,128)(2,1)S(1)}, bf16[1536,128]{1,0:T(8,128)(2,1)}, u32[]{:S(2)}) copy-start(bf16[1536,128]{1,0:T(8,128)(2,1)} %cot_hbm.1) | copy-start | bytes 1179652
  0.7 6.5 %copy-start = (s32[12,4,128,128]{3,2,1,0:T(8,128)S(1)}, s32[12,4,128,128]{3,2,1,0:T(8,128)}, u32[]{:S(2)}) copy-start(s32[12,4,128,128]{3,2,1,0:T(8,128)} %counts_ref.1) | copy-start | bytes 9437188
  0.7 6.5 %copy-start.8 = (f32[128]{0:T(128)S(1)}, f32[128]{0:T(128)}, u32[]{:S(2)}) copy-start(f32[128]{0:T(128)} %param.16) | copy-start | bytes 1540
  0.7 6.5 %copy-start.7 = (f32[128]{0:T(128)S(1)}, f32[128]{0:T(128)}, u32[]{:S(2)}) copy-start(f32[128]{0:T(128)} %param.15) | copy-start | bytes 1540
  0.7 6.5 %copy-start.5 = (bf16[128,128]{1,0:T(8,128)(2,1)S(1)}, bf16[128,128]{1,0:T(8,128)(2,1)}, u32[]{:S(2)}) copy-start(bf16[128,128]{1,0:T(8,128)(2,1)} %w_second_ref.1) | copy-start | bytes 98308
  0.7 6.5 %copy-start.6 = (f32[128]{0:T(128)S(1)}, f32[128]{0:T(128)}, u32[]{:S(2)}) copy-start(f32[128]{0:T(128)} %param.13) | copy-start | bytes 1540
  0.7 6.5 %copy-start.3 = (bf16[256,128]{1,0:T(8,128)(2,1)S(1)}, bf16[256,128]{1,0:T(8,128)(2,1)}, u32[]{:S(2)}) copy-start(bf16[256,128]{1,0:T(8,128)(2,1)} %w_first_ref.1) | copy-start | bytes 196612
  0.7 6.5 %copy-start.4 = (bf16[128,128]{1,0:T(8,128)(2,1)S(1)}, bf16[128,128]{1,0:T(8,128)(2,1)}, u32[]{:S(2)}) copy-start(bf16[128,128]{1,0:T(8,128)(2,1)} %w_msg_ref.1) | copy-start | bytes 98308
  1.8 5.3 %collective-permute-start = (bf16[256,128]{1,0:T(8,128)(2,1)S(1)}, bf16[256,128]{1,0:T(8,128)(2,1)S(1)}, u32[]{:S(2)}, u32[]{:S(2)}) collective-permute-start(bf16[256,128]{1,0:T(8,128)(2,1)S(1)} %get-tuple-element.44), channel_id=1, source_target_pairs={{0,1},{2,3},{4,5},{6,7},{8,9},{10,11},{12,13},{14,15},{16,17},{18,... | collective-permute-start | bytes 196616 | tf_op jit(solution)/shard_map/ppermute | solution.py:462
  4.9 6.3 %collective-permute-start.1 = (bf16[256,128]{1,0:T(8,128)(2,1)S(1)}, bf16[256,128]{1,0:T(8,128)(2,1)S(1)}, u32[]{:S(2)}, u32[]{:S(2)}) collective-permute-start(bf16[256,128]{1,0:T(8,128)(2,1)S(1)} %get-tuple-element.48), channel_id=1, source_target_pairs={{1,2},{3,4},{5,6},{7,8},{9,10},{11,12},{13,14},{15,16},{17,18},{19... | collective-permute-start | bytes 196616 | tf_op jit(solution)/shard_map/ppermute | solution.py:462
  13.7 15.7 %all-to-all-start = ((bf16[32,24,128]{2,1,0:T(8,128)(2,1)}), bf16[32,24,128]{2,1,0:T(8,128)(2,1)S(1)}, u32[]{:S(2)}, u32[]{:S(2)}) async-start(bf16[32,24,128]{2,1,0:T(8,128)(2,1)} %get-tuple-element.69), calls=%async_computation | async-start | bytes 393216 | tf_op jit(solution)/shard_map/all_to_all | solution.py:588
  20.9 11.8 %collective-permute-start.2 = (bf16[2,128,128]{2,1,0:T(8,128)(2,1)S(1)}, bf16[2,128,128]{2,1,0:T(8,128)(2,1)S(1)}, u32[]{:S(2)}, u32[]{:S(2)}) collective-permute-start(bf16[2,128,128]{2,1,0:T(8,128)(2,1)S(1)} %get-tuple-element.63), channel_id=1, source_target_pairs={{0,1},{2,3},{4,5},{6,7},{8,9},{10,11},{12,13},{14,15},{16,17},{18,... | collective-permute-start | bytes 196616 | tf_op jit(solution)/shard_map/ppermute | solution.py:462
  22.7 10.0 %collective-permute-start.3 = (bf16[2,128,128]{2,1,0:T(8,128)(2,1)S(1)}, bf16[2,128,128]{2,1,0:T(8,128)(2,1)S(1)}, u32[]{:S(2)}, u32[]{:S(2)}) collective-permute-start(bf16[2,128,128]{2,1,0:T(8,128)(2,1)S(1)} %get-tuple-element.64), channel_id=1, source_target_pairs={{1,2},{3,4},{5,6},{7,8},{9,10},{11,12},{13,14},{15,16},{17,18},{19... | collective-permute-start | bytes 196616 | tf_op jit(solution)/shard_map/ppermute | solution.py:462
  30.1 11.0 %all-to-all-start.1 = ((bf16[32,16,128]{2,1,0:T(8,128)(2,1)}), bf16[32,16,128]{2,1,0:T(8,128)(2,1)S(1)}, u32[]{:S(2)}, u32[]{:S(2)}) async-start(bf16[32,16,128]{2,1,0:T(8,128)(2,1)} %get-tuple-element.73), calls=%async_computation.1 | async-start | bytes 262144 | tf_op jit(solution)/shard_map/all_to_all | solution.py:632

commit v14 on v13

--- a/solution.py
+++ b/solution.py
@@ -24,10 +24,6 @@
     return jnp.dot(left, right, preferred_element_type=F32)
 
 
-def dot_nt(left, right):
-    return lax.dot_general(left, right, (((1,), (1,)), ((), ())), preferred_element_type=F32)
-
-
 def joined_lanes(parts):
     return jnp.concatenate(parts, axis=1)
 
@@ -44,6 +40,12 @@
 def blocks_turned(array):
     size = array.shape[1]
     return [array[k : k + size].T for k in range(0, array.shape[0], size)]
+
+
+def rows_of(array_t):
+    size = array_t.shape[0]
+    turned = [array_t[:, k : k + size].T for k in range(0, array_t.shape[1], size)]
+    return jnp.concatenate(turned, axis=0)
 
 
 def node_layer(state_t, aggregate_t, cot_t, first_t, second_t, w_second, columns):
@@ -75,14 +77,9 @@
     return dot(w_first[w_first.shape[1] :], d_hidden_t).astype(BF16)
 
 
-def first_products(d_hidden_t, state, aggregate):
-    ones = jnp.ones((state.shape[0], ONES), BF16)
-    return dot(d_hidden_t, joined_lanes([state, aggregate, ones]))
-
-
-def sums_over_nodes(lefts, right):
-    ones = jnp.ones((16, right.shape[1]), BF16)
-    return dot_nt(jnp.concatenate([*lefts, ones], axis=0), right)
+def sums_over_nodes(left_t, *rights):
+    ones = jnp.ones((rights[0].shape[0], ONES), BF16)
+    return dot(left_t, joined_lanes([*rights, ones]))
 
 
 def cut_kernel(state_hbm, even_side_ref, odd_side_ref, arrived):
@@ -121,6 +118,7 @@
     first_t_ref,
     second_t_ref,
     columns_ref,
+    side_state_ref,
     side_state_t_ref,
     side_cot_ref,
     side_sum_ref,
@@ -202,6 +200,7 @@
     end_cots_t = (joined_lanes(cot_t[:WIN]), joined_lanes(cot_t[blocks - WIN :]))
     side_sum_ref[...] = odd_side(*ends)
     side_far_ref[...] = odd_side(*fars)
+    side_state_ref[...] = odd_side(*end_states)
     side_state_t_ref[...] = odd_side(*end_states_t)
     side_cot_ref[...] = odd_side(*end_cots_t)
 
@@ -224,12 +223,12 @@
     updated_copy.start()
     d_hidden_ref[...] = d_hidden_t
     d_aggregate_t = d_aggregate_of(w_first, d_hidden_t)
-    first_sums_ref[...] = first_products(
+    first_sums_ref[...] = sums_over_nodes(
         d_hidden_t,
         stacked([state[WIN * size : (blocks - WIN) * size], even_side(*end_states)]),
         aggregate,
     )
-    second_sums_ref[...] = sums_over_nodes([active_t], d_norm_t)
+    second_sums_ref[...] = sums_over_nodes(d_norm_t, rows_of(active_t))
     msg_sums_ref[...] = dot(d_aggregate_t, summed)
     gain_sums_ref[...] = sum(
         terms[:, k * size : (k + 1) * size] for k in range(blocks - WIN)
@@ -246,6 +245,7 @@
     first_t_ref,
     second_t_ref,
     columns_ref,
+    side_state_ref,
     side_state_t_ref,
     side_cot_ref,
     side_sum_ref,
@@ -261,18 +261,13 @@
     left,
 ):
     features, size = w_msg_ref.shape[0], columns_ref.shape[2]
-    first_before = [first_sums_ref[:, pl.ds(k * size, size)].T for k in range(3)]
-    msg_before = msg_sums_ref[...].T
     halo = got_odd_ref[...]
     wide_halo = joined_lanes([dot(halo, w_msg_ref[...]).astype(BF16), halo])
     summed = (side_sum_ref[...] + dot(side_far_ref[...], wide_halo)).astype(BF16)
     aggregate, summed = summed[:, :features], summed[:, features:]
-    state_t = side_state_t_ref[...]
-    aggregate_t = joined_lanes(blocks_turned(aggregate))
-    summed_t = joined_lanes(blocks_turned(summed))
     updated_t, terms, active_t, d_norm_t, d_hidden_t = node_layer(
-        state_t,
-        aggregate_t,
+        side_state_t_ref[...],
+        joined_lanes(blocks_turned(aggregate)),
         side_cot_ref[...],
         first_t_ref[...],
         second_t_ref[...],
@@ -285,31 +280,24 @@
     d_hidden_ref[...] = d_hidden_t
     d_aggregate_t = d_aggregate_of(w_first_ref[...], d_hidden_t)
 
-    second_sums = second_sums_ref[...] + sums_over_nodes([active_t], d_norm_t)
-    first_sums = sums_over_nodes([state_t, aggregate_t], d_hidden_t)
-    msg_sums = msg_before + dot_nt(summed_t, d_aggregate_t)
+    second_sums = second_sums_ref[...] + sums_over_nodes(d_norm_t, rows_of(active_t))
+    first_sums = first_sums_ref[...] + sums_over_nodes(d_hidden_t, side_state_ref[...], aggregate)
+    msg_sums = msg_sums_ref[...] + dot(d_aggregate_t, summed)
     gain_sums = gain_sums_ref[...]
     for k in range(WIN):
         gain_sums = gain_sums + terms[:, k * size : (k + 1) * size]
 
     chunk = grads_ref.shape[1] - BIAS_ROWS
+    first = [first_sums[:, k * size : (k + 1) * size].T for k in range(3)]
+    second = [second_sums[:, k * size : (k + 1) * size].T for k in range(2)]
     sums = (
-        jnp.concatenate(
-            [
-                first_before[0] + first_sums[:features],
-                first_before[1] + first_sums[features : 2 * features],
-                second_sums[:features],
-                msg_sums,
-            ],
-            axis=0,
-        )
-        * grad_scale
+        jnp.concatenate([first[0], first[1], second[0], msg_sums.T], axis=0) * grad_scale
     ).astype(SENT)
     bias = (
         jnp.concatenate(
             [
-                first_before[2][:1] + first_sums[2 * features : 2 * features + 1],
-                second_sums[features : features + 1],
+                first[2][:1],
+                second[1][:1],
                 jnp.sum(gain_sums.T, axis=0, keepdims=True),
             ],
             axis=0,
@@ -525,6 +513,7 @@
                 vmem((features, 2 * features), BF16),
                 vmem((features, features), BF16),
                 vmem((3, features, size), F32),
+                vmem((side, features), BF16),
                 vmem((features, side), BF16),
                 vmem((features, side), BF16),
                 vmem((side, 2 * features), F32),
@@ -533,7 +522,7 @@
                 hbm((features, most), BF16),
                 vmem((features, most), BF16),
                 vmem((features, 2 * features + ONES), F32),
-                vmem((features + 16, features), F32),
+                vmem((features, features + ONES), F32),
                 vmem((features, features), F32),
                 vmem((features, size), F32),
             ),
@@ -563,9 +552,9 @@
             flops=700_000_000,
     )
     for_outer, (band, inner_updated, inner_d_hidden), sums = (
-        inner_results[:10],
-        inner_results[10:13],
-        inner_results[13:],
+        inner_results[:11],
+        inner_results[11:14],
+        inner_results[14:],
     )
     w_msg_here, w_first_here = inner_results[:2]
 

time: 42.1 us -> 42.2 us (level)
  no operation moved by 1% of the time
where the time goes in v14:
time: 42.2 us; the launch traced here: 41.9 us
  starting transfers between devices  15.1 us (36%)
  waiting for transfers between devices  13.5 us (32%)
  Pallas kernels  12.4 us (29%)
  between operations  0.86 us (2%)
    pallas_call x7, Pallas kernels, call(): pl.pallas_call(kernel, out_shape=tuple(outs), in_specs=specs, out_specs=t...  12.4 us
    all_to_all x1, starting transfers between devices, shards(): parts = lax.all_to_all(grads, AXES, 0, 0, tiled=True)  6.3 us
    ppermute x4, starting transfers between devices, swapped(): lax.ppermute(block, AXES, [(i, i + 1) for i in lower] + [(i + 1, i) for i...  6.24 us
    all_to_all x1, waiting for transfers between devices, shards(): parts = lax.all_to_all(grads, AXES, 0, 0, tiled=True)  6.01 us
    all_to_all x1, waiting for transfers between devices, shards(): whole = lax.all_to_all(spread, AXES, 0, 0, tiled=True)  5.9 us
    all_to_all x1, starting transfers between devices, shards(): whole = lax.all_to_all(spread, AXES, 0, 0, tiled=True)  2.58 us
    ppermute x4, waiting for transfers between devices, swapped(): lax.ppermute(block, AXES, [(i, i + 1) for i in lower] + [(i + 1, i) for i...  1.59 us
  transfers between devices with their start and end apart: 6, of which 3 were waited for; matrix products, arithmetic and copies ran while one was open for 0% of the time, Pallas kernels for 19%

profile of v14, /device:TPU:0, one launch (start us, length us, event | category | flops | bytes accessed | tf_op | source)
XLA Modules:
  0.0 41.9 jit_solution(5964852010147523735)
XLA Ops:
  0.6 0.0 copy-start.1
  0.6 0.0 copy-start.2
  0.7 0.0 copy-start
  0.7 0.0 copy-start.8
  0.7 0.0 copy-start.7
  0.7 0.0 copy-start.5
  0.7 0.0 copy-start.6
  0.7 0.0 copy-start.3
  0.7 0.0 copy-start.4
  0.7 1.1 %cut.1 = (bf16[256,128]{1,0:T(8,128)(2,1)S(1)}, bf16[256,128]{1,0:T(8,128)(2,1)S(1)}) custom-call(bf16[1536,128]{1,0:T(8,128)(2,1)} %state_ref.1), custom_call_target="tpu_custom_call" | custom-call | flops 49999998976 | bytes 1000000 | tf_op jit(solution)/shard_map/cut/pallas_call | solution.py:456
  1.8 3.1 %collective-permute-start = (bf16[256,128]{1,0:T(8,128)(2,1)S(1)}, bf16[256,128]{1,0:T(8,128)(2,1)S(1)}, u32[]{:S(2)}, u32[]{:S(2)}) collective-permute-start(bf16[256,128]{1,0:T(8,128)(2,1)S(1)} %get-tuple-element.45), channel_id=1, source_target_pairs={{0,1},{2,3},{4,5},{6,7},{8,9},{10,11},{12,13},{14,15},{16,17},{18,... | collective-permute-start | bytes 196616 | tf_op jit(solution)/shard_map/ppermute | solution.py:450
  4.9 0.7 %collective-permute-start.1 = (bf16[256,128]{1,0:T(8,128)(2,1)S(1)}, bf16[256,128]{1,0:T(8,128)(2,1)S(1)}, u32[]{:S(2)}, u32[]{:S(2)}) collective-permute-start(bf16[256,128]{1,0:T(8,128)(2,1)S(1)} %get-tuple-element.49), channel_id=1, source_target_pairs={{1,2},{3,4},{5,6},{7,8},{9,10},{11,12},{13,14},{15,16},{17,18},{19... | collective-permute-start | bytes 196616 | tf_op jit(solution)/shard_map/ppermute | solution.py:450
  5.5 1.6 %collective-permute-done.got_even_ref = bf16[256,128]{1,0:T(8,128)(2,1)S(1)} collective-permute-done((bf16[256,128]{1,0:T(8,128)(2,1)S(1)}, bf16[256,128]{1,0:T(8,128)(2,1)S(1)}, u32[]{:S(2)}, u32[]{:S(2)}) %collective-permute-start) | collective-permute-done | bytes 65568 | tf_op jit(solution)/shard_map/ppermute | solution.py:450
  7.1 0.0 copy-done.1
  7.1 0.0 copy-done.2
  7.1 0.0 copy-done
  7.1 0.0 copy-done.8
  7.2 4.1 %inner_rows.1 = (bf16[128,128]{1,0:T(8,128)(2,1)S(1)}, bf16[256,128]{1,0:T(8,128)(2,1)S(1)}, bf16[128,128]{1,0:T(8,128)(2,1)S(1)}, bf16[128,256]{1,0:T(8,128)(2,...) custom-call(s32[4,12]{1,0:T(4,128)} %bitcast.12, ...), custom_call_target="tpu_custom_call" | custom-call | flops 700000000 | bytes 1000000 | tf_op jit(solution)/shard_map/inner_rows/pallas_call | solution.py:456
  11.3 0.0 collective-permute-done.1.got_odd_ref
  11.3 2.6 %outer_rows.1 = (bf16[32,24,128]{2,1,0:T(8,128)(2,1)}, bf16[128,256]{1,0:T(8,128)(2,1)}, bf16[128,256]{1,0:T(8,128)(2,1)S(1)}) custom-call(bf16[256,128]{1,0:T(8,128)(2,1)S(1)} %collective-permute-done.1.got_odd_ref, bf16[128,128]{1,0:T(8,128)(2,1)S(1)} %get-tuple-element.50.w_msg_ref, bf16[256,128]{1,0:T(8,128)(2,1)S(1)} %get-tuple-element.47.w_first_ref, ...), custom_call_target="tpu_custom_call" | custom-call | flops 300000000 | bytes 1000000 | tf_op jit(solution)/shard_map/outer_rows/pallas_call | solution.py:456
  13.8 6.3 %all-to-all-start = ((bf16[32,24,128]{2,1,0:T(8,128)(2,1)}), bf16[32,24,128]{2,1,0:T(8,128)(2,1)S(1)}, u32[]{:S(2)}, u32[]{:S(2)}) async-start(bf16[32,24,128]{2,1,0:T(8,128)(2,1)} %get-tuple-element.71), calls=%async_computation | async-start | bytes 393216 | tf_op jit(solution)/shard_map/all_to_all | solution.py:577
  20.1 0.9 %owed.1 = (bf16[8,128,128]{2,1,0:T(8,128)(2,1)S(1)}, f32[4,128,128]{2,1,0:T(8,128)S(1)}, bf16[2,128,128]{2,1,0:T(8,128)(2,1)S(1)}, bf16[2,128,128]{2,1,0:T(8,128)(2,1)S(1)}) custom-call(bf16[12,5,128,128]{3,2,1,0:T(8,128)(2,1)S(1)} %get-tuple-element.46.band_ref, bf16[256,128]{1,0:T(8,128)(2,1)S(1)} %get-tuple-element.47.w_first_ref, ...), custom_call_target="tpu_custom_call" | custom-call | flops 200000000 | bytes 1000000 | tf_op jit(solution)/shard_map/owed/pallas_call | solution.py:456
  21.0 1.8 %collective-permute-start.2 = (bf16[2,128,128]{2,1,0:T(8,128)(2,1)S(1)}, bf16[2,128,128]{2,1,0:T(8,128)(2,1)S(1)}, u32[]{:S(2)}, u32[]{:S(2)}) collective-permute-start(bf16[2,128,128]{2,1,0:T(8,128)(2,1)S(1)} %get-tuple-element.65), channel_id=1, source_target_pairs={{0,1},{2,3},{4,5},{6,7},{8,9},{10,11},{12,13},{14,15},{16,17},{18,... | collective-permute-start | bytes 196616 | tf_op jit(solution)/shard_map/ppermute | solution.py:450
  22.9 0.7 %collective-permute-start.3 = (bf16[2,128,128]{2,1,0:T(8,128)(2,1)S(1)}, bf16[2,128,128]{2,1,0:T(8,128)(2,1)S(1)}, u32[]{:S(2)}, u32[]{:S(2)}) collective-permute-start(bf16[2,128,128]{2,1,0:T(8,128)(2,1)S(1)} %get-tuple-element.66), channel_id=1, source_target_pairs={{1,2},{3,4},{5,6},{7,8},{9,10},{11,12},{13,14},{15,16},{17,18},{19... | collective-permute-start | bytes 196616 | tf_op jit(solution)/shard_map/ppermute | solution.py:450
  23.5 6.0 %all-to-all-done.parts_ref = bf16[32,24,128]{2,1,0:T(8,128)(2,1)S(1)} async-done(((bf16[32,24,128]{2,1,0:T(8,128)(2,1)}), bf16[32,24,128]{2,1,0:T(8,128)(2,1)S(1)}, u32[]{:S(2)}, u32[]{:S(2)}) %all-to-all-start) | async-done | bytes 196640 | tf_op jit(solution)/shard_map/all_to_all | solution.py:577
  29.5 0.7 %sum.1 = (bf16[32,16,128]{2,1,0:T(8,128)(2,1)}, f32[8,128]{1,0:T(8,128)S(1)}) custom-call(bf16[32,24,128]{2,1,0:T(8,128)(2,1)S(1)} %all-to-all-done.parts_ref), custom_call_target="tpu_custom_call" | custom-call | flops 10000000000 | bytes 1000000 | tf_op jit(solution)/shard_map/sum/pallas_call | solution.py:456
  30.2 2.6 %all-to-all-start.1 = ((bf16[32,16,128]{2,1,0:T(8,128)(2,1)}), bf16[32,16,128]{2,1,0:T(8,128)(2,1)S(1)}, u32[]{:S(2)}, u32[]{:S(2)}) async-start(bf16[32,16,128]{2,1,0:T(8,128)(2,1)} %get-tuple-element.75), calls=%async_computation.1 | async-start | bytes 262144 | tf_op jit(solution)/shard_map/all_to_all | solution.py:621
  32.8 0.0 collective-permute-done.2.even_ref
  32.8 0.0 collective-permute-done.3.odd_ref
  32.9 2.5 %results.1 = (bf16[1536,128]{1,0:T(8,128)(2,1)}, bf16[1536,128]{1,0:T(8,128)(2,1)}, f32[1,128]{1,0:T(1,128)}, f32[1,128]{1,0:T(1,128)}, f32[1,128]{1,0:T(1,128)}) custom-call(bf16[2,128,128]{2,1,0:T(8,128)(2,1)S(1)} %collective-permute-done.2.even_ref, bf16[2,128,128]{2,1,0:T(8,128)(2,1)S(1)} %collective-permute-done.3.odd_ref, bf16[1536,128]{1,0:T(8,128)(2,1)} %cot_hbm.1, ...), custom_call_target="tpu_custom_call" | custom-call | flops 49999998976 | bytes 1000000 | tf_op jit(solution)/shard_map/results/pallas_call | solution.py:456
  35.3 5.9 %all-to-all-done.1 = bf16[32,16,128]{2,1,0:T(8,128)(2,1)S(1)} async-done(((bf16[32,16,128]{2,1,0:T(8,128)(2,1)}), bf16[32,16,128]{2,1,0:T(8,128)(2,1)S(1)}, u32[]{:S(2)}, u32[]{:S(2)}) %all-to-all-start.1) | async-done | bytes 131104 | tf_op jit(solution)/shard_map/all_to_all | solution.py:621
  41.2 0.7 %unpack.1 = (f32[128,128]{1,0:T(8,128)}, f32[256,128]{1,0:T(8,128)}, f32[128,128]{1,0:T(8,128)}) custom-call(bf16[512,128]{1,0:T(8,128)(2,1)S(1)} %bitcast.8), custom_call_target="tpu_custom_call" | custom-call | bytes 1000000 | tf_op jit(solution)/shard_map/unpack/pallas_call | solution.py:456
  (5 shorter events, 0.0 us)
Async XLA Ops:
  0.6 6.5 %copy-start.1 = (bf16[1536,128]{1,0:T(8,128)(2,1)S(1)}, bf16[1536,128]{1,0:T(8,128)(2,1)}, u32[]{:S(2)}) copy-start(bf16[1536,128]{1,0:T(8,128)(2,1)} %state_ref.1) | copy-start | bytes 1179652
  0.6 6.5 %copy-start.2 = (bf16[1536,128]{1,0:T(8,128)(2,1)S(1)}, bf16[1536,128]{1,0:T(8,128)(2,1)}, u32[]{:S(2)}) copy-start(bf16[1536,128]{1,0:T(8,128)(2,1)} %cot_hbm.1) | copy-start | bytes 1179652
  0.7 6.5 %copy-start = (s32[12,4,128,128]{3,2,1,0:T(8,128)S(1)}, s32[12,4,128,128]{3,2,1,0:T(8,128)}, u32[]{:S(2)}) copy-start(s32[12,4,128,128]{3,2,1,0:T(8,128)} %counts_ref.1) | copy-start | bytes 9437188
  0.7 6.5 %copy-start.8 = (f32[128]{0:T(128)S(1)}, f32[128]{0:T(128)}, u32[]{:S(2)}) copy-start(f32[128]{0:T(128)} %param.16) | copy-start | bytes 1540
  0.7 6.5 %copy-start.7 = (f32[128]{0:T(128)S(1)}, f32[128]{0:T(128)}, u32[]{:S(2)}) copy-start(f32[128]{0:T(128)} %param.15) | copy-start | bytes 1540
  0.7 6.5 %copy-start.5 = (bf16[128,128]{1,0:T(8,128)(2,1)S(1)}, bf16[128,128]{1,0:T(8,128)(2,1)}, u32[]{:S(2)}) copy-start(bf16[128,128]{1,0:T(8,128)(2,1)} %w_second_ref.1) | copy-start | bytes 98308
  0.7 6.5 %copy-start.6 = (f32[128]{0:T(128)S(1)}, f32[128]{0:T(128)}, u32[]{:S(2)}) copy-start(f32[128]{0:T(128)} %param.13) | copy-start | bytes 1540
  0.7 6.5 %copy-start.3 = (bf16[256,128]{1,0:T(8,128)(2,1)S(1)}, bf16[256,128]{1,0:T(8,128)(2,1)}, u32[]{:S(2)}) copy-start(bf16[256,128]{1,0:T(8,128)(2,1)} %w_first_ref.1) | copy-start | bytes 196612
  0.7 6.5 %copy-start.4 = (bf16[128,128]{1,0:T(8,128)(2,1)S(1)}, bf16[128,128]{1,0:T(8,128)(2,1)}, u32[]{:S(2)}) copy-start(bf16[128,128]{1,0:T(8,128)(2,1)} %w_msg_ref.1) | copy-start | bytes 98308
  1.8 5.3 %collective-permute-start = (bf16[256,128]{1,0:T(8,128)(2,1)S(1)}, bf16[256,128]{1,0:T(8,128)(2,1)S(1)}, u32[]{:S(2)}, u32[]{:S(2)}) collective-permute-start(bf16[256,128]{1,0:T(8,128)(2,1)S(1)} %get-tuple-element.45), channel_id=1, source_target_pairs={{0,1},{2,3},{4,5},{6,7},{8,9},{10,11},{12,13},{14,15},{16,17},{18,... | collective-permute-start | bytes 196616 | tf_op jit(solution)/shard_map/ppermute | solution.py:450
  4.9 6.4 %collective-permute-start.1 = (bf16[256,128]{1,0:T(8,128)(2,1)S(1)}, bf16[256,128]{1,0:T(8,128)(2,1)S(1)}, u32[]{:S(2)}, u32[]{:S(2)}) collective-permute-start(bf16[256,128]{1,0:T(8,128)(2,1)S(1)} %get-tuple-element.49), channel_id=1, source_target_pairs={{1,2},{3,4},{5,6},{7,8},{9,10},{11,12},{13,14},{15,16},{17,18},{19... | collective-permute-start | bytes 196616 | tf_op jit(solution)/shard_map/ppermute | solution.py:450
  13.8 15.7 %all-to-all-start = ((bf16[32,24,128]{2,1,0:T(8,128)(2,1)}), bf16[32,24,128]{2,1,0:T(8,128)(2,1)S(1)}, u32[]{:S(2)}, u32[]{:S(2)}) async-start(bf16[32,24,128]{2,1,0:T(8,128)(2,1)} %get-tuple-element.71), calls=%async_computation | async-start | bytes 393216 | tf_op jit(solution)/shard_map/all_to_all | solution.py:577
  21.0 11.8 %collective-permute-start.2 = (bf16[2,128,128]{2,1,0:T(8,128)(2,1)S(1)}, bf16[2,128,128]{2,1,0:T(8,128)(2,1)S(1)}, u32[]{:S(2)}, u32[]{:S(2)}) collective-permute-start(bf16[2,128,128]{2,1,0:T(8,128)(2,1)S(1)} %get-tuple-element.65), channel_id=1, source_target_pairs={{0,1},{2,3},{4,5},{6,7},{8,9},{10,11},{12,13},{14,15},{16,17},{18,... | collective-permute-start | bytes 196616 | tf_op jit(solution)/shard_map/ppermute | solution.py:450
  22.9 10.0 %collective-permute-start.3 = (bf16[2,128,128]{2,1,0:T(8,128)(2,1)S(1)}, bf16[2,128,128]{2,1,0:T(8,128)(2,1)S(1)}, u32[]{:S(2)}, u32[]{:S(2)}) collective-permute-start(bf16[2,128,128]{2,1,0:T(8,128)(2,1)S(1)} %get-tuple-element.66), channel_id=1, source_target_pairs={{1,2},{3,4},{5,6},{7,8},{9,10},{11,12},{13,14},{15,16},{17,18},{19... | collective-permute-start | bytes 196616 | tf_op jit(solution)/shard_map/ppermute | solution.py:450
  30.2 11.0 %all-to-all-start.1 = ((bf16[32,16,128]{2,1,0:T(8,128)(2,1)}), bf16[32,16,128]{2,1,0:T(8,128)(2,1)S(1)}, u32[]{:S(2)}, u32[]{:S(2)}) async-start(bf16[32,16,128]{2,1,0:T(8,128)(2,1)} %get-tuple-element.75), calls=%async_computation.1 | async-start | bytes 262144 | tf_op jit(solution)/shard_map/all_to_all | solution.py:621

commit v15 on v13

--- a/solution.py
+++ b/solution.py
@@ -37,8 +37,18 @@
     return index % 2 == 1
 
 
-def column(row_ref, width):
-    return jnp.broadcast_to(row_ref[...], (width, row_ref.shape[1])).T
+def column(row_ref):
+    features = row_ref.shape[1]
+    square = (features, features)
+    diagonal = lax.broadcasted_iota(jnp.int32, square, 0) == lax.broadcasted_iota(
+        jnp.int32, square, 1
+    )
+    rest, terms = row_ref[...], []
+    for _ in range(3):
+        term = rest.astype(BF16).astype(F32)
+        terms.append(jnp.where(diagonal, jnp.broadcast_to(term, square), 0.0).astype(BF16))
+        rest = rest - term
+    return dot(joined_lanes(terms), jnp.ones((3 * features, features), BF16))
 
 
 def blocks_turned(array):
@@ -158,7 +168,7 @@
     w_msg, w_first, w_second = w_msg_ref[...], w_first_ref[...], w_second_ref[...]
     first_t = joined_lanes([w_first[:features].T, w_first[features:].T])
     second_t = w_second.T
-    columns = [column(ref, size) for ref in (b_first_ref, b_second_ref, gain_ref)]
+    columns = [column(ref) for ref in (b_first_ref, b_second_ref, gain_ref)]
     w_msg_here_ref[...] = w_msg
     w_first_here_ref[...] = w_first
     w_second_here_ref[...] = w_second
@@ -224,13 +234,16 @@
     updated_copy.start()
     d_hidden_ref[...] = d_hidden_t
     d_aggregate_t = d_aggregate_of(w_first, d_hidden_t)
-    first_sums_ref[...] = first_products(
+    first_sums = first_products(
         d_hidden_t,
         stacked([state[WIN * size : (blocks - WIN) * size], even_side(*end_states)]),
         aggregate,
     )
+    for k in range(2):
+        first_sums_ref[rows(k), :] = first_sums[:, k * features : (k + 1) * features].T
+    first_sums_ref[pl.ds(2 * features, 16), :] = first_sums[:, 2 * features :].T[:16]
     second_sums_ref[...] = sums_over_nodes([active_t], d_norm_t)
-    msg_sums_ref[...] = dot(d_aggregate_t, summed)
+    msg_sums_ref[...] = dot(d_aggregate_t, summed).T
     gain_sums_ref[...] = sum(
         terms[:, k * size : (k + 1) * size] for k in range(blocks - WIN)
     )
@@ -261,15 +274,12 @@
     left,
 ):
     features, size = w_msg_ref.shape[0], columns_ref.shape[2]
-    first_before = [first_sums_ref[:, pl.ds(k * size, size)].T for k in range(3)]
-    msg_before = msg_sums_ref[...].T
     halo = got_odd_ref[...]
     wide_halo = joined_lanes([dot(halo, w_msg_ref[...]).astype(BF16), halo])
     summed = (side_sum_ref[...] + dot(side_far_ref[...], wide_halo)).astype(BF16)
     aggregate, summed = summed[:, :features], summed[:, features:]
     state_t = side_state_t_ref[...]
     aggregate_t = joined_lanes(blocks_turned(aggregate))
-    summed_t = joined_lanes(blocks_turned(summed))
     updated_t, terms, active_t, d_norm_t, d_hidden_t = node_layer(
         state_t,
         aggregate_t,
@@ -286,8 +296,8 @@
     d_aggregate_t = d_aggregate_of(w_first_ref[...], d_hidden_t)
 
     second_sums = second_sums_ref[...] + sums_over_nodes([active_t], d_norm_t)
-    first_sums = sums_over_nodes([state_t, aggregate_t], d_hidden_t)
-    msg_sums = msg_before + dot_nt(summed_t, d_aggregate_t)
+    first_sums = first_sums_ref[...] + sums_over_nodes([state_t, aggregate_t], d_hidden_t)
+    msg_sums = msg_sums_ref[...] + dot(d_aggregate_t, summed).T
     gain_sums = gain_sums_ref[...]
     for k in range(WIN):
         gain_sums = gain_sums + terms[:, k * size : (k + 1) * size]
@@ -296,8 +306,7 @@
     sums = (
         jnp.concatenate(
             [
-                first_before[0] + first_sums[:features],
-                first_before[1] + first_sums[features : 2 * features],
+                first_sums[: 2 * features],
                 second_sums[:features],
                 msg_sums,
             ],
@@ -308,7 +317,7 @@
     bias = (
         jnp.concatenate(
             [
-                first_before[2][:1] + first_sums[2 * features : 2 * features + 1],
+                first_sums[2 * features : 2 * features + 1],
                 second_sums[features : features + 1],
                 jnp.sum(gain_sums.T, axis=0, keepdims=True),
             ],
@@ -532,7 +541,7 @@
                 vmem((blocks, BAND, size, size), BF16),
                 hbm((features, most), BF16),
                 vmem((features, most), BF16),
-                vmem((features, 2 * features + ONES), F32),
+                vmem((2 * features + 16, features), F32),
                 vmem((features + 16, features), F32),
                 vmem((features, features), F32),
                 vmem((features, size), F32),

time: 42.1 us -> 42.1 us (level)
  no operation moved by 1% of the time
where the time goes in v15:
time: 42.1 us; the launch traced here: 41.8 us
  starting transfers between devices  15.1 us (36%)
  waiting for transfers between devices  13.5 us (32%)
  Pallas kernels  12.3 us (29%)
  between operations  0.86 us (2%)
    pallas_call x7, Pallas kernels, call(): pl.pallas_call(kernel, out_shape=tuple(outs), in_specs=specs, out_specs=t...  12.3 us
    all_to_all x1, starting transfers between devices, shards(): parts = lax.all_to_all(grads, AXES, 0, 0, tiled=True)  6.3 us
    ppermute x4, starting transfers between devices, swapped(): lax.ppermute(block, AXES, [(i, i + 1) for i in lower] + [(i + 1, i) for i...  6.23 us
    all_to_all x1, waiting for transfers between devices, shards(): parts = lax.all_to_all(grads, AXES, 0, 0, tiled=True)  6.02 us
    all_to_all x1, waiting for transfers between devices, shards(): whole = lax.all_to_all(spread, AXES, 0, 0, tiled=True)  5.91 us
    all_to_all x1, starting transfers between devices, shards(): whole = lax.all_to_all(spread, AXES, 0, 0, tiled=True)  2.58 us
    ppermute x4, waiting for transfers between devices, swapped(): lax.ppermute(block, AXES, [(i, i + 1) for i in lower] + [(i + 1, i) for i...  1.59 us
  transfers between devices with their start and end apart: 6, of which 3 were waited for; matrix products, arithmetic and copies ran while one was open for 0% of the time, Pallas kernels for 19%

profile of v15, /device:TPU:0, one launch (start us, length us, event | category | flops | bytes accessed | tf_op | source)
XLA Modules:
  0.0 41.8 jit_solution(2805285269681508134)
XLA Ops:
  0.6 0.0 copy-start.1
  0.6 0.0 copy-start.2
  0.7 0.0 copy-start
  0.7 0.0 copy-start.8
  0.7 0.0 copy-start.7
  0.7 0.0 copy-start.5
  0.7 0.0 copy-start.6
  0.7 0.0 copy-start.3
  0.7 0.0 copy-start.4
  0.7 1.1 %cut.1 = (bf16[256,128]{1,0:T(8,128)(2,1)S(1)}, bf16[256,128]{1,0:T(8,128)(2,1)S(1)}) custom-call(bf16[1536,128]{1,0:T(8,128)(2,1)} %state_ref.1), custom_call_target="tpu_custom_call" | custom-call | flops 49999998976 | bytes 1000000 | tf_op jit(solution)/shard_map/cut/pallas_call | solution.py:477
  1.8 3.1 %collective-permute-start = (bf16[256,128]{1,0:T(8,128)(2,1)S(1)}, bf16[256,128]{1,0:T(8,128)(2,1)S(1)}, u32[]{:S(2)}, u32[]{:S(2)}) collective-permute-start(bf16[256,128]{1,0:T(8,128)(2,1)S(1)} %get-tuple-element.44), channel_id=1, source_target_pairs={{0,1},{2,3},{4,5},{6,7},{8,9},{10,11},{12,13},{14,15},{16,17},{18,... | collective-permute-start | bytes 196616 | tf_op jit(solution)/shard_map/ppermute | solution.py:471
  4.9 0.7 %collective-permute-start.1 = (bf16[256,128]{1,0:T(8,128)(2,1)S(1)}, bf16[256,128]{1,0:T(8,128)(2,1)S(1)}, u32[]{:S(2)}, u32[]{:S(2)}) collective-permute-start(bf16[256,128]{1,0:T(8,128)(2,1)S(1)} %get-tuple-element.48), channel_id=1, source_target_pairs={{1,2},{3,4},{5,6},{7,8},{9,10},{11,12},{13,14},{15,16},{17,18},{19... | collective-permute-start | bytes 196616 | tf_op jit(solution)/shard_map/ppermute | solution.py:471
  5.5 1.6 %collective-permute-done.got_even_ref = bf16[256,128]{1,0:T(8,128)(2,1)S(1)} collective-permute-done((bf16[256,128]{1,0:T(8,128)(2,1)S(1)}, bf16[256,128]{1,0:T(8,128)(2,1)S(1)}, u32[]{:S(2)}, u32[]{:S(2)}) %collective-permute-start) | collective-permute-done | bytes 65568 | tf_op jit(solution)/shard_map/ppermute | solution.py:471
  7.1 0.0 copy-done.1
  7.1 0.0 copy-done.2
  7.1 0.0 copy-done
  7.1 0.0 copy-done.8
  7.2 4.0 %inner_rows.1 = (bf16[128,128]{1,0:T(8,128)(2,1)S(1)}, bf16[256,128]{1,0:T(8,128)(2,1)S(1)}, bf16[128,128]{1,0:T(8,128)(2,1)S(1)}, bf16[128,256]{1,0:T(8,128)(2,...) custom-call(s32[4,12]{1,0:T(4,128)} %bitcast.12, ...), custom_call_target="tpu_custom_call" | custom-call | flops 700000000 | bytes 1000000 | tf_op jit(solution)/shard_map/inner_rows/pallas_call | solution.py:477
  11.2 0.0 collective-permute-done.1.got_odd_ref
  11.2 2.5 %outer_rows.1 = (bf16[32,24,128]{2,1,0:T(8,128)(2,1)}, bf16[128,256]{1,0:T(8,128)(2,1)}, bf16[128,256]{1,0:T(8,128)(2,1)S(1)}) custom-call(bf16[256,128]{1,0:T(8,128)(2,1)S(1)} %collective-permute-done.1.got_odd_ref, bf16[128,128]{1,0:T(8,128)(2,1)S(1)} %get-tuple-element.49.w_msg_ref, bf16[256,128]{1,0:T(8,128)(2,1)S(1)} %get-tuple-element.46.w_first_ref, ...), custom_call_target="tpu_custom_call" | custom-call | flops 300000000 | bytes 1000000 | tf_op jit(solution)/shard_map/outer_rows/pallas_call | solution.py:477
  13.7 6.3 %all-to-all-start = ((bf16[32,24,128]{2,1,0:T(8,128)(2,1)}), bf16[32,24,128]{2,1,0:T(8,128)(2,1)S(1)}, u32[]{:S(2)}, u32[]{:S(2)}) async-start(bf16[32,24,128]{2,1,0:T(8,128)(2,1)} %get-tuple-element.69), calls=%async_computation | async-start | bytes 393216 | tf_op jit(solution)/shard_map/all_to_all | solution.py:597
  20.0 0.9 %owed.1 = (bf16[8,128,128]{2,1,0:T(8,128)(2,1)S(1)}, f32[4,128,128]{2,1,0:T(8,128)S(1)}, bf16[2,128,128]{2,1,0:T(8,128)(2,1)S(1)}, bf16[2,128,128]{2,1,0:T(8,128)(2,1)S(1)}) custom-call(bf16[12,5,128,128]{3,2,1,0:T(8,128)(2,1)S(1)} %get-tuple-element.45.band_ref, bf16[256,128]{1,0:T(8,128)(2,1)S(1)} %get-tuple-element.46.w_first_ref, ...), custom_call_target="tpu_custom_call" | custom-call | flops 200000000 | bytes 1000000 | tf_op jit(solution)/shard_map/owed/pallas_call | solution.py:477
  20.9 1.8 %collective-permute-start.2 = (bf16[2,128,128]{2,1,0:T(8,128)(2,1)S(1)}, bf16[2,128,128]{2,1,0:T(8,128)(2,1)S(1)}, u32[]{:S(2)}, u32[]{:S(2)}) collective-permute-start(bf16[2,128,128]{2,1,0:T(8,128)(2,1)S(1)} %get-tuple-element.63), channel_id=1, source_target_pairs={{0,1},{2,3},{4,5},{6,7},{8,9},{10,11},{12,13},{14,15},{16,17},{18,... | collective-permute-start | bytes 196616 | tf_op jit(solution)/shard_map/ppermute | solution.py:471
  22.8 0.7 %collective-permute-start.3 = (bf16[2,128,128]{2,1,0:T(8,128)(2,1)S(1)}, bf16[2,128,128]{2,1,0:T(8,128)(2,1)S(1)}, u32[]{:S(2)}, u32[]{:S(2)}) collective-permute-start(bf16[2,128,128]{2,1,0:T(8,128)(2,1)S(1)} %get-tuple-element.64), channel_id=1, source_target_pairs={{1,2},{3,4},{5,6},{7,8},{9,10},{11,12},{13,14},{15,16},{17,18},{19... | collective-permute-start | bytes 196616 | tf_op jit(solution)/shard_map/ppermute | solution.py:471
  23.4 6.0 %all-to-all-done.parts_ref = bf16[32,24,128]{2,1,0:T(8,128)(2,1)S(1)} async-done(((bf16[32,24,128]{2,1,0:T(8,128)(2,1)}), bf16[32,24,128]{2,1,0:T(8,128)(2,1)S(1)}, u32[]{:S(2)}, u32[]{:S(2)}) %all-to-all-start) | async-done | bytes 196640 | tf_op jit(solution)/shard_map/all_to_all | solution.py:597
  29.4 0.7 %sum.1 = (bf16[32,16,128]{2,1,0:T(8,128)(2,1)}, f32[8,128]{1,0:T(8,128)S(1)}) custom-call(bf16[32,24,128]{2,1,0:T(8,128)(2,1)S(1)} %all-to-all-done.parts_ref), custom_call_target="tpu_custom_call" | custom-call | flops 10000000000 | bytes 1000000 | tf_op jit(solution)/shard_map/sum/pallas_call | solution.py:477
  30.1 2.6 %all-to-all-start.1 = ((bf16[32,16,128]{2,1,0:T(8,128)(2,1)}), bf16[32,16,128]{2,1,0:T(8,128)(2,1)S(1)}, u32[]{:S(2)}, u32[]{:S(2)}) async-start(bf16[32,16,128]{2,1,0:T(8,128)(2,1)} %get-tuple-element.73), calls=%async_computation.1 | async-start | bytes 262144 | tf_op jit(solution)/shard_map/all_to_all | solution.py:641
  32.7 0.0 collective-permute-done.2.even_ref
  32.7 0.0 collective-permute-done.3.odd_ref
  32.7 2.5 %results.1 = (bf16[1536,128]{1,0:T(8,128)(2,1)}, bf16[1536,128]{1,0:T(8,128)(2,1)}, f32[1,128]{1,0:T(1,128)}, f32[1,128]{1,0:T(1,128)}, f32[1,128]{1,0:T(1,128)}) custom-call(bf16[2,128,128]{2,1,0:T(8,128)(2,1)S(1)} %collective-permute-done.2.even_ref, bf16[2,128,128]{2,1,0:T(8,128)(2,1)S(1)} %collective-permute-done.3.odd_ref, bf16[1536,128]{1,0:T(8,128)(2,1)} %cot_hbm.1, ...), custom_call_target="tpu_custom_call" | custom-call | flops 49999998976 | bytes 1000000 | tf_op jit(solution)/shard_map/results/pallas_call | solution.py:477
  35.2 5.9 %all-to-all-done.1 = bf16[32,16,128]{2,1,0:T(8,128)(2,1)S(1)} async-done(((bf16[32,16,128]{2,1,0:T(8,128)(2,1)}), bf16[32,16,128]{2,1,0:T(8,128)(2,1)S(1)}, u32[]{:S(2)}, u32[]{:S(2)}) %all-to-all-start.1) | async-done | bytes 131104 | tf_op jit(solution)/shard_map/all_to_all | solution.py:641
  41.1 0.7 %unpack.1 = (f32[128,128]{1,0:T(8,128)}, f32[256,128]{1,0:T(8,128)}, f32[128,128]{1,0:T(8,128)}) custom-call(bf16[512,128]{1,0:T(8,128)(2,1)S(1)} %bitcast.8), custom_call_target="tpu_custom_call" | custom-call | bytes 1000000 | tf_op jit(solution)/shard_map/unpack/pallas_call | solution.py:477
  (5 shorter events, 0.0 us)
Async XLA Ops:
  0.6 6.5 %copy-start.1 = (bf16[1536,128]{1,0:T(8,128)(2,1)S(1)}, bf16[1536,128]{1,0:T(8,128)(2,1)}, u32[]{:S(2)}) copy-start(bf16[1536,128]{1,0:T(8,128)(2,1)} %state_ref.1) | copy-start | bytes 1179652
  0.6 6.5 %copy-start.2 = (bf16[1536,128]{1,0:T(8,128)(2,1)S(1)}, bf16[1536,128]{1,0:T(8,128)(2,1)}, u32[]{:S(2)}) copy-start(bf16[1536,128]{1,0:T(8,128)(2,1)} %cot_hbm.1) | copy-start | bytes 1179652
  0.7 6.5 %copy-start = (s32[12,4,128,128]{3,2,1,0:T(8,128)S(1)}, s32[12,4,128,128]{3,2,1,0:T(8,128)}, u32[]{:S(2)}) copy-start(s32[12,4,128,128]{3,2,1,0:T(8,128)} %counts_ref.1) | copy-start | bytes 9437188
  0.7 6.5 %copy-start.8 = (f32[128]{0:T(128)S(1)}, f32[128]{0:T(128)}, u32[]{:S(2)}) copy-start(f32[128]{0:T(128)} %param.16) | copy-start | bytes 1540
  0.7 6.5 %copy-start.7 = (f32[128]{0:T(128)S(1)}, f32[128]{0:T(128)}, u32[]{:S(2)}) copy-start(f32[128]{0:T(128)} %param.15) | copy-start | bytes 1540
  0.7 6.5 %copy-start.5 = (bf16[128,128]{1,0:T(8,128)(2,1)S(1)}, bf16[128,128]{1,0:T(8,128)(2,1)}, u32[]{:S(2)}) copy-start(bf16[128,128]{1,0:T(8,128)(2,1)} %w_second_ref.1) | copy-start | bytes 98308
  0.7 6.5 %copy-start.6 = (f32[128]{0:T(128)S(1)}, f32[128]{0:T(128)}, u32[]{:S(2)}) copy-start(f32[128]{0:T(128)} %param.13) | copy-start | bytes 1540
  0.7 6.5 %copy-start.3 = (bf16[256,128]{1,0:T(8,128)(2,1)S(1)}, bf16[256,128]{1,0:T(8,128)(2,1)}, u32[]{:S(2)}) copy-start(bf16[256,128]{1,0:T(8,128)(2,1)} %w_first_ref.1) | copy-start | bytes 196612
  0.7 6.5 %copy-start.4 = (bf16[128,128]{1,0:T(8,128)(2,1)S(1)}, bf16[128,128]{1,0:T(8,128)(2,1)}, u32[]{:S(2)}) copy-start(bf16[128,128]{1,0:T(8,128)(2,1)} %w_msg_ref.1) | copy-start | bytes 98308
  1.8 5.3 %collective-permute-start = (bf16[256,128]{1,0:T(8,128)(2,1)S(1)}, bf16[256,128]{1,0:T(8,128)(2,1)S(1)}, u32[]{:S(2)}, u32[]{:S(2)}) collective-permute-start(bf16[256,128]{1,0:T(8,128)(2,1)S(1)} %get-tuple-element.44), channel_id=1, source_target_pairs={{0,1},{2,3},{4,5},{6,7},{8,9},{10,11},{12,13},{14,15},{16,17},{18,... | collective-permute-start | bytes 196616 | tf_op jit(solution)/shard_map/ppermute | solution.py:471
  4.9 6.3 %collective-permute-start.1 = (bf16[256,128]{1,0:T(8,128)(2,1)S(1)}, bf16[256,128]{1,0:T(8,128)(2,1)S(1)}, u32[]{:S(2)}, u32[]{:S(2)}) collective-permute-start(bf16[256,128]{1,0:T(8,128)(2,1)S(1)} %get-tuple-element.48), channel_id=1, source_target_pairs={{1,2},{3,4},{5,6},{7,8},{9,10},{11,12},{13,14},{15,16},{17,18},{19... | collective-permute-start | bytes 196616 | tf_op jit(solution)/shard_map/ppermute | solution.py:471
  13.7 15.7 %all-to-all-start = ((bf16[32,24,128]{2,1,0:T(8,128)(2,1)}), bf16[32,24,128]{2,1,0:T(8,128)(2,1)S(1)}, u32[]{:S(2)}, u32[]{:S(2)}) async-start(bf16[32,24,128]{2,1,0:T(8,128)(2,1)} %get-tuple-element.69), calls=%async_computation | async-start | bytes 393216 | tf_op jit(solution)/shard_map/all_to_all | solution.py:597
  20.9 11.8 %collective-permute-start.2 = (bf16[2,128,128]{2,1,0:T(8,128)(2,1)S(1)}, bf16[2,128,128]{2,1,0:T(8,128)(2,1)S(1)}, u32[]{:S(2)}, u32[]{:S(2)}) collective-permute-start(bf16[2,128,128]{2,1,0:T(8,128)(2,1)S(1)} %get-tuple-element.63), channel_id=1, source_target_pairs={{0,1},{2,3},{4,5},{6,7},{8,9},{10,11},{12,13},{14,15},{16,17},{18,... | collective-permute-start | bytes 196616 | tf_op jit(solution)/shard_map/ppermute | solution.py:471
  22.8 10.0 %collective-permute-start.3 = (bf16[2,128,128]{2,1,0:T(8,128)(2,1)S(1)}, bf16[2,128,128]{2,1,0:T(8,128)(2,1)S(1)}, u32[]{:S(2)}, u32[]{:S(2)}) collective-permute-start(bf16[2,128,128]{2,1,0:T(8,128)(2,1)S(1)} %get-tuple-element.64), channel_id=1, source_target_pairs={{1,2},{3,4},{5,6},{7,8},{9,10},{11,12},{13,14},{15,16},{17,18},{19... | collective-permute-start | bytes 196616 | tf_op jit(solution)/shard_map/ppermute | solution.py:471
  30.1 11.0 %all-to-all-start.1 = ((bf16[32,16,128]{2,1,0:T(8,128)(2,1)}), bf16[32,16,128]{2,1,0:T(8,128)(2,1)S(1)}, u32[]{:S(2)}, u32[]{:S(2)}) async-start(bf16[32,16,128]{2,1,0:T(8,128)(2,1)} %get-tuple-element.73), calls=%async_computation.1 | async-start | bytes 262144 | tf_op jit(solution)/shard_map/all_to_all | solution.py:641

commit v16 on v12

--- a/solution.py
+++ b/solution.py
@@ -258,10 +258,8 @@
     msg_sums_ref,
     gain_sums_ref,
     grads_ref,
-    updated_hbm,
+    updated_ref,
     d_hidden_ref,
-    updated_ref,
-    left,
 ):
     features, size = w_msg_ref.shape[0], columns_ref.shape[2]
     halo = got_odd_ref[...]
@@ -278,8 +276,6 @@
         [columns_ref[k] for k in range(3)],
     )
     updated_ref[...] = updated_t
-    updated_copy = pltpu.make_async_copy(updated_ref, updated_hbm, left)
-    updated_copy.start()
     d_hidden_ref[...] = d_hidden_t
     d_aggregate_t = d_aggregate_of(w_first_ref[...], d_hidden_t)
 
@@ -316,11 +312,10 @@
     for k in range(grads_ref.shape[0]):
         block = sums[k * chunk : (k + 1) * chunk] if k * chunk < sums.shape[0] else nothing
         grads_ref[k] = jnp.concatenate([block, bias], axis=0)
-    updated_copy.wait()
 
 
 def owed_kernel(
-    band_ref, w_first_ref, inner_ref, outer_ref, owed_ref, send_even_ref, send_odd_ref
+    band_ref, w_first_ref, inner_ref, outer_ref, done_ref, ends_ref, send_even_ref, send_odd_ref
 ):
     blocks, _, size, _ = band_ref.shape
     odd = device_is_odd()
@@ -348,8 +343,11 @@
         to_above = owed(blocks + k).astype(BF16)
         send_even_ref[k] = jnp.where(odd, to_below, to_above)
         send_odd_ref[k] = jnp.where(odd, to_above, to_below)
-    for b in range(blocks):
-        owed_ref[b] = owed(b)
+    for b in range(WIN, blocks - WIN):
+        done_ref[b - WIN] = owed(b).astype(BF16)
+    for k in range(WIN):
+        ends_ref[k] = owed(k)
+        ends_ref[WIN + k] = owed(blocks - WIN + k)
 
 
 def sum_kernel(parts_ref, spread_ref, bias_ref):
@@ -370,10 +368,11 @@
     w_msg_ref,
     w_first_ref,
     inner_updated_hbm,
-    outer_updated_hbm,
+    outer_updated_ref,
     inner_d_hidden_ref,
     outer_d_hidden_ref,
     owed_ref,
+    ends_ref,
     bias_ref,
     updated_ref,
     grad_state_ref,
@@ -382,17 +381,16 @@
     gain_ref,
     cot_ref,
     inner_updated_ref,
-    outer_updated_ref,
     arrived,
 ):
-    blocks, features, size = owed_ref.shape
+    inner, features, size = owed_ref.shape
+    blocks = inner + 2 * WIN
     copies = [
         pltpu.make_async_copy(source, target, arrived.at[k])
         for k, (source, target) in enumerate(
             (
                 (cot_hbm, cot_ref),
                 (inner_updated_hbm, inner_updated_ref),
-                (outer_updated_hbm, outer_updated_ref),
             )
         )
     ]
@@ -406,11 +404,13 @@
     for copy in copies:
         copy.wait()
     for b in range(blocks):
-        owed = owed_ref[b]
         if b < WIN:
-            owed = owed + from_below[b]
-        elif b >= blocks - WIN:
-            owed = owed + from_above[b - blocks + WIN]
+            owed = (ends_ref[b] + from_below[b]).astype(BF16)
+        elif b < blocks - WIN:
+            owed = owed_ref[b - WIN]
+        else:
+            k = b - blocks + WIN
+            owed = (ends_ref[WIN + k] + from_above[k]).astype(BF16)
         if WIN <= b < blocks - WIN:
             lanes = pl.ds((b - WIN) * size, size)
             updated, d_hidden = inner_updated_ref[:, lanes], inner_d_hidden_ref[:, lanes]
@@ -425,7 +425,7 @@
                 even_end, inner_d_hidden_ref[:, lanes], outer_d_hidden_ref[:, outer_lanes]
             )
         rows = pl.ds(b * size, size)
-        change = dot(weights, jnp.concatenate([d_hidden, owed.astype(BF16)], axis=0))
+        change = dot(weights, jnp.concatenate([d_hidden, owed], axis=0))
         grad_state_ref[rows, :] = (cot_ref[rows, :].astype(F32) + change.T).astype(BF16)
         updated_ref[rows, :] = updated.T
     for k, ref in enumerate((b_first_ref, b_second_ref, gain_ref)):
@@ -502,10 +502,7 @@
     got_even = swapped(even_side, 0)
     got_odd = swapped(odd_side, 1)
 
-    *outer_operands, band, inner_updated, inner_d_hidden = (
-        lambda *outs: (*outs[:8], *outs[11:], *outs[8:11])
-    )(
-        *call(
+    inner_results = call(
             inner_kernel,
             "inner_rows",
             (
@@ -538,31 +535,32 @@
             ),
             limit=32,
             flops=700_000_000,
-        )
-    )
+    )
+    band, inner_updated, inner_d_hidden = inner_results[8:11]
+    outer_operands = inner_results[:8] + inner_results[11:]
 
     grads, outer_updated, outer_d_hidden = call(
         functools.partial(outer_kernel, grad_scale),
         "outer_rows",
         (
             vmem((devices, chunk + BIAS_ROWS, features), SENT),
-            hbm((features, side), BF16),
+            vmem((features, side), BF16),
             vmem((features, side), BF16),
         ),
         [
             (array, vmem)
             for array in (got_odd, w_msg_here, w_first_here, w_second_here, *outer_operands)
         ],
-        scratch=(vmem((features, side), BF16), pltpu.SemaphoreType.DMA),
         flops=300_000_000,
     )
 
     parts = lax.all_to_all(grads, AXES, 0, 0, tiled=True)
-    owed, send_even, send_odd = call(
+    owed, owed_ends, send_even, send_odd = call(
         owed_kernel,
         "owed",
         (
-            vmem((blocks, features, size), F32),
+            vmem((blocks - 2 * WIN, features, size), BF16),
+            vmem((2 * WIN, features, size), F32),
             vmem((WIN, features, size), BF16),
             vmem((WIN, features, size), BF16),
         ),
@@ -589,13 +587,12 @@
             result((1, features), F32),
         ),
         [(owed_even, vmem), (owed_odd, vmem), (cotangent, hbm)]
-        + [(w_msg_here, vmem), (w_first_here, vmem), (inner_updated, hbm), (outer_updated, hbm)]
-        + [(array, vmem) for array in (inner_d_hidden, outer_d_hidden, owed, bias)],
+        + [(w_msg_here, vmem), (w_first_here, vmem), (inner_updated, hbm)]
+        + [(array, vmem) for array in (outer_updated, inner_d_hidden, outer_d_hidden, owed, owed_ends, bias)],
         scratch=(
             vmem((nodes, features), BF16),
             vmem((features, most), BF16),
-            vmem((features, side), BF16),
-            pltpu.SemaphoreType.DMA((3,)),
+            pltpu.SemaphoreType.DMA((2,)),
         ),
         flops=50_000_000_000,
     )

time: 41.8 us -> 41.6 us (level)
  waiting for transfers between devices: 12.5 us -> 13.5 us
  local copies, waits for them, and re-layouts: 0.9 us -> 0.01 us
    all_to_all x1, waiting for transfers between devices: 5.06 us -> 6.03 us  [shards(): parts = lax.all_to_all(grads, AXES, 0, 0, tiled=True)]
    unnamed x10 -> x6, local copies, waits for them, and re-layouts: 0.9 us -> 0.01 us
where the time goes in v16:
time: 41.6 us; the launch traced here: 41.4 us
  starting transfers between devices  15.3 us (37%)
  waiting for transfers between devices  13.5 us (32%)
  Pallas kernels  11.8 us (28%)
  between operations  0.75 us (2%)
    pallas_call x7, Pallas kernels, call(): pl.pallas_call(kernel, out_shape=tuple(outs), in_specs=specs, out_specs=t...  11.8 us
    all_to_all x1, starting transfers between devices, shards(): parts = lax.all_to_all(grads, AXES, 0, 0, tiled=True)  6.47 us
    ppermute x4, starting transfers between devices, swapped(): lax.ppermute(block, AXES, [(i, i + 1) for i in lower] + [(i + 1, i) for i...  6.23 us
    all_to_all x1, waiting for transfers between devices, shards(): parts = lax.all_to_all(grads, AXES, 0, 0, tiled=True)  6.03 us
    all_to_all x1, waiting for transfers between devices, shards(): whole = lax.all_to_all(spread, AXES, 0, 0, tiled=True)  5.92 us
    all_to_all x1, starting transfers between devices, shards(): whole = lax.all_to_all(spread, AXES, 0, 0, tiled=True)  2.58 us
    ppermute x4, waiting for transfers between devices, swapped(): lax.ppermute(block, AXES, [(i, i + 1) for i in lower] + [(i + 1, i) for i...  1.59 us
  transfers between devices with their start and end apart: 6, of which 3 were waited for; matrix products, arithmetic and copies ran while one was open for 0% of the time, Pallas kernels for 19%

profile of v16, /device:TPU:0, one launch (start us, length us, event | category | flops | bytes accessed | tf_op | source)
XLA Modules:
  0.0 41.4 jit_solution(13305021389299070087)
XLA Ops:
  0.6 0.0 copy-start
  0.6 0.0 copy-start.1
  0.7 0.0 copy-start.2
  0.7 1.2 %fetch.1 = (bf16[128,128]{1,0:T(8,128)(2,1)S(1)}, bf16[256,128]{1,0:T(8,128)(2,1)S(1)}, bf16[128,128]{1,0:T(8,128)(2,1)S(1)}, f32[1,128]{1,0:T(1,128)S(1)}, f32[...) custom-call(bf16[1536,128]{1,0:T(8,128)(2,1)} %state_ref.1, ...), custom_call_target="tpu_custom_call" | custom-call | flops 49999998976 | bytes 1000000 | tf_op jit(solution)/shard_map/fetch/pallas_call | solution.py:452
  1.8 3.1 %collective-permute-start = (bf16[256,128]{1,0:T(8,128)(2,1)S(1)}, bf16[256,128]{1,0:T(8,128)(2,1)S(1)}, u32[]{:S(2)}, u32[]{:S(2)}) collective-permute-start(bf16[256,128]{1,0:T(8,128)(2,1)S(1)} %get-tuple-element.48), channel_id=1, source_target_pairs={{0,1},{2,3},{4,5},{6,7},{8,9},{10,11},{12,13},{14,15},{16,17},{18,... | collective-permute-start | bytes 196616 | tf_op jit(solution)/shard_map/ppermute | solution.py:446
  4.9 0.7 %collective-permute-start.1 = (bf16[256,128]{1,0:T(8,128)(2,1)S(1)}, bf16[256,128]{1,0:T(8,128)(2,1)S(1)}, u32[]{:S(2)}, u32[]{:S(2)}) collective-permute-start(bf16[256,128]{1,0:T(8,128)(2,1)S(1)} %get-tuple-element.57), channel_id=1, source_target_pairs={{1,2},{3,4},{5,6},{7,8},{9,10},{11,12},{13,14},{15,16},{17,18},{19... | collective-permute-start | bytes 196616 | tf_op jit(solution)/shard_map/ppermute | solution.py:446
  5.6 1.6 %collective-permute-done.got_even_ref = bf16[256,128]{1,0:T(8,128)(2,1)S(1)} collective-permute-done((bf16[256,128]{1,0:T(8,128)(2,1)S(1)}, bf16[256,128]{1,0:T(8,128)(2,1)S(1)}, u32[]{:S(2)}, u32[]{:S(2)}) %collective-permute-start) | collective-permute-done | bytes 65568 | tf_op jit(solution)/shard_map/ppermute | solution.py:446
  7.2 0.0 copy-done
  7.2 0.0 copy-done.1
  7.2 0.0 copy-done.2
  7.2 3.9 %inner_rows.1 = (bf16[128,256]{1,0:T(8,128)(2,1)S(1)}, bf16[128,128]{1,0:T(8,128)(2,1)S(1)}, f32[3,128,128]{2,1,0:T(8,128)S(1)}, bf16[256,128]{1,0:T(8,128)(2,1)...) custom-call(s32[4,12]{1,0:T(4,128)} %bitcast.9, ...), custom_call_target="tpu_custom_call" | custom-call | flops 700000000 | bytes 1000000 | tf_op jit(solution)/shard_map/inner_rows/pallas_call | solution.py:452
  11.1 0.0 collective-permute-done.1.got_odd_ref
  11.1 2.0 %outer_rows.1 = (bf16[32,24,128]{2,1,0:T(8,128)(2,1)}, bf16[128,256]{1,0:T(8,128)(2,1)S(1)}, bf16[128,256]{1,0:T(8,128)(2,1)S(1)}) custom-call(bf16[256,128]{1,0:T(8,128)(2,1)S(1)} %collective-permute-done.1.got_odd_ref, bf16[128,128]{1,0:T(8,128)(2,1)S(1)} %get-tuple-element.49.w_msg_ref, bf16[256,128]{1,0:T(8,128)(2,1)S(1)} %get-tuple-element.50.w_first_ref, ...), custom_call_target="tpu_custom_call" | custom-call | flops 300000000 | bytes 1000000 | tf_op jit(solution)/shard_map/outer_rows/pallas_call | solution.py:452
  13.1 6.5 %all-to-all-start = ((bf16[32,24,128]{2,1,0:T(8,128)(2,1)}), bf16[32,24,128]{2,1,0:T(8,128)(2,1)S(1)}, u32[]{:S(2)}, u32[]{:S(2)}) async-start(bf16[32,24,128]{2,1,0:T(8,128)(2,1)} %get-tuple-element.77), calls=%async_computation | async-start | bytes 393216 | tf_op jit(solution)/shard_map/all_to_all | solution.py:557
  19.6 0.9 %owed.1 = (bf16[8,128,128]{2,1,0:T(8,128)(2,1)S(1)}, f32[4,128,128]{2,1,0:T(8,128)S(1)}, bf16[2,128,128]{2,1,0:T(8,128)(2,1)S(1)}, bf16[2,128,128]{2,1,0:T(8,128)(2,1)S(1)}) custom-call(bf16[12,5,128,128]{3,2,1,0:T(8,128)(2,1)S(1)} %get-tuple-element.55.band_ref, bf16[256,128]{1,0:T(8,128)(2,1)S(1)} %get-tuple-element.50.w_first_ref, ...), custom_call_target="tpu_custom_call" | custom-call | flops 200000000 | bytes 1000000 | tf_op jit(solution)/shard_map/owed/pallas_call | solution.py:452
  20.4 1.8 %collective-permute-start.2 = (bf16[2,128,128]{2,1,0:T(8,128)(2,1)S(1)}, bf16[2,128,128]{2,1,0:T(8,128)(2,1)S(1)}, u32[]{:S(2)}, u32[]{:S(2)}) collective-permute-start(bf16[2,128,128]{2,1,0:T(8,128)(2,1)S(1)} %get-tuple-element.71), channel_id=1, source_target_pairs={{0,1},{2,3},{4,5},{6,7},{8,9},{10,11},{12,13},{14,15},{16,17},{18,... | collective-permute-start | bytes 196616 | tf_op jit(solution)/shard_map/ppermute | solution.py:446
  22.3 0.7 %collective-permute-start.3 = (bf16[2,128,128]{2,1,0:T(8,128)(2,1)S(1)}, bf16[2,128,128]{2,1,0:T(8,128)(2,1)S(1)}, u32[]{:S(2)}, u32[]{:S(2)}) collective-permute-start(bf16[2,128,128]{2,1,0:T(8,128)(2,1)S(1)} %get-tuple-element.72), channel_id=1, source_target_pairs={{1,2},{3,4},{5,6},{7,8},{9,10},{11,12},{13,14},{15,16},{17,18},{19... | collective-permute-start | bytes 196616 | tf_op jit(solution)/shard_map/ppermute | solution.py:446
  22.9 6.0 %all-to-all-done.parts_ref = bf16[32,24,128]{2,1,0:T(8,128)(2,1)S(1)} async-done(((bf16[32,24,128]{2,1,0:T(8,128)(2,1)}), bf16[32,24,128]{2,1,0:T(8,128)(2,1)S(1)}, u32[]{:S(2)}, u32[]{:S(2)}) %all-to-all-start) | async-done | bytes 196640 | tf_op jit(solution)/shard_map/all_to_all | solution.py:557
  29.0 0.7 %sum.1 = (bf16[32,16,128]{2,1,0:T(8,128)(2,1)}, f32[8,128]{1,0:T(8,128)S(1)}) custom-call(bf16[32,24,128]{2,1,0:T(8,128)(2,1)S(1)} %all-to-all-done.parts_ref), custom_call_target="tpu_custom_call" | custom-call | flops 10000000000 | bytes 1000000 | tf_op jit(solution)/shard_map/sum/pallas_call | solution.py:452
  29.7 2.6 %all-to-all-start.1 = ((bf16[32,16,128]{2,1,0:T(8,128)(2,1)}), bf16[32,16,128]{2,1,0:T(8,128)(2,1)S(1)}, u32[]{:S(2)}, u32[]{:S(2)}) async-start(bf16[32,16,128]{2,1,0:T(8,128)(2,1)} %get-tuple-element.81), calls=%async_computation.1 | async-start | bytes 262144 | tf_op jit(solution)/shard_map/all_to_all | solution.py:600
  32.2 0.0 collective-permute-done.2.even_ref
  32.3 0.0 collective-permute-done.3.odd_ref
  32.3 2.5 %results.1 = (bf16[1536,128]{1,0:T(8,128)(2,1)}, bf16[1536,128]{1,0:T(8,128)(2,1)}, f32[1,128]{1,0:T(1,128)}, f32[1,128]{1,0:T(1,128)}, f32[1,128]{1,0:T(1,128)}) custom-call(bf16[2,128,128]{2,1,0:T(8,128)(2,1)S(1)} %collective-permute-done.2.even_ref, bf16[2,128,128]{2,1,0:T(8,128)(2,1)S(1)} %collective-permute-done.3.odd_ref, bf16[1536,128]{1,0:T(8,128)(2,1)} %cot_hbm.1, ...), custom_call_target="tpu_custom_call" | custom-call | flops 49999998976 | bytes 1000000 | tf_op jit(solution)/shard_map/results/pallas_call | solution.py:452
  34.7 5.9 %all-to-all-done.1 = bf16[32,16,128]{2,1,0:T(8,128)(2,1)S(1)} async-done(((bf16[32,16,128]{2,1,0:T(8,128)(2,1)}), bf16[32,16,128]{2,1,0:T(8,128)(2,1)S(1)}, u32[]{:S(2)}, u32[]{:S(2)}) %all-to-all-start.1) | async-done | bytes 131104 | tf_op jit(solution)/shard_map/all_to_all | solution.py:600
  40.6 0.7 %unpack.1 = (f32[128,128]{1,0:T(8,128)}, f32[256,128]{1,0:T(8,128)}, f32[128,128]{1,0:T(8,128)}) custom-call(bf16[512,128]{1,0:T(8,128)(2,1)S(1)} %bitcast.8), custom_call_target="tpu_custom_call" | custom-call | bytes 1000000 | tf_op jit(solution)/shard_map/unpack/pallas_call | solution.py:452
Async XLA Ops:
  0.6 6.5 %copy-start = (s32[12,4,128,128]{3,2,1,0:T(8,128)S(1)}, s32[12,4,128,128]{3,2,1,0:T(8,128)}, u32[]{:S(2)}) copy-start(s32[12,4,128,128]{3,2,1,0:T(8,128)} %counts_ref.1) | copy-start | bytes 9437188
  0.6 6.5 %copy-start.1 = (bf16[1536,128]{1,0:T(8,128)(2,1)S(1)}, bf16[1536,128]{1,0:T(8,128)(2,1)}, u32[]{:S(2)}) copy-start(bf16[1536,128]{1,0:T(8,128)(2,1)} %state_ref.1) | copy-start | bytes 1179652
  0.7 6.5 %copy-start.2 = (bf16[1536,128]{1,0:T(8,128)(2,1)S(1)}, bf16[1536,128]{1,0:T(8,128)(2,1)}, u32[]{:S(2)}) copy-start(bf16[1536,128]{1,0:T(8,128)(2,1)} %cot_hbm.1) | copy-start | bytes 1179652
  1.8 5.3 %collective-permute-start = (bf16[256,128]{1,0:T(8,128)(2,1)S(1)}, bf16[256,128]{1,0:T(8,128)(2,1)S(1)}, u32[]{:S(2)}, u32[]{:S(2)}) collective-permute-start(bf16[256,128]{1,0:T(8,128)(2,1)S(1)} %get-tuple-element.48), channel_id=1, source_target_pairs={{0,1},{2,3},{4,5},{6,7},{8,9},{10,11},{12,13},{14,15},{16,17},{18,... | collective-permute-start | bytes 196616 | tf_op jit(solution)/shard_map/ppermute | solution.py:446
  4.9 6.1 %collective-permute-start.1 = (bf16[256,128]{1,0:T(8,128)(2,1)S(1)}, bf16[256,128]{1,0:T(8,128)(2,1)S(1)}, u32[]{:S(2)}, u32[]{:S(2)}) collective-permute-start(bf16[256,128]{1,0:T(8,128)(2,1)S(1)} %get-tuple-element.57), channel_id=1, source_target_pairs={{1,2},{3,4},{5,6},{7,8},{9,10},{11,12},{13,14},{15,16},{17,18},{19... | collective-permute-start | bytes 196616 | tf_op jit(solution)/shard_map/ppermute | solution.py:446
  13.1 15.9 %all-to-all-start = ((bf16[32,24,128]{2,1,0:T(8,128)(2,1)}), bf16[32,24,128]{2,1,0:T(8,128)(2,1)S(1)}, u32[]{:S(2)}, u32[]{:S(2)}) async-start(bf16[32,24,128]{2,1,0:T(8,128)(2,1)} %get-tuple-element.77), calls=%async_computation | async-start | bytes 393216 | tf_op jit(solution)/shard_map/all_to_all | solution.py:557
  20.4 11.8 %collective-permute-start.2 = (bf16[2,128,128]{2,1,0:T(8,128)(2,1)S(1)}, bf16[2,128,128]{2,1,0:T(8,128)(2,1)S(1)}, u32[]{:S(2)}, u32[]{:S(2)}) collective-permute-start(bf16[2,128,128]{2,1,0:T(8,128)(2,1)S(1)} %get-tuple-element.71), channel_id=1, source_target_pairs={{0,1},{2,3},{4,5},{6,7},{8,9},{10,11},{12,13},{14,15},{16,17},{18,... | collective-permute-start | bytes 196616 | tf_op jit(solution)/shard_map/ppermute | solution.py:446
  22.3 10.0 %collective-permute-start.3 = (bf16[2,128,128]{2,1,0:T(8,128)(2,1)S(1)}, bf16[2,128,128]{2,1,0:T(8,128)(2,1)S(1)}, u32[]{:S(2)}, u32[]{:S(2)}) collective-permute-start(bf16[2,128,128]{2,1,0:T(8,128)(2,1)S(1)} %get-tuple-element.72), channel_id=1, source_target_pairs={{1,2},{3,4},{5,6},{7,8},{9,10},{11,12},{13,14},{15,16},{17,18},{19... | collective-permute-start | bytes 196616 | tf_op jit(solution)/shard_map/ppermute | solution.py:446
  29.7 11.0 %all-to-all-start.1 = ((bf16[32,16,128]{2,1,0:T(8,128)(2,1)}), bf16[32,16,128]{2,1,0:T(8,128)(2,1)S(1)}, u32[]{:S(2)}, u32[]{:S(2)}) async-start(bf16[32,16,128]{2,1,0:T(8,128)(2,1)} %get-tuple-element.81), calls=%async_computation.1 | async-start | bytes 262144 | tf_op jit(solution)/shard_map/all_to_all | solution.py:600

commit v17 on v11

--- a/solution.py
+++ b/solution.py
@@ -85,23 +85,27 @@
     return dot_nt(jnp.concatenate([active_t, ones], axis=0), d_norm_t)
 
 
-def fetch_kernel(*refs):
+def fetch_kernel(state_hbm, *refs):
     count = (len(refs) - 3) // 2
     sources, targets = refs[:count], refs[count : 2 * count]
     even_side_ref, odd_side_ref, arrived = refs[2 * count :]
+    edge = even_side_ref.shape[0]
+    odd = device_is_odd()
+    last = state_hbm.shape[0] - edge
+    even_start = pl.multiple_of(jnp.where(odd, 0, last), edge)
+    odd_start = pl.multiple_of(jnp.where(odd, last, 0), edge)
+    pairs = [
+        (state_hbm.at[pl.ds(even_start, edge)], even_side_ref),
+        (state_hbm.at[pl.ds(odd_start, edge)], odd_side_ref),
+        *zip(sources, targets),
+    ]
     copies = [
         pltpu.make_async_copy(source, target, arrived.at[k])
-        for k, (source, target) in enumerate(zip(sources, targets))
+        for k, (source, target) in enumerate(pairs)
     ]
     for copy in copies:
         copy.start()
-    copies[0].wait()
-    state, edge = targets[0], even_side_ref.shape[0]
-    odd = device_is_odd()
-    head, tail = state[pl.ds(0, edge), :], state[pl.ds(state.shape[0] - edge, edge), :]
-    even_side_ref[...] = jnp.where(odd, head, tail)
-    odd_side_ref[...] = jnp.where(odd, tail, head)
-    for copy in copies[1:]:
+    for copy in copies:
         copy.wait()
 
 
@@ -119,6 +123,7 @@
     first_t_ref,
     second_t_ref,
     columns_ref,
+    edge_rows_ref,
     edge_state_ref,
     edge_cot_ref,
     edge_sum_ref,
@@ -154,6 +159,7 @@
         columns_ref[k] = columns[k]
     state_t = [state_ref[rows(b), :].T for b in range(blocks)]
     for k, b in enumerate(edge_rows):
+        edge_rows_ref[rows(k), :] = state_ref[rows(b), :]
         edge_state_ref[:, rows(k)] = state_t[b]
 
     nothing = jnp.zeros((size, size), BF16)
@@ -210,15 +216,15 @@
 
 def outer_kernel(
     grad_scale,
+    got_odd_ref,
     got_even_ref,
-    got_odd_ref,
-    state_ref,
     w_msg_ref,
     w_first_ref,
     w_second_ref,
     first_t_ref,
     second_t_ref,
     columns_ref,
+    edge_rows_ref,
     edge_state_ref,
     edge_cot_ref,
     edge_sum_ref,
@@ -228,10 +234,8 @@
     msg_sums_ref,
     gain_sums_ref,
     grads_ref,
-    updated_hbm,
+    updated_ref,
     d_hidden_ref,
-    updated_ref,
-    left,
 ):
     blocks, _, size, _ = band_ref.shape
     features = w_msg_ref.shape[0]
@@ -263,16 +267,10 @@
         [columns_ref[k] for k in range(3)],
     )
     updated_ref[...] = updated_t
-    updated_copy = pltpu.make_async_copy(updated_ref, updated_hbm, left)
-    updated_copy.start()
     d_hidden_ref[...] = d_hidden_t
     d_aggregate_t = d_aggregate_of(w_first_ref[...], d_hidden_t)
 
-    width = WIN * size
-    ends = [state_ref[pl.ds(0, width), :], state_ref[pl.ds((blocks - WIN) * size, width), :]]
-    first_sums = first_sums_ref[...] + first_products(
-        d_hidden_t, jnp.concatenate(ends, axis=0), aggregate
-    )
+    first_sums = first_sums_ref[...] + first_products(d_hidden_t, edge_rows_ref[...], aggregate)
     second_sums = second_sums_ref[...] + second_products(active_t, d_norm_t)
     msg_sums = msg_sums_ref[...] + dot(d_aggregate_t, summed)
     gain_sums = gain_sums_ref[...]
@@ -305,11 +303,10 @@
     for k in range(grads_ref.shape[0]):
         block = sums[k * chunk : (k + 1) * chunk] if k * chunk < sums.shape[0] else nothing
         grads_ref[k] = jnp.concatenate([block, bias], axis=0)
-    updated_copy.wait()
 
 
 def owed_kernel(
-    band_ref, w_first_ref, inner_ref, outer_ref, owed_ref, send_even_ref, send_odd_ref
+    band_ref, w_first_ref, inner_ref, outer_ref, done_ref, ends_ref, send_even_ref, send_odd_ref
 ):
     blocks, _, size, _ = band_ref.shape
     odd = device_is_odd()
@@ -335,8 +332,11 @@
         to_above = owed(blocks + k).astype(BF16)
         send_even_ref[k] = jnp.where(odd, to_below, to_above)
         send_odd_ref[k] = jnp.where(odd, to_above, to_below)
-    for b in range(blocks):
-        owed_ref[b] = owed(b)
+    for b in range(WIN, blocks - WIN):
+        done_ref[b - WIN] = owed(b).astype(BF16)
+    for k in range(WIN):
+        ends_ref[k] = owed(k)
+        ends_ref[WIN + k] = owed(blocks - WIN + k)
 
 
 def sum_kernel(parts_ref, spread_ref, bias_ref):
@@ -357,10 +357,11 @@
     w_msg_ref,
     w_first_ref,
     inner_updated_hbm,
-    outer_updated_hbm,
+    outer_updated_ref,
     inner_d_hidden_ref,
     outer_d_hidden_ref,
     owed_ref,
+    ends_ref,
     bias_ref,
     updated_ref,
     grad_state_ref,
@@ -369,17 +370,16 @@
     gain_ref,
     cot_ref,
     inner_updated_ref,
-    outer_updated_ref,
     arrived,
 ):
-    blocks, features, size = owed_ref.shape
+    inner, features, size = owed_ref.shape
+    blocks = inner + 2 * WIN
     copies = [
         pltpu.make_async_copy(source, target, arrived.at[k])
         for k, (source, target) in enumerate(
             (
                 (cot_hbm, cot_ref),
                 (inner_updated_hbm, inner_updated_ref),
-                (outer_updated_hbm, outer_updated_ref),
             )
         )
     ]
@@ -393,18 +393,20 @@
     for copy in copies:
         copy.wait()
     for b in range(blocks):
-        owed = owed_ref[b]
         if b < WIN:
-            owed = owed + from_below[b]
-        elif b >= blocks - WIN:
-            owed = owed + from_above[b - blocks + WIN]
+            owed = (ends_ref[b] + from_below[b]).astype(BF16)
+        elif b < blocks - WIN:
+            owed = owed_ref[b - WIN]
+        else:
+            k = b - blocks + WIN
+            owed = (ends_ref[WIN + k] + from_above[k]).astype(BF16)
         if WIN <= b < blocks - WIN:
             k, updated, d_hidden = b - WIN, inner_updated_ref, inner_d_hidden_ref
         else:
             k = b if b < WIN else b - blocks + 2 * WIN
             updated, d_hidden = outer_updated_ref, outer_d_hidden_ref
         lanes, rows = pl.ds(k * size, size), pl.ds(b * size, size)
-        change = dot(weights, jnp.concatenate([d_hidden[:, lanes], owed.astype(BF16)], axis=0))
+        change = dot(weights, jnp.concatenate([d_hidden[:, lanes], owed], axis=0))
         grad_state_ref[rows, :] = (cot_ref[rows, :].astype(F32) + change.T).astype(BF16)
         updated_ref[rows, :] = updated[:, lanes].T
     for k, ref in enumerate((b_first_ref, b_second_ref, gain_ref)):
@@ -467,32 +469,26 @@
     result = jax.ShapeDtypeStruct
 
     row = lambda vector: vector.reshape(1, features)
-    sources = (
-        node_state,
-        w_msg,
-        w_first,
-        w_second,
-        row(b_first),
-        row(b_second),
-        row(ln_gain),
-    )
+    side = WIN * size
+    sources = (w_msg, w_first, w_second, row(b_first), row(b_second), row(ln_gain))
     *fetched, even_side, odd_side = call(
         fetch_kernel,
         "fetch",
         [vmem(array.shape, array.dtype) for array in sources]
-        + [vmem((WIN * size, features), BF16)] * 2,
-        [(array, hbm) for array in sources],
-        scratch=(pltpu.SemaphoreType.DMA((len(sources),)),),
+        + [vmem((side, features), BF16)] * 2,
+        [(array, hbm) for array in (node_state, *sources)],
+        scratch=(pltpu.SemaphoreType.DMA((len(sources) + 2,)),),
         flops=50_000_000_000,
     )
-    state, w_msg_here, w_first_here, w_second_here, *vectors = fetched
+    w_msg_here, w_first_here, w_second_here, *vectors = fetched
+    got_odd = swapped(odd_side, 1)
     got_even = swapped(even_side, 0)
-    got_odd = swapped(odd_side, 1)
 
     (
         first_t,
         second_t,
         columns,
+        edge_rows,
         edge_state,
         edge_cot,
         edge_sum,
@@ -510,6 +506,7 @@
             vmem((features, 2 * features), BF16),
             vmem((features, features), BF16),
             vmem((3, features, size), F32),
+            vmem((edge * size, features), BF16),
             vmem((features, edge * size), BF16),
             vmem((features, edge * size), BF16),
             vmem((edge, size, 2 * features), F32),
@@ -524,7 +521,7 @@
         [(col_index.T, hbm), (edge_counts, vmem), (cotangent, vmem)]
         + [
             (array, vmem)
-            for array in (state, w_msg_here, w_first_here, w_second_here, *vectors)
+            for array in (node_state, w_msg_here, w_first_here, w_second_here, *vectors)
         ],
         scratch=(
             pltpu.SMEM((tiles, blocks), jnp.int32),
@@ -541,21 +538,21 @@
         "outer_rows",
         (
             vmem((devices, chunk + BIAS_ROWS, features), SENT),
-            hbm((features, edge * size), BF16),
+            vmem((features, edge * size), BF16),
             vmem((features, edge * size), BF16),
         ),
         [
             (array, vmem)
             for array in (
+                got_odd,
                 got_even,
-                got_odd,
-                state,
                 w_msg_here,
                 w_first_here,
                 w_second_here,
                 first_t,
                 second_t,
                 columns,
+                edge_rows,
                 edge_state,
                 edge_cot,
                 edge_sum,
@@ -566,16 +563,16 @@
                 gain_sums,
             )
         ],
-        scratch=(vmem((features, edge * size), BF16), pltpu.SemaphoreType.DMA),
         flops=300_000_000,
     )
 
     parts = lax.all_to_all(grads, AXES, 0, 0, tiled=True)
-    owed, send_even, send_odd = call(
+    owed, owed_ends, send_even, send_odd = call(
         owed_kernel,
         "owed",
         (
-            vmem((blocks, features, size), F32),
+            vmem((blocks - 2 * WIN, features, size), BF16),
+            vmem((2 * WIN, features, size), F32),
             vmem((WIN, features, size), BF16),
             vmem((WIN, features, size), BF16),
         ),
@@ -602,13 +599,12 @@
             result((1, features), F32),
         ),
         [(owed_even, vmem), (owed_odd, vmem), (cotangent, hbm)]
-        + [(w_msg_here, vmem), (w_first_here, vmem), (inner_updated, hbm), (outer_updated, hbm)]
-        + [(array, vmem) for array in (inner_d_hidden, outer_d_hidden, owed, bias)],
+        + [(w_msg_here, vmem), (w_first_here, vmem), (inner_updated, hbm)]
+        + [(array, vmem) for array in (outer_updated, inner_d_hidden, outer_d_hidden, owed, owed_ends, bias)],
         scratch=(
             vmem((nodes, features), BF16),
             vmem((features, inner * size), BF16),
-            vmem((features, edge * size), BF16),
-            pltpu.SemaphoreType.DMA((3,)),
+            pltpu.SemaphoreType.DMA((2,)),
         ),
         flops=50_000_000_000,
     )

time: 41.9 us -> 41.7 us (level)
  Pallas kernels: 12.7 us -> 12 us
  waiting for transfers between devices: 11.5 us -> 12 us
    all_to_all x1, starting transfers between devices: 7.98 us -> 4.86 us  [shards(): parts = lax.all_to_all(grads, AXES, 0, 0, tiled=True)]
    ppermute x4, starting transfers between devices: 6.16 us -> 9.19 us  [swapped(): lax.ppermute(block, AXES, [(i, i + 1) for i in lower] + [(i + 1, i) for i...]
    pallas_call x7, Pallas kernels: 12.7 us -> 12 us  [call(): pl.pallas_call(kernel, out_shape=tuple(outs), in_specs=specs, out_specs=t...]
  transfers between devices with their start and end apart: 6 -> 6, of which waited for: 2 -> 2; matrix products, arithmetic and copies ran while one was open for 0% -> 0% of each run, Pallas kernels for 20% -> 19%
where the time goes in v17:
time: 41.7 us; the launch traced here: 41.4 us
  starting transfers between devices  16.6 us (40%)
  Pallas kernels  12 us (29%)
  waiting for transfers between devices  12 us (29%)
  between operations  0.76 us (2%)
    pallas_call x7, Pallas kernels, call(): pl.pallas_call(kernel, out_shape=tuple(outs), in_specs=specs, out_specs=t...  12 us
    ppermute x4, starting transfers between devices, swapped(): lax.ppermute(block, AXES, [(i, i + 1) for i in lower] + [(i + 1, i) for i...  9.19 us
    all_to_all x1, waiting for transfers between devices, shards(): parts = lax.all_to_all(grads, AXES, 0, 0, tiled=True)  6.01 us
    all_to_all x1, waiting for transfers between devices, shards(): whole = lax.all_to_all(spread, AXES, 0, 0, tiled=True)  5.94 us
    all_to_all x1, starting transfers between devices, shards(): parts = lax.all_to_all(grads, AXES, 0, 0, tiled=True)  4.86 us
    all_to_all x1, starting transfers between devices, shards(): whole = lax.all_to_all(spread, AXES, 0, 0, tiled=True)  2.58 us
  transfers between devices with their start and end apart: 6, of which 2 were waited for; matrix products, arithmetic and copies ran while one was open for 0% of the time, Pallas kernels for 19%

profile of v17, /device:TPU:0, one launch (start us, length us, event | category | flops | bytes accessed | tf_op | source)
XLA Modules:
  0.0 41.4 jit_solution(3016548159364004372)
XLA Ops:
  0.6 0.0 copy-start
  0.6 0.0 copy-start.1
  0.7 0.0 copy-start.2
  0.7 1.2 %fetch.1 = (bf16[128,128]{1,0:T(8,128)(2,1)S(1)}, bf16[256,128]{1,0:T(8,128)(2,1)S(1)}, bf16[128,128]{1,0:T(8,128)(2,1)S(1)}, f32[1,128]{1,0:T(1,128)S(1)}, f32[...) custom-call(bf16[1536,128]{1,0:T(8,128)(2,1)} %state_ref.1, ...), custom_call_target="tpu_custom_call" | custom-call | flops 49999998976 | bytes 1000000 | tf_op jit(solution)/shard_map/fetch/pallas_call | solution.py:433
  1.8 0.8 %collective-permute-start = (bf16[256,128]{1,0:T(8,128)(2,1)S(1)}, bf16[256,128]{1,0:T(8,128)(2,1)S(1)}, u32[]{:S(2)}, u32[]{:S(2)}) collective-permute-start(bf16[256,128]{1,0:T(8,128)(2,1)S(1)} %get-tuple-element.55), channel_id=1, source_target_pairs={{1,2},{3,4},{5,6},{7,8},{9,10},{11,12},{13,14},{15,16},{17,18},{19... | collective-permute-start | bytes 196616 | tf_op jit(solution)/shard_map/ppermute | solution.py:427
  2.6 5.9 %collective-permute-start.1 = (bf16[256,128]{1,0:T(8,128)(2,1)S(1)}, bf16[256,128]{1,0:T(8,128)(2,1)S(1)}, u32[]{:S(2)}, u32[]{:S(2)}) collective-permute-start(bf16[256,128]{1,0:T(8,128)(2,1)S(1)} %get-tuple-element.56), channel_id=1, source_target_pairs={{0,1},{2,3},{4,5},{6,7},{8,9},{10,11},{12,13},{14,15},{16,17},{18,... | collective-permute-start | bytes 196616 | tf_op jit(solution)/shard_map/ppermute | solution.py:427
  8.6 0.0 copy-done
  8.6 0.0 copy-done.1
  8.6 0.0 copy-done.2
  8.6 4.0 %inner_rows.1 = (bf16[128,256]{1,0:T(8,128)(2,1)S(1)}, bf16[128,128]{1,0:T(8,128)(2,1)S(1)}, f32[3,128,128]{2,1,0:T(8,128)S(1)}, bf16[512,128]{1,0:T(8,128)(2,1)...) custom-call(s32[4,12]{1,0:T(4,128)} %bitcast.9, ...), custom_call_target="tpu_custom_call" | custom-call | flops 700000000 | bytes 1000000 | tf_op jit(solution)/shard_map/inner_rows/pallas_call | solution.py:433
  12.6 0.0 collective-permute-done.got_odd_ref
  12.6 0.0 collective-permute-done.1.got_even_ref
  12.6 2.1 %outer_rows.1 = (bf16[32,24,128]{2,1,0:T(8,128)(2,1)}, bf16[128,512]{1,0:T(8,128)(2,1)S(1)}, bf16[128,512]{1,0:T(8,128)(2,1)S(1)}) custom-call(bf16[256,128]{1,0:T(8,128)(2,1)S(1)} %collective-permute-done.got_odd_ref, bf16[256,128]{1,0:T(8,128)(2,1)S(1)} %collective-permute-done.1.got_even_ref, bf16[128,128]{1,0:T(8,128)(2,1)S(1)} %get-tuple-element.47.w_msg_ref, ...), custom_call_target="tpu_custom_call" | custom-call | flops 300000000 | bytes 1000000 | tf_op jit(solution)/shard_map/outer_rows/pallas_call | solution.py:433
  14.7 4.9 %all-to-all-start = ((bf16[32,24,128]{2,1,0:T(8,128)(2,1)}), bf16[32,24,128]{2,1,0:T(8,128)(2,1)S(1)}, u32[]{:S(2)}, u32[]{:S(2)}) async-start(bf16[32,24,128]{2,1,0:T(8,128)(2,1)} %get-tuple-element.75), calls=%async_computation | async-start | bytes 393216 | tf_op jit(solution)/shard_map/all_to_all | solution.py:569
  19.6 0.9 %owed.1 = (bf16[8,128,128]{2,1,0:T(8,128)(2,1)S(1)}, f32[4,128,128]{2,1,0:T(8,128)S(1)}, bf16[2,128,128]{2,1,0:T(8,128)(2,1)S(1)}, bf16[2,128,128]{2,1,0:T(8,128)(2,1)S(1)}) custom-call(bf16[12,5,128,128]{3,2,1,0:T(8,128)(2,1)S(1)} %get-tuple-element.53.band_ref, bf16[256,128]{1,0:T(8,128)(2,1)S(1)} %get-tuple-element.48.w_first_ref, ...), custom_call_target="tpu_custom_call" | custom-call | flops 200000000 | bytes 1000000 | tf_op jit(solution)/shard_map/owed/pallas_call | solution.py:433
  20.5 1.8 %collective-permute-start.2 = (bf16[2,128,128]{2,1,0:T(8,128)(2,1)S(1)}, bf16[2,128,128]{2,1,0:T(8,128)(2,1)S(1)}, u32[]{:S(2)}, u32[]{:S(2)}) collective-permute-start(bf16[2,128,128]{2,1,0:T(8,128)(2,1)S(1)} %get-tuple-element.69), channel_id=1, source_target_pairs={{0,1},{2,3},{4,5},{6,7},{8,9},{10,11},{12,13},{14,15},{16,17},{18,... | collective-permute-start | bytes 196616 | tf_op jit(solution)/shard_map/ppermute | solution.py:427
  22.3 0.7 %collective-permute-start.3 = (bf16[2,128,128]{2,1,0:T(8,128)(2,1)S(1)}, bf16[2,128,128]{2,1,0:T(8,128)(2,1)S(1)}, u32[]{:S(2)}, u32[]{:S(2)}) collective-permute-start(bf16[2,128,128]{2,1,0:T(8,128)(2,1)S(1)} %get-tuple-element.70), channel_id=1, source_target_pairs={{1,2},{3,4},{5,6},{7,8},{9,10},{11,12},{13,14},{15,16},{17,18},{19... | collective-permute-start | bytes 196616 | tf_op jit(solution)/shard_map/ppermute | solution.py:427
  23.0 6.0 %all-to-all-done.parts_ref = bf16[32,24,128]{2,1,0:T(8,128)(2,1)S(1)} async-done(((bf16[32,24,128]{2,1,0:T(8,128)(2,1)}), bf16[32,24,128]{2,1,0:T(8,128)(2,1)S(1)}, u32[]{:S(2)}, u32[]{:S(2)}) %all-to-all-start) | async-done | bytes 196640 | tf_op jit(solution)/shard_map/all_to_all | solution.py:569
  29.0 0.7 %sum.1 = (bf16[32,16,128]{2,1,0:T(8,128)(2,1)}, f32[8,128]{1,0:T(8,128)S(1)}) custom-call(bf16[32,24,128]{2,1,0:T(8,128)(2,1)S(1)} %all-to-all-done.parts_ref), custom_call_target="tpu_custom_call" | custom-call | flops 10000000000 | bytes 1000000 | tf_op jit(solution)/shard_map/sum/pallas_call | solution.py:433
  29.7 2.6 %all-to-all-start.1 = ((bf16[32,16,128]{2,1,0:T(8,128)(2,1)}), bf16[32,16,128]{2,1,0:T(8,128)(2,1)S(1)}, u32[]{:S(2)}, u32[]{:S(2)}) async-start(bf16[32,16,128]{2,1,0:T(8,128)(2,1)} %get-tuple-element.79), calls=%async_computation.1 | async-start | bytes 262144 | tf_op jit(solution)/shard_map/all_to_all | solution.py:612
  32.3 0.0 collective-permute-done.2.even_ref
  32.3 0.0 collective-permute-done.3.odd_ref
  32.3 2.4 %results.1 = (bf16[1536,128]{1,0:T(8,128)(2,1)}, bf16[1536,128]{1,0:T(8,128)(2,1)}, f32[1,128]{1,0:T(1,128)}, f32[1,128]{1,0:T(1,128)}, f32[1,128]{1,0:T(1,128)}) custom-call(bf16[2,128,128]{2,1,0:T(8,128)(2,1)S(1)} %collective-permute-done.2.even_ref, bf16[2,128,128]{2,1,0:T(8,128)(2,1)S(1)} %collective-permute-done.3.odd_ref, bf16[1536,128]{1,0:T(8,128)(2,1)} %cot_hbm.1, ...), custom_call_target="tpu_custom_call" | custom-call | flops 49999998976 | bytes 1000000 | tf_op jit(solution)/shard_map/results/pallas_call | solution.py:433
  34.8 5.9 %all-to-all-done.1 = bf16[32,16,128]{2,1,0:T(8,128)(2,1)S(1)} async-done(((bf16[32,16,128]{2,1,0:T(8,128)(2,1)}), bf16[32,16,128]{2,1,0:T(8,128)(2,1)S(1)}, u32[]{:S(2)}, u32[]{:S(2)}) %all-to-all-start.1) | async-done | bytes 131104 | tf_op jit(solution)/shard_map/all_to_all | solution.py:612
  40.7 0.7 %unpack.1 = (f32[128,128]{1,0:T(8,128)}, f32[256,128]{1,0:T(8,128)}, f32[128,128]{1,0:T(8,128)}) custom-call(bf16[512,128]{1,0:T(8,128)(2,1)S(1)} %bitcast.8), custom_call_target="tpu_custom_call" | custom-call | bytes 1000000 | tf_op jit(solution)/shard_map/unpack/pallas_call | solution.py:433
Async XLA Ops:
  0.6 7.9 %copy-start = (s32[12,4,128,128]{3,2,1,0:T(8,128)S(1)}, s32[12,4,128,128]{3,2,1,0:T(8,128)}, u32[]{:S(2)}) copy-start(s32[12,4,128,128]{3,2,1,0:T(8,128)} %counts_ref.1) | copy-start | bytes 9437188
  0.6 7.9 %copy-start.1 = (bf16[1536,128]{1,0:T(8,128)(2,1)S(1)}, bf16[1536,128]{1,0:T(8,128)(2,1)}, u32[]{:S(2)}) copy-start(bf16[1536,128]{1,0:T(8,128)(2,1)} %state_ref.1) | copy-start | bytes 1179652
  0.7 7.9 %copy-start.2 = (bf16[1536,128]{1,0:T(8,128)(2,1)S(1)}, bf16[1536,128]{1,0:T(8,128)(2,1)}, u32[]{:S(2)}) copy-start(bf16[1536,128]{1,0:T(8,128)(2,1)} %cot_hbm.1) | copy-start | bytes 1179652
  1.8 10.7 %collective-permute-start = (bf16[256,128]{1,0:T(8,128)(2,1)S(1)}, bf16[256,128]{1,0:T(8,128)(2,1)S(1)}, u32[]{:S(2)}, u32[]{:S(2)}) collective-permute-start(bf16[256,128]{1,0:T(8,128)(2,1)S(1)} %get-tuple-element.55), channel_id=1, source_target_pairs={{1,2},{3,4},{5,6},{7,8},{9,10},{11,12},{13,14},{15,16},{17,18},{19... | collective-permute-start | bytes 196616 | tf_op jit(solution)/shard_map/ppermute | solution.py:427
  2.6 9.9 %collective-permute-start.1 = (bf16[256,128]{1,0:T(8,128)(2,1)S(1)}, bf16[256,128]{1,0:T(8,128)(2,1)S(1)}, u32[]{:S(2)}, u32[]{:S(2)}) collective-permute-start(bf16[256,128]{1,0:T(8,128)(2,1)S(1)} %get-tuple-element.56), channel_id=1, source_target_pairs={{0,1},{2,3},{4,5},{6,7},{8,9},{10,11},{12,13},{14,15},{16,17},{18,... | collective-permute-start | bytes 196616 | tf_op jit(solution)/shard_map/ppermute | solution.py:427
  14.7 14.3 %all-to-all-start = ((bf16[32,24,128]{2,1,0:T(8,128)(2,1)}), bf16[32,24,128]{2,1,0:T(8,128)(2,1)S(1)}, u32[]{:S(2)}, u32[]{:S(2)}) async-start(bf16[32,24,128]{2,1,0:T(8,128)(2,1)} %get-tuple-element.75), calls=%async_computation | async-start | bytes 393216 | tf_op jit(solution)/shard_map/all_to_all | solution.py:569
  20.5 11.8 %collective-permute-start.2 = (bf16[2,128,128]{2,1,0:T(8,128)(2,1)S(1)}, bf16[2,128,128]{2,1,0:T(8,128)(2,1)S(1)}, u32[]{:S(2)}, u32[]{:S(2)}) collective-permute-start(bf16[2,128,128]{2,1,0:T(8,128)(2,1)S(1)} %get-tuple-element.69), channel_id=1, source_target_pairs={{0,1},{2,3},{4,5},{6,7},{8,9},{10,11},{12,13},{14,15},{16,17},{18,... | collective-permute-start | bytes 196616 | tf_op jit(solution)/shard_map/ppermute | solution.py:427
  22.3 10.0 %collective-permute-start.3 = (bf16[2,128,128]{2,1,0:T(8,128)(2,1)S(1)}, bf16[2,128,128]{2,1,0:T(8,128)(2,1)S(1)}, u32[]{:S(2)}, u32[]{:S(2)}) collective-permute-start(bf16[2,128,128]{2,1,0:T(8,128)(2,1)S(1)} %get-tuple-element.70), channel_id=1, source_target_pairs={{1,2},{3,4},{5,6},{7,8},{9,10},{11,12},{13,14},{15,16},{17,18},{19... | collective-permute-start | bytes 196616 | tf_op jit(solution)/shard_map/ppermute | solution.py:427
  29.7 11.0 %all-to-all-start.1 = ((bf16[32,16,128]{2,1,0:T(8,128)(2,1)}), bf16[32,16,128]{2,1,0:T(8,128)(2,1)S(1)}, u32[]{:S(2)}, u32[]{:S(2)}) async-start(bf16[32,16,128]{2,1,0:T(8,128)(2,1)} %get-tuple-element.79), calls=%async_computation.1 | async-start | bytes 262144 | tf_op jit(solution)/shard_map/all_to_all | solution.py:612

commit v18 on v16

--- a/solution.py
+++ b/solution.py
@@ -11,7 +11,8 @@
 WIN = 2
 BAND = 2 * WIN + 1
 epsilon = 1e-05
-AXES = ("dom", "feat")
+AXES = ("dom", "feat_hi", "feat_lo")
+GATHERED = ("dom", "feat_lo")
 BF16, F32 = jnp.bfloat16, jnp.float32
 SENT = BF16
 ONES = 128
@@ -33,7 +34,9 @@
 
 
 def device_is_odd():
-    index = lax.axis_index("dom") * lax.axis_size("feat") + lax.axis_index("feat")
+    index = 0
+    for axis in AXES:
+        index = index * lax.axis_size(axis) + lax.axis_index(axis)
     return index % 2 == 1
 
 
@@ -241,6 +244,7 @@
 
 def outer_kernel(
     grad_scale,
+    copies,
     got_odd_ref,
     w_msg_ref,
     w_first_ref,
@@ -309,9 +313,12 @@
         [bias_high, bias_low, jnp.zeros((BIAS_ROWS - 6, features), SENT)], axis=0
     )
     nothing = jnp.zeros((chunk, features), SENT)
-    for k in range(grads_ref.shape[0]):
+    low = lax.axis_size("feat_lo")
+    for k in range(grads_ref.shape[0] // copies):
         block = sums[k * chunk : (k + 1) * chunk] if k * chunk < sums.shape[0] else nothing
-        grads_ref[k] = jnp.concatenate([block, bias], axis=0)
+        block = jnp.concatenate([block, bias], axis=0)
+        for copy in range(copies):
+            grads_ref[(k // low * copies + copy) * low + k % low] = block
 
 
 def owed_kernel(
@@ -481,7 +488,8 @@
     blocks, tiles, size, _ = edge_counts.shape
     devices = lax.axis_size(AXES)
     grad_scale = 1.0 / math.sqrt(nodes * devices)
-    chunk = -(-4 * features // (devices * 8)) * 8
+    gathered = lax.axis_size(GATHERED)
+    chunk = -(-4 * features // (gathered * 8)) * 8
     side = WIN * size
     most = nodes - side
     vmem, hbm = pltpu.VMEM, pltpu.HBM
@@ -540,7 +548,7 @@
     outer_operands = inner_results[:8] + inner_results[11:]
 
     grads, outer_updated, outer_d_hidden = call(
-        functools.partial(outer_kernel, grad_scale),
+        functools.partial(outer_kernel, grad_scale, devices // gathered),
         "outer_rows",
         (
             vmem((devices, chunk + BIAS_ROWS, features), SENT),
@@ -572,7 +580,7 @@
     spread, bias = call(
         sum_kernel,
         "sum",
-        (vmem((devices, chunk, features), SENT), vmem((BIAS_ROWS, features), F32)),
+        (vmem((gathered, chunk, features), SENT), vmem((BIAS_ROWS, features), F32)),
         [(parts, vmem)],
         flops=10_000_000_000,
     )
@@ -597,7 +605,7 @@
         flops=50_000_000_000,
     )
 
-    whole = lax.all_to_all(spread, AXES, 0, 0, tiled=True)
+    whole = lax.all_to_all(spread, GATHERED, 0, 0, tiled=True)
     g_msg, g_first, g_second = call(
         unpack_kernel,
         "unpack",
@@ -606,7 +614,7 @@
             result((2 * features, features), F32),
             result((features, features), F32),
         ),
-        [(whole.reshape(devices * chunk, features), vmem)],
+        [(whole.reshape(gathered * chunk, features), vmem)],
     )
     flat = lambda vector: vector.reshape(features)
     return (
@@ -622,6 +630,9 @@
 
 
 def solution(mesh):
+    dom, feat = mesh.devices.shape
+    low = 2 - feat % 2
+    mesh = jax.sharding.Mesh(mesh.devices.reshape(dom, feat // low, low), AXES)
     split = P(AXES, None)
     return jax.shard_map(
         shards,

time: 41.6 us -> 41.8 us (level)
  waiting for transfers between devices: 13.5 us -> 12.6 us
  starting transfers between devices: 15.3 us -> 16 us
    all_to_all x1, waiting for transfers between devices: 5.92 us -> 3.23 us  [shards(): whole = lax.all_to_all(spread, GATHERED, 0, 0, tiled=True)]
    all_to_all x1, waiting for transfers between devices: 6.03 us -> 7.75 us  [shards(): parts = lax.all_to_all(grads, AXES, 0, 0, tiled=True)]
    all_to_all x1, starting transfers between devices: 2.58 us -> 3.51 us  [shards(): whole = lax.all_to_all(spread, GATHERED, 0, 0, tiled=True)]
  transfers between devices with their start and end apart: 6 -> 6, of which waited for: 3 -> 3; matrix products, arithmetic and copies ran while one was open for 0% -> 0% of each run, Pallas kernels for 19% -> 20%
where the time goes in v18:
time: 41.8 us; the launch traced here: 41.4 us
  starting transfers between devices  16 us (38%)
  waiting for transfers between devices  12.6 us (30%)
  Pallas kernels  12 us (29%)
  between operations  0.75 us (2%)
    pallas_call x7, Pallas kernels, call(): pl.pallas_call(kernel, out_shape=tuple(outs), in_specs=specs, out_specs=t...  12 us
    all_to_all x1, waiting for transfers between devices, shards(): parts = lax.all_to_all(grads, AXES, 0, 0, tiled=True)  7.75 us
    all_to_all x1, starting transfers between devices, shards(): parts = lax.all_to_all(grads, AXES, 0, 0, tiled=True)  6.3 us
    ppermute x4, starting transfers between devices, swapped(): lax.ppermute(block, AXES, [(i, i + 1) for i in lower] + [(i + 1, i) for i...  6.23 us
    all_to_all x1, starting transfers between devices, shards(): whole = lax.all_to_all(spread, GATHERED, 0, 0, tiled=True)  3.51 us
    all_to_all x1, waiting for transfers between devices, shards(): whole = lax.all_to_all(spread, GATHERED, 0, 0, tiled=True)  3.23 us
    ppermute x4, waiting for transfers between devices, swapped(): lax.ppermute(block, AXES, [(i, i + 1) for i in lower] + [(i + 1, i) for i...  1.59 us
  transfers between devices with their start and end apart: 6, of which 3 were waited for; matrix products, arithmetic and copies ran while one was open for 0% of the time, Pallas kernels for 20%

profile of v18, /device:TPU:0, one launch (start us, length us, event | category | flops | bytes accessed | tf_op | source)
XLA Modules:
  0.0 41.4 jit_solution(9092285449661872025)
XLA Ops:
  0.6 0.0 copy-start
  0.6 0.0 copy-start.1
  0.7 0.0 copy-start.2
  0.7 1.2 %fetch.1 = (bf16[128,128]{1,0:T(8,128)(2,1)S(1)}, bf16[256,128]{1,0:T(8,128)(2,1)S(1)}, bf16[128,128]{1,0:T(8,128)(2,1)S(1)}, f32[1,128]{1,0:T(1,128)S(1)}, f32[...) custom-call(bf16[1536,128]{1,0:T(8,128)(2,1)} %state_ref.1, ...), custom_call_target="tpu_custom_call" | custom-call | flops 49999998976 | bytes 1000000 | tf_op jit(solution)/shard_map/fetch/pallas_call | solution.py:459
  1.8 3.1 %collective-permute-start = (bf16[256,128]{1,0:T(8,128)(2,1)S(1)}, bf16[256,128]{1,0:T(8,128)(2,1)S(1)}, u32[]{:S(2)}, u32[]{:S(2)}) collective-permute-start(bf16[256,128]{1,0:T(8,128)(2,1)S(1)} %get-tuple-element.48), channel_id=1, source_target_pairs={{0,1},{2,3},{4,5},{6,7},{8,9},{10,11},{12,13},{14,15},{16,17},{18,... | collective-permute-start | bytes 196616 | tf_op jit(solution)/shard_map/ppermute | solution.py:453
  4.9 0.7 %collective-permute-start.1 = (bf16[256,128]{1,0:T(8,128)(2,1)S(1)}, bf16[256,128]{1,0:T(8,128)(2,1)S(1)}, u32[]{:S(2)}, u32[]{:S(2)}) collective-permute-start(bf16[256,128]{1,0:T(8,128)(2,1)S(1)} %get-tuple-element.57), channel_id=1, source_target_pairs={{1,2},{3,4},{5,6},{7,8},{9,10},{11,12},{13,14},{15,16},{17,18},{19... | collective-permute-start | bytes 196616 | tf_op jit(solution)/shard_map/ppermute | solution.py:453
  5.6 1.6 %collective-permute-done.got_even_ref = bf16[256,128]{1,0:T(8,128)(2,1)S(1)} collective-permute-done((bf16[256,128]{1,0:T(8,128)(2,1)S(1)}, bf16[256,128]{1,0:T(8,128)(2,1)S(1)}, u32[]{:S(2)}, u32[]{:S(2)}) %collective-permute-start) | collective-permute-done | bytes 65568 | tf_op jit(solution)/shard_map/ppermute | solution.py:453
  7.2 0.0 copy-done
  7.2 0.0 copy-done.1
  7.2 0.0 copy-done.2
  7.2 4.1 %inner_rows.1 = (bf16[128,256]{1,0:T(8,128)(2,1)S(1)}, bf16[128,128]{1,0:T(8,128)(2,1)S(1)}, f32[3,128,128]{2,1,0:T(8,128)S(1)}, bf16[256,128]{1,0:T(8,128)(2,1)...) custom-call(s32[4,12]{1,0:T(4,128)} %bitcast.9, ...), custom_call_target="tpu_custom_call" | custom-call | flops 700000000 | bytes 1000000 | tf_op jit(solution)/shard_map/inner_rows/pallas_call | solution.py:459
  11.2 0.0 collective-permute-done.1.got_odd_ref
  11.3 2.1 %outer_rows.1 = (bf16[32,40,128]{2,1,0:T(8,128)(2,1)}, bf16[128,256]{1,0:T(8,128)(2,1)S(1)}, bf16[128,256]{1,0:T(8,128)(2,1)S(1)}) custom-call(bf16[256,128]{1,0:T(8,128)(2,1)S(1)} %collective-permute-done.1.got_odd_ref, bf16[128,128]{1,0:T(8,128)(2,1)S(1)} %get-tuple-element.49.w_msg_ref, bf16[256,128]{1,0:T(8,128)(2,1)S(1)} %get-tuple-element.50.w_first_ref, ...), custom_call_target="tpu_custom_call" | custom-call | flops 300000000 | bytes 1000000 | tf_op jit(solution)/shard_map/outer_rows/pallas_call | solution.py:459
  13.3 6.3 %all-to-all-start = ((bf16[32,40,128]{2,1,0:T(8,128)(2,1)}), bf16[32,40,128]{2,1,0:T(8,128)(2,1)S(1)}, u32[]{:S(2)}, u32[]{:S(2)}) async-start(bf16[32,40,128]{2,1,0:T(8,128)(2,1)} %get-tuple-element.77), calls=%async_computation | async-start | bytes 655360 | tf_op jit(solution)/shard_map/all_to_all | solution.py:565
  19.6 0.9 %owed.1 = (bf16[8,128,128]{2,1,0:T(8,128)(2,1)S(1)}, f32[4,128,128]{2,1,0:T(8,128)S(1)}, bf16[2,128,128]{2,1,0:T(8,128)(2,1)S(1)}, bf16[2,128,128]{2,1,0:T(8,128)(2,1)S(1)}) custom-call(bf16[12,5,128,128]{3,2,1,0:T(8,128)(2,1)S(1)} %get-tuple-element.55.band_ref, bf16[256,128]{1,0:T(8,128)(2,1)S(1)} %get-tuple-element.50.w_first_ref, ...), custom_call_target="tpu_custom_call" | custom-call | flops 200000000 | bytes 1000000 | tf_op jit(solution)/shard_map/owed/pallas_call | solution.py:459
  20.5 1.8 %collective-permute-start.2 = (bf16[2,128,128]{2,1,0:T(8,128)(2,1)S(1)}, bf16[2,128,128]{2,1,0:T(8,128)(2,1)S(1)}, u32[]{:S(2)}, u32[]{:S(2)}) collective-permute-start(bf16[2,128,128]{2,1,0:T(8,128)(2,1)S(1)} %get-tuple-element.71), channel_id=1, source_target_pairs={{0,1},{2,3},{4,5},{6,7},{8,9},{10,11},{12,13},{14,15},{16,17},{18,... | collective-permute-start | bytes 196616 | tf_op jit(solution)/shard_map/ppermute | solution.py:453
  22.4 0.7 %collective-permute-start.3 = (bf16[2,128,128]{2,1,0:T(8,128)(2,1)S(1)}, bf16[2,128,128]{2,1,0:T(8,128)(2,1)S(1)}, u32[]{:S(2)}, u32[]{:S(2)}) collective-permute-start(bf16[2,128,128]{2,1,0:T(8,128)(2,1)S(1)} %get-tuple-element.72), channel_id=1, source_target_pairs={{1,2},{3,4},{5,6},{7,8},{9,10},{11,12},{13,14},{15,16},{17,18},{19... | collective-permute-start | bytes 196616 | tf_op jit(solution)/shard_map/ppermute | solution.py:453
  23.0 7.8 %all-to-all-done.parts_ref = bf16[32,40,128]{2,1,0:T(8,128)(2,1)S(1)} async-done(((bf16[32,40,128]{2,1,0:T(8,128)(2,1)}), bf16[32,40,128]{2,1,0:T(8,128)(2,1)S(1)}, u32[]{:S(2)}, u32[]{:S(2)}) %all-to-all-start) | async-done | bytes 327712 | tf_op jit(solution)/shard_map/all_to_all | solution.py:565
  30.8 0.7 %sum.1 = (bf16[16,32,128]{2,1,0:T(8,128)(2,1)}, f32[8,128]{1,0:T(8,128)S(1)}) custom-call(bf16[32,40,128]{2,1,0:T(8,128)(2,1)S(1)} %all-to-all-done.parts_ref), custom_call_target="tpu_custom_call" | custom-call | flops 10000000000 | bytes 1000000 | tf_op jit(solution)/shard_map/sum/pallas_call | solution.py:459
  31.5 3.5 %all-to-all-start.1 = ((bf16[16,32,128]{2,1,0:T(8,128)(2,1)}), bf16[16,32,128]{2,1,0:T(8,128)(2,1)S(1)}, u32[]{:S(2)}, u32[]{:S(2)}) async-start(bf16[16,32,128]{2,1,0:T(8,128)(2,1)} %get-tuple-element.81), calls=%async_computation.1 | async-start | bytes 262144 | tf_op jit(solution)/shard_map/all_to_all | solution.py:608
  35.0 0.0 collective-permute-done.2.even_ref
  35.0 0.0 collective-permute-done.3.odd_ref
  35.0 2.5 %results.1 = (bf16[1536,128]{1,0:T(8,128)(2,1)}, bf16[1536,128]{1,0:T(8,128)(2,1)}, f32[1,128]{1,0:T(1,128)}, f32[1,128]{1,0:T(1,128)}, f32[1,128]{1,0:T(1,128)}) custom-call(bf16[2,128,128]{2,1,0:T(8,128)(2,1)S(1)} %collective-permute-done.2.even_ref, bf16[2,128,128]{2,1,0:T(8,128)(2,1)S(1)} %collective-permute-done.3.odd_ref, bf16[1536,128]{1,0:T(8,128)(2,1)} %cot_hbm.1, ...), custom_call_target="tpu_custom_call" | custom-call | flops 49999998976 | bytes 1000000 | tf_op jit(solution)/shard_map/results/pallas_call | solution.py:459
  37.5 3.2 %all-to-all-done.1 = bf16[16,32,128]{2,1,0:T(8,128)(2,1)S(1)} async-done(((bf16[16,32,128]{2,1,0:T(8,128)(2,1)}), bf16[16,32,128]{2,1,0:T(8,128)(2,1)S(1)}, u32[]{:S(2)}, u32[]{:S(2)}) %all-to-all-start.1) | async-done | bytes 131104 | tf_op jit(solution)/shard_map/all_to_all | solution.py:608
  40.7 0.7 %unpack.1 = (f32[128,128]{1,0:T(8,128)}, f32[256,128]{1,0:T(8,128)}, f32[128,128]{1,0:T(8,128)}) custom-call(bf16[512,128]{1,0:T(8,128)(2,1)S(1)} %bitcast.8), custom_call_target="tpu_custom_call" | custom-call | bytes 1000000 | tf_op jit(solution)/shard_map/unpack/pallas_call | solution.py:459
Async XLA Ops:
  0.6 6.5 %copy-start = (s32[12,4,128,128]{3,2,1,0:T(8,128)S(1)}, s32[12,4,128,128]{3,2,1,0:T(8,128)}, u32[]{:S(2)}) copy-start(s32[12,4,128,128]{3,2,1,0:T(8,128)} %counts_ref.1) | copy-start | bytes 9437188
  0.6 6.5 %copy-start.1 = (bf16[1536,128]{1,0:T(8,128)(2,1)S(1)}, bf16[1536,128]{1,0:T(8,128)(2,1)}, u32[]{:S(2)}) copy-start(bf16[1536,128]{1,0:T(8,128)(2,1)} %state_ref.1) | copy-start | bytes 1179652
  0.7 6.5 %copy-start.2 = (bf16[1536,128]{1,0:T(8,128)(2,1)S(1)}, bf16[1536,128]{1,0:T(8,128)(2,1)}, u32[]{:S(2)}) copy-start(bf16[1536,128]{1,0:T(8,128)(2,1)} %cot_hbm.1) | copy-start | bytes 1179652
  1.8 5.3 %collective-permute-start = (bf16[256,128]{1,0:T(8,128)(2,1)S(1)}, bf16[256,128]{1,0:T(8,128)(2,1)S(1)}, u32[]{:S(2)}, u32[]{:S(2)}) collective-permute-start(bf16[256,128]{1,0:T(8,128)(2,1)S(1)} %get-tuple-element.48), channel_id=1, source_target_pairs={{0,1},{2,3},{4,5},{6,7},{8,9},{10,11},{12,13},{14,15},{16,17},{18,... | collective-permute-start | bytes 196616 | tf_op jit(solution)/shard_map/ppermute | solution.py:453
  4.9 6.3 %collective-permute-start.1 = (bf16[256,128]{1,0:T(8,128)(2,1)S(1)}, bf16[256,128]{1,0:T(8,128)(2,1)S(1)}, u32[]{:S(2)}, u32[]{:S(2)}) collective-permute-start(bf16[256,128]{1,0:T(8,128)(2,1)S(1)} %get-tuple-element.57), channel_id=1, source_target_pairs={{1,2},{3,4},{5,6},{7,8},{9,10},{11,12},{13,14},{15,16},{17,18},{19... | collective-permute-start | bytes 196616 | tf_op jit(solution)/shard_map/ppermute | solution.py:453
  13.3 17.5 %all-to-all-start = ((bf16[32,40,128]{2,1,0:T(8,128)(2,1)}), bf16[32,40,128]{2,1,0:T(8,128)(2,1)S(1)}, u32[]{:S(2)}, u32[]{:S(2)}) async-start(bf16[32,40,128]{2,1,0:T(8,128)(2,1)} %get-tuple-element.77), calls=%async_computation | async-start | bytes 655360 | tf_op jit(solution)/shard_map/all_to_all | solution.py:565
  20.5 14.5 %collective-permute-start.2 = (bf16[2,128,128]{2,1,0:T(8,128)(2,1)S(1)}, bf16[2,128,128]{2,1,0:T(8,128)(2,1)S(1)}, u32[]{:S(2)}, u32[]{:S(2)}) collective-permute-start(bf16[2,128,128]{2,1,0:T(8,128)(2,1)S(1)} %get-tuple-element.71), channel_id=1, source_target_pairs={{0,1},{2,3},{4,5},{6,7},{8,9},{10,11},{12,13},{14,15},{16,17},{18,... | collective-permute-start | bytes 196616 | tf_op jit(solution)/shard_map/ppermute | solution.py:453
  22.4 12.7 %collective-permute-start.3 = (bf16[2,128,128]{2,1,0:T(8,128)(2,1)S(1)}, bf16[2,128,128]{2,1,0:T(8,128)(2,1)S(1)}, u32[]{:S(2)}, u32[]{:S(2)}) collective-permute-start(bf16[2,128,128]{2,1,0:T(8,128)(2,1)S(1)} %get-tuple-element.72), channel_id=1, source_target_pairs={{1,2},{3,4},{5,6},{7,8},{9,10},{11,12},{13,14},{15,16},{17,18},{19... | collective-permute-start | bytes 196616 | tf_op jit(solution)/shard_map/ppermute | solution.py:453
  31.5 9.2 %all-to-all-start.1 = ((bf16[16,32,128]{2,1,0:T(8,128)(2,1)}), bf16[16,32,128]{2,1,0:T(8,128)(2,1)S(1)}, u32[]{:S(2)}, u32[]{:S(2)}) async-start(bf16[16,32,128]{2,1,0:T(8,128)(2,1)} %get-tuple-element.81), calls=%async_computation.1 | async-start | bytes 262144 | tf_op jit(solution)/shard_map/all_to_all | solution.py:608

commit v19 on v16

--- a/solution.py
+++ b/solution.py
@@ -15,7 +15,7 @@
 BF16, F32 = jnp.bfloat16, jnp.float32
 SENT = BF16
 ONES = 128
-BIAS_ROWS = 8
+SLAB = 4
 
 kept = pltpu.with_memory_space_constraint
 
@@ -286,7 +286,7 @@
     for k in range(WIN):
         gain_sums = gain_sums + terms[:, k * size : (k + 1) * size]
 
-    chunk = grads_ref.shape[1] - BIAS_ROWS
+    slabs = grads_ref.shape[1] - 1
     turned = [first_sums[:, k * size : (k + 1) * size].T for k in range(3)]
     sums = (
         jnp.concatenate([turned[0], turned[1], second_sums[:features], msg_sums.T], axis=0)
@@ -303,15 +303,13 @@
         )
         * grad_scale
     )
-    bias_high = bias.astype(SENT)
-    bias_low = (bias - bias_high.astype(F32)).astype(SENT)
-    bias = jnp.concatenate(
-        [bias_high, bias_low, jnp.zeros((BIAS_ROWS - 6, features), SENT)], axis=0
-    )
-    nothing = jnp.zeros((chunk, features), SENT)
+    bias = jnp.concatenate([bias, jnp.zeros((SLAB - 3, features), F32)], axis=0).astype(SENT)
+    nothing = jnp.zeros((SLAB, features), SENT)
     for k in range(grads_ref.shape[0]):
-        block = sums[k * chunk : (k + 1) * chunk] if k * chunk < sums.shape[0] else nothing
-        grads_ref[k] = jnp.concatenate([block, bias], axis=0)
+        for slab in range(slabs):
+            row = (k * slabs + slab) * SLAB
+            grads_ref[k, slab] = sums[row : row + SLAB] if row < sums.shape[0] else nothing
+        grads_ref[k, slabs] = bias
 
 
 def owed_kernel(
@@ -351,14 +349,18 @@
 
 
 def sum_kernel(parts_ref, spread_ref, bias_ref):
-    total = parts_ref[0].astype(F32)
-    for k in range(1, parts_ref.shape[0]):
-        total = total + parts_ref[k].astype(F32)
-    chunk = spread_ref.shape[1]
-    weights = total[:chunk].astype(spread_ref.dtype)
+    def total(slab):
+        result = parts_ref[0, slab].astype(F32)
+        for k in range(1, parts_ref.shape[0]):
+            result = result + parts_ref[k, slab].astype(F32)
+        return result
+
+    slabs = parts_ref.shape[1] - 1
+    weights = jnp.concatenate([total(slab) for slab in range(slabs)], axis=0)
+    weights = weights.astype(spread_ref.dtype)
     for k in range(spread_ref.shape[0]):
         spread_ref[k] = weights
-    bias_ref[...] = total[chunk:]
+    bias_ref[...] = total(slabs)
 
 
 def result_kernel(
@@ -429,7 +431,7 @@
         grad_state_ref[rows, :] = (cot_ref[rows, :].astype(F32) + change.T).astype(BF16)
         updated_ref[rows, :] = updated.T
     for k, ref in enumerate((b_first_ref, b_second_ref, gain_ref)):
-        ref[...] = bias_ref[pl.ds(k, 1), :] + bias_ref[pl.ds(k + 3, 1), :]
+        ref[...] = bias_ref[pl.ds(k, 1), :]
 
 
 def unpack_kernel(rows_ref, msg_ref, first_ref, second_ref):
@@ -543,7 +545,7 @@
         functools.partial(outer_kernel, grad_scale),
         "outer_rows",
         (
-            vmem((devices, chunk + BIAS_ROWS, features), SENT),
+            vmem((devices, chunk // SLAB + 1, SLAB, features), SENT),
             vmem((features, side), BF16),
             vmem((features, side), BF16),
         ),
@@ -572,7 +574,7 @@
     spread, bias = call(
         sum_kernel,
         "sum",
-        (vmem((devices, chunk, features), SENT), vmem((BIAS_ROWS, features), F32)),
+        (vmem((devices, chunk, features), SENT), vmem((SLAB, features), F32)),
         [(parts, vmem)],
         flops=10_000_000_000,
     )

time: 41.6 us -> 41.3 us (level)
  no operation moved by 1% of the time
where the time goes in v19:
time: 41.3 us; the launch traced here: 41 us
  starting transfers between devices  15.3 us (37%)
  waiting for transfers between devices  13.1 us (32%)
  Pallas kernels  11.8 us (29%)
  between operations  0.75 us (2%)
    pallas_call x7, Pallas kernels, call(): pl.pallas_call(kernel, out_shape=tuple(outs), in_specs=specs, out_specs=t...  11.8 us
    all_to_all x1, starting transfers between devices, shards(): parts = lax.all_to_all(grads, AXES, 0, 0, tiled=True)  6.46 us
    ppermute x4, starting transfers between devices, swapped(): lax.ppermute(block, AXES, [(i, i + 1) for i in lower] + [(i + 1, i) for i...  6.23 us
    all_to_all x1, waiting for transfers between devices, shards(): whole = lax.all_to_all(spread, AXES, 0, 0, tiled=True)  5.92 us
    all_to_all x1, waiting for transfers between devices, shards(): parts = lax.all_to_all(grads, AXES, 0, 0, tiled=True)  5.62 us
    all_to_all x1, starting transfers between devices, shards(): whole = lax.all_to_all(spread, AXES, 0, 0, tiled=True)  2.58 us
    ppermute x4, waiting for transfers between devices, swapped(): lax.ppermute(block, AXES, [(i, i + 1) for i in lower] + [(i + 1, i) for i...  1.59 us
  transfers between devices with their start and end apart: 6, of which 3 were waited for; matrix products, arithmetic and copies ran while one was open for 0% of the time, Pallas kernels for 19%

profile of v19, /device:TPU:0, one launch (start us, length us, event | category | flops | bytes accessed | tf_op | source)
XLA Modules:
  0.0 41.0 jit_solution(6961281488532311568)
XLA Ops:
  0.6 0.0 copy-start
  0.6 0.0 copy-start.1
  0.7 0.0 copy-start.2
  0.7 1.2 %fetch.1 = (bf16[128,128]{1,0:T(8,128)(2,1)S(1)}, bf16[256,128]{1,0:T(8,128)(2,1)S(1)}, bf16[128,128]{1,0:T(8,128)(2,1)S(1)}, f32[1,128]{1,0:T(1,128)S(1)}, f32[...) custom-call(bf16[1536,128]{1,0:T(8,128)(2,1)} %state_ref.1, ...), custom_call_target="tpu_custom_call" | custom-call | flops 49999998976 | bytes 1000000 | tf_op jit(solution)/shard_map/fetch/pallas_call | solution.py:454
  1.8 3.1 %collective-permute-start = (bf16[256,128]{1,0:T(8,128)(2,1)S(1)}, bf16[256,128]{1,0:T(8,128)(2,1)S(1)}, u32[]{:S(2)}, u32[]{:S(2)}) collective-permute-start(bf16[256,128]{1,0:T(8,128)(2,1)S(1)} %get-tuple-element.48), channel_id=1, source_target_pairs={{0,1},{2,3},{4,5},{6,7},{8,9},{10,11},{12,13},{14,15},{16,17},{18,... | collective-permute-start | bytes 196616 | tf_op jit(solution)/shard_map/ppermute | solution.py:448
  4.9 0.7 %collective-permute-start.1 = (bf16[256,128]{1,0:T(8,128)(2,1)S(1)}, bf16[256,128]{1,0:T(8,128)(2,1)S(1)}, u32[]{:S(2)}, u32[]{:S(2)}) collective-permute-start(bf16[256,128]{1,0:T(8,128)(2,1)S(1)} %get-tuple-element.57), channel_id=1, source_target_pairs={{1,2},{3,4},{5,6},{7,8},{9,10},{11,12},{13,14},{15,16},{17,18},{19... | collective-permute-start | bytes 196616 | tf_op jit(solution)/shard_map/ppermute | solution.py:448
  5.6 1.6 %collective-permute-done.got_even_ref = bf16[256,128]{1,0:T(8,128)(2,1)S(1)} collective-permute-done((bf16[256,128]{1,0:T(8,128)(2,1)S(1)}, bf16[256,128]{1,0:T(8,128)(2,1)S(1)}, u32[]{:S(2)}, u32[]{:S(2)}) %collective-permute-start) | collective-permute-done | bytes 65568 | tf_op jit(solution)/shard_map/ppermute | solution.py:448
  7.2 0.0 copy-done
  7.2 0.0 copy-done.1
  7.2 0.0 copy-done.2
  7.2 3.9 %inner_rows.1 = (bf16[128,256]{1,0:T(8,128)(2,1)S(1)}, bf16[128,128]{1,0:T(8,128)(2,1)S(1)}, f32[3,128,128]{2,1,0:T(8,128)S(1)}, bf16[256,128]{1,0:T(8,128)(2,1)...) custom-call(s32[4,12]{1,0:T(4,128)} %bitcast.9, ...), custom_call_target="tpu_custom_call" | custom-call | flops 700000000 | bytes 1000000 | tf_op jit(solution)/shard_map/inner_rows/pallas_call | solution.py:454
  11.1 0.0 collective-permute-done.1.got_odd_ref
  11.1 2.0 %outer_rows.1 = (bf16[32,5,4,128]{3,2,1,0:T(4,128)(2,1)}, bf16[128,256]{1,0:T(8,128)(2,1)S(1)}, bf16[128,256]{1,0:T(8,128)(2,1)S(1)}) custom-call(bf16[256,128]{1,0:T(8,128)(2,1)S(1)} %collective-permute-done.1.got_odd_ref, bf16[128,128]{1,0:T(8,128)(2,1)S(1)} %get-tuple-element.49.w_msg_ref, bf16[256,128]{1,0:T(8,128)(2,1)S(1)} %get-tuple-element.50.w_first_ref, ...), custom_call_target="tpu_custom_call" | custom-call | flops 300000000 | bytes 1000000 | tf_op jit(solution)/shard_map/outer_rows/pallas_call | solution.py:454
  13.1 6.5 %all-to-all-start = ((bf16[32,5,4,128]{3,2,1,0:T(4,128)(2,1)}), bf16[32,5,4,128]{3,2,1,0:T(4,128)(2,1)S(1)}, u32[]{:S(2)}, u32[]{:S(2)}) async-start(bf16[32,5,4,128]{3,2,1,0:T(4,128)(2,1)} %get-tuple-element.77), calls=%async_computation | async-start | bytes 327680 | tf_op jit(solution)/shard_map/all_to_all | solution.py:559
  19.6 0.9 %owed.1 = (bf16[8,128,128]{2,1,0:T(8,128)(2,1)S(1)}, f32[4,128,128]{2,1,0:T(8,128)S(1)}, bf16[2,128,128]{2,1,0:T(8,128)(2,1)S(1)}, bf16[2,128,128]{2,1,0:T(8,128)(2,1)S(1)}) custom-call(bf16[12,5,128,128]{3,2,1,0:T(8,128)(2,1)S(1)} %get-tuple-element.55.band_ref, bf16[256,128]{1,0:T(8,128)(2,1)S(1)} %get-tuple-element.50.w_first_ref, ...), custom_call_target="tpu_custom_call" | custom-call | flops 200000000 | bytes 1000000 | tf_op jit(solution)/shard_map/owed/pallas_call | solution.py:454
  20.4 1.8 %collective-permute-start.2 = (bf16[2,128,128]{2,1,0:T(8,128)(2,1)S(1)}, bf16[2,128,128]{2,1,0:T(8,128)(2,1)S(1)}, u32[]{:S(2)}, u32[]{:S(2)}) collective-permute-start(bf16[2,128,128]{2,1,0:T(8,128)(2,1)S(1)} %get-tuple-element.71), channel_id=1, source_target_pairs={{0,1},{2,3},{4,5},{6,7},{8,9},{10,11},{12,13},{14,15},{16,17},{18,... | collective-permute-start | bytes 196616 | tf_op jit(solution)/shard_map/ppermute | solution.py:448
  22.3 0.7 %collective-permute-start.3 = (bf16[2,128,128]{2,1,0:T(8,128)(2,1)S(1)}, bf16[2,128,128]{2,1,0:T(8,128)(2,1)S(1)}, u32[]{:S(2)}, u32[]{:S(2)}) collective-permute-start(bf16[2,128,128]{2,1,0:T(8,128)(2,1)S(1)} %get-tuple-element.72), channel_id=1, source_target_pairs={{1,2},{3,4},{5,6},{7,8},{9,10},{11,12},{13,14},{15,16},{17,18},{19... | collective-permute-start | bytes 196616 | tf_op jit(solution)/shard_map/ppermute | solution.py:448
  22.9 5.6 %all-to-all-done.parts_ref = bf16[32,5,4,128]{3,2,1,0:T(4,128)(2,1)S(1)} async-done(((bf16[32,5,4,128]{3,2,1,0:T(4,128)(2,1)}), bf16[32,5,4,128]{3,2,1,0:T(4,128)(2,1)S(1)}, u32[]{:S(2)}, u32[]{:S(2)}) %all-to-all-start) | async-done | bytes 163872 | tf_op jit(solution)/shard_map/all_to_all | solution.py:559
  28.6 0.7 %sum.1 = (bf16[32,16,128]{2,1,0:T(8,128)(2,1)}, f32[4,128]{1,0:T(4,128)S(1)}) custom-call(bf16[32,5,4,128]{3,2,1,0:T(4,128)(2,1)S(1)} %all-to-all-done.parts_ref), custom_call_target="tpu_custom_call" | custom-call | flops 10000000000 | bytes 1000000 | tf_op jit(solution)/shard_map/sum/pallas_call | solution.py:454
  29.3 2.6 %all-to-all-start.1 = ((bf16[32,16,128]{2,1,0:T(8,128)(2,1)}), bf16[32,16,128]{2,1,0:T(8,128)(2,1)S(1)}, u32[]{:S(2)}, u32[]{:S(2)}) async-start(bf16[32,16,128]{2,1,0:T(8,128)(2,1)} %get-tuple-element.81), calls=%async_computation.1 | async-start | bytes 262144 | tf_op jit(solution)/shard_map/all_to_all | solution.py:602
  31.9 0.0 collective-permute-done.2.even_ref
  31.9 0.0 collective-permute-done.3.odd_ref
  31.9 2.5 %results.1 = (bf16[1536,128]{1,0:T(8,128)(2,1)}, bf16[1536,128]{1,0:T(8,128)(2,1)}, f32[1,128]{1,0:T(1,128)}, f32[1,128]{1,0:T(1,128)}, f32[1,128]{1,0:T(1,128)}) custom-call(bf16[2,128,128]{2,1,0:T(8,128)(2,1)S(1)} %collective-permute-done.2.even_ref, bf16[2,128,128]{2,1,0:T(8,128)(2,1)S(1)} %collective-permute-done.3.odd_ref, bf16[1536,128]{1,0:T(8,128)(2,1)} %cot_hbm.1, ...), custom_call_target="tpu_custom_call" | custom-call | flops 49999998976 | bytes 1000000 | tf_op jit(solution)/shard_map/results/pallas_call | solution.py:454
  34.3 5.9 %all-to-all-done.1 = bf16[32,16,128]{2,1,0:T(8,128)(2,1)S(1)} async-done(((bf16[32,16,128]{2,1,0:T(8,128)(2,1)}), bf16[32,16,128]{2,1,0:T(8,128)(2,1)S(1)}, u32[]{:S(2)}, u32[]{:S(2)}) %all-to-all-start.1) | async-done | bytes 131104 | tf_op jit(solution)/shard_map/all_to_all | solution.py:602
  40.3 0.7 %unpack.1 = (f32[128,128]{1,0:T(8,128)}, f32[256,128]{1,0:T(8,128)}, f32[128,128]{1,0:T(8,128)}) custom-call(bf16[512,128]{1,0:T(8,128)(2,1)S(1)} %bitcast.8), custom_call_target="tpu_custom_call" | custom-call | bytes 1000000 | tf_op jit(solution)/shard_map/unpack/pallas_call | solution.py:454
Async XLA Ops:
  0.6 6.5 %copy-start = (s32[12,4,128,128]{3,2,1,0:T(8,128)S(1)}, s32[12,4,128,128]{3,2,1,0:T(8,128)}, u32[]{:S(2)}) copy-start(s32[12,4,128,128]{3,2,1,0:T(8,128)} %counts_ref.1) | copy-start | bytes 9437188
  0.6 6.5 %copy-start.1 = (bf16[1536,128]{1,0:T(8,128)(2,1)S(1)}, bf16[1536,128]{1,0:T(8,128)(2,1)}, u32[]{:S(2)}) copy-start(bf16[1536,128]{1,0:T(8,128)(2,1)} %state_ref.1) | copy-start | bytes 1179652
  0.7 6.5 %copy-start.2 = (bf16[1536,128]{1,0:T(8,128)(2,1)S(1)}, bf16[1536,128]{1,0:T(8,128)(2,1)}, u32[]{:S(2)}) copy-start(bf16[1536,128]{1,0:T(8,128)(2,1)} %cot_hbm.1) | copy-start | bytes 1179652
  1.8 5.3 %collective-permute-start = (bf16[256,128]{1,0:T(8,128)(2,1)S(1)}, bf16[256,128]{1,0:T(8,128)(2,1)S(1)}, u32[]{:S(2)}, u32[]{:S(2)}) collective-permute-start(bf16[256,128]{1,0:T(8,128)(2,1)S(1)} %get-tuple-element.48), channel_id=1, source_target_pairs={{0,1},{2,3},{4,5},{6,7},{8,9},{10,11},{12,13},{14,15},{16,17},{18,... | collective-permute-start | bytes 196616 | tf_op jit(solution)/shard_map/ppermute | solution.py:448
  4.9 6.1 %collective-permute-start.1 = (bf16[256,128]{1,0:T(8,128)(2,1)S(1)}, bf16[256,128]{1,0:T(8,128)(2,1)S(1)}, u32[]{:S(2)}, u32[]{:S(2)}) collective-permute-start(bf16[256,128]{1,0:T(8,128)(2,1)S(1)} %get-tuple-element.57), channel_id=1, source_target_pairs={{1,2},{3,4},{5,6},{7,8},{9,10},{11,12},{13,14},{15,16},{17,18},{19... | collective-permute-start | bytes 196616 | tf_op jit(solution)/shard_map/ppermute | solution.py:448
  13.1 15.5 %all-to-all-start = ((bf16[32,5,4,128]{3,2,1,0:T(4,128)(2,1)}), bf16[32,5,4,128]{3,2,1,0:T(4,128)(2,1)S(1)}, u32[]{:S(2)}, u32[]{:S(2)}) async-start(bf16[32,5,4,128]{3,2,1,0:T(4,128)(2,1)} %get-tuple-element.77), calls=%async_computation | async-start | bytes 327680 | tf_op jit(solution)/shard_map/all_to_all | solution.py:559
  20.4 11.4 %collective-permute-start.2 = (bf16[2,128,128]{2,1,0:T(8,128)(2,1)S(1)}, bf16[2,128,128]{2,1,0:T(8,128)(2,1)S(1)}, u32[]{:S(2)}, u32[]{:S(2)}) collective-permute-start(bf16[2,128,128]{2,1,0:T(8,128)(2,1)S(1)} %get-tuple-element.71), channel_id=1, source_target_pairs={{0,1},{2,3},{4,5},{6,7},{8,9},{10,11},{12,13},{14,15},{16,17},{18,... | collective-permute-start | bytes 196616 | tf_op jit(solution)/shard_map/ppermute | solution.py:448
  22.3 9.6 %collective-permute-start.3 = (bf16[2,128,128]{2,1,0:T(8,128)(2,1)S(1)}, bf16[2,128,128]{2,1,0:T(8,128)(2,1)S(1)}, u32[]{:S(2)}, u32[]{:S(2)}) collective-permute-start(bf16[2,128,128]{2,1,0:T(8,128)(2,1)S(1)} %get-tuple-element.72), channel_id=1, source_target_pairs={{1,2},{3,4},{5,6},{7,8},{9,10},{11,12},{13,14},{15,16},{17,18},{19... | collective-permute-start | bytes 196616 | tf_op jit(solution)/shard_map/ppermute | solution.py:448
  29.3 11.0 %all-to-all-start.1 = ((bf16[32,16,128]{2,1,0:T(8,128)(2,1)}), bf16[32,16,128]{2,1,0:T(8,128)(2,1)S(1)}, u32[]{:S(2)}, u32[]{:S(2)}) async-start(bf16[32,16,128]{2,1,0:T(8,128)(2,1)} %get-tuple-element.81), calls=%async_computation.1 | async-start | bytes 262144 | tf_op jit(solution)/shard_map/all_to_all | solution.py:602

commit v20 on v19

--- a/solution.py
+++ b/solution.py
@@ -46,27 +46,29 @@
     return [array[k : k + size].T for k in range(0, array.shape[0], size)]
 
 
-def node_layer(state_t, aggregate_t, cot_t, first_t, second_t, w_second, columns):
-    features, width = state_t.shape
-    b_first, b_second, gain = (
-        joined_lanes([c] * (width // c.shape[1])) for c in columns
-    )
-    pre_hidden = dot(first_t, jnp.concatenate([state_t, aggregate_t], axis=0)) + b_first
+def widened(square, width):
+    return joined_lanes([square] * (width // square.shape[1]))
+
+
+def node_layer(pre_hidden, state_t, cot_t, second_t, w_second, b_second, gain):
+    width = state_t.shape[1]
+    b_second, gain = widened(b_second, width), widened(gain, width)
     sigmoid = 0.5 * jnp.tanh(0.5 * pre_hidden) + 0.5
     silu = pre_hidden * sigmoid
     active_t = silu.astype(BF16)
     slope = sigmoid + silu * (1.0 - sigmoid)
     pre_norm = dot(second_t, active_t) + b_second
     centred = pre_norm - jnp.mean(pre_norm, axis=0, keepdims=True)
+    cot = cot_t.astype(F32)
+    q = cot * gain
+    mean_q = jnp.mean(q, axis=0, keepdims=True)
+    mean_qc = jnp.mean(q * centred, axis=0, keepdims=True)
     inv_std = lax.rsqrt(jnp.mean(centred * centred, axis=0, keepdims=True) + epsilon)
+    share = inv_std * (inv_std * mean_qc)
+    d_norm_t = (inv_std * ((q - mean_q) - centred * share)).astype(BF16)
     normed = centred * inv_std
     updated_t = (state_t.astype(F32) + gain * normed).astype(BF16)
-    cot = cot_t.astype(F32)
     terms = cot * normed
-    q = cot * gain
-    mean_q = jnp.mean(q, axis=0, keepdims=True)
-    mean_qn = jnp.mean(q * normed, axis=0, keepdims=True)
-    d_norm_t = (inv_std * (q - mean_q - normed * mean_qn)).astype(BF16)
     d_hidden_t = (dot(w_second, d_norm_t) * slope).astype(BF16)
     return updated_t, terms, active_t, d_norm_t, d_hidden_t
 
@@ -124,6 +126,7 @@
     first_t_ref,
     second_t_ref,
     columns_ref,
+    side_hidden_ref,
     side_state_ref,
     side_state_t_ref,
     side_cot_ref,
@@ -162,11 +165,13 @@
     w_msg, w_first, w_second = w_msg_ref[...], w_first_ref[...], w_second_ref[...]
     first_t = joined_lanes([w_first[:features].T, w_first[features:].T])
     second_t = w_second.T
-    columns = [column(ref, size) for ref in (b_first_ref, b_second_ref, gain_ref)]
+    b_first, b_second, gain = (
+        column(ref, size) for ref in (b_first_ref, b_second_ref, gain_ref)
+    )
     first_t_ref[...] = first_t
     second_t_ref[...] = second_t
-    for k in range(3):
-        columns_ref[k] = columns[k]
+    columns_ref[0] = b_second
+    columns_ref[1] = gain
     state = state_ref[...]
     state_t = [state[b * size : (b + 1) * size].T for b in range(blocks)]
     cot_t = [cot_ref[rows(b), :].T for b in range(blocks)]
@@ -204,7 +209,11 @@
     side_sum_ref[...] = odd_side(*ends)
     side_far_ref[...] = odd_side(*fars)
     side_state_ref[...] = odd_side(*end_states)
-    side_state_t_ref[...] = odd_side(*end_states_t)
+    side_state_t = odd_side(*end_states_t)
+    side_state_t_ref[...] = side_state_t
+    side_hidden_ref[...] = dot(first_t[:, :features], side_state_t) + widened(
+        b_first, WIN * size
+    )
     side_cot_ref[...] = odd_side(*end_cots_t)
 
     halo = got_even_ref[...]
@@ -212,14 +221,16 @@
     end_sum = even_side(*ends) + dot(even_side(*fars), wide_halo)
     summed = stacked([*map(neighbour_sum, inner_rows), end_sum]).astype(BF16)
     aggregate, summed = summed[:, :features], summed[:, features:]
+    these_states_t = joined_lanes([*state_t[WIN : blocks - WIN], even_side(*end_states_t)])
+    joined_t = stacked([these_states_t, joined_lanes(blocks_turned(aggregate))])
     updated_t, terms, active_t, d_norm_t, d_hidden_t = node_layer(
-        joined_lanes([*state_t[WIN : blocks - WIN], even_side(*end_states_t)]),
-        joined_lanes(blocks_turned(aggregate)),
+        dot(first_t, joined_t) + widened(b_first, joined_t.shape[1]),
+        these_states_t,
         joined_lanes([*cot_t[WIN : blocks - WIN], even_side(*end_cots_t)]),
-        first_t,
         second_t,
         w_second,
-        columns,
+        b_second,
+        gain,
     )
     updated_ref[...] = updated_t
     updated_copy = pltpu.make_async_copy(updated_ref, updated_hbm, left)
@@ -248,6 +259,7 @@
     first_t_ref,
     second_t_ref,
     columns_ref,
+    side_hidden_ref,
     side_state_ref,
     side_state_t_ref,
     side_cot_ref,
@@ -266,14 +278,15 @@
     wide_halo = joined_lanes([dot(halo, w_msg_ref[...]).astype(BF16), halo])
     summed = (side_sum_ref[...] + dot(side_far_ref[...], wide_halo)).astype(BF16)
     aggregate, summed = summed[:, :features], summed[:, features:]
+    aggregate_t = joined_lanes(blocks_turned(aggregate))
     updated_t, terms, active_t, d_norm_t, d_hidden_t = node_layer(
+        side_hidden_ref[...] + dot(first_t_ref[:, pl.ds(features, features)], aggregate_t),
         side_state_t_ref[...],
-        joined_lanes(blocks_turned(aggregate)),
         side_cot_ref[...],
-        first_t_ref[...],
         second_t_ref[...],
         w_second_ref[...],
-        [columns_ref[k] for k in range(3)],
+        columns_ref[0],
+        columns_ref[1],
     )
     updated_ref[...] = updated_t
     d_hidden_ref[...] = d_hidden_t
@@ -510,7 +523,8 @@
             (
                 vmem((features, 2 * features), BF16),
                 vmem((features, features), BF16),
-                vmem((3, features, size), F32),
+                vmem((2, features, size), F32),
+                vmem((features, side), F32),
                 vmem((side, features), BF16),
                 vmem((features, side), BF16),
                 vmem((features, side), BF16),
@@ -538,8 +552,8 @@
             limit=32,
             flops=700_000_000,
     )
-    band, inner_updated, inner_d_hidden = inner_results[8:11]
-    outer_operands = inner_results[:8] + inner_results[11:]
+    band, inner_updated, inner_d_hidden = inner_results[9:12]
+    outer_operands = inner_results[:9] + inner_results[12:]
 
     grads, outer_updated, outer_d_hidden = call(
         functools.partial(outer_kernel, grad_scale),

time: 41.3 us -> 41.2 us (level)
  transfers between devices with their start and end apart: 6 -> 6, of which waited for: 3 -> 3; matrix products, arithmetic and copies ran while one was open for 0% -> 0% of each run, Pallas kernels for 19% -> 20%
where the time goes in v20:
time: 41.2 us; the launch traced here: 40.9 us
  starting transfers between devices  15.2 us (37%)
  waiting for transfers between devices  13.1 us (32%)
  Pallas kernels  11.8 us (29%)
  between operations  0.75 us (2%)
    pallas_call x7, Pallas kernels, call(): pl.pallas_call(kernel, out_shape=tuple(outs), in_specs=specs, out_specs=t...  11.8 us
    all_to_all x1, starting transfers between devices, shards(): parts = lax.all_to_all(grads, AXES, 0, 0, tiled=True)  6.37 us
    ppermute x4, starting transfers between devices, swapped(): lax.ppermute(block, AXES, [(i, i + 1) for i in lower] + [(i + 1, i) for i...  6.23 us
    all_to_all x1, waiting for transfers between devices, shards(): whole = lax.all_to_all(spread, AXES, 0, 0, tiled=True)  5.92 us
    all_to_all x1, waiting for transfers between devices, shards(): parts = lax.all_to_all(grads, AXES, 0, 0, tiled=True)  5.62 us
    all_to_all x1, starting transfers between devices, shards(): whole = lax.all_to_all(spread, AXES, 0, 0, tiled=True)  2.58 us
    ppermute x4, waiting for transfers between devices, swapped(): lax.ppermute(block, AXES, [(i, i + 1) for i in lower] + [(i + 1, i) for i...  1.59 us
  transfers between devices with their start and end apart: 6, of which 3 were waited for; matrix products, arithmetic and copies ran while one was open for 0% of the time, Pallas kernels for 20%

profile of v20, /device:TPU:0, one launch (start us, length us, event | category | flops | bytes accessed | tf_op | source)
XLA Modules:
  0.0 40.9 jit_solution(11078352773559689775)
XLA Ops:
  0.6 0.0 copy-start
  0.6 0.0 copy-start.1
  0.7 0.0 copy-start.2
  0.7 1.2 %fetch.1 = (bf16[128,128]{1,0:T(8,128)(2,1)S(1)}, bf16[256,128]{1,0:T(8,128)(2,1)S(1)}, bf16[128,128]{1,0:T(8,128)(2,1)S(1)}, f32[1,128]{1,0:T(1,128)S(1)}, f32[...) custom-call(bf16[1536,128]{1,0:T(8,128)(2,1)} %state_ref.1, ...), custom_call_target="tpu_custom_call" | custom-call | flops 49999998976 | bytes 1000000 | tf_op jit(solution)/shard_map/fetch/pallas_call | solution.py:467
  1.8 3.1 %collective-permute-start = (bf16[256,128]{1,0:T(8,128)(2,1)S(1)}, bf16[256,128]{1,0:T(8,128)(2,1)S(1)}, u32[]{:S(2)}, u32[]{:S(2)}) collective-permute-start(bf16[256,128]{1,0:T(8,128)(2,1)S(1)} %get-tuple-element.49), channel_id=1, source_target_pairs={{0,1},{2,3},{4,5},{6,7},{8,9},{10,11},{12,13},{14,15},{16,17},{18,... | collective-permute-start | bytes 196616 | tf_op jit(solution)/shard_map/ppermute | solution.py:461
  4.9 0.7 %collective-permute-start.1 = (bf16[256,128]{1,0:T(8,128)(2,1)S(1)}, bf16[256,128]{1,0:T(8,128)(2,1)S(1)}, u32[]{:S(2)}, u32[]{:S(2)}) collective-permute-start(bf16[256,128]{1,0:T(8,128)(2,1)S(1)} %get-tuple-element.58), channel_id=1, source_target_pairs={{1,2},{3,4},{5,6},{7,8},{9,10},{11,12},{13,14},{15,16},{17,18},{19... | collective-permute-start | bytes 196616 | tf_op jit(solution)/shard_map/ppermute | solution.py:461
  5.6 1.6 %collective-permute-done.got_even_ref = bf16[256,128]{1,0:T(8,128)(2,1)S(1)} collective-permute-done((bf16[256,128]{1,0:T(8,128)(2,1)S(1)}, bf16[256,128]{1,0:T(8,128)(2,1)S(1)}, u32[]{:S(2)}, u32[]{:S(2)}) %collective-permute-start) | collective-permute-done | bytes 65568 | tf_op jit(solution)/shard_map/ppermute | solution.py:461
  7.2 0.0 copy-done
  7.2 0.0 copy-done.1
  7.2 0.0 copy-done.2
  7.2 4.0 %inner_rows.1 = (bf16[128,256]{1,0:T(8,128)(2,1)S(1)}, bf16[128,128]{1,0:T(8,128)(2,1)S(1)}, f32[2,128,128]{2,1,0:T(8,128)S(1)}, f32[128,256]{1,0:T(8,128)S(1)},...) custom-call(s32[4,12]{1,0:T(4,128)} %bitcast.9, ...), custom_call_target="tpu_custom_call" | custom-call | flops 700000000 | bytes 1000000 | tf_op jit(solution)/shard_map/inner_rows/pallas_call | solution.py:467
  11.2 0.0 collective-permute-done.1.got_odd_ref
  11.2 2.0 %outer_rows.1 = (bf16[32,5,4,128]{3,2,1,0:T(4,128)(2,1)}, bf16[128,256]{1,0:T(8,128)(2,1)S(1)}, bf16[128,256]{1,0:T(8,128)(2,1)S(1)}) custom-call(bf16[256,128]{1,0:T(8,128)(2,1)S(1)} %collective-permute-done.1.got_odd_ref, bf16[128,128]{1,0:T(8,128)(2,1)S(1)} %get-tuple-element.50.w_msg_ref, bf16[256,128]{1,0:T(8,128)(2,1)S(1)} %get-tuple-element.51.w_first_ref, ...), custom_call_target="tpu_custom_call" | custom-call | flops 300000000 | bytes 1000000 | tf_op jit(solution)/shard_map/outer_rows/pallas_call | solution.py:467
  13.1 6.4 %all-to-all-start = ((bf16[32,5,4,128]{3,2,1,0:T(4,128)(2,1)}), bf16[32,5,4,128]{3,2,1,0:T(4,128)(2,1)S(1)}, u32[]{:S(2)}, u32[]{:S(2)}) async-start(bf16[32,5,4,128]{3,2,1,0:T(4,128)(2,1)} %get-tuple-element.79), calls=%async_computation | async-start | bytes 327680 | tf_op jit(solution)/shard_map/all_to_all | solution.py:573
  19.5 0.9 %owed.1 = (bf16[8,128,128]{2,1,0:T(8,128)(2,1)S(1)}, f32[4,128,128]{2,1,0:T(8,128)S(1)}, bf16[2,128,128]{2,1,0:T(8,128)(2,1)S(1)}, bf16[2,128,128]{2,1,0:T(8,128)(2,1)S(1)}) custom-call(bf16[12,5,128,128]{3,2,1,0:T(8,128)(2,1)S(1)} %get-tuple-element.56.band_ref, bf16[256,128]{1,0:T(8,128)(2,1)S(1)} %get-tuple-element.51.w_first_ref, ...), custom_call_target="tpu_custom_call" | custom-call | flops 200000000 | bytes 1000000 | tf_op jit(solution)/shard_map/owed/pallas_call | solution.py:467
  20.4 1.8 %collective-permute-start.2 = (bf16[2,128,128]{2,1,0:T(8,128)(2,1)S(1)}, bf16[2,128,128]{2,1,0:T(8,128)(2,1)S(1)}, u32[]{:S(2)}, u32[]{:S(2)}) collective-permute-start(bf16[2,128,128]{2,1,0:T(8,128)(2,1)S(1)} %get-tuple-element.73), channel_id=1, source_target_pairs={{0,1},{2,3},{4,5},{6,7},{8,9},{10,11},{12,13},{14,15},{16,17},{18,... | collective-permute-start | bytes 196616 | tf_op jit(solution)/shard_map/ppermute | solution.py:461
  22.2 0.7 %collective-permute-start.3 = (bf16[2,128,128]{2,1,0:T(8,128)(2,1)S(1)}, bf16[2,128,128]{2,1,0:T(8,128)(2,1)S(1)}, u32[]{:S(2)}, u32[]{:S(2)}) collective-permute-start(bf16[2,128,128]{2,1,0:T(8,128)(2,1)S(1)} %get-tuple-element.74), channel_id=1, source_target_pairs={{1,2},{3,4},{5,6},{7,8},{9,10},{11,12},{13,14},{15,16},{17,18},{19... | collective-permute-start | bytes 196616 | tf_op jit(solution)/shard_map/ppermute | solution.py:461
  22.9 5.6 %all-to-all-done.parts_ref = bf16[32,5,4,128]{3,2,1,0:T(4,128)(2,1)S(1)} async-done(((bf16[32,5,4,128]{3,2,1,0:T(4,128)(2,1)}), bf16[32,5,4,128]{3,2,1,0:T(4,128)(2,1)S(1)}, u32[]{:S(2)}, u32[]{:S(2)}) %all-to-all-start) | async-done | bytes 163872 | tf_op jit(solution)/shard_map/all_to_all | solution.py:573
  28.5 0.7 %sum.1 = (bf16[32,16,128]{2,1,0:T(8,128)(2,1)}, f32[4,128]{1,0:T(4,128)S(1)}) custom-call(bf16[32,5,4,128]{3,2,1,0:T(4,128)(2,1)S(1)} %all-to-all-done.parts_ref), custom_call_target="tpu_custom_call" | custom-call | flops 10000000000 | bytes 1000000 | tf_op jit(solution)/shard_map/sum/pallas_call | solution.py:467
  29.2 2.6 %all-to-all-start.1 = ((bf16[32,16,128]{2,1,0:T(8,128)(2,1)}), bf16[32,16,128]{2,1,0:T(8,128)(2,1)S(1)}, u32[]{:S(2)}, u32[]{:S(2)}) async-start(bf16[32,16,128]{2,1,0:T(8,128)(2,1)} %get-tuple-element.83), calls=%async_computation.1 | async-start | bytes 262144 | tf_op jit(solution)/shard_map/all_to_all | solution.py:616
  31.8 0.0 collective-permute-done.2.even_ref
  31.8 0.0 collective-permute-done.3.odd_ref
  31.8 2.5 %results.1 = (bf16[1536,128]{1,0:T(8,128)(2,1)}, bf16[1536,128]{1,0:T(8,128)(2,1)}, f32[1,128]{1,0:T(1,128)}, f32[1,128]{1,0:T(1,128)}, f32[1,128]{1,0:T(1,128)}) custom-call(bf16[2,128,128]{2,1,0:T(8,128)(2,1)S(1)} %collective-permute-done.2.even_ref, bf16[2,128,128]{2,1,0:T(8,128)(2,1)S(1)} %collective-permute-done.3.odd_ref, bf16[1536,128]{1,0:T(8,128)(2,1)} %cot_hbm.1, ...), custom_call_target="tpu_custom_call" | custom-call | flops 49999998976 | bytes 1000000 | tf_op jit(solution)/shard_map/results/pallas_call | solution.py:467
  34.3 5.9 %all-to-all-done.1 = bf16[32,16,128]{2,1,0:T(8,128)(2,1)S(1)} async-done(((bf16[32,16,128]{2,1,0:T(8,128)(2,1)}), bf16[32,16,128]{2,1,0:T(8,128)(2,1)S(1)}, u32[]{:S(2)}, u32[]{:S(2)}) %all-to-all-start.1) | async-done | bytes 131104 | tf_op jit(solution)/shard_map/all_to_all | solution.py:616
  40.2 0.7 %unpack.1 = (f32[128,128]{1,0:T(8,128)}, f32[256,128]{1,0:T(8,128)}, f32[128,128]{1,0:T(8,128)}) custom-call(bf16[512,128]{1,0:T(8,128)(2,1)S(1)} %bitcast.8), custom_call_target="tpu_custom_call" | custom-call | bytes 1000000 | tf_op jit(solution)/shard_map/unpack/pallas_call | solution.py:467
Async XLA Ops:
  0.6 6.5 %copy-start = (s32[12,4,128,128]{3,2,1,0:T(8,128)S(1)}, s32[12,4,128,128]{3,2,1,0:T(8,128)}, u32[]{:S(2)}) copy-start(s32[12,4,128,128]{3,2,1,0:T(8,128)} %counts_ref.1) | copy-start | bytes 9437188
  0.6 6.5 %copy-start.1 = (bf16[1536,128]{1,0:T(8,128)(2,1)S(1)}, bf16[1536,128]{1,0:T(8,128)(2,1)}, u32[]{:S(2)}) copy-start(bf16[1536,128]{1,0:T(8,128)(2,1)} %state_ref.1) | copy-start | bytes 1179652
  0.7 6.5 %copy-start.2 = (bf16[1536,128]{1,0:T(8,128)(2,1)S(1)}, bf16[1536,128]{1,0:T(8,128)(2,1)}, u32[]{:S(2)}) copy-start(bf16[1536,128]{1,0:T(8,128)(2,1)} %cot_hbm.1) | copy-start | bytes 1179652
  1.8 5.3 %collective-permute-start = (bf16[256,128]{1,0:T(8,128)(2,1)S(1)}, bf16[256,128]{1,0:T(8,128)(2,1)S(1)}, u32[]{:S(2)}, u32[]{:S(2)}) collective-permute-start(bf16[256,128]{1,0:T(8,128)(2,1)S(1)} %get-tuple-element.49), channel_id=1, source_target_pairs={{0,1},{2,3},{4,5},{6,7},{8,9},{10,11},{12,13},{14,15},{16,17},{18,... | collective-permute-start | bytes 196616 | tf_op jit(solution)/shard_map/ppermute | solution.py:461
  4.9 6.2 %collective-permute-start.1 = (bf16[256,128]{1,0:T(8,128)(2,1)S(1)}, bf16[256,128]{1,0:T(8,128)(2,1)S(1)}, u32[]{:S(2)}, u32[]{:S(2)}) collective-permute-start(bf16[256,128]{1,0:T(8,128)(2,1)S(1)} %get-tuple-element.58), channel_id=1, source_target_pairs={{1,2},{3,4},{5,6},{7,8},{9,10},{11,12},{13,14},{15,16},{17,18},{19... | collective-permute-start | bytes 196616 | tf_op jit(solution)/shard_map/ppermute | solution.py:461
  13.1 15.4 %all-to-all-start = ((bf16[32,5,4,128]{3,2,1,0:T(4,128)(2,1)}), bf16[32,5,4,128]{3,2,1,0:T(4,128)(2,1)S(1)}, u32[]{:S(2)}, u32[]{:S(2)}) async-start(bf16[32,5,4,128]{3,2,1,0:T(4,128)(2,1)} %get-tuple-element.79), calls=%async_computation | async-start | bytes 327680 | tf_op jit(solution)/shard_map/all_to_all | solution.py:573
  20.4 11.4 %collective-permute-start.2 = (bf16[2,128,128]{2,1,0:T(8,128)(2,1)S(1)}, bf16[2,128,128]{2,1,0:T(8,128)(2,1)S(1)}, u32[]{:S(2)}, u32[]{:S(2)}) collective-permute-start(bf16[2,128,128]{2,1,0:T(8,128)(2,1)S(1)} %get-tuple-element.73), channel_id=1, source_target_pairs={{0,1},{2,3},{4,5},{6,7},{8,9},{10,11},{12,13},{14,15},{16,17},{18,... | collective-permute-start | bytes 196616 | tf_op jit(solution)/shard_map/ppermute | solution.py:461
  22.2 9.6 %collective-permute-start.3 = (bf16[2,128,128]{2,1,0:T(8,128)(2,1)S(1)}, bf16[2,128,128]{2,1,0:T(8,128)(2,1)S(1)}, u32[]{:S(2)}, u32[]{:S(2)}) collective-permute-start(bf16[2,128,128]{2,1,0:T(8,128)(2,1)S(1)} %get-tuple-element.74), channel_id=1, source_target_pairs={{1,2},{3,4},{5,6},{7,8},{9,10},{11,12},{13,14},{15,16},{17,18},{19... | collective-permute-start | bytes 196616 | tf_op jit(solution)/shard_map/ppermute | solution.py:461
  29.2 11.0 %all-to-all-start.1 = ((bf16[32,16,128]{2,1,0:T(8,128)(2,1)}), bf16[32,16,128]{2,1,0:T(8,128)(2,1)S(1)}, u32[]{:S(2)}, u32[]{:S(2)}) async-start(bf16[32,16,128]{2,1,0:T(8,128)(2,1)} %get-tuple-element.83), calls=%async_computation.1 | async-start | bytes 262144 | tf_op jit(solution)/shard_map/all_to_all | solution.py:616

commit v21 on v19

--- a/solution.py
+++ b/solution.py
@@ -12,6 +12,7 @@
 BAND = 2 * WIN + 1
 epsilon = 1e-05
 AXES = ("dom", "feat")
+PARTNERS = ("feat", "dom")
 BF16, F32 = jnp.bfloat16, jnp.float32
 SENT = BF16
 ONES = 128
@@ -556,7 +557,7 @@
         flops=300_000_000,
     )
 
-    parts = lax.all_to_all(grads, AXES, 0, 0, tiled=True)
+    parts = lax.all_to_all(grads, PARTNERS, 0, 0, tiled=True)
     owed, owed_ends, send_even, send_odd = call(
         owed_kernel,
         "owed",
@@ -599,7 +600,7 @@
         flops=50_000_000_000,
     )
 
-    whole = lax.all_to_all(spread, AXES, 0, 0, tiled=True)
+    whole = lax.all_to_all(spread, PARTNERS, 0, 0, tiled=True)
     g_msg, g_first, g_second = call(
         unpack_kernel,
         "unpack",

time: 41.3 us -> 40.7 us (0.985)
  waiting for transfers between devices: 13.1 us -> 12.5 us
    all_to_all x2, waiting for transfers between devices: 11.5 us -> 10.9 us  [the longest x1 5.74 us: shards(): whole = lax.all_to_all(spread, PARTNERS, 0, 0, tiled=True)]
  transfers between devices with their start and end apart: 6 -> 6, of which waited for: 3 -> 3; matrix products, arithmetic and copies ran while one was open for 0% -> 0% of each run, Pallas kernels for 19% -> 20%
where the time goes in v21:
time: 40.7 us; the launch traced here: 40.4 us
  starting transfers between devices  15.3 us (38%)
  waiting for transfers between devices  12.5 us (31%)
  Pallas kernels  11.8 us (29%)
  between operations  0.75 us (2%)
    pallas_call x7, Pallas kernels, call(): pl.pallas_call(kernel, out_shape=tuple(outs), in_specs=specs, out_specs=t...  11.8 us
    all_to_all x1, starting transfers between devices, shards(): parts = lax.all_to_all(grads, PARTNERS, 0, 0, tiled=True)  6.46 us
    ppermute x4, starting transfers between devices, swapped(): lax.ppermute(block, AXES, [(i, i + 1) for i in lower] + [(i + 1, i) for i...  6.23 us
    all_to_all x1, waiting for transfers between devices, shards(): whole = lax.all_to_all(spread, PARTNERS, 0, 0, tiled=True)  5.74 us
    all_to_all x1, waiting for transfers between devices, shards(): parts = lax.all_to_all(grads, PARTNERS, 0, 0, tiled=True)  5.2 us
    all_to_all x1, starting transfers between devices, shards(): whole = lax.all_to_all(spread, PARTNERS, 0, 0, tiled=True)  2.58 us
    ppermute x4, waiting for transfers between devices, swapped(): lax.ppermute(block, AXES, [(i, i + 1) for i in lower] + [(i + 1, i) for i...  1.59 us
  transfers between devices with their start and end apart: 6, of which 3 were waited for; matrix products, arithmetic and copies ran while one was open for 0% of the time, Pallas kernels for 20%

profile of v21, /device:TPU:0, one launch (start us, length us, event | category | flops | bytes accessed | tf_op | source)
XLA Modules:
  0.0 40.4 jit_solution(12349461331580745257)
XLA Ops:
  0.6 0.0 copy-start
  0.6 0.0 copy-start.1
  0.7 0.0 copy-start.2
  0.7 1.2 %fetch.1 = (bf16[128,128]{1,0:T(8,128)(2,1)S(1)}, bf16[256,128]{1,0:T(8,128)(2,1)S(1)}, bf16[128,128]{1,0:T(8,128)(2,1)S(1)}, f32[1,128]{1,0:T(1,128)S(1)}, f32[...) custom-call(bf16[1536,128]{1,0:T(8,128)(2,1)} %state_ref.1, ...), custom_call_target="tpu_custom_call" | custom-call | flops 49999998976 | bytes 1000000 | tf_op jit(solution)/shard_map/fetch/pallas_call | solution.py:455
  1.8 3.1 %collective-permute-start = (bf16[256,128]{1,0:T(8,128)(2,1)S(1)}, bf16[256,128]{1,0:T(8,128)(2,1)S(1)}, u32[]{:S(2)}, u32[]{:S(2)}) collective-permute-start(bf16[256,128]{1,0:T(8,128)(2,1)S(1)} %get-tuple-element.48), channel_id=1, source_target_pairs={{0,1},{2,3},{4,5},{6,7},{8,9},{10,11},{12,13},{14,15},{16,17},{18,... | collective-permute-start | bytes 196616 | tf_op jit(solution)/shard_map/ppermute | solution.py:449
  4.9 0.7 %collective-permute-start.1 = (bf16[256,128]{1,0:T(8,128)(2,1)S(1)}, bf16[256,128]{1,0:T(8,128)(2,1)S(1)}, u32[]{:S(2)}, u32[]{:S(2)}) collective-permute-start(bf16[256,128]{1,0:T(8,128)(2,1)S(1)} %get-tuple-element.57), channel_id=1, source_target_pairs={{1,2},{3,4},{5,6},{7,8},{9,10},{11,12},{13,14},{15,16},{17,18},{19... | collective-permute-start | bytes 196616 | tf_op jit(solution)/shard_map/ppermute | solution.py:449
  5.6 1.6 %collective-permute-done.got_even_ref = bf16[256,128]{1,0:T(8,128)(2,1)S(1)} collective-permute-done((bf16[256,128]{1,0:T(8,128)(2,1)S(1)}, bf16[256,128]{1,0:T(8,128)(2,1)S(1)}, u32[]{:S(2)}, u32[]{:S(2)}) %collective-permute-start) | collective-permute-done | bytes 65568 | tf_op jit(solution)/shard_map/ppermute | solution.py:449
  7.2 0.0 copy-done
  7.2 0.0 copy-done.1
  7.2 0.0 copy-done.2
  7.2 3.9 %inner_rows.1 = (bf16[128,256]{1,0:T(8,128)(2,1)S(1)}, bf16[128,128]{1,0:T(8,128)(2,1)S(1)}, f32[3,128,128]{2,1,0:T(8,128)S(1)}, bf16[256,128]{1,0:T(8,128)(2,1)...) custom-call(s32[4,12]{1,0:T(4,128)} %bitcast.9, ...), custom_call_target="tpu_custom_call" | custom-call | flops 700000000 | bytes 1000000 | tf_op jit(solution)/shard_map/inner_rows/pallas_call | solution.py:455
  11.1 0.0 collective-permute-done.1.got_odd_ref
  11.1 2.0 %outer_rows.1 = (bf16[32,5,4,128]{3,2,1,0:T(4,128)(2,1)}, bf16[128,256]{1,0:T(8,128)(2,1)S(1)}, bf16[128,256]{1,0:T(8,128)(2,1)S(1)}) custom-call(bf16[256,128]{1,0:T(8,128)(2,1)S(1)} %collective-permute-done.1.got_odd_ref, bf16[128,128]{1,0:T(8,128)(2,1)S(1)} %get-tuple-element.49.w_msg_ref, bf16[256,128]{1,0:T(8,128)(2,1)S(1)} %get-tuple-element.50.w_first_ref, ...), custom_call_target="tpu_custom_call" | custom-call | flops 300000000 | bytes 1000000 | tf_op jit(solution)/shard_map/outer_rows/pallas_call | solution.py:455
  13.1 6.5 %all-to-all-start = ((bf16[32,5,4,128]{3,2,1,0:T(4,128)(2,1)}), bf16[32,5,4,128]{3,2,1,0:T(4,128)(2,1)S(1)}, u32[]{:S(2)}, u32[]{:S(2)}) async-start(bf16[32,5,4,128]{3,2,1,0:T(4,128)(2,1)} %get-tuple-element.77), calls=%async_computation | async-start | bytes 327680 | tf_op jit(solution)/shard_map/all_to_all | solution.py:560
  19.6 0.9 %owed.1 = (bf16[8,128,128]{2,1,0:T(8,128)(2,1)S(1)}, f32[4,128,128]{2,1,0:T(8,128)S(1)}, bf16[2,128,128]{2,1,0:T(8,128)(2,1)S(1)}, bf16[2,128,128]{2,1,0:T(8,128)(2,1)S(1)}) custom-call(bf16[12,5,128,128]{3,2,1,0:T(8,128)(2,1)S(1)} %get-tuple-element.55.band_ref, bf16[256,128]{1,0:T(8,128)(2,1)S(1)} %get-tuple-element.50.w_first_ref, ...), custom_call_target="tpu_custom_call" | custom-call | flops 200000000 | bytes 1000000 | tf_op jit(solution)/shard_map/owed/pallas_call | solution.py:455
  20.4 1.8 %collective-permute-start.2 = (bf16[2,128,128]{2,1,0:T(8,128)(2,1)S(1)}, bf16[2,128,128]{2,1,0:T(8,128)(2,1)S(1)}, u32[]{:S(2)}, u32[]{:S(2)}) collective-permute-start(bf16[2,128,128]{2,1,0:T(8,128)(2,1)S(1)} %get-tuple-element.71), channel_id=1, source_target_pairs={{0,1},{2,3},{4,5},{6,7},{8,9},{10,11},{12,13},{14,15},{16,17},{18,... | collective-permute-start | bytes 196616 | tf_op jit(solution)/shard_map/ppermute | solution.py:449
  22.3 0.7 %collective-permute-start.3 = (bf16[2,128,128]{2,1,0:T(8,128)(2,1)S(1)}, bf16[2,128,128]{2,1,0:T(8,128)(2,1)S(1)}, u32[]{:S(2)}, u32[]{:S(2)}) collective-permute-start(bf16[2,128,128]{2,1,0:T(8,128)(2,1)S(1)} %get-tuple-element.72), channel_id=1, source_target_pairs={{1,2},{3,4},{5,6},{7,8},{9,10},{11,12},{13,14},{15,16},{17,18},{19... | collective-permute-start | bytes 196616 | tf_op jit(solution)/shard_map/ppermute | solution.py:449
  22.9 5.2 %all-to-all-done.parts_ref = bf16[32,5,4,128]{3,2,1,0:T(4,128)(2,1)S(1)} async-done(((bf16[32,5,4,128]{3,2,1,0:T(4,128)(2,1)}), bf16[32,5,4,128]{3,2,1,0:T(4,128)(2,1)S(1)}, u32[]{:S(2)}, u32[]{:S(2)}) %all-to-all-start) | async-done | bytes 163872 | tf_op jit(solution)/shard_map/all_to_all | solution.py:560
  28.1 0.7 %sum.1 = (bf16[32,16,128]{2,1,0:T(8,128)(2,1)}, f32[4,128]{1,0:T(4,128)S(1)}) custom-call(bf16[32,5,4,128]{3,2,1,0:T(4,128)(2,1)S(1)} %all-to-all-done.parts_ref), custom_call_target="tpu_custom_call" | custom-call | flops 10000000000 | bytes 1000000 | tf_op jit(solution)/shard_map/sum/pallas_call | solution.py:455
  28.8 2.6 %all-to-all-start.1 = ((bf16[32,16,128]{2,1,0:T(8,128)(2,1)}), bf16[32,16,128]{2,1,0:T(8,128)(2,1)S(1)}, u32[]{:S(2)}, u32[]{:S(2)}) async-start(bf16[32,16,128]{2,1,0:T(8,128)(2,1)} %get-tuple-element.81), calls=%async_computation.1 | async-start | bytes 262144 | tf_op jit(solution)/shard_map/all_to_all | solution.py:603
  31.4 0.0 collective-permute-done.2.even_ref
  31.4 0.0 collective-permute-done.3.odd_ref
  31.5 2.5 %results.1 = (bf16[1536,128]{1,0:T(8,128)(2,1)}, bf16[1536,128]{1,0:T(8,128)(2,1)}, f32[1,128]{1,0:T(1,128)}, f32[1,128]{1,0:T(1,128)}, f32[1,128]{1,0:T(1,128)}) custom-call(bf16[2,128,128]{2,1,0:T(8,128)(2,1)S(1)} %collective-permute-done.2.even_ref, bf16[2,128,128]{2,1,0:T(8,128)(2,1)S(1)} %collective-permute-done.3.odd_ref, bf16[1536,128]{1,0:T(8,128)(2,1)} %cot_hbm.1, ...), custom_call_target="tpu_custom_call" | custom-call | flops 49999998976 | bytes 1000000 | tf_op jit(solution)/shard_map/results/pallas_call | solution.py:455
  33.9 5.7 %all-to-all-done.1 = bf16[32,16,128]{2,1,0:T(8,128)(2,1)S(1)} async-done(((bf16[32,16,128]{2,1,0:T(8,128)(2,1)}), bf16[32,16,128]{2,1,0:T(8,128)(2,1)S(1)}, u32[]{:S(2)}, u32[]{:S(2)}) %all-to-all-start.1) | async-done | bytes 131104 | tf_op jit(solution)/shard_map/all_to_all | solution.py:603
  39.7 0.7 %unpack.1 = (f32[128,128]{1,0:T(8,128)}, f32[256,128]{1,0:T(8,128)}, f32[128,128]{1,0:T(8,128)}) custom-call(bf16[512,128]{1,0:T(8,128)(2,1)S(1)} %bitcast.8), custom_call_target="tpu_custom_call" | custom-call | bytes 1000000 | tf_op jit(solution)/shard_map/unpack/pallas_call | solution.py:455
Async XLA Ops:
  0.6 6.5 %copy-start = (s32[12,4,128,128]{3,2,1,0:T(8,128)S(1)}, s32[12,4,128,128]{3,2,1,0:T(8,128)}, u32[]{:S(2)}) copy-start(s32[12,4,128,128]{3,2,1,0:T(8,128)} %counts_ref.1) | copy-start | bytes 9437188
  0.6 6.5 %copy-start.1 = (bf16[1536,128]{1,0:T(8,128)(2,1)S(1)}, bf16[1536,128]{1,0:T(8,128)(2,1)}, u32[]{:S(2)}) copy-start(bf16[1536,128]{1,0:T(8,128)(2,1)} %state_ref.1) | copy-start | bytes 1179652
  0.7 6.5 %copy-start.2 = (bf16[1536,128]{1,0:T(8,128)(2,1)S(1)}, bf16[1536,128]{1,0:T(8,128)(2,1)}, u32[]{:S(2)}) copy-start(bf16[1536,128]{1,0:T(8,128)(2,1)} %cot_hbm.1) | copy-start | bytes 1179652
  1.8 5.3 %collective-permute-start = (bf16[256,128]{1,0:T(8,128)(2,1)S(1)}, bf16[256,128]{1,0:T(8,128)(2,1)S(1)}, u32[]{:S(2)}, u32[]{:S(2)}) collective-permute-start(bf16[256,128]{1,0:T(8,128)(2,1)S(1)} %get-tuple-element.48), channel_id=1, source_target_pairs={{0,1},{2,3},{4,5},{6,7},{8,9},{10,11},{12,13},{14,15},{16,17},{18,... | collective-permute-start | bytes 196616 | tf_op jit(solution)/shard_map/ppermute | solution.py:449
  4.9 6.1 %collective-permute-start.1 = (bf16[256,128]{1,0:T(8,128)(2,1)S(1)}, bf16[256,128]{1,0:T(8,128)(2,1)S(1)}, u32[]{:S(2)}, u32[]{:S(2)}) collective-permute-start(bf16[256,128]{1,0:T(8,128)(2,1)S(1)} %get-tuple-element.57), channel_id=1, source_target_pairs={{1,2},{3,4},{5,6},{7,8},{9,10},{11,12},{13,14},{15,16},{17,18},{19... | collective-permute-start | bytes 196616 | tf_op jit(solution)/shard_map/ppermute | solution.py:449
  13.1 15.1 %all-to-all-start = ((bf16[32,5,4,128]{3,2,1,0:T(4,128)(2,1)}), bf16[32,5,4,128]{3,2,1,0:T(4,128)(2,1)S(1)}, u32[]{:S(2)}, u32[]{:S(2)}) async-start(bf16[32,5,4,128]{3,2,1,0:T(4,128)(2,1)} %get-tuple-element.77), calls=%async_computation | async-start | bytes 327680 | tf_op jit(solution)/shard_map/all_to_all | solution.py:560
  20.4 11.0 %collective-permute-start.2 = (bf16[2,128,128]{2,1,0:T(8,128)(2,1)S(1)}, bf16[2,128,128]{2,1,0:T(8,128)(2,1)S(1)}, u32[]{:S(2)}, u32[]{:S(2)}) collective-permute-start(bf16[2,128,128]{2,1,0:T(8,128)(2,1)S(1)} %get-tuple-element.71), channel_id=1, source_target_pairs={{0,1},{2,3},{4,5},{6,7},{8,9},{10,11},{12,13},{14,15},{16,17},{18,... | collective-permute-start | bytes 196616 | tf_op jit(solution)/shard_map/ppermute | solution.py:449
  22.3 9.2 %collective-permute-start.3 = (bf16[2,128,128]{2,1,0:T(8,128)(2,1)S(1)}, bf16[2,128,128]{2,1,0:T(8,128)(2,1)S(1)}, u32[]{:S(2)}, u32[]{:S(2)}) collective-permute-start(bf16[2,128,128]{2,1,0:T(8,128)(2,1)S(1)} %get-tuple-element.72), channel_id=1, source_target_pairs={{1,2},{3,4},{5,6},{7,8},{9,10},{11,12},{13,14},{15,16},{17,18},{19... | collective-permute-start | bytes 196616 | tf_op jit(solution)/shard_map/ppermute | solution.py:449
  28.8 10.8 %all-to-all-start.1 = ((bf16[32,16,128]{2,1,0:T(8,128)(2,1)}), bf16[32,16,128]{2,1,0:T(8,128)(2,1)S(1)}, u32[]{:S(2)}, u32[]{:S(2)}) async-start(bf16[32,16,128]{2,1,0:T(8,128)(2,1)} %get-tuple-element.81), calls=%async_computation.1 | async-start | bytes 262144 | tf_op jit(solution)/shard_map/all_to_all | solution.py:603

commit v22 on v21

--- a/solution.py
+++ b/solution.py
@@ -11,8 +11,8 @@
 WIN = 2
 BAND = 2 * WIN + 1
 epsilon = 1e-05
-AXES = ("dom", "feat")
-PARTNERS = ("feat", "dom")
+AXES = ("dom_hi", "dom_lo", "feat")
+PARTNERS = ("feat", "dom_lo", "dom_hi")
 BF16, F32 = jnp.bfloat16, jnp.float32
 SENT = BF16
 ONES = 128
@@ -34,7 +34,9 @@
 
 
 def device_is_odd():
-    index = lax.axis_index("dom") * lax.axis_size("feat") + lax.axis_index("feat")
+    index = 0
+    for axis in AXES:
+        index = index * lax.axis_size(axis) + lax.axis_index(axis)
     return index % 2 == 1
 
 
@@ -625,6 +627,9 @@
 
 
 def solution(mesh):
+    dom, feat = mesh.devices.shape
+    low = 2 - dom % 2
+    mesh = jax.sharding.Mesh(mesh.devices.reshape(dom // low, low, feat), AXES)
     split = P(AXES, None)
     return jax.shard_map(
         shards,

time: 40.7 us -> 41.3 us (1.015)
  waiting for transfers between devices: 12.5 us -> 13.1 us
    all_to_all x1, waiting for transfers between devices: 5.2 us -> 5.63 us  [shards(): parts = lax.all_to_all(grads, PARTNERS, 0, 0, tiled=True)]
where the time goes in v22:
time: 41.3 us; the launch traced here: 41 us
  starting transfers between devices  15.1 us (37%)
  waiting for transfers between devices  13.1 us (32%)
  Pallas kernels  12 us (29%)
  between operations  0.75 us (2%)
    pallas_call x7, Pallas kernels, call(): pl.pallas_call(kernel, out_shape=tuple(outs), in_specs=specs, out_specs=t...  12 us
    all_to_all x1, starting transfers between devices, shards(): parts = lax.all_to_all(grads, PARTNERS, 0, 0, tiled=True)  6.29 us
    ppermute x4, starting transfers between devices, swapped(): lax.ppermute(block, AXES, [(i, i + 1) for i in lower] + [(i + 1, i) for i...  6.23 us
    all_to_all x1, waiting for transfers between devices, shards(): whole = lax.all_to_all(spread, PARTNERS, 0, 0, tiled=True)  5.92 us
    all_to_all x1, waiting for transfers between devices, shards(): parts = lax.all_to_all(grads, PARTNERS, 0, 0, tiled=True)  5.63 us
    all_to_all x1, starting transfers between devices, shards(): whole = lax.all_to_all(spread, PARTNERS, 0, 0, tiled=True)  2.58 us
    ppermute x4, waiting for transfers between devices, swapped(): lax.ppermute(block, AXES, [(i, i + 1) for i in lower] + [(i + 1, i) for i...  1.59 us
  transfers between devices with their start and end apart: 6, of which 3 were waited for; matrix products, arithmetic and copies ran while one was open for 0% of the time, Pallas kernels for 20%

profile of v22, /device:TPU:0, one launch (start us, length us, event | category | flops | bytes accessed | tf_op | source)
XLA Modules:
  0.0 41.0 jit_solution(10666016298162385435)
XLA Ops:
  0.6 0.0 copy-start
  0.6 0.0 copy-start.1
  0.7 0.0 copy-start.2
  0.7 1.2 %fetch.1 = (bf16[128,128]{1,0:T(8,128)(2,1)S(1)}, bf16[256,128]{1,0:T(8,128)(2,1)S(1)}, bf16[128,128]{1,0:T(8,128)(2,1)S(1)}, f32[1,128]{1,0:T(1,128)S(1)}, f32[...) custom-call(bf16[1536,128]{1,0:T(8,128)(2,1)} %state_ref.1, ...), custom_call_target="tpu_custom_call" | custom-call | flops 49999998976 | bytes 1000000 | tf_op jit(solution)/shard_map/fetch/pallas_call | solution.py:457
  1.8 3.1 %collective-permute-start = (bf16[256,128]{1,0:T(8,128)(2,1)S(1)}, bf16[256,128]{1,0:T(8,128)(2,1)S(1)}, u32[]{:S(2)}, u32[]{:S(2)}) collective-permute-start(bf16[256,128]{1,0:T(8,128)(2,1)S(1)} %get-tuple-element.48), channel_id=1, source_target_pairs={{0,1},{2,3},{4,5},{6,7},{8,9},{10,11},{12,13},{14,15},{16,17},{18,... | collective-permute-start | bytes 196616 | tf_op jit(solution)/shard_map/ppermute | solution.py:451
  4.9 0.7 %collective-permute-start.1 = (bf16[256,128]{1,0:T(8,128)(2,1)S(1)}, bf16[256,128]{1,0:T(8,128)(2,1)S(1)}, u32[]{:S(2)}, u32[]{:S(2)}) collective-permute-start(bf16[256,128]{1,0:T(8,128)(2,1)S(1)} %get-tuple-element.57), channel_id=1, source_target_pairs={{1,2},{3,4},{5,6},{7,8},{9,10},{11,12},{13,14},{15,16},{17,18},{19... | collective-permute-start | bytes 196616 | tf_op jit(solution)/shard_map/ppermute | solution.py:451
  5.6 1.6 %collective-permute-done.got_even_ref = bf16[256,128]{1,0:T(8,128)(2,1)S(1)} collective-permute-done((bf16[256,128]{1,0:T(8,128)(2,1)S(1)}, bf16[256,128]{1,0:T(8,128)(2,1)S(1)}, u32[]{:S(2)}, u32[]{:S(2)}) %collective-permute-start) | collective-permute-done | bytes 65568 | tf_op jit(solution)/shard_map/ppermute | solution.py:451
  7.2 0.0 copy-done
  7.2 0.0 copy-done.1
  7.2 0.0 copy-done.2
  7.2 4.1 %inner_rows.1 = (bf16[128,256]{1,0:T(8,128)(2,1)S(1)}, bf16[128,128]{1,0:T(8,128)(2,1)S(1)}, f32[3,128,128]{2,1,0:T(8,128)S(1)}, bf16[256,128]{1,0:T(8,128)(2,1)...) custom-call(s32[4,12]{1,0:T(4,128)} %bitcast.9, ...), custom_call_target="tpu_custom_call" | custom-call | flops 700000000 | bytes 1000000 | tf_op jit(solution)/shard_map/inner_rows/pallas_call | solution.py:457
  11.2 0.0 collective-permute-done.1.got_odd_ref
  11.3 2.0 %outer_rows.1 = (bf16[32,5,4,128]{3,2,1,0:T(4,128)(2,1)}, bf16[128,256]{1,0:T(8,128)(2,1)S(1)}, bf16[128,256]{1,0:T(8,128)(2,1)S(1)}) custom-call(bf16[256,128]{1,0:T(8,128)(2,1)S(1)} %collective-permute-done.1.got_odd_ref, bf16[128,128]{1,0:T(8,128)(2,1)S(1)} %get-tuple-element.49.w_msg_ref, bf16[256,128]{1,0:T(8,128)(2,1)S(1)} %get-tuple-element.50.w_first_ref, ...), custom_call_target="tpu_custom_call" | custom-call | flops 300000000 | bytes 1000000 | tf_op jit(solution)/shard_map/outer_rows/pallas_call | solution.py:457
  13.3 6.3 %all-to-all-start = ((bf16[32,5,4,128]{3,2,1,0:T(4,128)(2,1)}), bf16[32,5,4,128]{3,2,1,0:T(4,128)(2,1)S(1)}, u32[]{:S(2)}, u32[]{:S(2)}) async-start(bf16[32,5,4,128]{3,2,1,0:T(4,128)(2,1)} %get-tuple-element.77), calls=%async_computation | async-start | bytes 327680 | tf_op jit(solution)/shard_map/all_to_all | solution.py:562
  19.6 0.9 %owed.1 = (bf16[8,128,128]{2,1,0:T(8,128)(2,1)S(1)}, f32[4,128,128]{2,1,0:T(8,128)S(1)}, bf16[2,128,128]{2,1,0:T(8,128)(2,1)S(1)}, bf16[2,128,128]{2,1,0:T(8,128)(2,1)S(1)}) custom-call(bf16[12,5,128,128]{3,2,1,0:T(8,128)(2,1)S(1)} %get-tuple-element.55.band_ref, bf16[256,128]{1,0:T(8,128)(2,1)S(1)} %get-tuple-element.50.w_first_ref, ...), custom_call_target="tpu_custom_call" | custom-call | flops 200000000 | bytes 1000000 | tf_op jit(solution)/shard_map/owed/pallas_call | solution.py:457
  20.5 1.8 %collective-permute-start.2 = (bf16[2,128,128]{2,1,0:T(8,128)(2,1)S(1)}, bf16[2,128,128]{2,1,0:T(8,128)(2,1)S(1)}, u32[]{:S(2)}, u32[]{:S(2)}) collective-permute-start(bf16[2,128,128]{2,1,0:T(8,128)(2,1)S(1)} %get-tuple-element.71), channel_id=1, source_target_pairs={{0,1},{2,3},{4,5},{6,7},{8,9},{10,11},{12,13},{14,15},{16,17},{18,... | collective-permute-start | bytes 196616 | tf_op jit(solution)/shard_map/ppermute | solution.py:451
  22.3 0.7 %collective-permute-start.3 = (bf16[2,128,128]{2,1,0:T(8,128)(2,1)S(1)}, bf16[2,128,128]{2,1,0:T(8,128)(2,1)S(1)}, u32[]{:S(2)}, u32[]{:S(2)}) collective-permute-start(bf16[2,128,128]{2,1,0:T(8,128)(2,1)S(1)} %get-tuple-element.72), channel_id=1, source_target_pairs={{1,2},{3,4},{5,6},{7,8},{9,10},{11,12},{13,14},{15,16},{17,18},{19... | collective-permute-start | bytes 196616 | tf_op jit(solution)/shard_map/ppermute | solution.py:451
  23.0 5.6 %all-to-all-done.parts_ref = bf16[32,5,4,128]{3,2,1,0:T(4,128)(2,1)S(1)} async-done(((bf16[32,5,4,128]{3,2,1,0:T(4,128)(2,1)}), bf16[32,5,4,128]{3,2,1,0:T(4,128)(2,1)S(1)}, u32[]{:S(2)}, u32[]{:S(2)}) %all-to-all-start) | async-done | bytes 163872 | tf_op jit(solution)/shard_map/all_to_all | solution.py:562
  28.6 0.7 %sum.1 = (bf16[32,16,128]{2,1,0:T(8,128)(2,1)}, f32[4,128]{1,0:T(4,128)S(1)}) custom-call(bf16[32,5,4,128]{3,2,1,0:T(4,128)(2,1)S(1)} %all-to-all-done.parts_ref), custom_call_target="tpu_custom_call" | custom-call | flops 10000000000 | bytes 1000000 | tf_op jit(solution)/shard_map/sum/pallas_call | solution.py:457
  29.3 2.6 %all-to-all-start.1 = ((bf16[32,16,128]{2,1,0:T(8,128)(2,1)}), bf16[32,16,128]{2,1,0:T(8,128)(2,1)S(1)}, u32[]{:S(2)}, u32[]{:S(2)}) async-start(bf16[32,16,128]{2,1,0:T(8,128)(2,1)} %get-tuple-element.81), calls=%async_computation.1 | async-start | bytes 262144 | tf_op jit(solution)/shard_map/all_to_all | solution.py:605
  31.9 0.0 collective-permute-done.2.even_ref
  31.9 0.0 collective-permute-done.3.odd_ref
  31.9 2.5 %results.1 = (bf16[1536,128]{1,0:T(8,128)(2,1)}, bf16[1536,128]{1,0:T(8,128)(2,1)}, f32[1,128]{1,0:T(1,128)}, f32[1,128]{1,0:T(1,128)}, f32[1,128]{1,0:T(1,128)}) custom-call(bf16[2,128,128]{2,1,0:T(8,128)(2,1)S(1)} %collective-permute-done.2.even_ref, bf16[2,128,128]{2,1,0:T(8,128)(2,1)S(1)} %collective-permute-done.3.odd_ref, bf16[1536,128]{1,0:T(8,128)(2,1)} %cot_hbm.1, ...), custom_call_target="tpu_custom_call" | custom-call | flops 49999998976 | bytes 1000000 | tf_op jit(solution)/shard_map/results/pallas_call | solution.py:457
  34.4 5.9 %all-to-all-done.1 = bf16[32,16,128]{2,1,0:T(8,128)(2,1)S(1)} async-done(((bf16[32,16,128]{2,1,0:T(8,128)(2,1)}), bf16[32,16,128]{2,1,0:T(8,128)(2,1)S(1)}, u32[]{:S(2)}, u32[]{:S(2)}) %all-to-all-start.1) | async-done | bytes 131104 | tf_op jit(solution)/shard_map/all_to_all | solution.py:605
  40.3 0.7 %unpack.1 = (f32[128,128]{1,0:T(8,128)}, f32[256,128]{1,0:T(8,128)}, f32[128,128]{1,0:T(8,128)}) custom-call(bf16[512,128]{1,0:T(8,128)(2,1)S(1)} %bitcast.8), custom_call_target="tpu_custom_call" | custom-call | bytes 1000000 | tf_op jit(solution)/shard_map/unpack/pallas_call | solution.py:457
Async XLA Ops:
  0.6 6.5 %copy-start = (s32[12,4,128,128]{3,2,1,0:T(8,128)S(1)}, s32[12,4,128,128]{3,2,1,0:T(8,128)}, u32[]{:S(2)}) copy-start(s32[12,4,128,128]{3,2,1,0:T(8,128)} %counts_ref.1) | copy-start | bytes 9437188
  0.6 6.5 %copy-start.1 = (bf16[1536,128]{1,0:T(8,128)(2,1)S(1)}, bf16[1536,128]{1,0:T(8,128)(2,1)}, u32[]{:S(2)}) copy-start(bf16[1536,128]{1,0:T(8,128)(2,1)} %state_ref.1) | copy-start | bytes 1179652
  0.7 6.5 %copy-start.2 = (bf16[1536,128]{1,0:T(8,128)(2,1)S(1)}, bf16[1536,128]{1,0:T(8,128)(2,1)}, u32[]{:S(2)}) copy-start(bf16[1536,128]{1,0:T(8,128)(2,1)} %cot_hbm.1) | copy-start | bytes 1179652
  1.8 5.3 %collective-permute-start = (bf16[256,128]{1,0:T(8,128)(2,1)S(1)}, bf16[256,128]{1,0:T(8,128)(2,1)S(1)}, u32[]{:S(2)}, u32[]{:S(2)}) collective-permute-start(bf16[256,128]{1,0:T(8,128)(2,1)S(1)} %get-tuple-element.48), channel_id=1, source_target_pairs={{0,1},{2,3},{4,5},{6,7},{8,9},{10,11},{12,13},{14,15},{16,17},{18,... | collective-permute-start | bytes 196616 | tf_op jit(solution)/shard_map/ppermute | solution.py:451
  4.9 6.3 %collective-permute-start.1 = (bf16[256,128]{1,0:T(8,128)(2,1)S(1)}, bf16[256,128]{1,0:T(8,128)(2,1)S(1)}, u32[]{:S(2)}, u32[]{:S(2)}) collective-permute-start(bf16[256,128]{1,0:T(8,128)(2,1)S(1)} %get-tuple-element.57), channel_id=1, source_target_pairs={{1,2},{3,4},{5,6},{7,8},{9,10},{11,12},{13,14},{15,16},{17,18},{19... | collective-permute-start | bytes 196616 | tf_op jit(solution)/shard_map/ppermute | solution.py:451
  13.3 15.3 %all-to-all-start = ((bf16[32,5,4,128]{3,2,1,0:T(4,128)(2,1)}), bf16[32,5,4,128]{3,2,1,0:T(4,128)(2,1)S(1)}, u32[]{:S(2)}, u32[]{:S(2)}) async-start(bf16[32,5,4,128]{3,2,1,0:T(4,128)(2,1)} %get-tuple-element.77), calls=%async_computation | async-start | bytes 327680 | tf_op jit(solution)/shard_map/all_to_all | solution.py:562
  20.5 11.4 %collective-permute-start.2 = (bf16[2,128,128]{2,1,0:T(8,128)(2,1)S(1)}, bf16[2,128,128]{2,1,0:T(8,128)(2,1)S(1)}, u32[]{:S(2)}, u32[]{:S(2)}) collective-permute-start(bf16[2,128,128]{2,1,0:T(8,128)(2,1)S(1)} %get-tuple-element.71), channel_id=1, source_target_pairs={{0,1},{2,3},{4,5},{6,7},{8,9},{10,11},{12,13},{14,15},{16,17},{18,... | collective-permute-start | bytes 196616 | tf_op jit(solution)/shard_map/ppermute | solution.py:451
  22.3 9.6 %collective-permute-start.3 = (bf16[2,128,128]{2,1,0:T(8,128)(2,1)S(1)}, bf16[2,128,128]{2,1,0:T(8,128)(2,1)S(1)}, u32[]{:S(2)}, u32[]{:S(2)}) collective-permute-start(bf16[2,128,128]{2,1,0:T(8,128)(2,1)S(1)} %get-tuple-element.72), channel_id=1, source_target_pairs={{1,2},{3,4},{5,6},{7,8},{9,10},{11,12},{13,14},{15,16},{17,18},{19... | collective-permute-start | bytes 196616 | tf_op jit(solution)/shard_map/ppermute | solution.py:451
  29.3 11.0 %all-to-all-start.1 = ((bf16[32,16,128]{2,1,0:T(8,128)(2,1)}), bf16[32,16,128]{2,1,0:T(8,128)(2,1)S(1)}, u32[]{:S(2)}, u32[]{:S(2)}) async-start(bf16[32,16,128]{2,1,0:T(8,128)(2,1)} %get-tuple-element.81), calls=%async_computation.1 | async-start | bytes 262144 | tf_op jit(solution)/shard_map/all_to_all | solution.py:605

commit v23 on v21

--- a/solution.py
+++ b/solution.py
@@ -365,8 +365,8 @@
 
 
 def result_kernel(
+    odd_ref,
     even_ref,
-    odd_ref,
     cot_hbm,
     w_msg_ref,
     w_first_ref,
@@ -589,7 +589,7 @@
             result((1, features), F32),
             result((1, features), F32),
         ),
-        [(owed_even, vmem), (owed_odd, vmem), (cotangent, hbm)]
+        [(owed_odd, vmem), (owed_even, vmem), (cotangent, hbm)]
         + [(w_msg_here, vmem), (w_first_here, vmem), (inner_updated, hbm)]
         + [(array, vmem) for array in (outer_updated, inner_d_hidden, outer_d_hidden, owed, owed_ends, bias)],
         scratch=(

time: 40.7 us -> 40.7 us (level)
  starting transfers between devices: 15.3 us -> 18 us
  waiting for transfers between devices: 12.5 us -> 9.8 us
    all_to_all x1, waiting for transfers between devices: 5.2 us -> 2.47 us  [shards(): parts = lax.all_to_all(grads, PARTNERS, 0, 0, tiled=True)]
    ppermute x4, starting transfers between devices: 6.23 us -> 8.95 us  [swapped(): lax.ppermute(block, AXES, [(i, i + 1) for i in lower] + [(i + 1, i) for i...]
where the time goes in v23:
time: 40.7 us; the launch traced here: 40.4 us
  starting transfers between devices  18 us (44%)
  Pallas kernels  11.8 us (29%)
  waiting for transfers between devices  9.8 us (24%)
  between operations  0.75 us (2%)
    pallas_call x7, Pallas kernels, call(): pl.pallas_call(kernel, out_shape=tuple(outs), in_specs=specs, out_specs=t...  11.8 us
    ppermute x4, starting transfers between devices, swapped(): lax.ppermute(block, AXES, [(i, i + 1) for i in lower] + [(i + 1, i) for i...  8.95 us
    all_to_all x1, starting transfers between devices, shards(): parts = lax.all_to_all(grads, PARTNERS, 0, 0, tiled=True)  6.47 us
    all_to_all x1, waiting for transfers between devices, shards(): whole = lax.all_to_all(spread, PARTNERS, 0, 0, tiled=True)  5.74 us
    all_to_all x1, starting transfers between devices, shards(): whole = lax.all_to_all(spread, PARTNERS, 0, 0, tiled=True)  2.58 us
    all_to_all x1, waiting for transfers between devices, shards(): parts = lax.all_to_all(grads, PARTNERS, 0, 0, tiled=True)  2.47 us
    ppermute x4, waiting for transfers between devices, swapped(): lax.ppermute(block, AXES, [(i, i + 1) for i in lower] + [(i + 1, i) for i...  1.59 us
  transfers between devices with their start and end apart: 6, of which 3 were waited for; matrix products, arithmetic and copies ran while one was open for 0% of the time, Pallas kernels for 20%

profile of v23, /device:TPU:0, one launch (start us, length us, event | category | flops | bytes accessed | tf_op | source)
XLA Modules:
  0.0 40.4 jit_solution(1766971231330604869)
XLA Ops:
  0.6 0.0 copy-start
  0.6 0.0 copy-start.1
  0.7 0.0 copy-start.2
  0.7 1.2 %fetch.1 = (bf16[128,128]{1,0:T(8,128)(2,1)S(1)}, bf16[256,128]{1,0:T(8,128)(2,1)S(1)}, bf16[128,128]{1,0:T(8,128)(2,1)S(1)}, f32[1,128]{1,0:T(1,128)S(1)}, f32[...) custom-call(bf16[1536,128]{1,0:T(8,128)(2,1)} %state_ref.1, ...), custom_call_target="tpu_custom_call" | custom-call | flops 49999998976 | bytes 1000000 | tf_op jit(solution)/shard_map/fetch/pallas_call | solution.py:455
  1.8 3.1 %collective-permute-start = (bf16[256,128]{1,0:T(8,128)(2,1)S(1)}, bf16[256,128]{1,0:T(8,128)(2,1)S(1)}, u32[]{:S(2)}, u32[]{:S(2)}) collective-permute-start(bf16[256,128]{1,0:T(8,128)(2,1)S(1)} %get-tuple-element.48), channel_id=1, source_target_pairs={{0,1},{2,3},{4,5},{6,7},{8,9},{10,11},{12,13},{14,15},{16,17},{18,... | collective-permute-start | bytes 196616 | tf_op jit(solution)/shard_map/ppermute | solution.py:449
  4.9 0.7 %collective-permute-start.1 = (bf16[256,128]{1,0:T(8,128)(2,1)S(1)}, bf16[256,128]{1,0:T(8,128)(2,1)S(1)}, u32[]{:S(2)}, u32[]{:S(2)}) collective-permute-start(bf16[256,128]{1,0:T(8,128)(2,1)S(1)} %get-tuple-element.57), channel_id=1, source_target_pairs={{1,2},{3,4},{5,6},{7,8},{9,10},{11,12},{13,14},{15,16},{17,18},{19... | collective-permute-start | bytes 196616 | tf_op jit(solution)/shard_map/ppermute | solution.py:449
  5.6 1.6 %collective-permute-done.got_even_ref = bf16[256,128]{1,0:T(8,128)(2,1)S(1)} collective-permute-done((bf16[256,128]{1,0:T(8,128)(2,1)S(1)}, bf16[256,128]{1,0:T(8,128)(2,1)S(1)}, u32[]{:S(2)}, u32[]{:S(2)}) %collective-permute-start) | collective-permute-done | bytes 65568 | tf_op jit(solution)/shard_map/ppermute | solution.py:449
  7.2 0.0 copy-done
  7.2 0.0 copy-done.1
  7.2 0.0 copy-done.2
  7.2 3.9 %inner_rows.1 = (bf16[128,256]{1,0:T(8,128)(2,1)S(1)}, bf16[128,128]{1,0:T(8,128)(2,1)S(1)}, f32[3,128,128]{2,1,0:T(8,128)S(1)}, bf16[256,128]{1,0:T(8,128)(2,1)...) custom-call(s32[4,12]{1,0:T(4,128)} %bitcast.9, ...), custom_call_target="tpu_custom_call" | custom-call | flops 700000000 | bytes 1000000 | tf_op jit(solution)/shard_map/inner_rows/pallas_call | solution.py:455
  11.1 0.0 collective-permute-done.1.got_odd_ref
  11.1 2.0 %outer_rows.1 = (bf16[32,5,4,128]{3,2,1,0:T(4,128)(2,1)}, bf16[128,256]{1,0:T(8,128)(2,1)S(1)}, bf16[128,256]{1,0:T(8,128)(2,1)S(1)}) custom-call(bf16[256,128]{1,0:T(8,128)(2,1)S(1)} %collective-permute-done.1.got_odd_ref, bf16[128,128]{1,0:T(8,128)(2,1)S(1)} %get-tuple-element.49.w_msg_ref, bf16[256,128]{1,0:T(8,128)(2,1)S(1)} %get-tuple-element.50.w_first_ref, ...), custom_call_target="tpu_custom_call" | custom-call | flops 300000000 | bytes 1000000 | tf_op jit(solution)/shard_map/outer_rows/pallas_call | solution.py:455
  13.1 6.5 %all-to-all-start = ((bf16[32,5,4,128]{3,2,1,0:T(4,128)(2,1)}), bf16[32,5,4,128]{3,2,1,0:T(4,128)(2,1)S(1)}, u32[]{:S(2)}, u32[]{:S(2)}) async-start(bf16[32,5,4,128]{3,2,1,0:T(4,128)(2,1)} %get-tuple-element.77), calls=%async_computation | async-start | bytes 327680 | tf_op jit(solution)/shard_map/all_to_all | solution.py:560
  19.6 0.9 %owed.1 = (bf16[8,128,128]{2,1,0:T(8,128)(2,1)S(1)}, f32[4,128,128]{2,1,0:T(8,128)S(1)}, bf16[2,128,128]{2,1,0:T(8,128)(2,1)S(1)}, bf16[2,128,128]{2,1,0:T(8,128)(2,1)S(1)}) custom-call(bf16[12,5,128,128]{3,2,1,0:T(8,128)(2,1)S(1)} %get-tuple-element.55.band_ref, bf16[256,128]{1,0:T(8,128)(2,1)S(1)} %get-tuple-element.50.w_first_ref, ...), custom_call_target="tpu_custom_call" | custom-call | flops 200000000 | bytes 1000000 | tf_op jit(solution)/shard_map/owed/pallas_call | solution.py:455
  20.4 0.7 %collective-permute-start.2 = (bf16[2,128,128]{2,1,0:T(8,128)(2,1)S(1)}, bf16[2,128,128]{2,1,0:T(8,128)(2,1)S(1)}, u32[]{:S(2)}, u32[]{:S(2)}) collective-permute-start(bf16[2,128,128]{2,1,0:T(8,128)(2,1)S(1)} %get-tuple-element.71), channel_id=1, source_target_pairs={{1,2},{3,4},{5,6},{7,8},{9,10},{11,12},{13,14},{15,16},{17,18},{19... | collective-permute-start | bytes 196616 | tf_op jit(solution)/shard_map/ppermute | solution.py:449
  21.1 4.5 %collective-permute-start.3 = (bf16[2,128,128]{2,1,0:T(8,128)(2,1)S(1)}, bf16[2,128,128]{2,1,0:T(8,128)(2,1)S(1)}, u32[]{:S(2)}, u32[]{:S(2)}) collective-permute-start(bf16[2,128,128]{2,1,0:T(8,128)(2,1)S(1)} %get-tuple-element.72), channel_id=1, source_target_pairs={{0,1},{2,3},{4,5},{6,7},{8,9},{10,11},{12,13},{14,15},{16,17},{18,... | collective-permute-start | bytes 196616 | tf_op jit(solution)/shard_map/ppermute | solution.py:449
  25.7 2.5 %all-to-all-done.parts_ref = bf16[32,5,4,128]{3,2,1,0:T(4,128)(2,1)S(1)} async-done(((bf16[32,5,4,128]{3,2,1,0:T(4,128)(2,1)}), bf16[32,5,4,128]{3,2,1,0:T(4,128)(2,1)S(1)}, u32[]{:S(2)}, u32[]{:S(2)}) %all-to-all-start) | async-done | bytes 163872 | tf_op jit(solution)/shard_map/all_to_all | solution.py:560
  28.1 0.7 %sum.1 = (bf16[32,16,128]{2,1,0:T(8,128)(2,1)}, f32[4,128]{1,0:T(4,128)S(1)}) custom-call(bf16[32,5,4,128]{3,2,1,0:T(4,128)(2,1)S(1)} %all-to-all-done.parts_ref), custom_call_target="tpu_custom_call" | custom-call | flops 10000000000 | bytes 1000000 | tf_op jit(solution)/shard_map/sum/pallas_call | solution.py:455
  28.8 2.6 %all-to-all-start.1 = ((bf16[32,16,128]{2,1,0:T(8,128)(2,1)}), bf16[32,16,128]{2,1,0:T(8,128)(2,1)S(1)}, u32[]{:S(2)}, u32[]{:S(2)}) async-start(bf16[32,16,128]{2,1,0:T(8,128)(2,1)} %get-tuple-element.81), calls=%async_computation.1 | async-start | bytes 262144 | tf_op jit(solution)/shard_map/all_to_all | solution.py:603
  31.4 0.0 collective-permute-done.2.odd_ref
  31.4 0.0 collective-permute-done.3.even_ref
  31.4 2.5 %results.1 = (bf16[1536,128]{1,0:T(8,128)(2,1)}, bf16[1536,128]{1,0:T(8,128)(2,1)}, f32[1,128]{1,0:T(1,128)}, f32[1,128]{1,0:T(1,128)}, f32[1,128]{1,0:T(1,128)}) custom-call(bf16[2,128,128]{2,1,0:T(8,128)(2,1)S(1)} %collective-permute-done.2.odd_ref, bf16[2,128,128]{2,1,0:T(8,128)(2,1)S(1)} %collective-permute-done.3.even_ref, bf16[1536,128]{1,0:T(8,128)(2,1)} %cot_hbm.1, ...), custom_call_target="tpu_custom_call" | custom-call | flops 49999998976 | bytes 1000000 | tf_op jit(solution)/shard_map/results/pallas_call | solution.py:455
  33.9 5.7 %all-to-all-done.1 = bf16[32,16,128]{2,1,0:T(8,128)(2,1)S(1)} async-done(((bf16[32,16,128]{2,1,0:T(8,128)(2,1)}), bf16[32,16,128]{2,1,0:T(8,128)(2,1)S(1)}, u32[]{:S(2)}, u32[]{:S(2)}) %all-to-all-start.1) | async-done | bytes 131104 | tf_op jit(solution)/shard_map/all_to_all | solution.py:603
  39.7 0.7 %unpack.1 = (f32[128,128]{1,0:T(8,128)}, f32[256,128]{1,0:T(8,128)}, f32[128,128]{1,0:T(8,128)}) custom-call(bf16[512,128]{1,0:T(8,128)(2,1)S(1)} %bitcast.8), custom_call_target="tpu_custom_call" | custom-call | bytes 1000000 | tf_op jit(solution)/shard_map/unpack/pallas_call | solution.py:455
Async XLA Ops:
  0.6 6.5 %copy-start = (s32[12,4,128,128]{3,2,1,0:T(8,128)S(1)}, s32[12,4,128,128]{3,2,1,0:T(8,128)}, u32[]{:S(2)}) copy-start(s32[12,4,128,128]{3,2,1,0:T(8,128)} %counts_ref.1) | copy-start | bytes 9437188
  0.6 6.5 %copy-start.1 = (bf16[1536,128]{1,0:T(8,128)(2,1)S(1)}, bf16[1536,128]{1,0:T(8,128)(2,1)}, u32[]{:S(2)}) copy-start(bf16[1536,128]{1,0:T(8,128)(2,1)} %state_ref.1) | copy-start | bytes 1179652
  0.7 6.5 %copy-start.2 = (bf16[1536,128]{1,0:T(8,128)(2,1)S(1)}, bf16[1536,128]{1,0:T(8,128)(2,1)}, u32[]{:S(2)}) copy-start(bf16[1536,128]{1,0:T(8,128)(2,1)} %cot_hbm.1) | copy-start | bytes 1179652
  1.8 5.3 %collective-permute-start = (bf16[256,128]{1,0:T(8,128)(2,1)S(1)}, bf16[256,128]{1,0:T(8,128)(2,1)S(1)}, u32[]{:S(2)}, u32[]{:S(2)}) collective-permute-start(bf16[256,128]{1,0:T(8,128)(2,1)S(1)} %get-tuple-element.48), channel_id=1, source_target_pairs={{0,1},{2,3},{4,5},{6,7},{8,9},{10,11},{12,13},{14,15},{16,17},{18,... | collective-permute-start | bytes 196616 | tf_op jit(solution)/shard_map/ppermute | solution.py:449
  4.9 6.1 %collective-permute-start.1 = (bf16[256,128]{1,0:T(8,128)(2,1)S(1)}, bf16[256,128]{1,0:T(8,128)(2,1)S(1)}, u32[]{:S(2)}, u32[]{:S(2)}) collective-permute-start(bf16[256,128]{1,0:T(8,128)(2,1)S(1)} %get-tuple-element.57), channel_id=1, source_target_pairs={{1,2},{3,4},{5,6},{7,8},{9,10},{11,12},{13,14},{15,16},{17,18},{19... | collective-permute-start | bytes 196616 | tf_op jit(solution)/shard_map/ppermute | solution.py:449
  13.1 15.1 %all-to-all-start = ((bf16[32,5,4,128]{3,2,1,0:T(4,128)(2,1)}), bf16[32,5,4,128]{3,2,1,0:T(4,128)(2,1)S(1)}, u32[]{:S(2)}, u32[]{:S(2)}) async-start(bf16[32,5,4,128]{3,2,1,0:T(4,128)(2,1)} %get-tuple-element.77), calls=%async_computation | async-start | bytes 327680 | tf_op jit(solution)/shard_map/all_to_all | solution.py:560
  20.4 11.0 %collective-permute-start.2 = (bf16[2,128,128]{2,1,0:T(8,128)(2,1)S(1)}, bf16[2,128,128]{2,1,0:T(8,128)(2,1)S(1)}, u32[]{:S(2)}, u32[]{:S(2)}) collective-permute-start(bf16[2,128,128]{2,1,0:T(8,128)(2,1)S(1)} %get-tuple-element.71), channel_id=1, source_target_pairs={{1,2},{3,4},{5,6},{7,8},{9,10},{11,12},{13,14},{15,16},{17,18},{19... | collective-permute-start | bytes 196616 | tf_op jit(solution)/shard_map/ppermute | solution.py:449
  21.1 10.3 %collective-permute-start.3 = (bf16[2,128,128]{2,1,0:T(8,128)(2,1)S(1)}, bf16[2,128,128]{2,1,0:T(8,128)(2,1)S(1)}, u32[]{:S(2)}, u32[]{:S(2)}) collective-permute-start(bf16[2,128,128]{2,1,0:T(8,128)(2,1)S(1)} %get-tuple-element.72), channel_id=1, source_target_pairs={{0,1},{2,3},{4,5},{6,7},{8,9},{10,11},{12,13},{14,15},{16,17},{18,... | collective-permute-start | bytes 196616 | tf_op jit(solution)/shard_map/ppermute | solution.py:449
  28.8 10.8 %all-to-all-start.1 = ((bf16[32,16,128]{2,1,0:T(8,128)(2,1)}), bf16[32,16,128]{2,1,0:T(8,128)(2,1)S(1)}, u32[]{:S(2)}, u32[]{:S(2)}) async-start(bf16[32,16,128]{2,1,0:T(8,128)(2,1)} %get-tuple-element.81), calls=%async_computation.1 | async-start | bytes 262144 | tf_op jit(solution)/shard_map/all_to_all | solution.py:603

commit v24 on v23

--- a/solution.py
+++ b/solution.py
@@ -435,12 +435,16 @@
         ref[...] = bias_ref[pl.ds(k, 1), :]
 
 
-def unpack_kernel(rows_ref, msg_ref, first_ref, second_ref):
-    place = 0
-    for ref in (first_ref, second_ref, msg_ref):
-        count = ref.shape[0]
-        ref[...] = rows_ref[pl.ds(place, count), :].astype(F32)
-        place += count
+def unpack_kernel(rows_ref, msg_hbm, first_hbm, second_hbm, wide_ref, left):
+    place, copies = 0, []
+    for k, target in enumerate((first_hbm, second_hbm, msg_hbm)):
+        here = pl.ds(place, target.shape[0])
+        wide_ref[here, :] = rows_ref[here, :].astype(F32)
+        copies.append(pltpu.make_async_copy(wide_ref.at[here], target, left.at[k]))
+        copies[-1].start()
+        place += target.shape[0]
+    for copy in copies:
+        copy.wait()
 
 
 def swapped(block, parity):
@@ -605,11 +609,12 @@
         unpack_kernel,
         "unpack",
         (
-            result((features, features), F32),
-            result((2 * features, features), F32),
-            result((features, features), F32),
+            hbm((features, features), F32),
+            hbm((2 * features, features), F32),
+            hbm((features, features), F32),
         ),
         [(whole.reshape(devices * chunk, features), vmem)],
+        scratch=(vmem((4 * features, features), F32), pltpu.SemaphoreType.DMA((3,))),
     )
     flat = lambda vector: vector.reshape(features)
     return (

time: 40.7 us -> 40.7 us (level)
  no operation moved by 1% of the time
where the time goes in v24:
time: 40.7 us; the launch traced here: 40.4 us
  starting transfers between devices  18 us (44%)
  Pallas kernels  11.8 us (29%)
  waiting for transfers between devices  9.8 us (24%)
  between operations  0.75 us (2%)
    pallas_call x7, Pallas kernels, call(): pl.pallas_call(kernel, out_shape=tuple(outs), in_specs=specs, out_specs=t...  11.8 us
    ppermute x4, starting transfers between devices, swapped(): lax.ppermute(block, AXES, [(i, i + 1) for i in lower] + [(i + 1, i) for i...  8.95 us
    all_to_all x1, starting transfers between devices, shards(): parts = lax.all_to_all(grads, PARTNERS, 0, 0, tiled=True)  6.46 us
    all_to_all x1, waiting for transfers between devices, shards(): whole = lax.all_to_all(spread, PARTNERS, 0, 0, tiled=True)  5.74 us
    all_to_all x1, starting transfers between devices, shards(): whole = lax.all_to_all(spread, PARTNERS, 0, 0, tiled=True)  2.58 us
    all_to_all x1, waiting for transfers between devices, shards(): parts = lax.all_to_all(grads, PARTNERS, 0, 0, tiled=True)  2.47 us
    ppermute x4, waiting for transfers between devices, swapped(): lax.ppermute(block, AXES, [(i, i + 1) for i in lower] + [(i + 1, i) for i...  1.59 us
  transfers between devices with their start and end apart: 6, of which 3 were waited for; matrix products, arithmetic and copies ran while one was open for 0% of the time, Pallas kernels for 20%

profile of v24, /device:TPU:0, one launch (start us, length us, event | category | flops | bytes accessed | tf_op | source)
XLA Modules:
  0.0 40.4 jit_solution(16879756242460450214)
XLA Ops:
  0.6 0.0 copy-start
  0.6 0.0 copy-start.1
  0.7 0.0 copy-start.2
  0.7 1.2 %fetch.1 = (bf16[128,128]{1,0:T(8,128)(2,1)S(1)}, bf16[256,128]{1,0:T(8,128)(2,1)S(1)}, bf16[128,128]{1,0:T(8,128)(2,1)S(1)}, f32[1,128]{1,0:T(1,128)S(1)}, f32[...) custom-call(bf16[1536,128]{1,0:T(8,128)(2,1)} %state_ref.1, ...), custom_call_target="tpu_custom_call" | custom-call | flops 49999998976 | bytes 1000000 | tf_op jit(solution)/shard_map/fetch/pallas_call | solution.py:459
  1.8 3.1 %collective-permute-start = (bf16[256,128]{1,0:T(8,128)(2,1)S(1)}, bf16[256,128]{1,0:T(8,128)(2,1)S(1)}, u32[]{:S(2)}, u32[]{:S(2)}) collective-permute-start(bf16[256,128]{1,0:T(8,128)(2,1)S(1)} %get-tuple-element.48), channel_id=1, source_target_pairs={{0,1},{2,3},{4,5},{6,7},{8,9},{10,11},{12,13},{14,15},{16,17},{18,... | collective-permute-start | bytes 196616 | tf_op jit(solution)/shard_map/ppermute | solution.py:453
  4.9 0.7 %collective-permute-start.1 = (bf16[256,128]{1,0:T(8,128)(2,1)S(1)}, bf16[256,128]{1,0:T(8,128)(2,1)S(1)}, u32[]{:S(2)}, u32[]{:S(2)}) collective-permute-start(bf16[256,128]{1,0:T(8,128)(2,1)S(1)} %get-tuple-element.57), channel_id=1, source_target_pairs={{1,2},{3,4},{5,6},{7,8},{9,10},{11,12},{13,14},{15,16},{17,18},{19... | collective-permute-start | bytes 196616 | tf_op jit(solution)/shard_map/ppermute | solution.py:453
  5.6 1.6 %collective-permute-done.got_even_ref = bf16[256,128]{1,0:T(8,128)(2,1)S(1)} collective-permute-done((bf16[256,128]{1,0:T(8,128)(2,1)S(1)}, bf16[256,128]{1,0:T(8,128)(2,1)S(1)}, u32[]{:S(2)}, u32[]{:S(2)}) %collective-permute-start) | collective-permute-done | bytes 65568 | tf_op jit(solution)/shard_map/ppermute | solution.py:453
  7.2 0.0 copy-done
  7.2 0.0 copy-done.1
  7.2 0.0 copy-done.2
  7.2 3.9 %inner_rows.1 = (bf16[128,256]{1,0:T(8,128)(2,1)S(1)}, bf16[128,128]{1,0:T(8,128)(2,1)S(1)}, f32[3,128,128]{2,1,0:T(8,128)S(1)}, bf16[256,128]{1,0:T(8,128)(2,1)...) custom-call(s32[4,12]{1,0:T(4,128)} %bitcast.9, ...), custom_call_target="tpu_custom_call" | custom-call | flops 700000000 | bytes 1000000 | tf_op jit(solution)/shard_map/inner_rows/pallas_call | solution.py:459
  11.1 0.0 collective-permute-done.1.got_odd_ref
  11.1 2.0 %outer_rows.1 = (bf16[32,5,4,128]{3,2,1,0:T(4,128)(2,1)}, bf16[128,256]{1,0:T(8,128)(2,1)S(1)}, bf16[128,256]{1,0:T(8,128)(2,1)S(1)}) custom-call(bf16[256,128]{1,0:T(8,128)(2,1)S(1)} %collective-permute-done.1.got_odd_ref, bf16[128,128]{1,0:T(8,128)(2,1)S(1)} %get-tuple-element.49.w_msg_ref, bf16[256,128]{1,0:T(8,128)(2,1)S(1)} %get-tuple-element.50.w_first_ref, ...), custom_call_target="tpu_custom_call" | custom-call | flops 300000000 | bytes 1000000 | tf_op jit(solution)/shard_map/outer_rows/pallas_call | solution.py:459
  13.1 6.5 %all-to-all-start = ((bf16[32,5,4,128]{3,2,1,0:T(4,128)(2,1)}), bf16[32,5,4,128]{3,2,1,0:T(4,128)(2,1)S(1)}, u32[]{:S(2)}, u32[]{:S(2)}) async-start(bf16[32,5,4,128]{3,2,1,0:T(4,128)(2,1)} %get-tuple-element.77), calls=%async_computation | async-start | bytes 327680 | tf_op jit(solution)/shard_map/all_to_all | solution.py:564
  19.6 0.9 %owed.1 = (bf16[8,128,128]{2,1,0:T(8,128)(2,1)S(1)}, f32[4,128,128]{2,1,0:T(8,128)S(1)}, bf16[2,128,128]{2,1,0:T(8,128)(2,1)S(1)}, bf16[2,128,128]{2,1,0:T(8,128)(2,1)S(1)}) custom-call(bf16[12,5,128,128]{3,2,1,0:T(8,128)(2,1)S(1)} %get-tuple-element.55.band_ref, bf16[256,128]{1,0:T(8,128)(2,1)S(1)} %get-tuple-element.50.w_first_ref, ...), custom_call_target="tpu_custom_call" | custom-call | flops 200000000 | bytes 1000000 | tf_op jit(solution)/shard_map/owed/pallas_call | solution.py:459
  20.4 0.7 %collective-permute-start.2 = (bf16[2,128,128]{2,1,0:T(8,128)(2,1)S(1)}, bf16[2,128,128]{2,1,0:T(8,128)(2,1)S(1)}, u32[]{:S(2)}, u32[]{:S(2)}) collective-permute-start(bf16[2,128,128]{2,1,0:T(8,128)(2,1)S(1)} %get-tuple-element.71), channel_id=1, source_target_pairs={{1,2},{3,4},{5,6},{7,8},{9,10},{11,12},{13,14},{15,16},{17,18},{19... | collective-permute-start | bytes 196616 | tf_op jit(solution)/shard_map/ppermute | solution.py:453
  21.1 4.5 %collective-permute-start.3 = (bf16[2,128,128]{2,1,0:T(8,128)(2,1)S(1)}, bf16[2,128,128]{2,1,0:T(8,128)(2,1)S(1)}, u32[]{:S(2)}, u32[]{:S(2)}) collective-permute-start(bf16[2,128,128]{2,1,0:T(8,128)(2,1)S(1)} %get-tuple-element.72), channel_id=1, source_target_pairs={{0,1},{2,3},{4,5},{6,7},{8,9},{10,11},{12,13},{14,15},{16,17},{18,... | collective-permute-start | bytes 196616 | tf_op jit(solution)/shard_map/ppermute | solution.py:453
  25.7 2.5 %all-to-all-done.parts_ref = bf16[32,5,4,128]{3,2,1,0:T(4,128)(2,1)S(1)} async-done(((bf16[32,5,4,128]{3,2,1,0:T(4,128)(2,1)}), bf16[32,5,4,128]{3,2,1,0:T(4,128)(2,1)S(1)}, u32[]{:S(2)}, u32[]{:S(2)}) %all-to-all-start) | async-done | bytes 163872 | tf_op jit(solution)/shard_map/all_to_all | solution.py:564
  28.1 0.7 %sum.1 = (bf16[32,16,128]{2,1,0:T(8,128)(2,1)}, f32[4,128]{1,0:T(4,128)S(1)}) custom-call(bf16[32,5,4,128]{3,2,1,0:T(4,128)(2,1)S(1)} %all-to-all-done.parts_ref), custom_call_target="tpu_custom_call" | custom-call | flops 10000000000 | bytes 1000000 | tf_op jit(solution)/shard_map/sum/pallas_call | solution.py:459
  28.8 2.6 %all-to-all-start.1 = ((bf16[32,16,128]{2,1,0:T(8,128)(2,1)}), bf16[32,16,128]{2,1,0:T(8,128)(2,1)S(1)}, u32[]{:S(2)}, u32[]{:S(2)}) async-start(bf16[32,16,128]{2,1,0:T(8,128)(2,1)} %get-tuple-element.81), calls=%async_computation.1 | async-start | bytes 262144 | tf_op jit(solution)/shard_map/all_to_all | solution.py:607
  31.4 0.0 collective-permute-done.2.odd_ref
  31.4 0.0 collective-permute-done.3.even_ref
  31.4 2.5 %results.1 = (bf16[1536,128]{1,0:T(8,128)(2,1)}, bf16[1536,128]{1,0:T(8,128)(2,1)}, f32[1,128]{1,0:T(1,128)}, f32[1,128]{1,0:T(1,128)}, f32[1,128]{1,0:T(1,128)}) custom-call(bf16[2,128,128]{2,1,0:T(8,128)(2,1)S(1)} %collective-permute-done.2.odd_ref, bf16[2,128,128]{2,1,0:T(8,128)(2,1)S(1)} %collective-permute-done.3.even_ref, bf16[1536,128]{1,0:T(8,128)(2,1)} %cot_hbm.1, ...), custom_call_target="tpu_custom_call" | custom-call | flops 49999998976 | bytes 1000000 | tf_op jit(solution)/shard_map/results/pallas_call | solution.py:459
  33.9 5.7 %all-to-all-done.1 = bf16[32,16,128]{2,1,0:T(8,128)(2,1)S(1)} async-done(((bf16[32,16,128]{2,1,0:T(8,128)(2,1)}), bf16[32,16,128]{2,1,0:T(8,128)(2,1)S(1)}, u32[]{:S(2)}, u32[]{:S(2)}) %all-to-all-start.1) | async-done | bytes 131104 | tf_op jit(solution)/shard_map/all_to_all | solution.py:607
  39.7 0.7 %unpack.1 = (f32[128,128]{1,0:T(8,128)}, f32[256,128]{1,0:T(8,128)}, f32[128,128]{1,0:T(8,128)}) custom-call(bf16[512,128]{1,0:T(8,128)(2,1)S(1)} %bitcast.8), custom_call_target="tpu_custom_call" | custom-call | bytes 1000000 | tf_op jit(solution)/shard_map/unpack/pallas_call | solution.py:459
Async XLA Ops:
  0.6 6.5 %copy-start = (s32[12,4,128,128]{3,2,1,0:T(8,128)S(1)}, s32[12,4,128,128]{3,2,1,0:T(8,128)}, u32[]{:S(2)}) copy-start(s32[12,4,128,128]{3,2,1,0:T(8,128)} %counts_ref.1) | copy-start | bytes 9437188
  0.6 6.5 %copy-start.1 = (bf16[1536,128]{1,0:T(8,128)(2,1)S(1)}, bf16[1536,128]{1,0:T(8,128)(2,1)}, u32[]{:S(2)}) copy-start(bf16[1536,128]{1,0:T(8,128)(2,1)} %state_ref.1) | copy-start | bytes 1179652
  0.7 6.5 %copy-start.2 = (bf16[1536,128]{1,0:T(8,128)(2,1)S(1)}, bf16[1536,128]{1,0:T(8,128)(2,1)}, u32[]{:S(2)}) copy-start(bf16[1536,128]{1,0:T(8,128)(2,1)} %cot_hbm.1) | copy-start | bytes 1179652
  1.8 5.3 %collective-permute-start = (bf16[256,128]{1,0:T(8,128)(2,1)S(1)}, bf16[256,128]{1,0:T(8,128)(2,1)S(1)}, u32[]{:S(2)}, u32[]{:S(2)}) collective-permute-start(bf16[256,128]{1,0:T(8,128)(2,1)S(1)} %get-tuple-element.48), channel_id=1, source_target_pairs={{0,1},{2,3},{4,5},{6,7},{8,9},{10,11},{12,13},{14,15},{16,17},{18,... | collective-permute-start | bytes 196616 | tf_op jit(solution)/shard_map/ppermute | solution.py:453
  4.9 6.1 %collective-permute-start.1 = (bf16[256,128]{1,0:T(8,128)(2,1)S(1)}, bf16[256,128]{1,0:T(8,128)(2,1)S(1)}, u32[]{:S(2)}, u32[]{:S(2)}) collective-permute-start(bf16[256,128]{1,0:T(8,128)(2,1)S(1)} %get-tuple-element.57), channel_id=1, source_target_pairs={{1,2},{3,4},{5,6},{7,8},{9,10},{11,12},{13,14},{15,16},{17,18},{19... | collective-permute-start | bytes 196616 | tf_op jit(solution)/shard_map/ppermute | solution.py:453
  13.1 15.0 %all-to-all-start = ((bf16[32,5,4,128]{3,2,1,0:T(4,128)(2,1)}), bf16[32,5,4,128]{3,2,1,0:T(4,128)(2,1)S(1)}, u32[]{:S(2)}, u32[]{:S(2)}) async-start(bf16[32,5,4,128]{3,2,1,0:T(4,128)(2,1)} %get-tuple-element.77), calls=%async_computation | async-start | bytes 327680 | tf_op jit(solution)/shard_map/all_to_all | solution.py:564
  20.4 11.0 %collective-permute-start.2 = (bf16[2,128,128]{2,1,0:T(8,128)(2,1)S(1)}, bf16[2,128,128]{2,1,0:T(8,128)(2,1)S(1)}, u32[]{:S(2)}, u32[]{:S(2)}) collective-permute-start(bf16[2,128,128]{2,1,0:T(8,128)(2,1)S(1)} %get-tuple-element.71), channel_id=1, source_target_pairs={{1,2},{3,4},{5,6},{7,8},{9,10},{11,12},{13,14},{15,16},{17,18},{19... | collective-permute-start | bytes 196616 | tf_op jit(solution)/shard_map/ppermute | solution.py:453
  21.1 10.3 %collective-permute-start.3 = (bf16[2,128,128]{2,1,0:T(8,128)(2,1)S(1)}, bf16[2,128,128]{2,1,0:T(8,128)(2,1)S(1)}, u32[]{:S(2)}, u32[]{:S(2)}) collective-permute-start(bf16[2,128,128]{2,1,0:T(8,128)(2,1)S(1)} %get-tuple-element.72), channel_id=1, source_target_pairs={{0,1},{2,3},{4,5},{6,7},{8,9},{10,11},{12,13},{14,15},{16,17},{18,... | collective-permute-start | bytes 196616 | tf_op jit(solution)/shard_map/ppermute | solution.py:453
  28.8 10.8 %all-to-all-start.1 = ((bf16[32,16,128]{2,1,0:T(8,128)(2,1)}), bf16[32,16,128]{2,1,0:T(8,128)(2,1)S(1)}, u32[]{:S(2)}, u32[]{:S(2)}) async-start(bf16[32,16,128]{2,1,0:T(8,128)(2,1)} %get-tuple-element.81), calls=%async_computation.1 | async-start | bytes 262144 | tf_op jit(solution)/shard_map/all_to_all | solution.py:607
